TPU v7x, 512 devices: a whole 4x8x8 slice. The times are simulated.
512 devices in a mesh: vc: 16 (over z, x_hi), vd: 32 (over x_lo, y, core).
Axes of the slice: x: 4 (x_hi: 2, x_lo: 2; x = x_hi * 2 + x_lo), y: 8, z: 8, core: 2. Of those that a mesh axis runs over, the one named last changes fastest.
Arguments:
- vectors_left: float32 [8, 1024, 4096], P(None, 'vc', 'vd'), may hold values from -0.8 to 0.8
- vectors_right: float32 [16, 1024, 4096], P(None, 'vd', 'vc'), may hold values from -0.8 to 0.8
- amplitudes: float32 [1024, 1024, 128], P('vc', 'vd'), may hold values from -0.005859375 to 0.005859375
Outputs:
- ladder: float32 [128, 8, 16], P('vd', None, 'vc')
All inputs are finite; a program needn't handle non-finite values.
Results may differ from a plain program's by a relative error of at most 0.000094.
Values sent between devices are 32-bit elements; how exact they have to be, the bound alone decides.
No kernel may reach another device: no remote copies, remote signals or barrier semaphores. Data moves between devices by JAX's collectives and lax.ppermute only.
A program may use at most 64 MiB of HBM per device.

v0:
```python
import jax
import jax.numpy as jnp
from jax import lax
from jax.sharding import PartitionSpec as P


def contract(left_rows, right_rows):
    return lax.dot_general(
        left_rows,
        right_rows,
        (((1,), (1,)), ((), ())),
        precision=lax.Precision.HIGHEST,
        preferred_element_type=jnp.float32,
    )


def shards(vectors_left, vectors_right, amplitudes):
    count_a, count_c, left_q = vectors_left.shape
    count_b, count_d, right_q = vectors_right.shape
    left_whole = lax.all_gather(vectors_left, "vd", axis=2, tiled=True)
    left_flat = left_whole.reshape(count_a * count_c, left_whole.shape[2])
    piece = lax.all_gather(vectors_right, "vc", axis=2, tiled=True)
    width = piece.shape[2]
    tile = contract(left_flat, piece.reshape(count_b * count_d, width))
    tile = tile.reshape(count_a, count_c, count_b, count_d)
    partial_sum = jnp.einsum("acbd,cdi->iab", tile, amplitudes, precision=lax.Precision.HIGHEST)
    reduced = lax.psum_scatter(partial_sum, "vd", scatter_dimension=0, tiled=True)
    ladder = lax.psum_scatter(reduced, "vc", scatter_dimension=2, tiled=True)
    return ladder


def solution(mesh):
    return jax.shard_map(
        shards,
        mesh=mesh,
        in_specs=(P(None, "vc", "vd"), P(None, "vd", "vc"), P("vc", "vd", None)),
        out_specs=P("vd", None, "vc"),
        check_vma=False,
    )
```

profile of v0, /device:TPU:2, one launch (start us, length us, event | category | flops | bytes accessed | tf_op | source)
XLA Modules:
  0.0 498.5 jit_solution(13409341898188266008)
XLA Ops:
  6.5 0.0 all-gather.5.cloned.1.call-start
  6.5 0.7 all-gather.5.cloned.1.call-update
  7.3 0.0 all-gather.3.cloned.1.call-start
  7.3 0.7 all-gather.3.cloned.1.call-update
  8.0 0.0 reduce-scatter.2.cloned.1.call-start
  8.1 160.1 %all-gather.5.cloned.1.call-done = f32[16,32,4096]{2,1,0:T(8,128)} async-done(((f32[16,32,256]{2,1,0:T(8,128)}), f32[16,32,4096]{2,1,0:T(8,128)}) %all-gather.5.cloned.1.call-update) | async-done | bytes 8388624 | tf_op jit(solution)/shard_map/all_gather | solution.py:22
  168.2 90.7 %all-gather.3.cloned.1.call-done = f32[8,64,4096]{2,1,0:T(8,128)} async-done(((f32[8,64,128]{2,1,0:T(8,128)}), f32[8,64,4096]{2,1,0:T(8,128)}) %all-gather.3.cloned.1.call-update) | async-done | bytes 8388624 | tf_op jit(solution)/shard_map/all_gather | solution.py:20
  258.9 0.0 copy-start
  258.9 33.9 %fusion = f32[8,64,16,32]{1,2,3,0:T(8,128)S(1)} fusion(f32[8,64,4096]{2,1,0:T(8,128)} %all-gather.3.cloned.1.call-done, f32[16,32,4096,1]{2,1,0,3:T(8,128)} %bitcast.17), kind=kOutput, calls=%fused_computation | convolution fusion | flops 12884901888 | bytes 17825792 | tf_op jit(solution)/shard_map/dot_general | solution.py:8
  292.9 0.0 copy-done
  292.9 2.4 convolution_bitcast_fusion
  295.3 1.0 copy.7
  296.3 0.0 reduce-scatter.2.cloned.1.call-update
  296.3 1.3 dynamic-slice
  297.6 115.0 %reduce-scatter.2.cloned.1.call-done = f32[4,8,16]{2,1,0:T(8,128)} async-done(((f32[128,8,16]{2,1,0:T(8,128)}), f32[4,8,16]{2,1,0:T(8,128)}) %reduce-scatter.2.cloned.1.call-update) | async-done | bytes 2064 | tf_op jit(solution)/shard_map/reduce_scatter | solution.py:27
  412.6 0.8 copy.8
  413.4 77.3 %all-reduce = f32[4,8,16]{1,0,2:T(4,128)S(1)} all-reduce(f32[4,8,16]{1,0,2:T(4,128)S(1)} %copy.8), channel_id=3, replica_groups=mesh['vc'=16,'vd'=32] {'vc'}, use_global_device_ids=true, to_apply=%region_1.0.clone | all-reduce | flops 512 | bytes 4096
  490.7 1.3 constant_dynamic-slice_fusion
Async XLA Ops:
  6.5 161.7 %all-gather.5.cloned.1.call-start = ((), (), s32[]{:S(2)}) async-start(), calls=%async_computation.2 | async-start | bytes 8912896 | tf_op jit(solution)/shard_map/all_gather | solution.py:22
  7.3 251.7 %all-gather.3.cloned.1.call-start = ((), (), s32[]{:S(2)}) async-start(), calls=%async_computation.1 | async-start | bytes 8650752 | tf_op jit(solution)/shard_map/all_gather | solution.py:20
  8.0 404.6 %reduce-scatter.2.cloned.1.call-start = ((), (), s32[]{:S(2)}) async-start(), calls=%async_computation.3 | async-start | bytes 540672 | tf_op jit(solution)/shard_map/reduce_scatter | solution.py:27
  258.9 33.9 %copy-start = (f32[64,32,128]{2,1,0:T(8,128)S(1)}, f32[64,32,128]{2,1,0:T(8,128)}, u32[]{:S(2)}) copy-start(f32[64,32,128]{2,1,0:T(8,128)} %param.5) | copy-start | bytes 3145732
Sparse Core Ops, SparseCore 0:
  10.4 157.7 all-gather.4
  170.2 88.6 all-gather.2
  296.4 116.1 reduce-scatter.1
where the time goes:
time: 499 us
  waiting for transfers between devices  367 us (74%)
  blocking collectives  77.3 us (15%)
  matrix products  36.3 us (7%)
  between operations  13.1 us (3%)
    all_gather x1, waiting for transfers between devices, shards(): piece = lax.all_gather(vectors_right, 'vc', axis=2, tiled=True)  160 us
    reduce_scatter x1, waiting for transfers between devices, shards(): lax.psum_scatter(partial_sum, 'vd', scatter_dimension=0, tiled=True)  115 us
    all_gather x1, waiting for transfers between devices, shards(): left_whole = lax.all_gather(vectors_left, 'vd', axis=2, tiled=True)  90.7 us
    unnamed x1, blocking collectives  77.3 us
    dot_general x1, matrix products, contract(): lax.dot_general(left_rows, right_rows, (((1,), (1,)), ((), ())), precisio...  33.9 us
  transfers between devices with their start and end apart: 3, of which 3 were waited for; matrix products, arithmetic and copies ran while one was open for 0% of the time, Pallas kernels for 0%

commit v1 on v0

v1 whole, which is shorter than its diff:
```python
import jax
import jax.numpy as jnp
from jax import lax
from jax.experimental import pallas as pl
from jax.experimental.pallas import tpu as pltpu
from jax.sharding import Mesh, PartitionSpec as P

AXES = ("z", "xh", "xl", "y", "core")
SIZES = (8, 2, 2, 8, 2)


def linear(z, xh, xl, y, core):
    return (((z % 8) * 2 + xh) * 2 + xl) * 16 + (y % 8) * 2 + core


def table(target):
    pairs = []
    for z in range(8):
        for xh in range(2):
            for xl in range(2):
                for y in range(8):
                    for core in range(2):
                        pairs.append((linear(z, xh, xl, y, core), linear(*target(z, xh, xl, y, core))))
    return pairs


SAME_XL = table(lambda z, xh, xl, y, core: (z, y % 2, xl, y // 2 * 2 + xh, core))
OTHER_XL = table(lambda z, xh, xl, y, core: (z, y % 2, 1 - xl, y // 2 * 2 + xh, core))
RING_X = table(lambda z, xh, xl, y, core: (z, xh, xl, y + 1 - 2 * core, core))
RING_Y = table(lambda z, xh, xl, y, core: (z, xh, xl, y - 1 + 2 * core, core))
SWAP_CORE = table(lambda z, xh, xl, y, core: (z, xh, xl, y, 1 - core))
SWAP_XH = table(lambda z, xh, xl, y, core: (z, 1 - xh, xl, y, core))


def send(array, pairs):
    return lax.ppermute(array, AXES, pairs)


def split(value):
    high = value.astype(jnp.bfloat16)
    low = (value - high.astype(jnp.float32)).astype(jnp.bfloat16)
    return high, low


def dot_nt(a, b):
    return lax.dot_general(a, b, (((1,), (1,)), ((), ())), preferred_element_type=jnp.float32)


def dot_nn(a, b):
    return lax.dot_general(a, b, (((1,), (0,)), ((), ())), preferred_element_type=jnp.float32)


def ladder_kernel(place, r_own, r_oth, lo0, lo1, lx0, lx1, t_own, t_oth, out, acc):
    step = pl.program_id(0)
    left_own = jnp.concatenate([lo0[...].reshape(8, 64, 128), lo1[...].reshape(8, 64, 128)], axis=1).reshape(1024, 128)
    left_oth = jnp.concatenate([lx0[...].reshape(8, 64, 128), lx1[...].reshape(8, 64, 128)], axis=1).reshape(1024, 128)
    left = jnp.concatenate([left_own, left_oth], axis=1)
    right = jnp.concatenate([r_own[...].reshape(512, 128), r_oth[...].reshape(512, 128)], axis=1)
    left_high, left_low = split(left)
    right_high, right_low = split(right)
    product = dot_nt(
        jnp.concatenate([right_high, right_high, right_low], axis=1),
        jnp.concatenate([left_high, left_low, left_high], axis=1),
    )

    for a in range(8):
        part = product[:, a * 128 : a * 128 + 128]

        @pl.when(step == 0)
        def _():
            acc[a] = part

        @pl.when(step > 0)
        def _():
            acc[a] += part

    @pl.when(step == 7)
    def _():
        total = jnp.zeros((128, 128), jnp.float32)
        for d in range(0, 32, 2):
            highs, lows, t_highs, t_lows = [], [], [], []
            for one in (d, d + 1):
                rows = jnp.concatenate([acc[a, pl.ds(one, 16, 32), :] for a in range(8)], axis=0)
                high, low = split(rows)
                highs.append(high)
                lows.append(low)
                for ref in (t_own, t_oth):
                    high, low = split(ref[:, one, :])
                    t_highs.append(high)
                    t_lows.append(low)
            total += dot_nn(
                jnp.concatenate(highs + highs + lows, axis=1),
                jnp.concatenate(t_highs + t_lows + t_highs, axis=0),
            )
        out[...] = total


def contract(place, right, left_own, left_oth, t_own, t_oth):
    def slot(place, y_wanted, sign):
        return lax.bitwise_and((place[0] - y_wanted) * sign + 8, 7)

    def left_map(half, sign):
        def index(step, place):
            parity = place[3] if half == 0 else 1 - place[3]
            wanted = 2 * lax.rem(step, 4) + parity
            order = lax.bitwise_xor(step // 4, place[2])
            return slot(place, wanted, place[1] * sign), order, 0, 0, 0

        return index

    left_block = (1, 1, 8, 64, 128)
    right_block = (1, 16, 32, 128)
    return pl.pallas_call(
        ladder_kernel,
        out_shape=jax.ShapeDtypeStruct((128, 128), jnp.float32),
        grid_spec=pltpu.PrefetchScalarGridSpec(
            num_scalar_prefetch=1,
            grid=(8,),
            in_specs=[
                pl.BlockSpec(right_block, lambda step, place: (step, 0, 0, place[4])),
                pl.BlockSpec(right_block, lambda step, place: (step, 0, 0, 1 - place[4])),
                pl.BlockSpec(left_block, left_map(0, 1)),
                pl.BlockSpec(left_block, left_map(1, 1)),
                pl.BlockSpec(left_block, left_map(0, -1)),
                pl.BlockSpec(left_block, left_map(1, -1)),
                pl.BlockSpec((64, 32, 128), lambda step, place: (0, 0, 0)),
                pl.BlockSpec((64, 32, 128), lambda step, place: (0, 0, 0)),
            ],
            out_specs=pl.BlockSpec((128, 128), lambda step, place: (0, 0)),
            scratch_shapes=[pltpu.VMEM((8, 512, 128), jnp.float32)],
        ),
        compiler_params=pltpu.CompilerParams(vmem_limit_bytes=40 * 1024 * 1024),
        cost_estimate=pl.CostEstimate(flops=6 << 30, bytes_accessed=16 << 20, transcendentals=0),
        name="ladder",
    )(place, right, right, left_own, left_own, left_oth, left_oth, t_own, t_oth)


def shards(vectors_left, vectors_right, amplitudes):
    y, core = lax.axis_index("y"), lax.axis_index("core")
    place = jnp.stack([y, 1 - 2 * core, lax.axis_index("xl"), lax.axis_index("xh"), core]).astype(jnp.int32)
    right = lax.all_gather(vectors_right, "z", axis=0)
    own = jnp.stack([send(vectors_left, SAME_XL), send(vectors_left, OTHER_XL)])
    ahead, behind = [own], []
    for step in range(4):
        ahead.append(send(ahead[-1], RING_X))
        if step < 3:
            behind.append(send(behind[-1] if behind else own, RING_Y))
    left_own = jnp.stack(ahead + behind[::-1])
    left_oth = send(left_own, SWAP_CORE)
    t_oth = send(amplitudes, SWAP_XH)
    partial = contract(place, right, left_own, left_oth, amplitudes, t_oth)
    partial = partial.reshape(8, 8, 2, 2, 8, 2, 4).transpose(2, 3, 5, 1, 4, 6, 0).reshape(8, 16, 128)
    near = lax.all_to_all(partial, ("xh", "xl", "core"), 0, 0, tiled=True)
    near = jnp.sum(near, axis=0).reshape(64, 32)
    far = lax.all_to_all(near, ("z", "y"), 0, 0, tiled=True)
    return jnp.sum(far, axis=0).reshape(4, 8, 1)


def solution(mesh):
    fine = Mesh(mesh.devices.reshape(SIZES), AXES)
    c_axes, d_axes = ("z", "xh"), ("xl", "y", "core")
    return jax.shard_map(
        shards,
        mesh=fine,
        in_specs=(P(None, c_axes, d_axes), P(None, d_axes, c_axes), P(c_axes, d_axes, None)),
        out_specs=P(d_axes, None, c_axes),
        check_vma=False,
    )
```

time: 499 us -> 196 us (0.39)
  the two profiles are of different devices: /device:TPU:2 before, /device:TPU:1 now
where the time goes in v1:
time: 196 us
  waiting for transfers between devices  69.6 us (36%)
  starting transfers between devices  40.2 us (21%)
  blocking collectives  34.6 us (18%)
  Pallas kernels  19.9 us (10%)
  local copies, waits for them, and re-layouts  16.8 us (9%)
  between operations  13.5 us (7%)
    ppermute x11, waiting for transfers between devices, send(): return lax.ppermute(array, AXES, pairs)  69.6 us
    ppermute x11, starting transfers between devices, send(): return lax.ppermute(array, AXES, pairs)  40.2 us
    all_to_all x1, blocking collectives, shards(): far = lax.all_to_all(near, ('z', 'y'), 0, 0, tiled=True)  24.3 us
    pallas_call x1, Pallas kernels, contract(): pl.pallas_call(ladder_kernel, out_shape=jax.ShapeDtypeStruct((128, 128),...  19.9 us
    all_to_all x1, blocking collectives, shards(): near = lax.all_to_all(partial, ('xh', 'xl', 'core'), 0, 0, tiled=True)  10.3 us
    unnamed x10, local copies, waits for them, and re-layouts  7.27 us
    reshape x2, local copies, waits for them, and re-layouts, shards(): partial.reshape(8, 8, 2, 2, 8, 2, 4).transpose(2, 3, 5, 1, 4, 6, 0)  4.27 us
  transfers between devices with their start and end apart: 12, of which 7 were waited for; matrix products, arithmetic and copies ran while one was open for 4% of the time, Pallas kernels for 0%

profile of v1, /device:TPU:1, one launch (start us, length us, event | category | flops | bytes accessed | tf_op | source)
XLA Modules:
  0.0 195.6 jit_solution(866993049686296412)
XLA Ops:
  6.5 0.0 all-gather.3.cloned.1.call-start
  6.5 1.6 collective-permute-start
  8.1 3.9 %collective-permute-start.1 = (f32[8,64,128]{2,1,0:T(8,128)}, f32[8,64,128]{2,1,0:T(8,128)S(1)}, u32[]{:S(2)}, u32[]{:S(2)}) collective-permute-start(f32[8,64,128]{2,1,0:T(8,128)} %param.3), channel_id=1, source_target_pairs={{0,16},{1,17},{2,48},{3,49},{4,20},{5,21},{6,52},{7,53},{8,24},{9,... | collective-permute-start | bytes 786440 | tf_op jit(solution)/shard_map/ppermute | solution.py:36
  12.1 0.0 collective-permute-done
  12.1 11.0 %collective-permute-done.1 = f32[8,64,128]{2,1,0:T(8,128)S(1)} collective-permute-done((f32[8,64,128]{2,1,0:T(8,128)}, f32[8,64,128]{2,1,0:T(8,128)S(1)}, u32[]{:S(2)}, u32[]{:S(2)}) %collective-permute-start.1) | collective-permute-done | bytes 262176 | tf_op jit(solution)/shard_map/ppermute | solution.py:36
  23.2 7.4 %collective-permute-start.2 = (f32[2,8,64,128]{3,2,1,0:T(8,128)S(1)}, f32[2,8,64,128]{3,2,1,0:T(8,128)S(1)}, u32[]{:S(2)}, u32[]{:S(2)}) collective-permute-start(f32[2,8,64,128]{3,2,1,0:T(8,128)S(1)} %pad_maximum_fusion), channel_id=1, source_target_pairs={{0,2},{1,15},{2,4},{3,1},{4,6},{5,3},{6,8},{7,5},{8,10},{9,7},{10,... | collective-permute-start | bytes 1572872 | tf_op jit(solution)/shard_map/ppermute | solution.py:36
  30.6 0.0 all-gather.3.cloned.1.call-update
  30.6 0.0 copy-start.1
  30.6 6.1 %collective-permute-done.2 = f32[2,8,64,128]{3,2,1,0:T(8,128)S(1)} collective-permute-done((f32[2,8,64,128]{3,2,1,0:T(8,128)S(1)}, f32[2,8,64,128]{3,2,1,0:T(8,128)S(1)}, u32[]{:S(2)}, u32[]{:S(2)}) %collective-permute-start.2) | collective-permute-done | bytes 524320 | tf_op jit(solution)/shard_map/ppermute | solution.py:36
  36.7 5.0 %collective-permute-start.3 = (f32[2,8,64,128]{3,2,1,0:T(8,128)S(1)}, f32[2,8,64,128]{3,2,1,0:T(8,128)S(1)}, u32[]{:S(2)}, u32[]{:S(2)}) collective-permute-start(f32[2,8,64,128]{3,2,1,0:T(8,128)S(1)} %collective-permute-done.2), channel_id=1, source_target_pairs={{0,2},{1,15},{2,4},{3,1},{4,6},{5,3},{6,8},{7,5},{8,10},{9,7},{10,... | collective-permute-start | bytes 1572872 | tf_op jit(solution)/shard_map/ppermute | solution.py:36
  41.7 1.9 collective-permute-start.6
  43.6 4.7 %collective-permute-done.3 = f32[2,8,64,128]{3,2,1,0:T(8,128)S(1)} collective-permute-done((f32[2,8,64,128]{3,2,1,0:T(8,128)S(1)}, f32[2,8,64,128]{3,2,1,0:T(8,128)S(1)}, u32[]{:S(2)}, u32[]{:S(2)}) %collective-permute-start.3) | collective-permute-done | bytes 524320 | tf_op jit(solution)/shard_map/ppermute | solution.py:36
  48.3 5.3 %collective-permute-start.4 = (f32[2,8,64,128]{3,2,1,0:T(8,128)S(1)}, f32[2,8,64,128]{3,2,1,0:T(8,128)S(1)}, u32[]{:S(2)}, u32[]{:S(2)}) collective-permute-start(f32[2,8,64,128]{3,2,1,0:T(8,128)S(1)} %collective-permute-done.3), channel_id=1, source_target_pairs={{0,2},{1,15},{2,4},{3,1},{4,6},{5,3},{6,8},{7,5},{8,10},{9,7},{10,... | collective-permute-start | bytes 1572872 | tf_op jit(solution)/shard_map/ppermute | solution.py:36
  53.6 3.4 %collective-permute-done.6 = f32[2,8,64,128]{3,2,1,0:T(8,128)S(1)} collective-permute-done((f32[2,8,64,128]{3,2,1,0:T(8,128)S(1)}, f32[2,8,64,128]{3,2,1,0:T(8,128)S(1)}, u32[]{:S(2)}, u32[]{:S(2)}) %collective-permute-start.6) | collective-permute-done | bytes 524320 | tf_op jit(solution)/shard_map/ppermute | solution.py:36
  57.1 1.9 collective-permute-start.7
  59.0 0.9 bitcast_dynamic-update-slice_fusion.7
  59.9 0.0 collective-permute-done.4
  59.9 5.3 %collective-permute-start.5 = (f32[2,8,64,128]{3,2,1,0:T(8,128)S(1)}, f32[2,8,64,128]{3,2,1,0:T(8,128)S(1)}, u32[]{:S(2)}, u32[]{:S(2)}) collective-permute-start(f32[2,8,64,128]{3,2,1,0:T(8,128)S(1)} %collective-permute-done.4), channel_id=1, source_target_pairs={{0,2},{1,15},{2,4},{3,1},{4,6},{5,3},{6,8},{7,5},{8,10},{9,7},{10,... | collective-permute-start | bytes 1572872 | tf_op jit(solution)/shard_map/ppermute | solution.py:36
  65.2 0.9 bitcast_dynamic-update-slice_fusion.6
  66.0 7.1 %collective-permute-done.7 = f32[2,8,64,128]{3,2,1,0:T(8,128)S(1)} collective-permute-done((f32[2,8,64,128]{3,2,1,0:T(8,128)S(1)}, f32[2,8,64,128]{3,2,1,0:T(8,128)S(1)}, u32[]{:S(2)}, u32[]{:S(2)}) %collective-permute-start.7) | collective-permute-done | bytes 524320 | tf_op jit(solution)/shard_map/ppermute | solution.py:36
  73.1 1.9 collective-permute-start.8
  75.0 0.8 bitcast_dynamic-update-slice_fusion.5
  75.9 0.8 bitcast_dynamic-update-slice_fusion.4
  76.7 0.0 collective-permute-done.5
  76.7 0.8 bitcast_dynamic-update-slice_fusion.3
  77.6 12.3 %collective-permute-done.8 = f32[2,8,64,128]{3,2,1,0:T(8,128)S(1)} collective-permute-done((f32[2,8,64,128]{3,2,1,0:T(8,128)S(1)}, f32[2,8,64,128]{3,2,1,0:T(8,128)S(1)}, u32[]{:S(2)}, u32[]{:S(2)}) %collective-permute-start.8) | collective-permute-done | bytes 524320 | tf_op jit(solution)/shard_map/ppermute | solution.py:36
  89.9 0.8 bitcast_dynamic-update-slice_fusion.2
  90.7 0.8 bitcast_dynamic-update-slice_fusion.1
  91.6 0.8 bitcast_dynamic-update-slice_fusion.lo0.lo1
  92.4 2.8 %collective-permute-start.9 = (f32[8,2,8,64,128]{4,3,2,1,0:T(8,128)}, f32[8,2,8,64,128]{4,3,2,1,0:T(8,128)}, u32[]{:S(2)}, u32[]{:S(2)}) collective-permute-start(f32[8,2,8,64,128]{4,3,2,1,0:T(8,128)} %bitcast_dynamic-update-slice_fusion.lo0.lo1), channel_id=1, source_target_pairs={{0,1},{1,0},{2,3},{3,2},{4,5},{5,4},{6,7},{7,6},{8,9},{9,8},{10,11... | collective-permute-start | bytes 12582920 | tf_op jit(solution)/shard_map/ppermute | solution.py:36
  95.2 0.0 copy-done.1
  95.2 3.2 %collective-permute-start.10 = (f32[64,32,128]{2,1,0:T(8,128)S(1)}, f32[64,32,128]{2,1,0:T(8,128)S(1)}, u32[]{:S(2)}, u32[]{:S(2)}) collective-permute-start(f32[64,32,128]{2,1,0:T(8,128)S(1)} %copy-done.1), channel_id=1, source_target_pairs={{0,32},{1,33},{2,34},{3,35},{4,36},{5,37},{6,38},{7,39},{8,40},{9,... | collective-permute-start | bytes 3145736 | tf_op jit(solution)/shard_map/ppermute | solution.py:36
  98.4 0.1 stack.59.place
  98.4 24.9 %collective-permute-done.10.t_oth = f32[64,32,128]{2,1,0:T(8,128)S(1)} collective-permute-done((f32[64,32,128]{2,1,0:T(8,128)S(1)}, f32[64,32,128]{2,1,0:T(8,128)S(1)}, u32[]{:S(2)}, u32[]{:S(2)}) %collective-permute-start.10) | collective-permute-done | bytes 1048608 | tf_op jit(solution)/shard_map/ppermute | solution.py:36
  123.4 0.0 collective-permute-done.9.lx0.lx1
  123.4 0.0 all-gather.3.cloned.1.call-done
  123.4 0.0 copy-start
  123.4 2.2 %copy-done = f32[128,32,256]{2,1,0:T(8,128)S(1)} copy-done((f32[128,32,256]{2,1,0:T(8,128)S(1)}, f32[128,32,256]{2,1,0:T(8,128)}, u32[]{:S(2)}) %copy-start) | copy-done | bytes 4194328
  125.6 19.9 %ladder.1 = f32[128,128]{1,0:T(8,128)S(1)} custom-call(s32[5]{0:T(128)S(1)} %stack.59.place, f32[8,16,32,256]{3,2,1,0:T(8,128)S(1)} %bitcast.27, f32[8,16,32,256]{3,2,1,0:T(8,128)S(1)} %bitcast.28, f32[8,2,8,64,128]{4,3,2,1,0:T(8,128)} %bitcast_dynamic-update-slice_fusion.lo0.lo1, f32[8,2,8,64,128]{4,3,2,1,0:T(8,128)} %bitcast_dynamic-update-slice_fusion.lo0.lo1, ...), custom_call_target="tpu_custom_call" | custom-call | flops 6442450944 | bytes 16777216 | tf_op jit(solution)/shard_map/ladder/pallas_call | solution.py:113
  145.5 3.2 %reshape.13 = f32[8,8,2,2,8,2,4]{6,5,4,3,2,1,0:T(2,128)S(1)} reshape(f32[128,128]{1,0:T(8,128)S(1)} %ladder.1) | data formatting | bytes 131072 | tf_op jit(solution)/shard_map/reshape | solution.py:152
  148.7 3.6 %copy.7 = f32[2,2,2,8,8,4,8]{6,5,4,3,2,1,0:T(4,128)S(1)} copy(f32[2,2,2,8,8,4,8]{5,2,4,1,0,3,6:T(2,128)S(1)} %bitcast.29) | data formatting | bytes 131072 | tf_op jit(solution)/shard_map/transpose | solution.py:152
  152.3 1.0 reshape.14
  153.4 10.3 %all_to_all.14 = f32[8,16,128]{2,1,0:T(8,128)S(1)} all-to-all(f32[8,16,128]{2,1,0:T(8,128)S(1)} %reshape.14), channel_id=1, replica_groups=mesh['z'=8,'xh'=2,'xl'=2,'y'=8,'core'=2] {'xh','xl','core'}, dimensions={0} | all-to-all | bytes 131072 | tf_op jit(solution)/shard_map/all_to_all | solution.py:153
  163.7 0.1 all_to_all.10
  163.7 24.3 %all_to_all.15 = f32[64,1,32]{2,1,0:T(1,128)S(1)} all-to-all(f32[64,1,32]{2,1,0:T(1,128)S(1)} %bitcast.34), channel_id=1, replica_groups=mesh['z'=8,'xh'=2,'xl'=2,'y'=8,'core'=2] {'z','y'}, dimensions={0} | all-to-all | bytes 16384 | tf_op jit(solution)/shard_map/all_to_all | solution.py:155
  188.1 0.1 reduce_sum.19
  188.1 0.7 reshape.15
  (2 shorter events, 0.1 us)
Async XLA Ops:
  6.5 116.8 %all-gather.3.cloned.1.call-start = ((), (), s32[]{:S(2)}) async-start(), calls=%async_computation.2 | async-start | bytes 4718592 | tf_op jit(solution)/shard_map/all_gather | solution.py:141
  6.5 5.5 %collective-permute-start = (f32[8,64,128]{2,1,0:T(8,128)}, f32[8,64,128]{2,1,0:T(8,128)S(1)}, u32[]{:S(2)}, u32[]{:S(2)}) collective-permute-start(f32[8,64,128]{2,1,0:T(8,128)} %param.3), channel_id=1, source_target_pairs={{0,0},{1,1},{2,32},{3,33},{4,4},{5,5},{6,36},{7,37},{8,8},{9,9},{1... | collective-permute-start | bytes 786440 | tf_op jit(solution)/shard_map/ppermute | solution.py:36
  8.1 15.0 %collective-permute-start.1 = (f32[8,64,128]{2,1,0:T(8,128)}, f32[8,64,128]{2,1,0:T(8,128)S(1)}, u32[]{:S(2)}, u32[]{:S(2)}) collective-permute-start(f32[8,64,128]{2,1,0:T(8,128)} %param.3), channel_id=1, source_target_pairs={{0,16},{1,17},{2,48},{3,49},{4,20},{5,21},{6,52},{7,53},{8,24},{9,... | collective-permute-start | bytes 786440 | tf_op jit(solution)/shard_map/ppermute | solution.py:36
  23.2 13.5 %collective-permute-start.2 = (f32[2,8,64,128]{3,2,1,0:T(8,128)S(1)}, f32[2,8,64,128]{3,2,1,0:T(8,128)S(1)}, u32[]{:S(2)}, u32[]{:S(2)}) collective-permute-start(f32[2,8,64,128]{3,2,1,0:T(8,128)S(1)} %pad_maximum_fusion), channel_id=1, source_target_pairs={{0,2},{1,15},{2,4},{3,1},{4,6},{5,3},{6,8},{7,5},{8,10},{9,7},{10,... | collective-permute-start | bytes 1572872 | tf_op jit(solution)/shard_map/ppermute | solution.py:36
  30.6 64.6 %copy-start.1 = (f32[64,32,128]{2,1,0:T(8,128)S(1)}, f32[64,32,128]{2,1,0:T(8,128)}, u32[]{:S(2)}) copy-start(f32[64,32,128]{2,1,0:T(8,128)} %t_own.1) | copy-start | bytes 3145732
  36.7 11.7 %collective-permute-start.3 = (f32[2,8,64,128]{3,2,1,0:T(8,128)S(1)}, f32[2,8,64,128]{3,2,1,0:T(8,128)S(1)}, u32[]{:S(2)}, u32[]{:S(2)}) collective-permute-start(f32[2,8,64,128]{3,2,1,0:T(8,128)S(1)} %collective-permute-done.2), channel_id=1, source_target_pairs={{0,2},{1,15},{2,4},{3,1},{4,6},{5,3},{6,8},{7,5},{8,10},{9,7},{10,... | collective-permute-start | bytes 1572872 | tf_op jit(solution)/shard_map/ppermute | solution.py:36
  41.7 15.4 %collective-permute-start.6 = (f32[2,8,64,128]{3,2,1,0:T(8,128)S(1)}, f32[2,8,64,128]{3,2,1,0:T(8,128)S(1)}, u32[]{:S(2)}, u32[]{:S(2)}) collective-permute-start(f32[2,8,64,128]{3,2,1,0:T(8,128)S(1)} %pad_maximum_fusion), channel_id=1, source_target_pairs={{0,14},{1,3},{2,0},{3,5},{4,2},{5,7},{6,4},{7,9},{8,6},{9,11},{10,... | collective-permute-start | bytes 1572872 | tf_op jit(solution)/shard_map/ppermute | solution.py:36
  48.3 11.5 %collective-permute-start.4 = (f32[2,8,64,128]{3,2,1,0:T(8,128)S(1)}, f32[2,8,64,128]{3,2,1,0:T(8,128)S(1)}, u32[]{:S(2)}, u32[]{:S(2)}) collective-permute-start(f32[2,8,64,128]{3,2,1,0:T(8,128)S(1)} %collective-permute-done.3), channel_id=1, source_target_pairs={{0,2},{1,15},{2,4},{3,1},{4,6},{5,3},{6,8},{7,5},{8,10},{9,7},{10,... | collective-permute-start | bytes 1572872 | tf_op jit(solution)/shard_map/ppermute | solution.py:36
  57.1 16.0 %collective-permute-start.7 = (f32[2,8,64,128]{3,2,1,0:T(8,128)S(1)}, f32[2,8,64,128]{3,2,1,0:T(8,128)S(1)}, u32[]{:S(2)}, u32[]{:S(2)}) collective-permute-start(f32[2,8,64,128]{3,2,1,0:T(8,128)S(1)} %collective-permute-done.6), channel_id=1, source_target_pairs={{0,14},{1,3},{2,0},{3,5},{4,2},{5,7},{6,4},{7,9},{8,6},{9,11},{10,... | collective-permute-start | bytes 1572872 | tf_op jit(solution)/shard_map/ppermute | solution.py:36
  59.9 16.8 %collective-permute-start.5 = (f32[2,8,64,128]{3,2,1,0:T(8,128)S(1)}, f32[2,8,64,128]{3,2,1,0:T(8,128)S(1)}, u32[]{:S(2)}, u32[]{:S(2)}) collective-permute-start(f32[2,8,64,128]{3,2,1,0:T(8,128)S(1)} %collective-permute-done.4), channel_id=1, source_target_pairs={{0,2},{1,15},{2,4},{3,1},{4,6},{5,3},{6,8},{7,5},{8,10},{9,7},{10,... | collective-permute-start | bytes 1572872 | tf_op jit(solution)/shard_map/ppermute | solution.py:36
  73.1 16.8 %collective-permute-start.8 = (f32[2,8,64,128]{3,2,1,0:T(8,128)S(1)}, f32[2,8,64,128]{3,2,1,0:T(8,128)S(1)}, u32[]{:S(2)}, u32[]{:S(2)}) collective-permute-start(f32[2,8,64,128]{3,2,1,0:T(8,128)S(1)} %collective-permute-done.7), channel_id=1, source_target_pairs={{0,14},{1,3},{2,0},{3,5},{4,2},{5,7},{6,4},{7,9},{8,6},{9,11},{10,... | collective-permute-start | bytes 1572872 | tf_op jit(solution)/shard_map/ppermute | solution.py:36
  92.4 31.0 %collective-permute-start.9 = (f32[8,2,8,64,128]{4,3,2,1,0:T(8,128)}, f32[8,2,8,64,128]{4,3,2,1,0:T(8,128)}, u32[]{:S(2)}, u32[]{:S(2)}) collective-permute-start(f32[8,2,8,64,128]{4,3,2,1,0:T(8,128)} %bitcast_dynamic-update-slice_fusion.lo0.lo1), channel_id=1, source_target_pairs={{0,1},{1,0},{2,3},{3,2},{4,5},{5,4},{6,7},{7,6},{8,9},{9,8},{10,11... | collective-permute-start | bytes 12582920 | tf_op jit(solution)/shard_map/ppermute | solution.py:36
  95.2 28.2 %collective-permute-start.10 = (f32[64,32,128]{2,1,0:T(8,128)S(1)}, f32[64,32,128]{2,1,0:T(8,128)S(1)}, u32[]{:S(2)}, u32[]{:S(2)}) collective-permute-start(f32[64,32,128]{2,1,0:T(8,128)S(1)} %copy-done.1), channel_id=1, source_target_pairs={{0,32},{1,33},{2,34},{3,35},{4,36},{5,37},{6,38},{7,39},{8,40},{9,... | collective-permute-start | bytes 3145736 | tf_op jit(solution)/shard_map/ppermute | solution.py:36
  123.4 2.2 %copy-start = (f32[128,32,256]{2,1,0:T(8,128)S(1)}, f32[128,32,256]{2,1,0:T(8,128)}, u32[]{:S(2)}) copy-start(f32[128,32,256]{2,1,0:T(8,128)} %all-gather.3.cloned.1.call-done) | copy-start | bytes 12582916
Sparse Core Ops, SparseCore 0:
  30.7 60.5 all-gather.2

commit v2 on v0

v2 whole, which is shorter than its diff:
```python
import jax
import jax.numpy as jnp
from jax import lax
from jax.experimental import pallas as pl
from jax.experimental.pallas import tpu as pltpu
from jax.sharding import Mesh, PartitionSpec as P

AXES = ("z", "xh", "xl", "y", "core")
SIZES = (8, 2, 2, 8, 2)


def linear(z, xh, xl, y, core):
    return (((z % 8) * 2 + xh) * 2 + xl) * 16 + (y % 8) * 2 + core


def table(target):
    pairs = []
    for z in range(8):
        for xh in range(2):
            for xl in range(2):
                for y in range(8):
                    for core in range(2):
                        pairs.append((linear(z, xh, xl, y, core), linear(*target(z, xh, xl, y, core))))
    return pairs


SAME_XL = table(lambda z, xh, xl, y, core: (z, y % 2, xl, y // 2 * 2 + xh, core))
OTHER_XL = table(lambda z, xh, xl, y, core: (z, y % 2, 1 - xl, y // 2 * 2 + xh, core))
RING_X = table(lambda z, xh, xl, y, core: (z, xh, xl, y + 1 - 2 * core, core))
RING_Y = table(lambda z, xh, xl, y, core: (z, xh, xl, y - 1 + 2 * core, core))
SWAP_CORE = table(lambda z, xh, xl, y, core: (z, xh, xl, y, 1 - core))
SWAP_XH = table(lambda z, xh, xl, y, core: (z, 1 - xh, xl, y, core))


def send(array, pairs):
    return lax.ppermute(array, AXES, pairs)


def split(value):
    high = value.astype(jnp.bfloat16)
    low = (value - high.astype(jnp.float32)).astype(jnp.bfloat16)
    return high, low

def dot_nt(a, b):
    return lax.dot_general(a, b, (((1,), (1,)), ((), ())), preferred_element_type=jnp.float32)

def dot_nn(a, b):
    return lax.dot_general(a, b, (((1,), (0,)), ((), ())), preferred_element_type=jnp.float32)

PAIRS = (0, 1, 3, 2)
ARRIVAL = (0, 1, 7, 2, 6, 3, 5, 4)

def ladder_kernel(place, right, *refs):
    own, oth = refs[:8], refs[8:16]
    t_own, t_oth, out = refs[16:19]
    r_buf, l_buf, t_buf, r_mul, l_mul, acc, y_high, y_low, t_high, t_low, r_sem, l_sem, t_sem = refs[19:]
    y, sign, xl_here, xh, core = (place[i] for i in range(5))

    def pair(k):
        return lax.rem(y // 2 + PAIRS[k], 4)

    def right_copy(k, xl):
        return pltpu.make_async_copy(right.at[lax.bitwise_xor(xl, xl_here) * 4 + pair(k)], r_buf.at[2 * k + xl], r_sem.at[2 * k + xl])

    def left_copy(side, slot):
        at = lax.bitwise_and(y + (8 - slot if side == 0 else slot) * sign + 8, 7)
        return pltpu.make_async_copy((own, oth)[side][slot], l_buf.at[side, at], l_sem.at[side, at])

    def left_wait(side, at):
        pltpu.make_async_copy(own[0], l_buf.at[side, at], l_sem.at[side, at]).wait()

    for xl in range(2):
        right_copy(0, xl).start()
    for slot in ARRIVAL:
        left_copy(0, slot).start()
        left_copy(1, slot).start()
    for k in range(1, 4):
        for xl in range(2):
            right_copy(k, xl).start()
    t_copies = [pltpu.make_async_copy(ref, t_buf.at[i], t_sem.at[i]) for i, ref in enumerate((t_own, t_oth))]
    for copy in t_copies:
        copy.start()

    def prepare(k, part):
        xl, side = part // 2, part % 2
        if part == 0:
            for each in range(2):
                right_copy(k, each).wait()
                left_wait(each, 2 * pair(k))
                left_wait(each, 2 * pair(k) + 1)
        slot = k % 2
        lanes = jnp.where(side == 0, core, 1 - core) * 128
        value = r_buf[2 * k + xl, :, :, pl.ds(pl.multiple_of(lanes, 128), 128)].reshape(512, 128)
        high, low = split(value)
        at = part * 128
        r_mul[slot, :, at : at + 128] = high
        r_mul[slot, :, 512 + at : 512 + at + 128] = low
        for half, where in enumerate((2 * pair(k) + xh, 2 * pair(k) + 1 - xh)):
            high, low = split(l_buf[side, where, xl])
            l_mul[slot, :, half * 64 : half * 64 + 64, at : at + 128] = high
            l_mul[slot, :, half * 64 : half * 64 + 64, 512 + at : 512 + at + 128] = low

    def multiply(k, part):
        slot, a = k % 2, part * 2
        left = l_mul[slot, a : a + 2].reshape(256, 1024)
        both = r_mul[slot]
        product = dot_nt(
            jnp.concatenate([both, both[:, :512]], axis=1),
            jnp.concatenate([left[:, :512], left], axis=1),
        )
        for i in range(2):
            piece = product[:, i * 128 : i * 128 + 128]
            if k == 0:
                acc[a + i] = piece
            else:
                acc[a + i] += piece

    def prepare_t(d):
        for half in range(2):
            high, low = split(t_buf[half, pl.ds(d, 64, 32), :])
            t_high[d * 128 + half * 64 : d * 128 + half * 64 + 64, :] = high
            t_low[d * 128 + half * 64 : d * 128 + half * 64 + 64, :] = low

    for part in range(4):
        prepare(0, part)
    for k in range(4):
        if k == 1:
            for copy in t_copies:
                copy.wait()
        for part in range(4):
            multiply(k, part)
            if k < 3:
                prepare(k + 1, part)
            if k >= 1:
                for d in range((k - 1) * 12 + part * 3, min((k - 1) * 12 + part * 3 + 3, 32)):
                    prepare_t(d)
    for d in range(32):
        for a in range(8):
            high, low = split(acc[a, pl.ds(d, 16, 32), :])
            y_high[a * 16 : a * 16 + 16, d * 128 : d * 128 + 128] = high
            y_low[a * 16 : a * 16 + 16, d * 128 : d * 128 + 128] = low
    total = dot_nn(y_high[...], t_high[...]) + dot_nn(y_high[...], t_low[...]) + dot_nn(y_low[...], t_high[...])
    total = total.T
    for xl in range(2):
        for each in range(2):
            for row in range(8):
                first = xl * 64 + row * 8 + each * 4
                for xh_to in range(2):
                    out[xh_to * 4 + xl * 2 + each, row] = total[first : first + 4]

def contract(place, right, own, oth, t_own, t_oth):
    any_spec = pl.BlockSpec(memory_space=pl.ANY)
    return pl.pallas_call(
        ladder_kernel,
        out_shape=jax.ShapeDtypeStruct((8, 8, 4, 128), jnp.float32),
        in_specs=[pl.BlockSpec(memory_space=pltpu.SMEM)] + [any_spec] * 19,
        out_specs=pl.BlockSpec(memory_space=pltpu.VMEM),
        scratch_shapes=[
            pltpu.VMEM((8, 16, 32, 256), jnp.float32),
            pltpu.VMEM((2, 8, 2, 8, 64, 128), jnp.float32),
            pltpu.VMEM((2, 2048, 128), jnp.float32),
            pltpu.VMEM((2, 512, 1024), jnp.bfloat16),
            pltpu.VMEM((2, 8, 128, 1024), jnp.bfloat16),
            pltpu.VMEM((8, 512, 128), jnp.float32),
            pltpu.VMEM((128, 4096), jnp.bfloat16),
            pltpu.VMEM((128, 4096), jnp.bfloat16),
            pltpu.VMEM((4096, 128), jnp.bfloat16),
            pltpu.VMEM((4096, 128), jnp.bfloat16),
            pltpu.SemaphoreType.DMA((8,)),
            pltpu.SemaphoreType.DMA((2, 8)),
            pltpu.SemaphoreType.DMA((2,)),
        ],
        compiler_params=pltpu.CompilerParams(vmem_limit_bytes=56 * 1024 * 1024),
        cost_estimate=pl.CostEstimate(flops=6 << 30, bytes_accessed=16 << 20, transcendentals=0),
        name="ladder",
    )(place, right, *own, *oth, t_own.reshape(2048, 128), t_oth.reshape(2048, 128))


def after(array, *earlier):
    return lax.optimization_barrier((array, *earlier))[0]


def shards(vectors_left, vectors_right, amplitudes):
    z, xh, y, core = (lax.axis_index(name) for name in ("z", "xh", "y", "core"))
    place = jnp.stack([y, 1 - 2 * core, lax.axis_index("xl"), xh, core]).astype(jnp.int32)
    right = lax.all_gather(vectors_right, "z", axis=0)
    same, other = send(vectors_left, SAME_XL), send(vectors_left, OTHER_XL)
    own = jnp.stack([same, other])
    x1 = send(own, RING_X)
    t_oth = send(amplitudes, SWAP_XH)
    y1 = send(own, RING_Y)
    own_swapped = send(own, SWAP_CORE)
    x2 = send(x1, RING_X)
    y2 = send(after(y1, x1), RING_Y)
    x1_swapped = send(after(x1, own_swapped), SWAP_CORE)
    x3 = send(after(x2, y1), RING_X)
    y1_swapped = send(y1, SWAP_CORE)
    y3 = send(after(y2, x2), RING_Y)
    x2_swapped = send(x2, SWAP_CORE)
    x4 = send(after(x3, y2, t_oth), RING_X)
    y2_swapped = send(y2, SWAP_CORE)
    x3_swapped = send(x3, SWAP_CORE)
    y3_swapped = send(y3, SWAP_CORE)
    x4_swapped = send(x4, SWAP_CORE)
    left_own = [own, x1, x2, x3, x4, y3, y2, y1]
    left_oth = [own_swapped, x1_swapped, x2_swapped, x3_swapped, x4_swapped, y3_swapped, y2_swapped, y1_swapped]
    partial = contract(place, right, left_own, left_oth, amplitudes, t_oth)
    near = lax.all_to_all(partial, ("xh", "xl", "core"), 0, 0, tiled=True)
    near = jnp.broadcast_to(jnp.sum(near, axis=0)[None], (8, 8, 4, 128)).reshape(64, 4, 128)
    far = jnp.sum(lax.all_to_all(near, ("z", "y"), 0, 0, tiled=True), axis=0)
    return lax.dynamic_slice(far.reshape(4, 8, 16), (0, 0, z * 2 + xh), (4, 8, 1))


def solution(mesh):
    fine = Mesh(mesh.devices.reshape(SIZES), AXES)
    c_axes, d_axes = ("z", "xh"), ("xl", "y", "core")
    return jax.shard_map(
        shards,
        mesh=fine,
        in_specs=(P(None, c_axes, d_axes), P(None, d_axes, c_axes), P(c_axes, d_axes, None)),
        out_specs=P(d_axes, None, c_axes),
        check_vma=False,
    )
```

time: 499 us -> 159 us (0.32)
  the two profiles are of different devices: /device:TPU:2 before, /device:TPU:1 now
where the time goes in v2:
time: 159 us; the launch traced here: 158 us
  starting transfers between devices  90.5 us (57%)
  waiting for transfers between devices  23.7 us (15%)
  Pallas kernels  18.9 us (12%)
  between operations  13.8 us (9%)
  blocking collectives  9.17 us (6%)
  local copies, waits for them, and re-layouts  2.17 us (1%)
    ppermute x18, starting transfers between devices, send(): return lax.ppermute(array, AXES, pairs)  70.8 us
    all_to_all x1, starting transfers between devices, shards(): far = jnp.sum(lax.all_to_all(near, ('z', 'y'), 0, 0, tiled=True), axis=0)  19.7 us
    pallas_call x1, Pallas kernels, contract(): pl.pallas_call(ladder_kernel, out_shape=jax.ShapeDtypeStruct((8, 8, 4, 12...  18.9 us
    all_to_all x1, waiting for transfers between devices, shards(): far = jnp.sum(lax.all_to_all(near, ('z', 'y'), 0, 0, tiled=True), axis=0)  11.6 us
    ppermute x18, waiting for transfers between devices, send(): return lax.ppermute(array, AXES, pairs)  11.4 us
    all_to_all x1, blocking collectives, shards(): near = lax.all_to_all(partial, ('xh', 'xl', 'core'), 0, 0, tiled=True)  9.17 us
  transfers between devices with their start and end apart: 20, of which 5 were waited for; matrix products, arithmetic and copies ran while one was open for 0% of the time, Pallas kernels for 0%

profile of v2, /device:TPU:1, one launch (start us, length us, event | category | flops | bytes accessed | tf_op | source)
XLA Modules:
  0.0 158.4 jit_solution(7835061764552882369)
XLA Ops:
  6.5 0.7 all-gather.3.cloned.1.call-update
  7.3 3.9 %collective-permute-start.1 = (f32[8,64,128]{2,1,0:T(8,128)}, f32[8,64,128]{2,1,0:T(8,128)S(1)}, u32[]{:S(2)}, u32[]{:S(2)}) collective-permute-start(f32[8,64,128]{2,1,0:T(8,128)} %param.3), channel_id=1, source_target_pairs={{0,16},{1,17},{2,48},{3,49},{4,20},{5,21},{6,52},{7,53},{8,24},{9,... | collective-permute-start | bytes 786440 | tf_op jit(solution)/shard_map/ppermute | solution.py:36
  11.2 1.6 %collective-permute-start = (f32[8,64,128]{2,1,0:T(8,128)}, f32[8,64,128]{2,1,0:T(8,128)S(1)}, u32[]{:S(2)}, u32[]{:S(2)}) collective-permute-start(f32[8,64,128]{2,1,0:T(8,128)} %param.3), channel_id=1, source_target_pairs={{0,0},{1,1},{2,32},{3,33},{4,4},{5,5},{6,36},{7,37},{8,8},{9,9},{1... | collective-permute-start | bytes 786440 | tf_op jit(solution)/shard_map/ppermute | solution.py:36
  12.8 2.3 %collective-permute-done.1 = f32[8,64,128]{2,1,0:T(8,128)S(1)} collective-permute-done((f32[8,64,128]{2,1,0:T(8,128)}, f32[8,64,128]{2,1,0:T(8,128)S(1)}, u32[]{:S(2)}, u32[]{:S(2)}) %collective-permute-start.1) | collective-permute-done | bytes 262176 | tf_op jit(solution)/shard_map/ppermute | solution.py:36
  15.2 0.0 collective-permute-done
  15.2 15.5 %collective-permute-start.2 = (f32[2,8,64,128]{3,2,1,0:T(8,128)S(1)}, f32[2,8,64,128]{3,2,1,0:T(8,128)S(1)}, u32[]{:S(2)}, u32[]{:S(2)}) collective-permute-start(f32[2,8,64,128]{3,2,1,0:T(8,128)S(1)} %pad_maximum_fusion.refs_0_), channel_id=1, source_target_pairs={{0,2},{1,15},{2,4},{3,1},{4,6},{5,3},{6,8},{7,5},{8,10},{9,7},{10,... | collective-permute-start | bytes 1572872 | tf_op jit(solution)/shard_map/ppermute | solution.py:36
  30.7 1.9 %collective-permute-start.4 = (f32[2,8,64,128]{3,2,1,0:T(8,128)S(1)}, f32[2,8,64,128]{3,2,1,0:T(8,128)S(1)}, u32[]{:S(2)}, u32[]{:S(2)}) collective-permute-start(f32[2,8,64,128]{3,2,1,0:T(8,128)S(1)} %pad_maximum_fusion.refs_0_), channel_id=1, source_target_pairs={{0,14},{1,3},{2,0},{3,5},{4,2},{5,7},{6,4},{7,9},{8,6},{9,11},{10,... | collective-permute-start | bytes 1572872 | tf_op jit(solution)/shard_map/ppermute | solution.py:36
  32.6 5.0 %collective-permute-done.2.refs_1_ = f32[2,8,64,128]{3,2,1,0:T(8,128)S(1)} collective-permute-done((f32[2,8,64,128]{3,2,1,0:T(8,128)S(1)}, f32[2,8,64,128]{3,2,1,0:T(8,128)S(1)}, u32[]{:S(2)}, u32[]{:S(2)}) %collective-permute-start.2) | collective-permute-done | bytes 524320 | tf_op jit(solution)/shard_map/ppermute | solution.py:36
  37.7 5.4 %collective-permute-start.3 = (f32[2,8,64,128]{3,2,1,0:T(8,128)S(1)}, f32[2,8,64,128]{3,2,1,0:T(8,128)S(1)}, u32[]{:S(2)}, u32[]{:S(2)}) collective-permute-start(f32[2,8,64,128]{3,2,1,0:T(8,128)S(1)} %collective-permute-done.2.refs_1_), channel_id=1, source_target_pairs={{0,2},{1,15},{2,4},{3,1},{4,6},{5,3},{6,8},{7,5},{8,10},{9,7},{10,... | collective-permute-start | bytes 1572872 | tf_op jit(solution)/shard_map/ppermute | solution.py:36
  43.1 2.5 %collective-permute-start.7 = (f32[64,32,128]{2,1,0:T(8,128)}, f32[64,32,128]{2,1,0:T(8,128)S(1)}, u32[]{:S(2)}, u32[]{:S(2)}) collective-permute-start(f32[64,32,128]{2,1,0:T(8,128)} %param.5), channel_id=1, source_target_pairs={{0,32},{1,33},{2,34},{3,35},{4,36},{5,37},{6,38},{7,39},{8,40},{9,... | collective-permute-start | bytes 3145736 | tf_op jit(solution)/shard_map/ppermute | solution.py:36
  45.6 7.1 %collective-permute-start.10 = (f32[2,8,64,128]{3,2,1,0:T(8,128)S(1)}, f32[2,8,64,128]{3,2,1,0:T(8,128)S(1)}, u32[]{:S(2)}, u32[]{:S(2)}) collective-permute-start(f32[2,8,64,128]{3,2,1,0:T(8,128)S(1)} %pad_maximum_fusion.refs_0_), channel_id=1, source_target_pairs={{0,1},{1,0},{2,3},{3,2},{4,5},{5,4},{6,7},{7,6},{8,9},{9,8},{10,11... | collective-permute-start | bytes 1572872 | tf_op jit(solution)/shard_map/ppermute | solution.py:36
  52.8 0.0 collective-permute-done.4.refs_7_
  52.8 4.1 %collective-permute-start.6 = (f32[2,8,64,128]{3,2,1,0:T(8,128)S(1)}, f32[2,8,64,128]{3,2,1,0:T(8,128)}, u32[]{:S(2)}, u32[]{:S(2)}) collective-permute-start(f32[2,8,64,128]{3,2,1,0:T(8,128)S(1)} %collective-permute-done.4.refs_7_), channel_id=1, source_target_pairs={{0,14},{1,3},{2,0},{3,5},{4,2},{5,7},{6,4},{7,9},{8,6},{9,11},{10,... | collective-permute-start | bytes 1572872 | tf_op jit(solution)/shard_map/ppermute | solution.py:36
  56.9 0.0 collective-permute-done.3.refs_2_
  56.9 0.0 copy-start.4
  56.9 2.4 %collective-permute-start.5 = (f32[2,8,64,128]{3,2,1,0:T(8,128)S(1)}, f32[2,8,64,128]{3,2,1,0:T(8,128)}, u32[]{:S(2)}, u32[]{:S(2)}) collective-permute-start(f32[2,8,64,128]{3,2,1,0:T(8,128)S(1)} %collective-permute-done.3.refs_2_), channel_id=1, source_target_pairs={{0,2},{1,15},{2,4},{3,1},{4,6},{5,3},{6,8},{7,5},{8,10},{9,7},{10,... | collective-permute-start | bytes 1572872 | tf_op jit(solution)/shard_map/ppermute | solution.py:36
  59.3 0.0 collective-permute-done.10.refs_8_
  59.3 1.9 %collective-permute-start.11 = (f32[2,8,64,128]{3,2,1,0:T(8,128)S(1)}, f32[2,8,64,128]{3,2,1,0:T(8,128)S(1)}, u32[]{:S(2)}, u32[]{:S(2)}) collective-permute-start(f32[2,8,64,128]{3,2,1,0:T(8,128)S(1)} %collective-permute-done.2.refs_1_), channel_id=1, source_target_pairs={{0,1},{1,0},{2,3},{3,2},{4,5},{5,4},{6,7},{7,6},{8,9},{9,8},{10,11... | collective-permute-start | bytes 1572872 | tf_op jit(solution)/shard_map/ppermute | solution.py:36
  61.3 2.4 %collective-permute-start.17 = (f32[2,8,64,128]{3,2,1,0:T(8,128)S(1)}, f32[2,8,64,128]{3,2,1,0:T(8,128)S(1)}, u32[]{:S(2)}, u32[]{:S(2)}) collective-permute-start(f32[2,8,64,128]{3,2,1,0:T(8,128)S(1)} %collective-permute-done.4.refs_7_), channel_id=1, source_target_pairs={{0,1},{1,0},{2,3},{3,2},{4,5},{5,4},{6,7},{7,6},{8,9},{9,8},{10,11... | collective-permute-start | bytes 1572872 | tf_op jit(solution)/shard_map/ppermute | solution.py:36
  63.7 2.5 %collective-permute-done.6.refs_6_ = f32[2,8,64,128]{3,2,1,0:T(8,128)} collective-permute-done((f32[2,8,64,128]{3,2,1,0:T(8,128)S(1)}, f32[2,8,64,128]{3,2,1,0:T(8,128)}, u32[]{:S(2)}, u32[]{:S(2)}) %collective-permute-start.6) | collective-permute-done | bytes 524320 | tf_op jit(solution)/shard_map/ppermute | solution.py:36
  66.1 4.2 %collective-permute-start.9 = (f32[2,8,64,128]{3,2,1,0:T(8,128)}, f32[2,8,64,128]{3,2,1,0:T(8,128)}, u32[]{:S(2)}, u32[]{:S(2)}) collective-permute-start(f32[2,8,64,128]{3,2,1,0:T(8,128)} %collective-permute-done.6.refs_6_), channel_id=1, source_target_pairs={{0,14},{1,3},{2,0},{3,5},{4,2},{5,7},{6,4},{7,9},{8,6},{9,11},{10,... | collective-permute-start | bytes 1572872 | tf_op jit(solution)/shard_map/ppermute | solution.py:36
  70.3 0.0 collective-permute-done.7
  70.4 0.0 collective-permute-done.5.refs_3_
  70.4 4.1 %collective-permute-start.8 = (f32[2,8,64,128]{3,2,1,0:T(8,128)}, f32[2,8,64,128]{3,2,1,0:T(8,128)}, u32[]{:S(2)}, u32[]{:S(2)}) collective-permute-start(f32[2,8,64,128]{3,2,1,0:T(8,128)} %collective-permute-done.5.refs_3_), channel_id=1, source_target_pairs={{0,2},{1,15},{2,4},{3,1},{4,6},{5,3},{6,8},{7,5},{8,10},{9,7},{10,... | collective-permute-start | bytes 1572872 | tf_op jit(solution)/shard_map/ppermute | solution.py:36
  74.4 2.5 %collective-permute-start.16 = (f32[2,8,64,128]{3,2,1,0:T(8,128)}, f32[2,8,64,128]{3,2,1,0:T(8,128)}, u32[]{:S(2)}, u32[]{:S(2)}) collective-permute-start(f32[2,8,64,128]{3,2,1,0:T(8,128)} %collective-permute-done.6.refs_6_), channel_id=1, source_target_pairs={{0,1},{1,0},{2,3},{3,2},{4,5},{5,4},{6,7},{7,6},{8,9},{9,8},{10,11... | collective-permute-start | bytes 1572872 | tf_op jit(solution)/shard_map/ppermute | solution.py:36
  76.9 0.0 collective-permute-done.17.refs_15_
  76.9 1.9 %collective-permute-start.12 = (f32[2,8,64,128]{3,2,1,0:T(8,128)S(1)}, f32[2,8,64,128]{3,2,1,0:T(8,128)}, u32[]{:S(2)}, u32[]{:S(2)}) collective-permute-start(f32[2,8,64,128]{3,2,1,0:T(8,128)S(1)} %collective-permute-done.3.refs_2_), channel_id=1, source_target_pairs={{0,1},{1,0},{2,3},{3,2},{4,5},{5,4},{6,7},{7,6},{8,9},{9,8},{10,11... | collective-permute-start | bytes 1572872 | tf_op jit(solution)/shard_map/ppermute | solution.py:36
  78.9 0.0 collective-permute-done.11.refs_9_
  78.9 2.4 %collective-permute-start.13 = (f32[2,8,64,128]{3,2,1,0:T(8,128)}, f32[2,8,64,128]{3,2,1,0:T(8,128)}, u32[]{:S(2)}, u32[]{:S(2)}) collective-permute-start(f32[2,8,64,128]{3,2,1,0:T(8,128)} %collective-permute-done.5.refs_3_), channel_id=1, source_target_pairs={{0,1},{1,0},{2,3},{3,2},{4,5},{5,4},{6,7},{7,6},{8,9},{9,8},{10,11... | collective-permute-start | bytes 1572872 | tf_op jit(solution)/shard_map/ppermute | solution.py:36
  81.3 0.0 collective-permute-done.9.refs_5_
  81.3 4.9 %collective-permute-start.15 = (f32[2,8,64,128]{3,2,1,0:T(8,128)}, f32[2,8,64,128]{3,2,1,0:T(8,128)}, u32[]{:S(2)}, u32[]{:S(2)}) collective-permute-start(f32[2,8,64,128]{3,2,1,0:T(8,128)} %collective-permute-done.9.refs_5_), channel_id=1, source_target_pairs={{0,1},{1,0},{2,3},{3,2},{4,5},{5,4},{6,7},{7,6},{8,9},{9,8},{10,11... | collective-permute-start | bytes 1572872 | tf_op jit(solution)/shard_map/ppermute | solution.py:36
  86.3 0.0 collective-permute-done.8.refs_4_
  86.3 1.9 %collective-permute-start.14 = (f32[2,8,64,128]{3,2,1,0:T(8,128)}, f32[2,8,64,128]{3,2,1,0:T(8,128)}, u32[]{:S(2)}, u32[]{:S(2)}) collective-permute-start(f32[2,8,64,128]{3,2,1,0:T(8,128)} %collective-permute-done.8.refs_4_), channel_id=1, source_target_pairs={{0,1},{1,0},{2,3},{3,2},{4,5},{5,4},{6,7},{7,6},{8,9},{9,8},{10,11... | collective-permute-start | bytes 1572872 | tf_op jit(solution)/shard_map/ppermute | solution.py:36
  88.2 0.7 stack.32.place
  88.9 0.0 collective-permute-done.16.refs_14_
  88.9 0.0 collective-permute-done.12.refs_10_
  88.9 0.0 collective-permute-done.13.refs_11_
  88.9 0.0 collective-permute-done.15.refs_13_
  88.9 1.5 collective-permute-done.14.refs_12_
  90.5 18.9 %ladder.1 = f32[8,8,4,128]{3,2,1,0:T(4,128)} custom-call(s32[5]{0:T(128)} %stack.32.place, f32[8,16,32,256]{3,2,1,0:T(8,128)} %bitcast.13, f32[2,8,64,128]{3,2,1,0:T(8,128)} %copy-done, f32[2,8,64,128]{3,2,1,0:T(8,128)} %copy-done.2, f32[2,8,64,128]{3,2,1,0:T(8,128)} %copy-done.4, f32[2,8,64,128]{3,2,1,0:T(8,128)} %collective-permute-done.5.refs_3_, ...), custom_call_target="tpu_custom_call" | custom-call | flops 6442450944 | bytes 16777216 | tf_op jit(solution)/shard_map/ladder/pallas_call | solution.py:153
  109.4 9.2 %all_to_all.10 = f32[8,8,4,128]{3,2,1,0:T(4,128)S(1)} all-to-all(f32[8,8,4,128]{3,2,1,0:T(4,128)} %ladder.1), channel_id=1, replica_groups=mesh['z'=8,'xh'=2,'xl'=2,'y'=8,'core'=2] {'xh','xl','core'}, dimensions={0} | all-to-all | bytes 262144 | tf_op jit(solution)/shard_map/all_to_all | solution.py:208
  118.6 0.7 broadcast_in_dim.2
  119.3 19.7 %all-to-all-start.1 = ((f32[64,4,128]{2,1,0:T(4,128)}), f32[64,4,128]{2,1,0:T(4,128)S(1)}, u32[]{:S(2)}, u32[]{:S(2)}) async-start(f32[64,4,128]{2,1,0:T(4,128)} %bitcast.10), calls=%async_computation.1 | async-start | bytes 262144 | tf_op jit(solution)/shard_map/all_to_all | solution.py:210
  139.0 11.6 %all-to-all-done.1 = f32[64,4,128]{2,1,0:T(4,128)S(1)} async-done(((f32[64,4,128]{2,1,0:T(4,128)}), f32[64,4,128]{2,1,0:T(4,128)S(1)}, u32[]{:S(2)}, u32[]{:S(2)}) %all-to-all-start.1) | async-done | bytes 131104 | tf_op jit(solution)/shard_map/all_to_all | solution.py:210
  150.6 0.1 reduce_sum.19
  150.7 0.1 reshape.16
  150.8 0.1 constant_dynamic-slice_fusion
  150.9 0.7 copy.8
  (19 shorter events, 0.1 us)
Async XLA Ops:
  6.5 83.9 %all-gather.3.cloned.1.call-start = ((), (), s32[]{:S(2)}) async-start(), calls=%async_computation.2 | async-start | bytes 4718592 | tf_op jit(solution)/shard_map/all_gather | solution.py:186
  7.3 7.9 %collective-permute-start.1 = (f32[8,64,128]{2,1,0:T(8,128)}, f32[8,64,128]{2,1,0:T(8,128)S(1)}, u32[]{:S(2)}, u32[]{:S(2)}) collective-permute-start(f32[8,64,128]{2,1,0:T(8,128)} %param.3), channel_id=1, source_target_pairs={{0,16},{1,17},{2,48},{3,49},{4,20},{5,21},{6,52},{7,53},{8,24},{9,... | collective-permute-start | bytes 786440 | tf_op jit(solution)/shard_map/ppermute | solution.py:36
  11.2 4.0 %collective-permute-start = (f32[8,64,128]{2,1,0:T(8,128)}, f32[8,64,128]{2,1,0:T(8,128)S(1)}, u32[]{:S(2)}, u32[]{:S(2)}) collective-permute-start(f32[8,64,128]{2,1,0:T(8,128)} %param.3), channel_id=1, source_target_pairs={{0,0},{1,1},{2,32},{3,33},{4,4},{5,5},{6,36},{7,37},{8,8},{9,9},{1... | collective-permute-start | bytes 786440 | tf_op jit(solution)/shard_map/ppermute | solution.py:36
  15.2 75.2 %copy-start = (f32[2,8,64,128]{3,2,1,0:T(8,128)}, f32[2,8,64,128]{3,2,1,0:T(8,128)S(1)}, u32[]{:S(2)}) copy-start(f32[2,8,64,128]{3,2,1,0:T(8,128)S(1)} %pad_maximum_fusion.refs_0_) | copy-start | bytes 1572868
  15.2 22.4 %collective-permute-start.2 = (f32[2,8,64,128]{3,2,1,0:T(8,128)S(1)}, f32[2,8,64,128]{3,2,1,0:T(8,128)S(1)}, u32[]{:S(2)}, u32[]{:S(2)}) collective-permute-start(f32[2,8,64,128]{3,2,1,0:T(8,128)S(1)} %pad_maximum_fusion.refs_0_), channel_id=1, source_target_pairs={{0,2},{1,15},{2,4},{3,1},{4,6},{5,3},{6,8},{7,5},{8,10},{9,7},{10,... | collective-permute-start | bytes 1572872 | tf_op jit(solution)/shard_map/ppermute | solution.py:36
  30.7 22.1 %collective-permute-start.4 = (f32[2,8,64,128]{3,2,1,0:T(8,128)S(1)}, f32[2,8,64,128]{3,2,1,0:T(8,128)S(1)}, u32[]{:S(2)}, u32[]{:S(2)}) collective-permute-start(f32[2,8,64,128]{3,2,1,0:T(8,128)S(1)} %pad_maximum_fusion.refs_0_), channel_id=1, source_target_pairs={{0,14},{1,3},{2,0},{3,5},{4,2},{5,7},{6,4},{7,9},{8,6},{9,11},{10,... | collective-permute-start | bytes 1572872 | tf_op jit(solution)/shard_map/ppermute | solution.py:36
  37.6 52.8 %copy-start.2 = (f32[2,8,64,128]{3,2,1,0:T(8,128)}, f32[2,8,64,128]{3,2,1,0:T(8,128)S(1)}, u32[]{:S(2)}) copy-start(f32[2,8,64,128]{3,2,1,0:T(8,128)S(1)} %collective-permute-done.2.refs_1_) | copy-start | bytes 1572868
  37.7 19.3 %collective-permute-start.3 = (f32[2,8,64,128]{3,2,1,0:T(8,128)S(1)}, f32[2,8,64,128]{3,2,1,0:T(8,128)S(1)}, u32[]{:S(2)}, u32[]{:S(2)}) collective-permute-start(f32[2,8,64,128]{3,2,1,0:T(8,128)S(1)} %collective-permute-done.2.refs_1_), channel_id=1, source_target_pairs={{0,2},{1,15},{2,4},{3,1},{4,6},{5,3},{6,8},{7,5},{8,10},{9,7},{10,... | collective-permute-start | bytes 1572872 | tf_op jit(solution)/shard_map/ppermute | solution.py:36
  43.1 27.3 %collective-permute-start.7 = (f32[64,32,128]{2,1,0:T(8,128)}, f32[64,32,128]{2,1,0:T(8,128)S(1)}, u32[]{:S(2)}, u32[]{:S(2)}) collective-permute-start(f32[64,32,128]{2,1,0:T(8,128)} %param.5), channel_id=1, source_target_pairs={{0,32},{1,33},{2,34},{3,35},{4,36},{5,37},{6,38},{7,39},{8,40},{9,... | collective-permute-start | bytes 3145736 | tf_op jit(solution)/shard_map/ppermute | solution.py:36
  45.6 13.7 %collective-permute-start.10 = (f32[2,8,64,128]{3,2,1,0:T(8,128)S(1)}, f32[2,8,64,128]{3,2,1,0:T(8,128)S(1)}, u32[]{:S(2)}, u32[]{:S(2)}) collective-permute-start(f32[2,8,64,128]{3,2,1,0:T(8,128)S(1)} %pad_maximum_fusion.refs_0_), channel_id=1, source_target_pairs={{0,1},{1,0},{2,3},{3,2},{4,5},{5,4},{6,7},{7,6},{8,9},{9,8},{10,11... | collective-permute-start | bytes 1572872 | tf_op jit(solution)/shard_map/ppermute | solution.py:36
  52.8 37.7 %copy-start.3 = (f32[2,8,64,128]{3,2,1,0:T(8,128)}, f32[2,8,64,128]{3,2,1,0:T(8,128)S(1)}, u32[]{:S(2)}) copy-start(f32[2,8,64,128]{3,2,1,0:T(8,128)S(1)} %collective-permute-done.4.refs_7_) | copy-start | bytes 1572868
  52.8 13.3 %collective-permute-start.6 = (f32[2,8,64,128]{3,2,1,0:T(8,128)S(1)}, f32[2,8,64,128]{3,2,1,0:T(8,128)}, u32[]{:S(2)}, u32[]{:S(2)}) collective-permute-start(f32[2,8,64,128]{3,2,1,0:T(8,128)S(1)} %collective-permute-done.4.refs_7_), channel_id=1, source_target_pairs={{0,14},{1,3},{2,0},{3,5},{4,2},{5,7},{6,4},{7,9},{8,6},{9,11},{10,... | collective-permute-start | bytes 1572872 | tf_op jit(solution)/shard_map/ppermute | solution.py:36
  56.9 33.5 %copy-start.4 = (f32[2,8,64,128]{3,2,1,0:T(8,128)}, f32[2,8,64,128]{3,2,1,0:T(8,128)S(1)}, u32[]{:S(2)}) copy-start(f32[2,8,64,128]{3,2,1,0:T(8,128)S(1)} %collective-permute-done.3.refs_2_) | copy-start | bytes 1572868
  56.9 13.4 %collective-permute-start.5 = (f32[2,8,64,128]{3,2,1,0:T(8,128)S(1)}, f32[2,8,64,128]{3,2,1,0:T(8,128)}, u32[]{:S(2)}, u32[]{:S(2)}) collective-permute-start(f32[2,8,64,128]{3,2,1,0:T(8,128)S(1)} %collective-permute-done.3.refs_2_), channel_id=1, source_target_pairs={{0,2},{1,15},{2,4},{3,1},{4,6},{5,3},{6,8},{7,5},{8,10},{9,7},{10,... | collective-permute-start | bytes 1572872 | tf_op jit(solution)/shard_map/ppermute | solution.py:36
  59.3 19.5 %copy-start.5 = (f32[2,8,64,128]{3,2,1,0:T(8,128)}, f32[2,8,64,128]{3,2,1,0:T(8,128)S(1)}, u32[]{:S(2)}) copy-start(f32[2,8,64,128]{3,2,1,0:T(8,128)S(1)} %collective-permute-done.10.refs_8_) | copy-start | bytes 1572868
  59.3 19.5 %collective-permute-start.11 = (f32[2,8,64,128]{3,2,1,0:T(8,128)S(1)}, f32[2,8,64,128]{3,2,1,0:T(8,128)S(1)}, u32[]{:S(2)}, u32[]{:S(2)}) collective-permute-start(f32[2,8,64,128]{3,2,1,0:T(8,128)S(1)} %collective-permute-done.2.refs_1_), channel_id=1, source_target_pairs={{0,1},{1,0},{2,3},{3,2},{4,5},{5,4},{6,7},{7,6},{8,9},{9,8},{10,11... | collective-permute-start | bytes 1572872 | tf_op jit(solution)/shard_map/ppermute | solution.py:36
  61.3 15.6 %collective-permute-start.17 = (f32[2,8,64,128]{3,2,1,0:T(8,128)S(1)}, f32[2,8,64,128]{3,2,1,0:T(8,128)S(1)}, u32[]{:S(2)}, u32[]{:S(2)}) collective-permute-start(f32[2,8,64,128]{3,2,1,0:T(8,128)S(1)} %collective-permute-done.4.refs_7_), channel_id=1, source_target_pairs={{0,1},{1,0},{2,3},{3,2},{4,5},{5,4},{6,7},{7,6},{8,9},{9,8},{10,11... | collective-permute-start | bytes 1572872 | tf_op jit(solution)/shard_map/ppermute | solution.py:36
  66.1 15.2 %collective-permute-start.9 = (f32[2,8,64,128]{3,2,1,0:T(8,128)}, f32[2,8,64,128]{3,2,1,0:T(8,128)}, u32[]{:S(2)}, u32[]{:S(2)}) collective-permute-start(f32[2,8,64,128]{3,2,1,0:T(8,128)} %collective-permute-done.6.refs_6_), channel_id=1, source_target_pairs={{0,14},{1,3},{2,0},{3,5},{4,2},{5,7},{6,4},{7,9},{8,6},{9,11},{10,... | collective-permute-start | bytes 1572872 | tf_op jit(solution)/shard_map/ppermute | solution.py:36
  70.4 20.1 %copy-start.1 = (f32[64,32,128]{2,1,0:T(8,128)}, f32[64,32,128]{2,1,0:T(8,128)S(1)}, u32[]{:S(2)}) copy-start(f32[64,32,128]{2,1,0:T(8,128)S(1)} %collective-permute-done.7) | copy-start | bytes 3145732
  70.4 15.9 %collective-permute-start.8 = (f32[2,8,64,128]{3,2,1,0:T(8,128)}, f32[2,8,64,128]{3,2,1,0:T(8,128)}, u32[]{:S(2)}, u32[]{:S(2)}) collective-permute-start(f32[2,8,64,128]{3,2,1,0:T(8,128)} %collective-permute-done.5.refs_3_), channel_id=1, source_target_pairs={{0,2},{1,15},{2,4},{3,1},{4,6},{5,3},{6,8},{7,5},{8,10},{9,7},{10,... | collective-permute-start | bytes 1572872 | tf_op jit(solution)/shard_map/ppermute | solution.py:36
  74.4 14.4 %collective-permute-start.16 = (f32[2,8,64,128]{3,2,1,0:T(8,128)}, f32[2,8,64,128]{3,2,1,0:T(8,128)}, u32[]{:S(2)}, u32[]{:S(2)}) collective-permute-start(f32[2,8,64,128]{3,2,1,0:T(8,128)} %collective-permute-done.6.refs_6_), channel_id=1, source_target_pairs={{0,1},{1,0},{2,3},{3,2},{4,5},{5,4},{6,7},{7,6},{8,9},{9,8},{10,11... | collective-permute-start | bytes 1572872 | tf_op jit(solution)/shard_map/ppermute | solution.py:36
  76.9 4.4 %copy-start.7 = (f32[2,8,64,128]{3,2,1,0:T(8,128)}, f32[2,8,64,128]{3,2,1,0:T(8,128)S(1)}, u32[]{:S(2)}) copy-start(f32[2,8,64,128]{3,2,1,0:T(8,128)S(1)} %collective-permute-done.17.refs_15_) | copy-start | bytes 1572868
  76.9 12.0 %collective-permute-start.12 = (f32[2,8,64,128]{3,2,1,0:T(8,128)S(1)}, f32[2,8,64,128]{3,2,1,0:T(8,128)}, u32[]{:S(2)}, u32[]{:S(2)}) collective-permute-start(f32[2,8,64,128]{3,2,1,0:T(8,128)S(1)} %collective-permute-done.3.refs_2_), channel_id=1, source_target_pairs={{0,1},{1,0},{2,3},{3,2},{4,5},{5,4},{6,7},{7,6},{8,9},{9,8},{10,11... | collective-permute-start | bytes 1572872 | tf_op jit(solution)/shard_map/ppermute | solution.py:36
  78.9 2.4 %copy-start.6 = (f32[2,8,64,128]{3,2,1,0:T(8,128)}, f32[2,8,64,128]{3,2,1,0:T(8,128)S(1)}, u32[]{:S(2)}) copy-start(f32[2,8,64,128]{3,2,1,0:T(8,128)S(1)} %collective-permute-done.11.refs_9_) | copy-start | bytes 1572868
  78.9 10.0 %collective-permute-start.13 = (f32[2,8,64,128]{3,2,1,0:T(8,128)}, f32[2,8,64,128]{3,2,1,0:T(8,128)}, u32[]{:S(2)}, u32[]{:S(2)}) collective-permute-start(f32[2,8,64,128]{3,2,1,0:T(8,128)} %collective-permute-done.5.refs_3_), channel_id=1, source_target_pairs={{0,1},{1,0},{2,3},{3,2},{4,5},{5,4},{6,7},{7,6},{8,9},{9,8},{10,11... | collective-permute-start | bytes 1572872 | tf_op jit(solution)/shard_map/ppermute | solution.py:36
  81.3 7.6 %collective-permute-start.15 = (f32[2,8,64,128]{3,2,1,0:T(8,128)}, f32[2,8,64,128]{3,2,1,0:T(8,128)}, u32[]{:S(2)}, u32[]{:S(2)}) collective-permute-start(f32[2,8,64,128]{3,2,1,0:T(8,128)} %collective-permute-done.9.refs_5_), channel_id=1, source_target_pairs={{0,1},{1,0},{2,3},{3,2},{4,5},{5,4},{6,7},{7,6},{8,9},{9,8},{10,11... | collective-permute-start | bytes 1572872 | tf_op jit(solution)/shard_map/ppermute | solution.py:36
  86.3 4.1 %collective-permute-start.14 = (f32[2,8,64,128]{3,2,1,0:T(8,128)}, f32[2,8,64,128]{3,2,1,0:T(8,128)}, u32[]{:S(2)}, u32[]{:S(2)}) collective-permute-start(f32[2,8,64,128]{3,2,1,0:T(8,128)} %collective-permute-done.8.refs_4_), channel_id=1, source_target_pairs={{0,1},{1,0},{2,3},{3,2},{4,5},{5,4},{6,7},{7,6},{8,9},{9,8},{10,11... | collective-permute-start | bytes 1572872 | tf_op jit(solution)/shard_map/ppermute | solution.py:36
  119.3 31.4 %all-to-all-start.1 = ((f32[64,4,128]{2,1,0:T(4,128)}), f32[64,4,128]{2,1,0:T(4,128)S(1)}, u32[]{:S(2)}, u32[]{:S(2)}) async-start(f32[64,4,128]{2,1,0:T(4,128)} %bitcast.10), calls=%async_computation.1 | async-start | bytes 262144 | tf_op jit(solution)/shard_map/all_to_all | solution.py:210
Sparse Core Ops, SparseCore 0:
  9.4 63.7 all-gather.2

commit v3 on v0

v3 whole, which is shorter than its diff:
```python
import jax
import jax.numpy as jnp
from jax import lax
from jax.experimental import pallas as pl
from jax.experimental.pallas import tpu as pltpu
from jax.sharding import Mesh, PartitionSpec as P

AXES = ("z", "xh", "xl", "y", "core")
SIZES = (8, 2, 2, 8, 2)


def linear(z, xh, xl, y, core):
    return (((z % 8) * 2 + xh) * 2 + xl) * 16 + (y % 8) * 2 + core


def table(target):
    pairs = []
    for z in range(8):
        for xh in range(2):
            for xl in range(2):
                for y in range(8):
                    for core in range(2):
                        pairs.append((linear(z, xh, xl, y, core), linear(*target(z, xh, xl, y, core))))
    return pairs


SAME_XL = table(lambda z, xh, xl, y, core: (z, y % 2, xl, y // 2 * 2 + xh, core))
OTHER_XL = table(lambda z, xh, xl, y, core: (z, y % 2, 1 - xl, y // 2 * 2 + xh, core))
RING_X = table(lambda z, xh, xl, y, core: (z, xh, xl, y + 1 - 2 * core, core))
RING_Y = table(lambda z, xh, xl, y, core: (z, xh, xl, y - 1 + 2 * core, core))
SWAP_CORE = table(lambda z, xh, xl, y, core: (z, xh, xl, y, 1 - core))
SWAP_XH = table(lambda z, xh, xl, y, core: (z, 1 - xh, xl, y, core))
GROUPS = ((0, 1, 7, 2), (6, 3, 5, 4))
PAIRS = (0, 1, 3, 2)
IN_HBM = pl.BlockSpec(memory_space=pltpu.HBM)


def send(array, pairs):
    return lax.ppermute(array, AXES, pairs)


def after(array, *earlier):
    return lax.optimization_barrier((array, *earlier))[0]


def split(value):
    high = value.astype(jnp.bfloat16)
    low = (value - high.astype(jnp.float32)).astype(jnp.bfloat16)
    return high, low


def dot_nt(a, b):
    return lax.dot_general(a, b, (((1,), (1,)), ((), ())), preferred_element_type=jnp.float32)


def dot_nn(a, b):
    return lax.dot_general(a, b, (((1,), (0,)), ((), ())), preferred_element_type=jnp.float32)


def pieces_kernel(piece, out):
    high, low = split(piece[...])
    out[..., :128] = high
    out[..., 128:] = low


def split_pieces(group):
    count = group.shape[0]
    return pl.pallas_call(
        pieces_kernel,
        out_shape=pltpu.HBM((count, 2, 8, 64, 256), jnp.bfloat16),
        grid=(count, 2),
        in_specs=[pl.BlockSpec((1, 1, 8, 64, 128), lambda i, j: (i, j, 0, 0, 0))],
        out_specs=pl.BlockSpec((1, 1, 8, 64, 256), lambda i, j: (i, j, 0, 0, 0)),
        compiler_params=pltpu.CompilerParams(vmem_limit_bytes=8 * 1024 * 1024),
        cost_estimate=pl.CostEstimate(flops=1 << 20, bytes_accessed=4 << 20, transcendentals=0),
        name="split_pieces",
    )(group)


def amplitudes_kernel(t_own, t_oth, high_out, low_out):
    for d in range(32):
        for half, ref in enumerate((t_own, t_oth)):
            high, low = split(ref[pl.ds(d, 64, 32), :])
            high_out[d * 128 + half * 64 : d * 128 + half * 64 + 64, :] = high
            low_out[d * 128 + half * 64 : d * 128 + half * 64 + 64, :] = low


def split_amplitudes(t_own, t_oth):
    shape = pltpu.HBM((4096, 128), jnp.bfloat16)
    whole = pl.BlockSpec((4096, 128), lambda: (0, 0))
    return pl.pallas_call(
        amplitudes_kernel,
        out_shape=(shape, shape),
        out_specs=(whole, whole),
        compiler_params=pltpu.CompilerParams(vmem_limit_bytes=8 * 1024 * 1024),
        cost_estimate=pl.CostEstimate(flops=1 << 20, bytes_accessed=4 << 20, transcendentals=0),
        name="split_amplitudes",
    )(t_own.reshape(2048, 128), t_oth.reshape(2048, 128))


def ladder_kernel(place, right, own0, own1, oth0, oth1, t_high_in, t_low_in, out, r_buf, l_buf, t_high, t_low, acc, y_high, y_low, flip, r_sem, l_sem, t_sem):
    y, sign, xl_here, xh, core = (place[i] for i in range(5))

    def pair(k):
        return lax.rem(y // 2 + PAIRS[k], 4)

    def right_copy(k, order):
        where = lax.bitwise_xor(order, xl_here) * 4 + pair(k)
        return pltpu.make_async_copy(right.at[where], r_buf.at[k, order], r_sem.at[k, order])

    def left_copy(source, side, group, index):
        slot = GROUPS[group][index]
        at = lax.bitwise_and(y + (8 - slot if side == 0 else slot) * sign + 8, 7)
        half = lax.bitwise_xor(lax.bitwise_and(at, 1), xh)
        return pltpu.make_async_copy(
            source.at[index], l_buf.at[at // 2, side, half], l_sem.at[at // 2, side, half]
        )

    t_copies = [
        pltpu.make_async_copy(t_high_in, t_high, t_sem.at[0]),
        pltpu.make_async_copy(t_low_in, t_low, t_sem.at[1]),
    ]
    for order in range(2):
        right_copy(0, order).start()
    for group, sources in enumerate(((own0, oth0), (own1, oth1))):
        for index in range(4):
            for side in range(2):
                left_copy(sources[side], side, group, index).start()
        for k in (1, 2) if group == 0 else (3,):
            for order in range(2):
                right_copy(k, order).start()
    for copy in t_copies:
        copy.start()

    for k in range(4):
        for order in range(2):
            right_copy(k, order).wait()
        for side in range(2):
            for half in range(2):
                pltpu.make_async_copy(own0.at[0], l_buf.at[pair(k), side, half], l_sem.at[pair(k), side, half]).wait()
        r_high, r_low, l_high, l_low = [], [], [], []
        for order in range(2):
            high, low = split(r_buf[k, order].reshape(512, 256))
            r_high.append(high)
            r_low.append(low)
            for q_half in range(2):
                side = lax.bitwise_xor(core, q_half)
                both = jnp.concatenate([l_buf[pair(k), side, half, order] for half in range(2)], axis=1).reshape(1024, 256)
                l_high.append(both[:, :128])
                l_low.append(both[:, 128:])
        product = dot_nt(
            jnp.concatenate(r_high + r_low + r_high, axis=1),
            jnp.concatenate(l_high + l_high + l_low, axis=1),
        )
        for a in range(8):
            piece = product[:, a * 128 : a * 128 + 128]
            if k == 0:
                acc[a] = piece
            else:
                acc[a] += piece
    for copy in t_copies:
        copy.wait()
    for d in range(32):
        for a in range(8):
            high, low = split(acc[a, pl.ds(d, 16, 32), :])
            y_high[a * 16 : a * 16 + 16, d * 128 : d * 128 + 128] = high
            y_low[a * 16 : a * 16 + 16, d * 128 : d * 128 + 128] = low
    total = dot_nn(y_high[...], t_high[...]) + dot_nn(y_high[...], t_low[...]) + dot_nn(y_low[...], t_high[...])
    for a in range(8):
        flip[pl.ds(a, 16, 8), :] = total[a * 16 : a * 16 + 16]
    total = flip[...].T
    for xl in range(2):
        for each in range(2):
            for row in range(8):
                first = xl * 64 + row * 8 + each * 4
                for xh_to in range(2):
                    out[xh_to * 4 + xl * 2 + each, row * 4 : row * 4 + 4] = total[first : first + 4]


def contract(place, right, own, oth, t_split):
    return pl.pallas_call(
        ladder_kernel,
        out_shape=jax.ShapeDtypeStruct((8, 32, 128), jnp.float32),
        in_specs=[pl.BlockSpec(memory_space=pltpu.SMEM)] + [IN_HBM] * 7,
        out_specs=pl.BlockSpec(memory_space=pltpu.VMEM),
        scratch_shapes=[
            pltpu.VMEM((4, 2, 16, 32, 256), jnp.float32),
            pltpu.VMEM((4, 2, 2, 2, 8, 64, 256), jnp.bfloat16),
            pltpu.VMEM((4096, 128), jnp.bfloat16),
            pltpu.VMEM((4096, 128), jnp.bfloat16),
            pltpu.VMEM((8, 512, 128), jnp.float32),
            pltpu.VMEM((128, 4096), jnp.bfloat16),
            pltpu.VMEM((128, 4096), jnp.bfloat16),
            pltpu.VMEM((128, 128), jnp.float32),
            pltpu.SemaphoreType.DMA((4, 2)),
            pltpu.SemaphoreType.DMA((4, 2, 2)),
            pltpu.SemaphoreType.DMA((2,)),
        ],
        compiler_params=pltpu.CompilerParams(vmem_limit_bytes=60 * 1024 * 1024),
        cost_estimate=pl.CostEstimate(flops=6 << 30, bytes_accessed=16 << 20, transcendentals=0),
        name="ladder",
    )(place, right, *own, *oth, *t_split)


def pack_kernel(near, out, total):
    value = near[0]
    for part in range(1, 8):
        value += near[part]
    total[...] = value
    lane = lax.broadcasted_iota(jnp.int32, (8, 128), 1) // 16
    for z in range(8):
        packed = jnp.zeros((8, 128), jnp.float32)
        for k in range(4):
            rows = total[pl.ds(k, 8, 4), :]
            shift = (k - z) * 16 % 128
            packed = jnp.where(lane == k, pltpu.roll(rows, shift, 1) if shift else rows, packed)
        out[z * 8 : z * 8 + 8, :] = packed


def pack(near):
    return pl.pallas_call(
        pack_kernel,
        out_shape=jax.ShapeDtypeStruct((64, 128), jnp.float32),
        scratch_shapes=[pltpu.VMEM((32, 128), jnp.float32)],
        name="pack",
    )(near)


def shards(vectors_left, vectors_right, amplitudes):
    xh, y, core = (lax.axis_index(name) for name in ("xh", "y", "core"))
    place = jnp.stack([y, 1 - 2 * core, lax.axis_index("xl"), xh, core]).astype(jnp.int32)
    right = lax.all_gather(vectors_right, "z", axis=0)
    own = jnp.stack([send(vectors_left, SAME_XL), send(vectors_left, OTHER_XL)])
    x1 = send(own, RING_X)
    y1 = send(own, RING_Y)
    t_oth = send(amplitudes, SWAP_XH)
    x2 = send(x1, RING_X)
    y2 = send(after(y1, x1), RING_Y)
    own0 = jnp.stack([own, x1, y1, x2])
    oth0 = send(own0, SWAP_CORE)
    x3 = send(after(x2, y1), RING_X)
    y3 = send(after(y2, x2), RING_Y)
    x4 = send(after(x3, y2, t_oth), RING_X)
    own1 = jnp.stack([y2, x3, y3, x4])
    oth1 = send(own1, SWAP_CORE)
    t_split = split_amplitudes(amplitudes, t_oth)
    partial = contract(
        place, right, (split_pieces(own0), split_pieces(own1)), (split_pieces(oth0), split_pieces(oth1)), t_split
    )
    near = pack(lax.all_to_all(partial, ("xh", "xl", "core"), 0, 0, tiled=True))
    far = jnp.sum(lax.all_to_all(near, ("z", "y"), 0, 0, tiled=True), axis=0)
    return lax.dynamic_slice(far[:64].reshape(4, 2, 8), (0, xh, 0), (4, 1, 8)).reshape(4, 8, 1)


def solution(mesh):
    fine = Mesh(mesh.devices.reshape(SIZES), AXES)
    c_axes, d_axes = ("z", "xh"), ("xl", "y", "core")
    return jax.shard_map(
        shards,
        mesh=fine,
        in_specs=(P(None, c_axes, d_axes), P(None, d_axes, c_axes), P(c_axes, d_axes, None)),
        out_specs=P(d_axes, None, c_axes),
        check_vma=False,
    )
```

time: 499 us -> 181 us (0.36)
  the two profiles are of different devices: /device:TPU:2 before, /device:TPU:1 now
where the time goes in v3:
time: 181 us; the launch traced here: 180 us
  starting transfers between devices  68.3 us (38%)
  waiting for transfers between devices  44.3 us (24%)
  Pallas kernels  38.9 us (21%)
  between operations  13.6 us (8%)
  blocking collectives  9.52 us (5%)
  local copies, waits for them, and re-layouts  3.55 us (2%)
  other arithmetic  1.84 us (1%)
    ppermute x12, starting transfers between devices, send(): return lax.ppermute(array, AXES, pairs)  48.6 us
    ppermute x12, waiting for transfers between devices, send(): return lax.ppermute(array, AXES, pairs)  32.7 us
    pallas_call x4, Pallas kernels, split_pieces(): pl.pallas_call(pieces_kernel, out_shape=pltpu.HBM((count, 2, 8, 64, 256),...  20.4 us
    all_to_all x1, starting transfers between devices, shards(): far = jnp.sum(lax.all_to_all(near, ('z', 'y'), 0, 0, tiled=True), axis=0)  19.8 us
    pallas_call x1, Pallas kernels, contract(): pl.pallas_call(ladder_kernel, out_shape=jax.ShapeDtypeStruct((8, 32, 128)...  13.7 us
    all_to_all x1, waiting for transfers between devices, shards(): far = jnp.sum(lax.all_to_all(near, ('z', 'y'), 0, 0, tiled=True), axis=0)  10.9 us
    all_to_all x1, blocking collectives, shards(): near = pack(lax.all_to_all(partial, ('xh', 'xl', 'core'), 0, 0, tiled=True))  9.52 us
  transfers between devices with their start and end apart: 14, of which 6 were waited for; matrix products, arithmetic and copies ran while one was open for 1% of the time, Pallas kernels for 13%

profile of v3, /device:TPU:1, one launch (start us, length us, event | category | flops | bytes accessed | tf_op | source)
XLA Modules:
  0.0 180.0 jit_solution(18116237798263878160)
XLA Ops:
  6.5 0.0 copy-start
  6.5 0.0 all-gather.3.cloned.1.call-start
  6.5 0.7 all-gather.3.cloned.1.call-update
  7.3 1.6 collective-permute-start
  8.9 3.9 %collective-permute-start.1 = (f32[8,64,128]{2,1,0:T(8,128)}, f32[8,64,128]{2,1,0:T(8,128)S(1)}, u32[]{:S(2)}, u32[]{:S(2)}) collective-permute-start(f32[8,64,128]{2,1,0:T(8,128)} %param.3), channel_id=1, source_target_pairs={{0,16},{1,17},{2,48},{3,49},{4,20},{5,21},{6,52},{7,53},{8,24},{9,... | collective-permute-start | bytes 786440 | tf_op jit(solution)/shard_map/ppermute | solution.py:39
  12.8 0.0 collective-permute-done
  12.8 11.0 %collective-permute-done.1 = f32[8,64,128]{2,1,0:T(8,128)S(1)} collective-permute-done((f32[8,64,128]{2,1,0:T(8,128)}, f32[8,64,128]{2,1,0:T(8,128)S(1)}, u32[]{:S(2)}, u32[]{:S(2)}) %collective-permute-start.1) | collective-permute-done | bytes 262176 | tf_op jit(solution)/shard_map/ppermute | solution.py:39
  23.8 0.1 fusion
  24.0 7.4 %collective-permute-start.2 = (f32[2,8,64,128]{3,2,1,0:T(8,128)S(1)}, f32[2,8,64,128]{3,2,1,0:T(8,128)S(1)}, u32[]{:S(2)}, u32[]{:S(2)}) collective-permute-start(f32[2,8,64,128]{3,2,1,0:T(8,128)S(1)} %get-tuple-element.18), channel_id=1, source_target_pairs={{0,2},{1,15},{2,4},{3,1},{4,6},{5,3},{6,8},{7,5},{8,10},{9,7},{10,... | collective-permute-start | bytes 1572872 | tf_op jit(solution)/shard_map/ppermute | solution.py:39
  31.4 1.9 %collective-permute-start.3 = (f32[2,8,64,128]{3,2,1,0:T(8,128)S(1)}, f32[2,8,64,128]{3,2,1,0:T(8,128)S(1)}, u32[]{:S(2)}, u32[]{:S(2)}) collective-permute-start(f32[2,8,64,128]{3,2,1,0:T(8,128)S(1)} %get-tuple-element.18), channel_id=1, source_target_pairs={{0,14},{1,3},{2,0},{3,5},{4,2},{5,7},{6,4},{7,9},{8,6},{9,11},{10,... | collective-permute-start | bytes 1572872 | tf_op jit(solution)/shard_map/ppermute | solution.py:39
  33.3 5.9 %collective-permute-done.2 = f32[2,8,64,128]{3,2,1,0:T(8,128)S(1)} collective-permute-done((f32[2,8,64,128]{3,2,1,0:T(8,128)S(1)}, f32[2,8,64,128]{3,2,1,0:T(8,128)S(1)}, u32[]{:S(2)}, u32[]{:S(2)}) %collective-permute-start.2) | collective-permute-done | bytes 524320 | tf_op jit(solution)/shard_map/ppermute | solution.py:39
  39.2 5.4 %collective-permute-start.4 = (f32[2,8,64,128]{3,2,1,0:T(8,128)S(1)}, f32[2,8,64,128]{3,2,1,0:T(8,128)S(1)}, u32[]{:S(2)}, u32[]{:S(2)}) collective-permute-start(f32[2,8,64,128]{3,2,1,0:T(8,128)S(1)} %collective-permute-done.2), channel_id=1, source_target_pairs={{0,2},{1,15},{2,4},{3,1},{4,6},{5,3},{6,8},{7,5},{8,10},{9,7},{10,... | collective-permute-start | bytes 1572872 | tf_op jit(solution)/shard_map/ppermute | solution.py:39
  44.6 0.0 copy-done
  44.6 4.2 %collective-permute-start.8 = (f32[64,32,128]{2,1,0:T(8,128)S(1)}, f32[64,32,128]{2,1,0:T(8,128)S(1)}, u32[]{:S(2)}, u32[]{:S(2)}) collective-permute-start(f32[64,32,128]{2,1,0:T(8,128)S(1)} %copy-done), channel_id=1, source_target_pairs={{0,32},{1,33},{2,34},{3,35},{4,36},{5,37},{6,38},{7,39},{8,40},{9,... | collective-permute-start | bytes 3145736 | tf_op jit(solution)/shard_map/ppermute | solution.py:39
  48.8 0.0 collective-permute-done.3
  48.8 1.9 %collective-permute-start.5 = (f32[2,8,64,128]{3,2,1,0:T(8,128)S(1)}, f32[2,8,64,128]{3,2,1,0:T(8,128)S(1)}, u32[]{:S(2)}, u32[]{:S(2)}) collective-permute-start(f32[2,8,64,128]{3,2,1,0:T(8,128)S(1)} %collective-permute-done.3), channel_id=1, source_target_pairs={{0,14},{1,3},{2,0},{3,5},{4,2},{5,7},{6,4},{7,9},{8,6},{9,11},{10,... | collective-permute-start | bytes 1572872 | tf_op jit(solution)/shard_map/ppermute | solution.py:39
  50.8 0.0 collective-permute-done.4
  50.8 5.3 %collective-permute-start.6 = (f32[2,8,64,128]{3,2,1,0:T(8,128)S(1)}, f32[2,8,64,128]{3,2,1,0:T(8,128)S(1)}, u32[]{:S(2)}, u32[]{:S(2)}) collective-permute-start(f32[2,8,64,128]{3,2,1,0:T(8,128)S(1)} %collective-permute-done.4), channel_id=1, source_target_pairs={{0,2},{1,15},{2,4},{3,1},{4,6},{5,3},{6,8},{7,5},{8,10},{9,7},{10,... | collective-permute-start | bytes 1572872 | tf_op jit(solution)/shard_map/ppermute | solution.py:39
  56.1 5.6 %collective-permute-done.5 = f32[2,8,64,128]{3,2,1,0:T(8,128)S(1)} collective-permute-done((f32[2,8,64,128]{3,2,1,0:T(8,128)S(1)}, f32[2,8,64,128]{3,2,1,0:T(8,128)S(1)}, u32[]{:S(2)}, u32[]{:S(2)}) %collective-permute-start.5) | collective-permute-done | bytes 524320 | tf_op jit(solution)/shard_map/ppermute | solution.py:39
  61.7 1.9 %collective-permute-start.7 = (f32[2,8,64,128]{3,2,1,0:T(8,128)S(1)}, f32[2,8,64,128]{3,2,1,0:T(8,128)S(1)}, u32[]{:S(2)}, u32[]{:S(2)}) collective-permute-start(f32[2,8,64,128]{3,2,1,0:T(8,128)S(1)} %collective-permute-done.5), channel_id=1, source_target_pairs={{0,14},{1,3},{2,0},{3,5},{4,2},{5,7},{6,4},{7,9},{8,6},{9,11},{10,... | collective-permute-start | bytes 1572872 | tf_op jit(solution)/shard_map/ppermute | solution.py:39
  63.6 7.7 %collective-permute-done.8 = f32[64,32,128]{2,1,0:T(8,128)S(1)} collective-permute-done((f32[64,32,128]{2,1,0:T(8,128)S(1)}, f32[64,32,128]{2,1,0:T(8,128)S(1)}, u32[]{:S(2)}, u32[]{:S(2)}) %collective-permute-start.8) | collective-permute-done | bytes 1048608 | tf_op jit(solution)/shard_map/ppermute | solution.py:39
  71.3 0.0 copy-start.1
  71.3 1.0 copy-done.1
  72.2 0.0 collective-permute-done.6
  72.2 1.9 %collective-permute-start.9 = (f32[2,8,64,128]{3,2,1,0:T(8,128)S(1)}, f32[2,8,64,128]{3,2,1,0:T(8,128)S(1)}, u32[]{:S(2)}, u32[]{:S(2)}) collective-permute-start(f32[2,8,64,128]{3,2,1,0:T(8,128)S(1)} %collective-permute-done.6), channel_id=1, source_target_pairs={{0,2},{1,15},{2,4},{3,1},{4,6},{5,3},{6,8},{7,5},{8,10},{9,7},{10,... | collective-permute-start | bytes 1572872 | tf_op jit(solution)/shard_map/ppermute | solution.py:39
  74.1 0.1 pad_maximum_fusion.piece
  74.3 6.4 %collective-permute-start.10 = (f32[4,2,8,64,128]{4,3,2,1,0:T(8,128)S(1)}, f32[4,2,8,64,128]{4,3,2,1,0:T(8,128)}, u32[]{:S(2)}, u32[]{:S(2)}) collective-permute-start(f32[4,2,8,64,128]{4,3,2,1,0:T(8,128)S(1)} %pad_maximum_fusion.piece), channel_id=1, source_target_pairs={{0,1},{1,0},{2,3},{3,2},{4,5},{5,4},{6,7},{7,6},{8,9},{9,8},{10,11... | collective-permute-start | bytes 6291464 | tf_op jit(solution)/shard_map/ppermute | solution.py:39
  80.7 0.0 collective-permute-done.7
  80.7 2.6 %collective-permute-done.9 = f32[2,8,64,128]{3,2,1,0:T(8,128)S(1)} collective-permute-done((f32[2,8,64,128]{3,2,1,0:T(8,128)S(1)}, f32[2,8,64,128]{3,2,1,0:T(8,128)S(1)}, u32[]{:S(2)}, u32[]{:S(2)}) %collective-permute-start.9) | collective-permute-done | bytes 524320 | tf_op jit(solution)/shard_map/ppermute | solution.py:39
  83.3 1.5 pad_maximum_fusion.1.piece
  84.8 6.6 %collective-permute-start.11 = (f32[4,2,8,64,128]{4,3,2,1,0:T(8,128)}, f32[4,2,8,64,128]{4,3,2,1,0:T(8,128)}, u32[]{:S(2)}, u32[]{:S(2)}) collective-permute-start(f32[4,2,8,64,128]{4,3,2,1,0:T(8,128)} %pad_maximum_fusion.1.piece), channel_id=1, source_target_pairs={{0,1},{1,0},{2,3},{3,2},{4,5},{5,4},{6,7},{7,6},{8,9},{9,8},{10,11... | collective-permute-start | bytes 6291464 | tf_op jit(solution)/shard_map/ppermute | solution.py:39
  91.4 0.7 stack.62.place
  92.1 1.2 copy-done.2
  93.3 3.1 %split_amplitudes.1 = (bf16[4096,128]{1,0:T(8,128)(2,1)}, bf16[4096,128]{1,0:T(8,128)(2,1)}) custom-call(f32[2048,128]{1,0:T(8,128)S(1)} %bitcast.27, f32[2048,128]{1,0:T(8,128)S(1)} %bitcast.28), custom_call_target="tpu_custom_call" | custom-call | flops 1048576 | bytes 4194304 | tf_op jit(solution)/shard_map/split_amplitudes/pallas_call | solution.py:91
  96.4 3.1 %split_pieces.4.own0 = bf16[4,2,8,64,256]{4,3,2,1,0:T(8,128)(2,1)} custom-call(f32[4,2,8,64,128]{4,3,2,1,0:T(8,128)S(1)} %pad_maximum_fusion.piece), custom_call_target="tpu_custom_call" | custom-call | flops 1048576 | bytes 4194304 | tf_op jit(solution)/shard_map/split_pieces/pallas_call | solution.py:68
  99.5 5.8 %split_pieces.5.own1 = bf16[4,2,8,64,256]{4,3,2,1,0:T(8,128)(2,1)} custom-call(f32[4,2,8,64,128]{4,3,2,1,0:T(8,128)} %pad_maximum_fusion.1.piece), custom_call_target="tpu_custom_call" | custom-call | flops 1048576 | bytes 4194304 | tf_op jit(solution)/shard_map/split_pieces/pallas_call | solution.py:68
  105.3 0.0 collective-permute-done.10.piece
  105.3 5.8 %split_pieces.6.oth0 = bf16[4,2,8,64,256]{4,3,2,1,0:T(8,128)(2,1)} custom-call(f32[4,2,8,64,128]{4,3,2,1,0:T(8,128)} %collective-permute-done.10.piece), custom_call_target="tpu_custom_call" | custom-call | flops 1048576 | bytes 4194304 | tf_op jit(solution)/shard_map/split_pieces/pallas_call | solution.py:68
  111.0 0.0 collective-permute-done.11.piece
  111.0 5.8 %split_pieces.7.oth1 = bf16[4,2,8,64,256]{4,3,2,1,0:T(8,128)(2,1)} custom-call(f32[4,2,8,64,128]{4,3,2,1,0:T(8,128)} %collective-permute-done.11.piece), custom_call_target="tpu_custom_call" | custom-call | flops 1048576 | bytes 4194304 | tf_op jit(solution)/shard_map/split_pieces/pallas_call | solution.py:68
  116.8 13.7 %ladder.1 = f32[8,32,128]{2,1,0:T(8,128)} custom-call(s32[5]{0:T(128)} %stack.62.place, f32[8,16,32,256]{3,2,1,0:T(8,128)} %bitcast.40, bf16[4,2,8,64,256]{4,3,2,1,0:T(8,128)(2,1)} %split_pieces.4.own0, bf16[4,2,8,64,256]{4,3,2,1,0:T(8,128)(2,1)} %split_pieces.5.own1, bf16[4,2,8,64,256]{4,3,2,1,0:T(8,128)(2,1)} %split_pieces.6.oth0, ...), custom_call_target="tpu_custom_call" | custom-call | flops 6442450944 | bytes 16777216 | tf_op jit(solution)/shard_map/ladder/pallas_call | solution.py:181
  130.6 9.5 %all_to_all.14.near = f32[8,32,128]{2,1,0:T(8,128)} all-to-all(f32[8,32,128]{2,1,0:T(8,128)} %ladder.1), channel_id=1, replica_groups=mesh['z'=8,'xh'=2,'xl'=2,'y'=8,'core'=2] {'xh','xl','core'}, dimensions={0} | all-to-all | bytes 262144 | tf_op jit(solution)/shard_map/all_to_all | solution.py:250
  140.1 1.6 pack.1
  141.7 19.8 %all-to-all-start.1 = ((f32[64,1,128]{2,1,0:T(1,128)}), f32[64,1,128]{2,1,0:T(1,128)S(1)}, u32[]{:S(2)}, u32[]{:S(2)}) async-start(f32[64,1,128]{2,1,0:T(1,128)} %bitcast.38), calls=%async_computation.1 | async-start | bytes 65536 | tf_op jit(solution)/shard_map/all_to_all | solution.py:251
  161.5 10.9 %all-to-all-done.1 = f32[64,1,128]{2,1,0:T(1,128)S(1)} async-done(((f32[64,1,128]{2,1,0:T(1,128)}), f32[64,1,128]{2,1,0:T(1,128)S(1)}, u32[]{:S(2)}, u32[]{:S(2)}) %all-to-all-start.1) | async-done | bytes 32800 | tf_op jit(solution)/shard_map/all_to_all | solution.py:251
  172.3 0.1 reduce_sum.9
  172.4 0.1 reshape.24
  172.5 0.6 dynamic-slice_bitcast_fusion
  (2 shorter events, 0.0 us)
Async XLA Ops:
  6.5 38.0 %copy-start = (f32[64,32,128]{2,1,0:T(8,128)S(1)}, f32[64,32,128]{2,1,0:T(8,128)}, u32[]{:S(2)}) copy-start(f32[64,32,128]{2,1,0:T(8,128)} %param.5) | copy-start | bytes 3145732
  6.5 110.3 %all-gather.3.cloned.1.call-start = ((), (), s32[]{:S(2)}) async-start(), calls=%async_computation.2 | async-start | bytes 4718592 | tf_op jit(solution)/shard_map/all_gather | solution.py:232
  7.3 5.6 %collective-permute-start = (f32[8,64,128]{2,1,0:T(8,128)}, f32[8,64,128]{2,1,0:T(8,128)S(1)}, u32[]{:S(2)}, u32[]{:S(2)}) collective-permute-start(f32[8,64,128]{2,1,0:T(8,128)} %param.3), channel_id=1, source_target_pairs={{0,0},{1,1},{2,32},{3,33},{4,4},{5,5},{6,36},{7,37},{8,8},{9,9},{1... | collective-permute-start | bytes 786440 | tf_op jit(solution)/shard_map/ppermute | solution.py:39
  8.9 15.0 %collective-permute-start.1 = (f32[8,64,128]{2,1,0:T(8,128)}, f32[8,64,128]{2,1,0:T(8,128)S(1)}, u32[]{:S(2)}, u32[]{:S(2)}) collective-permute-start(f32[8,64,128]{2,1,0:T(8,128)} %param.3), channel_id=1, source_target_pairs={{0,16},{1,17},{2,48},{3,49},{4,20},{5,21},{6,52},{7,53},{8,24},{9,... | collective-permute-start | bytes 786440 | tf_op jit(solution)/shard_map/ppermute | solution.py:39
  24.0 15.2 %collective-permute-start.2 = (f32[2,8,64,128]{3,2,1,0:T(8,128)S(1)}, f32[2,8,64,128]{3,2,1,0:T(8,128)S(1)}, u32[]{:S(2)}, u32[]{:S(2)}) collective-permute-start(f32[2,8,64,128]{3,2,1,0:T(8,128)S(1)} %get-tuple-element.18), channel_id=1, source_target_pairs={{0,2},{1,15},{2,4},{3,1},{4,6},{5,3},{6,8},{7,5},{8,10},{9,7},{10,... | collective-permute-start | bytes 1572872 | tf_op jit(solution)/shard_map/ppermute | solution.py:39
  31.4 17.5 %collective-permute-start.3 = (f32[2,8,64,128]{3,2,1,0:T(8,128)S(1)}, f32[2,8,64,128]{3,2,1,0:T(8,128)S(1)}, u32[]{:S(2)}, u32[]{:S(2)}) collective-permute-start(f32[2,8,64,128]{3,2,1,0:T(8,128)S(1)} %get-tuple-element.18), channel_id=1, source_target_pairs={{0,14},{1,3},{2,0},{3,5},{4,2},{5,7},{6,4},{7,9},{8,6},{9,11},{10,... | collective-permute-start | bytes 1572872 | tf_op jit(solution)/shard_map/ppermute | solution.py:39
  39.2 11.6 %collective-permute-start.4 = (f32[2,8,64,128]{3,2,1,0:T(8,128)S(1)}, f32[2,8,64,128]{3,2,1,0:T(8,128)S(1)}, u32[]{:S(2)}, u32[]{:S(2)}) collective-permute-start(f32[2,8,64,128]{3,2,1,0:T(8,128)S(1)} %collective-permute-done.2), channel_id=1, source_target_pairs={{0,2},{1,15},{2,4},{3,1},{4,6},{5,3},{6,8},{7,5},{8,10},{9,7},{10,... | collective-permute-start | bytes 1572872 | tf_op jit(solution)/shard_map/ppermute | solution.py:39
  44.6 26.7 %collective-permute-start.8 = (f32[64,32,128]{2,1,0:T(8,128)S(1)}, f32[64,32,128]{2,1,0:T(8,128)S(1)}, u32[]{:S(2)}, u32[]{:S(2)}) collective-permute-start(f32[64,32,128]{2,1,0:T(8,128)S(1)} %copy-done), channel_id=1, source_target_pairs={{0,32},{1,33},{2,34},{3,35},{4,36},{5,37},{6,38},{7,39},{8,40},{9,... | collective-permute-start | bytes 3145736 | tf_op jit(solution)/shard_map/ppermute | solution.py:39
  48.8 12.8 %collective-permute-start.5 = (f32[2,8,64,128]{3,2,1,0:T(8,128)S(1)}, f32[2,8,64,128]{3,2,1,0:T(8,128)S(1)}, u32[]{:S(2)}, u32[]{:S(2)}) collective-permute-start(f32[2,8,64,128]{3,2,1,0:T(8,128)S(1)} %collective-permute-done.3), channel_id=1, source_target_pairs={{0,14},{1,3},{2,0},{3,5},{4,2},{5,7},{6,4},{7,9},{8,6},{9,11},{10,... | collective-permute-start | bytes 1572872 | tf_op jit(solution)/shard_map/ppermute | solution.py:39
  50.8 21.5 %collective-permute-start.6 = (f32[2,8,64,128]{3,2,1,0:T(8,128)S(1)}, f32[2,8,64,128]{3,2,1,0:T(8,128)S(1)}, u32[]{:S(2)}, u32[]{:S(2)}) collective-permute-start(f32[2,8,64,128]{3,2,1,0:T(8,128)S(1)} %collective-permute-done.4), channel_id=1, source_target_pairs={{0,2},{1,15},{2,4},{3,1},{4,6},{5,3},{6,8},{7,5},{8,10},{9,7},{10,... | collective-permute-start | bytes 1572872 | tf_op jit(solution)/shard_map/ppermute | solution.py:39
  61.7 19.0 %collective-permute-start.7 = (f32[2,8,64,128]{3,2,1,0:T(8,128)S(1)}, f32[2,8,64,128]{3,2,1,0:T(8,128)S(1)}, u32[]{:S(2)}, u32[]{:S(2)}) collective-permute-start(f32[2,8,64,128]{3,2,1,0:T(8,128)S(1)} %collective-permute-done.5), channel_id=1, source_target_pairs={{0,14},{1,3},{2,0},{3,5},{4,2},{5,7},{6,4},{7,9},{8,6},{9,11},{10,... | collective-permute-start | bytes 1572872 | tf_op jit(solution)/shard_map/ppermute | solution.py:39
  71.3 1.0 copy-start.1
  72.2 11.1 %collective-permute-start.9 = (f32[2,8,64,128]{3,2,1,0:T(8,128)S(1)}, f32[2,8,64,128]{3,2,1,0:T(8,128)S(1)}, u32[]{:S(2)}, u32[]{:S(2)}) collective-permute-start(f32[2,8,64,128]{3,2,1,0:T(8,128)S(1)} %collective-permute-done.6), channel_id=1, source_target_pairs={{0,2},{1,15},{2,4},{3,1},{4,6},{5,3},{6,8},{7,5},{8,10},{9,7},{10,... | collective-permute-start | bytes 1572872 | tf_op jit(solution)/shard_map/ppermute | solution.py:39
  74.3 31.0 %collective-permute-start.10 = (f32[4,2,8,64,128]{4,3,2,1,0:T(8,128)S(1)}, f32[4,2,8,64,128]{4,3,2,1,0:T(8,128)}, u32[]{:S(2)}, u32[]{:S(2)}) collective-permute-start(f32[4,2,8,64,128]{4,3,2,1,0:T(8,128)S(1)} %pad_maximum_fusion.piece), channel_id=1, source_target_pairs={{0,1},{1,0},{2,3},{3,2},{4,5},{5,4},{6,7},{7,6},{8,9},{9,8},{10,11... | collective-permute-start | bytes 6291464 | tf_op jit(solution)/shard_map/ppermute | solution.py:39
  84.8 26.2 %collective-permute-start.11 = (f32[4,2,8,64,128]{4,3,2,1,0:T(8,128)}, f32[4,2,8,64,128]{4,3,2,1,0:T(8,128)}, u32[]{:S(2)}, u32[]{:S(2)}) collective-permute-start(f32[4,2,8,64,128]{4,3,2,1,0:T(8,128)} %pad_maximum_fusion.1.piece), channel_id=1, source_target_pairs={{0,1},{1,0},{2,3},{3,2},{4,5},{5,4},{6,7},{7,6},{8,9},{9,8},{10,11... | collective-permute-start | bytes 6291464 | tf_op jit(solution)/shard_map/ppermute | solution.py:39
  92.1 1.2 copy-start.2
  141.7 30.6 %all-to-all-start.1 = ((f32[64,1,128]{2,1,0:T(1,128)}), f32[64,1,128]{2,1,0:T(1,128)S(1)}, u32[]{:S(2)}, u32[]{:S(2)}) async-start(f32[64,1,128]{2,1,0:T(1,128)} %bitcast.38), calls=%async_computation.1 | async-start | bytes 65536 | tf_op jit(solution)/shard_map/all_to_all | solution.py:251
Sparse Core Ops, SparseCore 0:
  9.4 63.7 all-gather.2

commit v4 on v3

--- a/solution.py
+++ b/solution.py
@@ -30,9 +30,8 @@
 RING_Y = table(lambda z, xh, xl, y, core: (z, xh, xl, y - 1 + 2 * core, core))
 SWAP_CORE = table(lambda z, xh, xl, y, core: (z, xh, xl, y, 1 - core))
 SWAP_XH = table(lambda z, xh, xl, y, core: (z, 1 - xh, xl, y, core))
-GROUPS = ((0, 1, 7, 2), (6, 3, 5, 4))
 PAIRS = (0, 1, 3, 2)
-IN_HBM = pl.BlockSpec(memory_space=pltpu.HBM)
+NEEDED = ((0, 1, 7), (2, 6, 3, 5), (4,), ())
 
 
 def send(array, pairs):
@@ -55,26 +54,6 @@
 
 def dot_nn(a, b):
     return lax.dot_general(a, b, (((1,), (0,)), ((), ())), preferred_element_type=jnp.float32)
-
-
-def pieces_kernel(piece, out):
-    high, low = split(piece[...])
-    out[..., :128] = high
-    out[..., 128:] = low
-
-
-def split_pieces(group):
-    count = group.shape[0]
-    return pl.pallas_call(
-        pieces_kernel,
-        out_shape=pltpu.HBM((count, 2, 8, 64, 256), jnp.bfloat16),
-        grid=(count, 2),
-        in_specs=[pl.BlockSpec((1, 1, 8, 64, 128), lambda i, j: (i, j, 0, 0, 0))],
-        out_specs=pl.BlockSpec((1, 1, 8, 64, 256), lambda i, j: (i, j, 0, 0, 0)),
-        compiler_params=pltpu.CompilerParams(vmem_limit_bytes=8 * 1024 * 1024),
-        cost_estimate=pl.CostEstimate(flops=1 << 20, bytes_accessed=4 << 20, transcendentals=0),
-        name="split_pieces",
-    )(group)
 
 
 def amplitudes_kernel(t_own, t_oth, high_out, low_out):
@@ -86,19 +65,19 @@
 
 
 def split_amplitudes(t_own, t_oth):
-    shape = pltpu.HBM((4096, 128), jnp.bfloat16)
-    whole = pl.BlockSpec((4096, 128), lambda: (0, 0))
+    shape = jax.ShapeDtypeStruct((4096, 128), jnp.bfloat16)
     return pl.pallas_call(
         amplitudes_kernel,
         out_shape=(shape, shape),
-        out_specs=(whole, whole),
         compiler_params=pltpu.CompilerParams(vmem_limit_bytes=8 * 1024 * 1024),
         cost_estimate=pl.CostEstimate(flops=1 << 20, bytes_accessed=4 << 20, transcendentals=0),
         name="split_amplitudes",
     )(t_own.reshape(2048, 128), t_oth.reshape(2048, 128))
 
 
-def ladder_kernel(place, right, own0, own1, oth0, oth1, t_high_in, t_low_in, out, r_buf, l_buf, t_high, t_low, acc, y_high, y_low, flip, r_sem, l_sem, t_sem):
+def ladder_kernel(place, right, *refs):
+    pieces, (t_high_in, t_low_in, out) = (refs[:8], refs[8:16]), refs[16:19]
+    r_buf, raw, parts, t_high, t_low, acc, y_high, y_low, flip, r_sem, l_sem, t_sem = refs[19:]
     y, sign, xl_here, xh, core = (place[i] for i in range(5))
 
     def pair(k):
@@ -108,44 +87,44 @@
         where = lax.bitwise_xor(order, xl_here) * 4 + pair(k)
         return pltpu.make_async_copy(right.at[where], r_buf.at[k, order], r_sem.at[k, order])
 
-    def left_copy(source, side, group, index):
-        slot = GROUPS[group][index]
-        at = lax.bitwise_and(y + (8 - slot if side == 0 else slot) * sign + 8, 7)
-        half = lax.bitwise_xor(lax.bitwise_and(at, 1), xh)
-        return pltpu.make_async_copy(
-            source.at[index], l_buf.at[at // 2, side, half], l_sem.at[at // 2, side, half]
-        )
+    def left_copy(side, slot):
+        return pltpu.make_async_copy(pieces[side][slot], raw.at[side, slot], l_sem.at[side, slot])
+
+    def left(k, q_half, half, order):
+        at = 2 * pair(k) + lax.bitwise_xor(half, xh)
+        steps = (y - at) * sign
+        side = lax.bitwise_xor(core, q_half)
+        slot = lax.bitwise_and(8 + steps - 2 * side * steps, 7)
+        return parts[side, slot, order]
 
     t_copies = [
         pltpu.make_async_copy(t_high_in, t_high, t_sem.at[0]),
         pltpu.make_async_copy(t_low_in, t_low, t_sem.at[1]),
     ]
-    for order in range(2):
-        right_copy(0, order).start()
-    for group, sources in enumerate(((own0, oth0), (own1, oth1))):
-        for index in range(4):
+    for k in range(4):
+        for slot in NEEDED[k]:
             for side in range(2):
-                left_copy(sources[side], side, group, index).start()
-        for k in (1, 2) if group == 0 else (3,):
-            for order in range(2):
-                right_copy(k, order).start()
+                left_copy(side, slot).start()
+        for order in range(2):
+            right_copy(k, order).start()
     for copy in t_copies:
         copy.start()
-
     for k in range(4):
+        for slot in NEEDED[k]:
+            for side in range(2):
+                left_copy(side, slot).wait()
+                high, low = split(raw[side, slot])
+                parts[side, slot, :, :, :, :128] = high
+                parts[side, slot, :, :, :, 128:] = low
         for order in range(2):
             right_copy(k, order).wait()
-        for side in range(2):
-            for half in range(2):
-                pltpu.make_async_copy(own0.at[0], l_buf.at[pair(k), side, half], l_sem.at[pair(k), side, half]).wait()
         r_high, r_low, l_high, l_low = [], [], [], []
         for order in range(2):
             high, low = split(r_buf[k, order].reshape(512, 256))
             r_high.append(high)
             r_low.append(low)
             for q_half in range(2):
-                side = lax.bitwise_xor(core, q_half)
-                both = jnp.concatenate([l_buf[pair(k), side, half, order] for half in range(2)], axis=1).reshape(1024, 256)
+                both = jnp.concatenate([left(k, q_half, half, order) for half in range(2)], axis=1).reshape(1024, 256)
                 l_high.append(both[:, :128])
                 l_low.append(both[:, 128:])
         product = dot_nt(
@@ -181,11 +160,12 @@
     return pl.pallas_call(
         ladder_kernel,
         out_shape=jax.ShapeDtypeStruct((8, 32, 128), jnp.float32),
-        in_specs=[pl.BlockSpec(memory_space=pltpu.SMEM)] + [IN_HBM] * 7,
+        in_specs=[pl.BlockSpec(memory_space=pltpu.SMEM)] + [pl.BlockSpec(memory_space=pl.ANY)] * 19,
         out_specs=pl.BlockSpec(memory_space=pltpu.VMEM),
         scratch_shapes=[
             pltpu.VMEM((4, 2, 16, 32, 256), jnp.float32),
-            pltpu.VMEM((4, 2, 2, 2, 8, 64, 256), jnp.bfloat16),
+            pltpu.VMEM((2, 8, 2, 8, 64, 128), jnp.float32),
+            pltpu.VMEM((2, 8, 2, 8, 64, 256), jnp.bfloat16),
             pltpu.VMEM((4096, 128), jnp.bfloat16),
             pltpu.VMEM((4096, 128), jnp.bfloat16),
             pltpu.VMEM((8, 512, 128), jnp.float32),
@@ -193,7 +173,7 @@
             pltpu.VMEM((128, 4096), jnp.bfloat16),
             pltpu.VMEM((128, 128), jnp.float32),
             pltpu.SemaphoreType.DMA((4, 2)),
-            pltpu.SemaphoreType.DMA((4, 2, 2)),
+            pltpu.SemaphoreType.DMA((2, 8)),
             pltpu.SemaphoreType.DMA((2,)),
         ],
         compiler_params=pltpu.CompilerParams(vmem_limit_bytes=60 * 1024 * 1024),
@@ -231,22 +211,18 @@
     place = jnp.stack([y, 1 - 2 * core, lax.axis_index("xl"), xh, core]).astype(jnp.int32)
     right = lax.all_gather(vectors_right, "z", axis=0)
     own = jnp.stack([send(vectors_left, SAME_XL), send(vectors_left, OTHER_XL)])
+    t_oth = send(amplitudes, SWAP_XH)
     x1 = send(own, RING_X)
     y1 = send(own, RING_Y)
-    t_oth = send(amplitudes, SWAP_XH)
     x2 = send(x1, RING_X)
     y2 = send(after(y1, x1), RING_Y)
-    own0 = jnp.stack([own, x1, y1, x2])
-    oth0 = send(own0, SWAP_CORE)
-    x3 = send(after(x2, y1), RING_X)
+    x3 = send(after(x2, y1, t_oth), RING_X)
     y3 = send(after(y2, x2), RING_Y)
-    x4 = send(after(x3, y2, t_oth), RING_X)
-    own1 = jnp.stack([y2, x3, y3, x4])
-    oth1 = send(own1, SWAP_CORE)
+    x4 = send(after(x3, y2), RING_X)
+    left_own = [own, x1, x2, x3, x4, y3, y2, y1]
     t_split = split_amplitudes(amplitudes, t_oth)
-    partial = contract(
-        place, right, (split_pieces(own0), split_pieces(own1)), (split_pieces(oth0), split_pieces(oth1)), t_split
-    )
+    left_oth = [send(after(piece, *t_split) if piece is y3 else piece, SWAP_CORE) for piece in left_own]
+    partial = contract(place, right, left_own, left_oth, t_split)
     near = pack(lax.all_to_all(partial, ("xh", "xl", "core"), 0, 0, tiled=True))
     far = jnp.sum(lax.all_to_all(near, ("z", "y"), 0, 0, tiled=True), axis=0)
     return lax.dynamic_slice(far[:64].reshape(4, 2, 8), (0, xh, 0), (4, 1, 8)).reshape(4, 8, 1)

time: 181 us -> 161 us (0.89)
  Pallas kernels: 38.9 us -> 18.3 us
  starting transfers between devices: 68.3 us -> 80 us
  waiting for transfers between devices: 44.3 us -> 33.6 us
    pallas_call x5 -> x1, Pallas kernels: 23.5 us -> 1.76 us  [split_amplitudes(): pl.pallas_call(amplitudes_kernel, out_shape=(shape, shape), compiler_para...]
    ppermute x12 -> x18, starting transfers between devices: 48.6 us -> 64.4 us  [send(): return lax.ppermute(array, AXES, pairs)]
    ppermute x12 -> x18, waiting for transfers between devices: 32.7 us -> 22.1 us  [send(): return lax.ppermute(array, AXES, pairs)]
    all_to_all x1, starting transfers between devices: 19.8 us -> 15.7 us  [shards(): far = jnp.sum(lax.all_to_all(near, ('z', 'y'), 0, 0, tiled=True), axis=0)]
  transfers between devices with their start and end apart: 14 -> 20, of which waited for: 6 -> 7; matrix products, arithmetic and copies ran while one was open for 1% -> 0% of each run, Pallas kernels for 13% -> 1%
where the time goes in v4:
time: 161 us; the launch traced here: 160 us
  starting transfers between devices  80 us (50%)
  waiting for transfers between devices  33.6 us (21%)
  Pallas kernels  18.3 us (11%)
  between operations  13.7 us (9%)
  blocking collectives  9.64 us (6%)
  local copies, waits for them, and re-layouts  4.63 us (3%)
    ppermute x18, starting transfers between devices, send(): return lax.ppermute(array, AXES, pairs)  64.4 us
    ppermute x18, waiting for transfers between devices, send(): return lax.ppermute(array, AXES, pairs)  22.1 us
    all_to_all x1, starting transfers between devices, shards(): far = jnp.sum(lax.all_to_all(near, ('z', 'y'), 0, 0, tiled=True), axis=0)  15.7 us
    pallas_call x1, Pallas kernels, contract(): pl.pallas_call(ladder_kernel, out_shape=jax.ShapeDtypeStruct((8, 32, 128)...  14.9 us
    all_to_all x1, waiting for transfers between devices, shards(): far = jnp.sum(lax.all_to_all(near, ('z', 'y'), 0, 0, tiled=True), axis=0)  10.8 us
    all_to_all x1, blocking collectives, shards(): near = pack(lax.all_to_all(partial, ('xh', 'xl', 'core'), 0, 0, tiled=True))  9.64 us
    unnamed x24, local copies, waits for them, and re-layouts  3.27 us
  transfers between devices with their start and end apart: 20, of which 7 were waited for; matrix products, arithmetic and copies ran while one was open for 0% of the time, Pallas kernels for 1%

profile of v4, /device:TPU:1, one launch (start us, length us, event | category | flops | bytes accessed | tf_op | source)
XLA Modules:
  0.0 160.1 jit_solution(9234623152616423240)
XLA Ops:
  6.5 0.7 all-gather.3.cloned.1.call-update
  7.3 1.6 %collective-permute-start = (f32[8,64,128]{2,1,0:T(8,128)}, f32[8,64,128]{2,1,0:T(8,128)S(1)}, u32[]{:S(2)}, u32[]{:S(2)}) collective-permute-start(f32[8,64,128]{2,1,0:T(8,128)} %param.3), channel_id=1, source_target_pairs={{0,0},{1,1},{2,32},{3,33},{4,4},{5,5},{6,36},{7,37},{8,8},{9,9},{1... | collective-permute-start | bytes 786440 | tf_op jit(solution)/shard_map/ppermute | solution.py:38
  8.9 3.9 %collective-permute-start.1 = (f32[8,64,128]{2,1,0:T(8,128)}, f32[8,64,128]{2,1,0:T(8,128)S(1)}, u32[]{:S(2)}, u32[]{:S(2)}) collective-permute-start(f32[8,64,128]{2,1,0:T(8,128)} %param.3), channel_id=1, source_target_pairs={{0,16},{1,17},{2,48},{3,49},{4,20},{5,21},{6,52},{7,53},{8,24},{9,... | collective-permute-start | bytes 786440 | tf_op jit(solution)/shard_map/ppermute | solution.py:38
  12.8 6.8 %collective-permute-start.5 = (f32[64,32,128]{2,1,0:T(8,128)}, f32[64,32,128]{2,1,0:T(8,128)S(1)}, u32[]{:S(2)}, u32[]{:S(2)}) collective-permute-start(f32[64,32,128]{2,1,0:T(8,128)} %param.5), channel_id=1, source_target_pairs={{0,32},{1,33},{2,34},{3,35},{4,36},{5,37},{6,38},{7,39},{8,40},{9,... | collective-permute-start | bytes 3145736 | tf_op jit(solution)/shard_map/ppermute | solution.py:38
  19.6 0.0 collective-permute-done
  19.6 4.3 %collective-permute-done.1 = f32[8,64,128]{2,1,0:T(8,128)S(1)} collective-permute-done((f32[8,64,128]{2,1,0:T(8,128)}, f32[8,64,128]{2,1,0:T(8,128)S(1)}, u32[]{:S(2)}, u32[]{:S(2)}) %collective-permute-start.1) | collective-permute-done | bytes 262176 | tf_op jit(solution)/shard_map/ppermute | solution.py:38
  23.9 7.4 %collective-permute-start.2 = (f32[2,8,64,128]{3,2,1,0:T(8,128)S(1)}, f32[2,8,64,128]{3,2,1,0:T(8,128)S(1)}, u32[]{:S(2)}, u32[]{:S(2)}) collective-permute-start(f32[2,8,64,128]{3,2,1,0:T(8,128)S(1)} %pad_maximum_fusion.refs_0_), channel_id=1, source_target_pairs={{0,2},{1,15},{2,4},{3,1},{4,6},{5,3},{6,8},{7,5},{8,10},{9,7},{10,... | collective-permute-start | bytes 1572872 | tf_op jit(solution)/shard_map/ppermute | solution.py:38
  31.3 1.9 %collective-permute-start.4 = (f32[2,8,64,128]{3,2,1,0:T(8,128)S(1)}, f32[2,8,64,128]{3,2,1,0:T(8,128)S(1)}, u32[]{:S(2)}, u32[]{:S(2)}) collective-permute-start(f32[2,8,64,128]{3,2,1,0:T(8,128)S(1)} %pad_maximum_fusion.refs_0_), channel_id=1, source_target_pairs={{0,14},{1,3},{2,0},{3,5},{4,2},{5,7},{6,4},{7,9},{8,6},{9,11},{10,... | collective-permute-start | bytes 1572872 | tf_op jit(solution)/shard_map/ppermute | solution.py:38
  33.2 5.2 %collective-permute-done.2.refs_1_ = f32[2,8,64,128]{3,2,1,0:T(8,128)S(1)} collective-permute-done((f32[2,8,64,128]{3,2,1,0:T(8,128)S(1)}, f32[2,8,64,128]{3,2,1,0:T(8,128)S(1)}, u32[]{:S(2)}, u32[]{:S(2)}) %collective-permute-start.2) | collective-permute-done | bytes 524320 | tf_op jit(solution)/shard_map/ppermute | solution.py:38
  38.4 5.4 %collective-permute-start.3 = (f32[2,8,64,128]{3,2,1,0:T(8,128)S(1)}, f32[2,8,64,128]{3,2,1,0:T(8,128)S(1)}, u32[]{:S(2)}, u32[]{:S(2)}) collective-permute-start(f32[2,8,64,128]{3,2,1,0:T(8,128)S(1)} %collective-permute-done.2.refs_1_), channel_id=1, source_target_pairs={{0,2},{1,15},{2,4},{3,1},{4,6},{5,3},{6,8},{7,5},{8,10},{9,7},{10,... | collective-permute-start | bytes 1572872 | tf_op jit(solution)/shard_map/ppermute | solution.py:38
  43.8 2.4 %collective-permute-done.4.refs_7_ = f32[2,8,64,128]{3,2,1,0:T(8,128)S(1)} collective-permute-done((f32[2,8,64,128]{3,2,1,0:T(8,128)S(1)}, f32[2,8,64,128]{3,2,1,0:T(8,128)S(1)}, u32[]{:S(2)}, u32[]{:S(2)}) %collective-permute-start.4) | collective-permute-done | bytes 524320 | tf_op jit(solution)/shard_map/ppermute | solution.py:38
  46.2 1.9 %collective-permute-start.7 = (f32[2,8,64,128]{3,2,1,0:T(8,128)S(1)}, f32[2,8,64,128]{3,2,1,0:T(8,128)S(1)}, u32[]{:S(2)}, u32[]{:S(2)}) collective-permute-start(f32[2,8,64,128]{3,2,1,0:T(8,128)S(1)} %collective-permute-done.4.refs_7_), channel_id=1, source_target_pairs={{0,14},{1,3},{2,0},{3,5},{4,2},{5,7},{6,4},{7,9},{8,6},{9,11},{10,... | collective-permute-start | bytes 1572872 | tf_op jit(solution)/shard_map/ppermute | solution.py:38
  48.1 0.0 collective-permute-done.5
  48.1 1.8 %collective-permute-done.3.refs_2_ = f32[2,8,64,128]{3,2,1,0:T(8,128)S(1)} collective-permute-done((f32[2,8,64,128]{3,2,1,0:T(8,128)S(1)}, f32[2,8,64,128]{3,2,1,0:T(8,128)S(1)}, u32[]{:S(2)}, u32[]{:S(2)}) %collective-permute-start.3) | collective-permute-done | bytes 524320 | tf_op jit(solution)/shard_map/ppermute | solution.py:38
  49.9 5.4 %collective-permute-start.6 = (f32[2,8,64,128]{3,2,1,0:T(8,128)S(1)}, f32[2,8,64,128]{3,2,1,0:T(8,128)S(1)}, u32[]{:S(2)}, u32[]{:S(2)}) collective-permute-start(f32[2,8,64,128]{3,2,1,0:T(8,128)S(1)} %collective-permute-done.3.refs_2_), channel_id=1, source_target_pairs={{0,2},{1,15},{2,4},{3,1},{4,6},{5,3},{6,8},{7,5},{8,10},{9,7},{10,... | collective-permute-start | bytes 1572872 | tf_op jit(solution)/shard_map/ppermute | solution.py:38
  55.4 7.5 %collective-permute-done.7.refs_6_ = f32[2,8,64,128]{3,2,1,0:T(8,128)S(1)} collective-permute-done((f32[2,8,64,128]{3,2,1,0:T(8,128)S(1)}, f32[2,8,64,128]{3,2,1,0:T(8,128)S(1)}, u32[]{:S(2)}, u32[]{:S(2)}) %collective-permute-start.7) | collective-permute-done | bytes 524320 | tf_op jit(solution)/shard_map/ppermute | solution.py:38
  62.9 1.9 %collective-permute-start.9 = (f32[2,8,64,128]{3,2,1,0:T(8,128)S(1)}, f32[2,8,64,128]{3,2,1,0:T(8,128)}, u32[]{:S(2)}, u32[]{:S(2)}) collective-permute-start(f32[2,8,64,128]{3,2,1,0:T(8,128)S(1)} %collective-permute-done.7.refs_6_), channel_id=1, source_target_pairs={{0,14},{1,3},{2,0},{3,5},{4,2},{5,7},{6,4},{7,9},{8,6},{9,11},{10,... | collective-permute-start | bytes 1572872 | tf_op jit(solution)/shard_map/ppermute | solution.py:38
  64.8 7.0 %collective-permute-start.10 = (f32[2,8,64,128]{3,2,1,0:T(8,128)S(1)}, f32[2,8,64,128]{3,2,1,0:T(8,128)S(1)}, u32[]{:S(2)}, u32[]{:S(2)}) collective-permute-start(f32[2,8,64,128]{3,2,1,0:T(8,128)S(1)} %pad_maximum_fusion.refs_0_), channel_id=1, source_target_pairs={{0,1},{1,0},{2,3},{3,2},{4,5},{5,4},{6,7},{7,6},{8,9},{9,8},{10,11... | collective-permute-start | bytes 1572872 | tf_op jit(solution)/shard_map/ppermute | solution.py:38
  71.8 1.9 %collective-permute-start.11 = (f32[2,8,64,128]{3,2,1,0:T(8,128)S(1)}, f32[2,8,64,128]{3,2,1,0:T(8,128)S(1)}, u32[]{:S(2)}, u32[]{:S(2)}) collective-permute-start(f32[2,8,64,128]{3,2,1,0:T(8,128)S(1)} %collective-permute-done.2.refs_1_), channel_id=1, source_target_pairs={{0,1},{1,0},{2,3},{3,2},{4,5},{5,4},{6,7},{7,6},{8,9},{9,8},{10,11... | collective-permute-start | bytes 1572872 | tf_op jit(solution)/shard_map/ppermute | solution.py:38
  73.7 2.4 %collective-permute-start.17 = (f32[2,8,64,128]{3,2,1,0:T(8,128)S(1)}, f32[2,8,64,128]{3,2,1,0:T(8,128)S(1)}, u32[]{:S(2)}, u32[]{:S(2)}) collective-permute-start(f32[2,8,64,128]{3,2,1,0:T(8,128)S(1)} %collective-permute-done.4.refs_7_), channel_id=1, source_target_pairs={{0,1},{1,0},{2,3},{3,2},{4,5},{5,4},{6,7},{7,6},{8,9},{9,8},{10,11... | collective-permute-start | bytes 1572872 | tf_op jit(solution)/shard_map/ppermute | solution.py:38
  76.1 0.0 collective-permute-done.6.refs_3_
  76.1 2.1 %collective-permute-start.8 = (f32[2,8,64,128]{3,2,1,0:T(8,128)S(1)}, f32[2,8,64,128]{3,2,1,0:T(8,128)}, u32[]{:S(2)}, u32[]{:S(2)}) collective-permute-start(f32[2,8,64,128]{3,2,1,0:T(8,128)S(1)} %collective-permute-done.6.refs_3_), channel_id=1, source_target_pairs={{0,2},{1,15},{2,4},{3,1},{4,6},{5,3},{6,8},{7,5},{8,10},{9,7},{10,... | collective-permute-start | bytes 1572872 | tf_op jit(solution)/shard_map/ppermute | solution.py:38
  78.2 0.0 copy-start
  78.2 1.2 copy-done
  79.4 1.8 %split_amplitudes.1 = (bf16[4096,128]{1,0:T(8,128)(2,1)S(1)}, bf16[4096,128]{1,0:T(8,128)(2,1)S(1)}) custom-call(f32[2048,128]{1,0:T(8,128)S(1)} %bitcast.18, f32[2048,128]{1,0:T(8,128)S(1)} %bitcast.19), custom_call_target="tpu_custom_call" | custom-call | flops 1048576 | bytes 4194304 | tf_op jit(solution)/shard_map/split_amplitudes/pallas_call | solution.py:69
  81.2 1.0 copy-done.1
  82.2 1.0 copy-done.2
  83.2 0.0 collective-permute-done.9.refs_5_
  83.2 5.9 %collective-permute-start.16 = (f32[2,8,64,128]{3,2,1,0:T(8,128)S(1)}, f32[2,8,64,128]{3,2,1,0:T(8,128)}, u32[]{:S(2)}, u32[]{:S(2)}) collective-permute-start(f32[2,8,64,128]{3,2,1,0:T(8,128)S(1)} %collective-permute-done.7.refs_6_), channel_id=1, source_target_pairs={{0,1},{1,0},{2,3},{3,2},{4,5},{5,4},{6,7},{7,6},{8,9},{9,8},{10,11... | collective-permute-start | bytes 1572872 | tf_op jit(solution)/shard_map/ppermute | solution.py:38
  89.1 0.0 collective-permute-done.10.refs_8_
  89.2 1.9 %collective-permute-start.12 = (f32[2,8,64,128]{3,2,1,0:T(8,128)S(1)}, f32[2,8,64,128]{3,2,1,0:T(8,128)}, u32[]{:S(2)}, u32[]{:S(2)}) collective-permute-start(f32[2,8,64,128]{3,2,1,0:T(8,128)S(1)} %collective-permute-done.3.refs_2_), channel_id=1, source_target_pairs={{0,1},{1,0},{2,3},{3,2},{4,5},{5,4},{6,7},{7,6},{8,9},{9,8},{10,11... | collective-permute-start | bytes 1572872 | tf_op jit(solution)/shard_map/ppermute | solution.py:38
  91.1 0.0 collective-permute-done.11.refs_9_
  91.1 2.4 %collective-permute-start.15 = (f32[2,8,64,128]{3,2,1,0:T(8,128)}, f32[2,8,64,128]{3,2,1,0:T(8,128)}, u32[]{:S(2)}, u32[]{:S(2)}) collective-permute-start(f32[2,8,64,128]{3,2,1,0:T(8,128)} %collective-permute-done.9.refs_5_), channel_id=1, source_target_pairs={{0,1},{1,0},{2,3},{3,2},{4,5},{5,4},{6,7},{7,6},{8,9},{9,8},{10,11... | collective-permute-start | bytes 1572872 | tf_op jit(solution)/shard_map/ppermute | solution.py:38
  93.5 0.0 collective-permute-done.17.refs_15_
  93.6 1.9 %collective-permute-start.13 = (f32[2,8,64,128]{3,2,1,0:T(8,128)S(1)}, f32[2,8,64,128]{3,2,1,0:T(8,128)}, u32[]{:S(2)}, u32[]{:S(2)}) collective-permute-start(f32[2,8,64,128]{3,2,1,0:T(8,128)S(1)} %collective-permute-done.6.refs_3_), channel_id=1, source_target_pairs={{0,1},{1,0},{2,3},{3,2},{4,5},{5,4},{6,7},{7,6},{8,9},{9,8},{10,11... | collective-permute-start | bytes 1572872 | tf_op jit(solution)/shard_map/ppermute | solution.py:38
  95.5 0.0 collective-permute-done.8.refs_4_
  95.5 2.6 %collective-permute-start.14 = (f32[2,8,64,128]{3,2,1,0:T(8,128)}, f32[2,8,64,128]{3,2,1,0:T(8,128)}, u32[]{:S(2)}, u32[]{:S(2)}) collective-permute-start(f32[2,8,64,128]{3,2,1,0:T(8,128)} %collective-permute-done.8.refs_4_), channel_id=1, source_target_pairs={{0,1},{1,0},{2,3},{3,2},{4,5},{5,4},{6,7},{7,6},{8,9},{9,8},{10,11... | collective-permute-start | bytes 1572872 | tf_op jit(solution)/shard_map/ppermute | solution.py:38
  98.1 0.7 stack.32.place
  98.8 0.0 collective-permute-done.13.refs_11_
  98.8 0.9 collective-permute-done.14.refs_12_
  99.8 14.9 %ladder.1 = f32[8,32,128]{2,1,0:T(8,128)} custom-call(s32[5]{0:T(128)} %stack.32.place, f32[8,16,32,256]{3,2,1,0:T(8,128)} %bitcast.24, f32[2,8,64,128]{3,2,1,0:T(8,128)} %copy-done.3, f32[2,8,64,128]{3,2,1,0:T(8,128)} %copy-done.4, f32[2,8,64,128]{3,2,1,0:T(8,128)} %copy-done.6, f32[2,8,64,128]{3,2,1,0:T(8,128)} %copy-done.8, ...), custom_call_target="tpu_custom_call" | custom-call | flops 6442450944 | bytes 16777216 | tf_op jit(solution)/shard_map/ladder/pallas_call | solution.py:160
  114.7 9.6 %all_to_all.14.near = f32[8,32,128]{2,1,0:T(8,128)} all-to-all(f32[8,32,128]{2,1,0:T(8,128)} %ladder.1), channel_id=1, replica_groups=mesh['z'=8,'xh'=2,'xl'=2,'y'=8,'core'=2] {'xh','xl','core'}, dimensions={0} | all-to-all | bytes 262144 | tf_op jit(solution)/shard_map/all_to_all | solution.py:226
  124.3 1.6 %pack.1 = f32[64,128]{1,0:T(8,128)} custom-call(f32[8,32,128]{2,1,0:T(8,128)} %all_to_all.14.near), custom_call_target="tpu_custom_call" | custom-call | tf_op jit(solution)/shard_map/pack/pallas_call | solution.py:201
  126.0 15.7 %all-to-all-start.1 = ((f32[64,1,128]{2,1,0:T(1,128)}), f32[64,1,128]{2,1,0:T(1,128)S(1)}, u32[]{:S(2)}, u32[]{:S(2)}) async-start(f32[64,1,128]{2,1,0:T(1,128)} %bitcast.22), calls=%async_computation.1 | async-start | bytes 65536 | tf_op jit(solution)/shard_map/all_to_all | solution.py:227
  141.6 10.8 %all-to-all-done.1 = f32[64,1,128]{2,1,0:T(1,128)S(1)} async-done(((f32[64,1,128]{2,1,0:T(1,128)}), f32[64,1,128]{2,1,0:T(1,128)S(1)}, u32[]{:S(2)}, u32[]{:S(2)}) %all-to-all-start.1) | async-done | bytes 32800 | tf_op jit(solution)/shard_map/all_to_all | solution.py:227
  152.5 0.1 reduce_sum.9
  152.6 0.1 reshape.24
  152.6 0.6 dynamic-slice_bitcast_fusion
  (26 shorter events, 0.1 us)
Async XLA Ops:
  6.5 93.2 %all-gather.3.cloned.1.call-start = ((), (), s32[]{:S(2)}) async-start(), calls=%async_computation.2 | async-start | bytes 4718592 | tf_op jit(solution)/shard_map/all_gather | solution.py:212
  7.3 12.3 %collective-permute-start = (f32[8,64,128]{2,1,0:T(8,128)}, f32[8,64,128]{2,1,0:T(8,128)S(1)}, u32[]{:S(2)}, u32[]{:S(2)}) collective-permute-start(f32[8,64,128]{2,1,0:T(8,128)} %param.3), channel_id=1, source_target_pairs={{0,0},{1,1},{2,32},{3,33},{4,4},{5,5},{6,36},{7,37},{8,8},{9,9},{1... | collective-permute-start | bytes 786440 | tf_op jit(solution)/shard_map/ppermute | solution.py:38
  8.9 15.0 %collective-permute-start.1 = (f32[8,64,128]{2,1,0:T(8,128)}, f32[8,64,128]{2,1,0:T(8,128)S(1)}, u32[]{:S(2)}, u32[]{:S(2)}) collective-permute-start(f32[8,64,128]{2,1,0:T(8,128)} %param.3), channel_id=1, source_target_pairs={{0,16},{1,17},{2,48},{3,49},{4,20},{5,21},{6,52},{7,53},{8,24},{9,... | collective-permute-start | bytes 786440 | tf_op jit(solution)/shard_map/ppermute | solution.py:38
  12.8 35.3 %collective-permute-start.5 = (f32[64,32,128]{2,1,0:T(8,128)}, f32[64,32,128]{2,1,0:T(8,128)S(1)}, u32[]{:S(2)}, u32[]{:S(2)}) collective-permute-start(f32[64,32,128]{2,1,0:T(8,128)} %param.5), channel_id=1, source_target_pairs={{0,32},{1,33},{2,34},{3,35},{4,36},{5,37},{6,38},{7,39},{8,40},{9,... | collective-permute-start | bytes 3145736 | tf_op jit(solution)/shard_map/ppermute | solution.py:38
  23.9 75.9 %copy-start.3 = (f32[2,8,64,128]{3,2,1,0:T(8,128)}, f32[2,8,64,128]{3,2,1,0:T(8,128)S(1)}, u32[]{:S(2)}) copy-start(f32[2,8,64,128]{3,2,1,0:T(8,128)S(1)} %pad_maximum_fusion.refs_0_) | copy-start | bytes 1572868
  23.9 14.5 %collective-permute-start.2 = (f32[2,8,64,128]{3,2,1,0:T(8,128)S(1)}, f32[2,8,64,128]{3,2,1,0:T(8,128)S(1)}, u32[]{:S(2)}, u32[]{:S(2)}) collective-permute-start(f32[2,8,64,128]{3,2,1,0:T(8,128)S(1)} %pad_maximum_fusion.refs_0_), channel_id=1, source_target_pairs={{0,2},{1,15},{2,4},{3,1},{4,6},{5,3},{6,8},{7,5},{8,10},{9,7},{10,... | collective-permute-start | bytes 1572872 | tf_op jit(solution)/shard_map/ppermute | solution.py:38
  31.3 14.9 %collective-permute-start.4 = (f32[2,8,64,128]{3,2,1,0:T(8,128)S(1)}, f32[2,8,64,128]{3,2,1,0:T(8,128)S(1)}, u32[]{:S(2)}, u32[]{:S(2)}) collective-permute-start(f32[2,8,64,128]{3,2,1,0:T(8,128)S(1)} %pad_maximum_fusion.refs_0_), channel_id=1, source_target_pairs={{0,14},{1,3},{2,0},{3,5},{4,2},{5,7},{6,4},{7,9},{8,6},{9,11},{10,... | collective-permute-start | bytes 1572872 | tf_op jit(solution)/shard_map/ppermute | solution.py:38
  38.4 61.4 %copy-start.4 = (f32[2,8,64,128]{3,2,1,0:T(8,128)}, f32[2,8,64,128]{3,2,1,0:T(8,128)S(1)}, u32[]{:S(2)}) copy-start(f32[2,8,64,128]{3,2,1,0:T(8,128)S(1)} %collective-permute-done.2.refs_1_) | copy-start | bytes 1572868
  38.4 11.5 %collective-permute-start.3 = (f32[2,8,64,128]{3,2,1,0:T(8,128)S(1)}, f32[2,8,64,128]{3,2,1,0:T(8,128)S(1)}, u32[]{:S(2)}, u32[]{:S(2)}) collective-permute-start(f32[2,8,64,128]{3,2,1,0:T(8,128)S(1)} %collective-permute-done.2.refs_1_), channel_id=1, source_target_pairs={{0,2},{1,15},{2,4},{3,1},{4,6},{5,3},{6,8},{7,5},{8,10},{9,7},{10,... | collective-permute-start | bytes 1572872 | tf_op jit(solution)/shard_map/ppermute | solution.py:38
  46.2 53.6 %copy-start.5 = (f32[2,8,64,128]{3,2,1,0:T(8,128)}, f32[2,8,64,128]{3,2,1,0:T(8,128)S(1)}, u32[]{:S(2)}) copy-start(f32[2,8,64,128]{3,2,1,0:T(8,128)S(1)} %collective-permute-done.4.refs_7_) | copy-start | bytes 1572868
  46.2 16.7 %collective-permute-start.7 = (f32[2,8,64,128]{3,2,1,0:T(8,128)S(1)}, f32[2,8,64,128]{3,2,1,0:T(8,128)S(1)}, u32[]{:S(2)}, u32[]{:S(2)}) collective-permute-start(f32[2,8,64,128]{3,2,1,0:T(8,128)S(1)} %collective-permute-done.4.refs_7_), channel_id=1, source_target_pairs={{0,14},{1,3},{2,0},{3,5},{4,2},{5,7},{6,4},{7,9},{8,6},{9,11},{10,... | collective-permute-start | bytes 1572872 | tf_op jit(solution)/shard_map/ppermute | solution.py:38
  49.9 49.9 %copy-start.6 = (f32[2,8,64,128]{3,2,1,0:T(8,128)}, f32[2,8,64,128]{3,2,1,0:T(8,128)S(1)}, u32[]{:S(2)}) copy-start(f32[2,8,64,128]{3,2,1,0:T(8,128)S(1)} %collective-permute-done.3.refs_2_) | copy-start | bytes 1572868
  49.9 26.2 %collective-permute-start.6 = (f32[2,8,64,128]{3,2,1,0:T(8,128)S(1)}, f32[2,8,64,128]{3,2,1,0:T(8,128)S(1)}, u32[]{:S(2)}, u32[]{:S(2)}) collective-permute-start(f32[2,8,64,128]{3,2,1,0:T(8,128)S(1)} %collective-permute-done.3.refs_2_), channel_id=1, source_target_pairs={{0,2},{1,15},{2,4},{3,1},{4,6},{5,3},{6,8},{7,5},{8,10},{9,7},{10,... | collective-permute-start | bytes 1572872 | tf_op jit(solution)/shard_map/ppermute | solution.py:38
  62.9 36.9 %copy-start.7 = (f32[2,8,64,128]{3,2,1,0:T(8,128)}, f32[2,8,64,128]{3,2,1,0:T(8,128)S(1)}, u32[]{:S(2)}) copy-start(f32[2,8,64,128]{3,2,1,0:T(8,128)S(1)} %collective-permute-done.7.refs_6_) | copy-start | bytes 1572868
  62.9 20.3 %collective-permute-start.9 = (f32[2,8,64,128]{3,2,1,0:T(8,128)S(1)}, f32[2,8,64,128]{3,2,1,0:T(8,128)}, u32[]{:S(2)}, u32[]{:S(2)}) collective-permute-start(f32[2,8,64,128]{3,2,1,0:T(8,128)S(1)} %collective-permute-done.7.refs_6_), channel_id=1, source_target_pairs={{0,14},{1,3},{2,0},{3,5},{4,2},{5,7},{6,4},{7,9},{8,6},{9,11},{10,... | collective-permute-start | bytes 1572872 | tf_op jit(solution)/shard_map/ppermute | solution.py:38
  64.8 24.4 %collective-permute-start.10 = (f32[2,8,64,128]{3,2,1,0:T(8,128)S(1)}, f32[2,8,64,128]{3,2,1,0:T(8,128)S(1)}, u32[]{:S(2)}, u32[]{:S(2)}) collective-permute-start(f32[2,8,64,128]{3,2,1,0:T(8,128)S(1)} %pad_maximum_fusion.refs_0_), channel_id=1, source_target_pairs={{0,1},{1,0},{2,3},{3,2},{4,5},{5,4},{6,7},{7,6},{8,9},{9,8},{10,11... | collective-permute-start | bytes 1572872 | tf_op jit(solution)/shard_map/ppermute | solution.py:38
  71.8 19.3 %collective-permute-start.11 = (f32[2,8,64,128]{3,2,1,0:T(8,128)S(1)}, f32[2,8,64,128]{3,2,1,0:T(8,128)S(1)}, u32[]{:S(2)}, u32[]{:S(2)}) collective-permute-start(f32[2,8,64,128]{3,2,1,0:T(8,128)S(1)} %collective-permute-done.2.refs_1_), channel_id=1, source_target_pairs={{0,1},{1,0},{2,3},{3,2},{4,5},{5,4},{6,7},{7,6},{8,9},{9,8},{10,11... | collective-permute-start | bytes 1572872 | tf_op jit(solution)/shard_map/ppermute | solution.py:38
  73.7 19.9 %collective-permute-start.17 = (f32[2,8,64,128]{3,2,1,0:T(8,128)S(1)}, f32[2,8,64,128]{3,2,1,0:T(8,128)S(1)}, u32[]{:S(2)}, u32[]{:S(2)}) collective-permute-start(f32[2,8,64,128]{3,2,1,0:T(8,128)S(1)} %collective-permute-done.4.refs_7_), channel_id=1, source_target_pairs={{0,1},{1,0},{2,3},{3,2},{4,5},{5,4},{6,7},{7,6},{8,9},{9,8},{10,11... | collective-permute-start | bytes 1572872 | tf_op jit(solution)/shard_map/ppermute | solution.py:38
  76.1 23.7 %copy-start.8 = (f32[2,8,64,128]{3,2,1,0:T(8,128)}, f32[2,8,64,128]{3,2,1,0:T(8,128)S(1)}, u32[]{:S(2)}) copy-start(f32[2,8,64,128]{3,2,1,0:T(8,128)S(1)} %collective-permute-done.6.refs_3_) | copy-start | bytes 1572868
  76.1 19.4 %collective-permute-start.8 = (f32[2,8,64,128]{3,2,1,0:T(8,128)S(1)}, f32[2,8,64,128]{3,2,1,0:T(8,128)}, u32[]{:S(2)}, u32[]{:S(2)}) collective-permute-start(f32[2,8,64,128]{3,2,1,0:T(8,128)S(1)} %collective-permute-done.6.refs_3_), channel_id=1, source_target_pairs={{0,2},{1,15},{2,4},{3,1},{4,6},{5,3},{6,8},{7,5},{8,10},{9,7},{10,... | collective-permute-start | bytes 1572872 | tf_op jit(solution)/shard_map/ppermute | solution.py:38
  78.2 1.2 copy-start
  81.2 1.0 copy-start.1
  82.2 1.0 copy-start.2
  83.2 15.6 %collective-permute-start.16 = (f32[2,8,64,128]{3,2,1,0:T(8,128)S(1)}, f32[2,8,64,128]{3,2,1,0:T(8,128)}, u32[]{:S(2)}, u32[]{:S(2)}) collective-permute-start(f32[2,8,64,128]{3,2,1,0:T(8,128)S(1)} %collective-permute-done.7.refs_6_), channel_id=1, source_target_pairs={{0,1},{1,0},{2,3},{3,2},{4,5},{5,4},{6,7},{7,6},{8,9},{9,8},{10,11... | collective-permute-start | bytes 1572872 | tf_op jit(solution)/shard_map/ppermute | solution.py:38
  89.2 6.3 %copy-start.9 = (f32[2,8,64,128]{3,2,1,0:T(8,128)}, f32[2,8,64,128]{3,2,1,0:T(8,128)S(1)}, u32[]{:S(2)}) copy-start(f32[2,8,64,128]{3,2,1,0:T(8,128)S(1)} %collective-permute-done.10.refs_8_) | copy-start | bytes 1572868
  89.2 9.6 %collective-permute-start.12 = (f32[2,8,64,128]{3,2,1,0:T(8,128)S(1)}, f32[2,8,64,128]{3,2,1,0:T(8,128)}, u32[]{:S(2)}, u32[]{:S(2)}) collective-permute-start(f32[2,8,64,128]{3,2,1,0:T(8,128)S(1)} %collective-permute-done.3.refs_2_), channel_id=1, source_target_pairs={{0,1},{1,0},{2,3},{3,2},{4,5},{5,4},{6,7},{7,6},{8,9},{9,8},{10,11... | collective-permute-start | bytes 1572872 | tf_op jit(solution)/shard_map/ppermute | solution.py:38
  91.1 7.0 %copy-start.10 = (f32[2,8,64,128]{3,2,1,0:T(8,128)}, f32[2,8,64,128]{3,2,1,0:T(8,128)S(1)}, u32[]{:S(2)}) copy-start(f32[2,8,64,128]{3,2,1,0:T(8,128)S(1)} %collective-permute-done.11.refs_9_) | copy-start | bytes 1572868
  91.1 7.7 %collective-permute-start.15 = (f32[2,8,64,128]{3,2,1,0:T(8,128)}, f32[2,8,64,128]{3,2,1,0:T(8,128)}, u32[]{:S(2)}, u32[]{:S(2)}) collective-permute-start(f32[2,8,64,128]{3,2,1,0:T(8,128)} %collective-permute-done.9.refs_5_), channel_id=1, source_target_pairs={{0,1},{1,0},{2,3},{3,2},{4,5},{5,4},{6,7},{7,6},{8,9},{9,8},{10,11... | collective-permute-start | bytes 1572872 | tf_op jit(solution)/shard_map/ppermute | solution.py:38
  93.5 4.6 %copy-start.11 = (f32[2,8,64,128]{3,2,1,0:T(8,128)}, f32[2,8,64,128]{3,2,1,0:T(8,128)S(1)}, u32[]{:S(2)}) copy-start(f32[2,8,64,128]{3,2,1,0:T(8,128)S(1)} %collective-permute-done.17.refs_15_) | copy-start | bytes 1572868
  93.6 5.3 %collective-permute-start.13 = (f32[2,8,64,128]{3,2,1,0:T(8,128)S(1)}, f32[2,8,64,128]{3,2,1,0:T(8,128)}, u32[]{:S(2)}, u32[]{:S(2)}) collective-permute-start(f32[2,8,64,128]{3,2,1,0:T(8,128)S(1)} %collective-permute-done.6.refs_3_), channel_id=1, source_target_pairs={{0,1},{1,0},{2,3},{3,2},{4,5},{5,4},{6,7},{7,6},{8,9},{9,8},{10,11... | collective-permute-start | bytes 1572872 | tf_op jit(solution)/shard_map/ppermute | solution.py:38
  95.5 4.3 %collective-permute-start.14 = (f32[2,8,64,128]{3,2,1,0:T(8,128)}, f32[2,8,64,128]{3,2,1,0:T(8,128)}, u32[]{:S(2)}, u32[]{:S(2)}) collective-permute-start(f32[2,8,64,128]{3,2,1,0:T(8,128)} %collective-permute-done.8.refs_4_), channel_id=1, source_target_pairs={{0,1},{1,0},{2,3},{3,2},{4,5},{5,4},{6,7},{7,6},{8,9},{9,8},{10,11... | collective-permute-start | bytes 1572872 | tf_op jit(solution)/shard_map/ppermute | solution.py:38
  126.0 26.5 %all-to-all-start.1 = ((f32[64,1,128]{2,1,0:T(1,128)}), f32[64,1,128]{2,1,0:T(1,128)S(1)}, u32[]{:S(2)}, u32[]{:S(2)}) async-start(f32[64,1,128]{2,1,0:T(1,128)} %bitcast.22), calls=%async_computation.1 | async-start | bytes 65536 | tf_op jit(solution)/shard_map/all_to_all | solution.py:227
Sparse Core Ops, SparseCore 0:
  9.4 63.7 all-gather.2

commit v5 on v4

--- a/solution.py
+++ b/solution.py
@@ -56,23 +56,42 @@
     return lax.dot_general(a, b, (((1,), (0,)), ((), ())), preferred_element_type=jnp.float32)
 
 
-def amplitudes_kernel(t_own, t_oth, high_out, low_out):
-    for d in range(32):
-        for half, ref in enumerate((t_own, t_oth)):
-            high, low = split(ref[pl.ds(d, 64, 32), :])
-            high_out[d * 128 + half * 64 : d * 128 + half * 64 + 64, :] = high
-            low_out[d * 128 + half * 64 : d * 128 + half * 64 + 64, :] = low
+def amplitudes_kernel(t_own, t_oth, high_out, low_out, first, second, t_high, t_low, in_sem, out_sem):
+    blocks = ((t_own, first), (t_oth, second))
+    copies = [pltpu.make_async_copy(ref, buf, in_sem.at[half]) for half, (ref, buf) in enumerate(blocks)]
+    for copy in copies:
+        copy.start()
+    for half, (_, buf) in enumerate(blocks):
+        copies[half].wait()
+        for d in range(32):
+            high, low = split(buf[pl.ds(d, 64, 32), :])
+            t_high[d * 128 + half * 64 : d * 128 + half * 64 + 64, :] = high
+            t_low[d * 128 + half * 64 : d * 128 + half * 64 + 64, :] = low
+    results = [
+        pltpu.make_async_copy(t_high, high_out, out_sem.at[0]),
+        pltpu.make_async_copy(t_low, low_out, out_sem.at[1]),
+    ]
+    for copy in results:
+        copy.start()
+    for copy in results:
+        copy.wait()
 
 
 def split_amplitudes(t_own, t_oth):
-    shape = jax.ShapeDtypeStruct((4096, 128), jnp.bfloat16)
+    shape = pltpu.HBM((4096, 128), jnp.bfloat16)
+    anywhere = pl.BlockSpec(memory_space=pl.ANY)
     return pl.pallas_call(
         amplitudes_kernel,
         out_shape=(shape, shape),
+        in_specs=[anywhere] * 2,
+        out_specs=[pl.BlockSpec(memory_space=pltpu.HBM)] * 2,
+        scratch_shapes=[pltpu.VMEM((2048, 128), jnp.float32)] * 2
+        + [pltpu.VMEM((4096, 128), jnp.bfloat16)] * 2
+        + [pltpu.SemaphoreType.DMA((2,))] * 2,
         compiler_params=pltpu.CompilerParams(vmem_limit_bytes=8 * 1024 * 1024),
         cost_estimate=pl.CostEstimate(flops=1 << 20, bytes_accessed=4 << 20, transcendentals=0),
         name="split_amplitudes",
-    )(t_own.reshape(2048, 128), t_oth.reshape(2048, 128))
+    )(*(pltpu.with_memory_space_constraint(block.reshape(2048, 128), pltpu.HBM) for block in (t_own, t_oth)))
 
 
 def ladder_kernel(place, right, *refs):
@@ -211,16 +230,16 @@
     place = jnp.stack([y, 1 - 2 * core, lax.axis_index("xl"), xh, core]).astype(jnp.int32)
     right = lax.all_gather(vectors_right, "z", axis=0)
     own = jnp.stack([send(vectors_left, SAME_XL), send(vectors_left, OTHER_XL)])
+    x1 = send(own, RING_X)
     t_oth = send(amplitudes, SWAP_XH)
-    x1 = send(own, RING_X)
     y1 = send(own, RING_Y)
     x2 = send(x1, RING_X)
     y2 = send(after(y1, x1), RING_Y)
-    x3 = send(after(x2, y1, t_oth), RING_X)
+    x3 = send(after(x2, y1), RING_X)
     y3 = send(after(y2, x2), RING_Y)
-    x4 = send(after(x3, y2), RING_X)
+    x4 = send(after(x3, y2, t_oth), RING_X)
+    t_split = split_amplitudes(amplitudes, t_oth)
     left_own = [own, x1, x2, x3, x4, y3, y2, y1]
-    t_split = split_amplitudes(amplitudes, t_oth)
     left_oth = [send(after(piece, *t_split) if piece is y3 else piece, SWAP_CORE) for piece in left_own]
     partial = contract(place, right, left_own, left_oth, t_split)
     near = pack(lax.all_to_all(partial, ("xh", "xl", "core"), 0, 0, tiled=True))

time: 161 us -> 160 us (level)
  local copies, waits for them, and re-layouts: 4.63 us -> 1.34 us
  Pallas kernels: 18.3 us -> 20.7 us
  waiting for transfers between devices: 33.6 us -> 35.4 us
    unnamed x24 -> x20, local copies, waits for them, and re-layouts: 3.27 us -> 0.04 us
    ppermute x18, starting transfers between devices: 64.4 us -> 61.6 us  [send(): return lax.ppermute(array, AXES, pairs)]
    pallas_call x1, Pallas kernels: 1.76 us -> 4.19 us  [split_amplitudes(): pl.pallas_call(amplitudes_kernel, out_shape=(shape, shape), in_specs=[any...]
    ppermute x18, waiting for transfers between devices: 22.1 us -> 23.8 us  [send(): return lax.ppermute(array, AXES, pairs)]
  transfers between devices with their start and end apart: 20 -> 20, of which waited for: 7 -> 5; matrix products, arithmetic and copies ran while one was open for 0% -> 0% of each run, Pallas kernels for 1% -> 3%
where the time goes in v5:
time: 160 us; the launch traced here: 159 us
  starting transfers between devices  78.7 us (49%)
  waiting for transfers between devices  35.4 us (22%)
  Pallas kernels  20.7 us (13%)
  between operations  13.8 us (9%)
  blocking collectives  9.39 us (6%)
    ppermute x18, starting transfers between devices, send(): return lax.ppermute(array, AXES, pairs)  61.6 us
    ppermute x18, waiting for transfers between devices, send(): return lax.ppermute(array, AXES, pairs)  23.8 us
    all_to_all x1, starting transfers between devices, shards(): far = jnp.sum(lax.all_to_all(near, ('z', 'y'), 0, 0, tiled=True), axis=0)  17.1 us
    pallas_call x1, Pallas kernels, contract(): pl.pallas_call(ladder_kernel, out_shape=jax.ShapeDtypeStruct((8, 32, 128)...  14.9 us
    all_to_all x1, waiting for transfers between devices, shards(): far = jnp.sum(lax.all_to_all(near, ('z', 'y'), 0, 0, tiled=True), axis=0)  10.8 us
    all_to_all x1, blocking collectives, shards(): near = pack(lax.all_to_all(partial, ('xh', 'xl', 'core'), 0, 0, tiled=True))  9.39 us
    pallas_call x1, Pallas kernels, split_amplitudes(): pl.pallas_call(amplitudes_kernel, out_shape=(shape, shape), in_specs=[any...  4.19 us
  transfers between devices with their start and end apart: 20, of which 5 were waited for; matrix products, arithmetic and copies ran while one was open for 0% of the time, Pallas kernels for 3%

profile of v5, /device:TPU:1, one launch (start us, length us, event | category | flops | bytes accessed | tf_op | source)
XLA Modules:
  0.0 159.4 jit_solution(4401301935329091161)
XLA Ops:
  6.5 0.7 all-gather.3.cloned.1.call-update
  7.3 1.6 %collective-permute-start = (f32[8,64,128]{2,1,0:T(8,128)}, f32[8,64,128]{2,1,0:T(8,128)S(1)}, u32[]{:S(2)}, u32[]{:S(2)}) collective-permute-start(f32[8,64,128]{2,1,0:T(8,128)} %param.3), channel_id=1, source_target_pairs={{0,0},{1,1},{2,32},{3,33},{4,4},{5,5},{6,36},{7,37},{8,8},{9,9},{1... | collective-permute-start | bytes 786440 | tf_op jit(solution)/shard_map/ppermute | solution.py:38
  8.9 3.9 %collective-permute-start.1 = (f32[8,64,128]{2,1,0:T(8,128)}, f32[8,64,128]{2,1,0:T(8,128)S(1)}, u32[]{:S(2)}, u32[]{:S(2)}) collective-permute-start(f32[8,64,128]{2,1,0:T(8,128)} %param.3), channel_id=1, source_target_pairs={{0,16},{1,17},{2,48},{3,49},{4,20},{5,21},{6,52},{7,53},{8,24},{9,... | collective-permute-start | bytes 786440 | tf_op jit(solution)/shard_map/ppermute | solution.py:38
  12.8 0.0 collective-permute-done
  12.8 11.0 %collective-permute-done.1 = f32[8,64,128]{2,1,0:T(8,128)S(1)} collective-permute-done((f32[8,64,128]{2,1,0:T(8,128)}, f32[8,64,128]{2,1,0:T(8,128)S(1)}, u32[]{:S(2)}, u32[]{:S(2)}) %collective-permute-start.1) | collective-permute-done | bytes 262176 | tf_op jit(solution)/shard_map/ppermute | solution.py:38
  23.9 7.4 %collective-permute-start.2 = (f32[2,8,64,128]{3,2,1,0:T(8,128)S(1)}, f32[2,8,64,128]{3,2,1,0:T(8,128)S(1)}, u32[]{:S(2)}, u32[]{:S(2)}) collective-permute-start(f32[2,8,64,128]{3,2,1,0:T(8,128)S(1)} %pad_maximum_fusion.refs_0_), channel_id=1, source_target_pairs={{0,2},{1,15},{2,4},{3,1},{4,6},{5,3},{6,8},{7,5},{8,10},{9,7},{10,... | collective-permute-start | bytes 1572872 | tf_op jit(solution)/shard_map/ppermute | solution.py:38
  31.3 1.9 %collective-permute-start.4 = (f32[2,8,64,128]{3,2,1,0:T(8,128)S(1)}, f32[2,8,64,128]{3,2,1,0:T(8,128)S(1)}, u32[]{:S(2)}, u32[]{:S(2)}) collective-permute-start(f32[2,8,64,128]{3,2,1,0:T(8,128)S(1)} %pad_maximum_fusion.refs_0_), channel_id=1, source_target_pairs={{0,14},{1,3},{2,0},{3,5},{4,2},{5,7},{6,4},{7,9},{8,6},{9,11},{10,... | collective-permute-start | bytes 1572872 | tf_op jit(solution)/shard_map/ppermute | solution.py:38
  33.2 5.9 %collective-permute-done.2.refs_1_ = f32[2,8,64,128]{3,2,1,0:T(8,128)S(1)} collective-permute-done((f32[2,8,64,128]{3,2,1,0:T(8,128)S(1)}, f32[2,8,64,128]{3,2,1,0:T(8,128)S(1)}, u32[]{:S(2)}, u32[]{:S(2)}) %collective-permute-start.2) | collective-permute-done | bytes 524320 | tf_op jit(solution)/shard_map/ppermute | solution.py:38
  39.1 5.4 %collective-permute-start.3 = (f32[2,8,64,128]{3,2,1,0:T(8,128)S(1)}, f32[2,8,64,128]{3,2,1,0:T(8,128)S(1)}, u32[]{:S(2)}, u32[]{:S(2)}) collective-permute-start(f32[2,8,64,128]{3,2,1,0:T(8,128)S(1)} %collective-permute-done.2.refs_1_), channel_id=1, source_target_pairs={{0,2},{1,15},{2,4},{3,1},{4,6},{5,3},{6,8},{7,5},{8,10},{9,7},{10,... | collective-permute-start | bytes 1572872 | tf_op jit(solution)/shard_map/ppermute | solution.py:38
  44.5 4.2 %collective-permute-start.7 = (f32[64,32,128]{2,1,0:T(8,128)}, f32[64,32,128]{2,1,0:T(8,128)S(1)}, u32[]{:S(2)}, u32[]{:S(2)}) collective-permute-start(f32[64,32,128]{2,1,0:T(8,128)} %param.5), channel_id=1, source_target_pairs={{0,32},{1,33},{2,34},{3,35},{4,36},{5,37},{6,38},{7,39},{8,40},{9,... | collective-permute-start | bytes 3145736 | tf_op jit(solution)/shard_map/ppermute | solution.py:38
  48.7 0.0 collective-permute-done.4.refs_7_
  48.8 1.9 %collective-permute-start.6 = (f32[2,8,64,128]{3,2,1,0:T(8,128)S(1)}, f32[2,8,64,128]{3,2,1,0:T(8,128)S(1)}, u32[]{:S(2)}, u32[]{:S(2)}) collective-permute-start(f32[2,8,64,128]{3,2,1,0:T(8,128)S(1)} %collective-permute-done.4.refs_7_), channel_id=1, source_target_pairs={{0,14},{1,3},{2,0},{3,5},{4,2},{5,7},{6,4},{7,9},{8,6},{9,11},{10,... | collective-permute-start | bytes 1572872 | tf_op jit(solution)/shard_map/ppermute | solution.py:38
  50.7 0.0 collective-permute-done.3.refs_2_
  50.7 0.0 copy-start.4
  50.7 5.3 %collective-permute-start.5 = (f32[2,8,64,128]{3,2,1,0:T(8,128)S(1)}, f32[2,8,64,128]{3,2,1,0:T(8,128)S(1)}, u32[]{:S(2)}, u32[]{:S(2)}) collective-permute-start(f32[2,8,64,128]{3,2,1,0:T(8,128)S(1)} %collective-permute-done.3.refs_2_), channel_id=1, source_target_pairs={{0,2},{1,15},{2,4},{3,1},{4,6},{5,3},{6,8},{7,5},{8,10},{9,7},{10,... | collective-permute-start | bytes 1572872 | tf_op jit(solution)/shard_map/ppermute | solution.py:38
  56.0 5.6 %collective-permute-done.6.refs_6_ = f32[2,8,64,128]{3,2,1,0:T(8,128)S(1)} collective-permute-done((f32[2,8,64,128]{3,2,1,0:T(8,128)S(1)}, f32[2,8,64,128]{3,2,1,0:T(8,128)S(1)}, u32[]{:S(2)}, u32[]{:S(2)}) %collective-permute-start.6) | collective-permute-done | bytes 524320 | tf_op jit(solution)/shard_map/ppermute | solution.py:38
  61.6 1.9 %collective-permute-start.9 = (f32[2,8,64,128]{3,2,1,0:T(8,128)S(1)}, f32[2,8,64,128]{3,2,1,0:T(8,128)}, u32[]{:S(2)}, u32[]{:S(2)}) collective-permute-start(f32[2,8,64,128]{3,2,1,0:T(8,128)S(1)} %collective-permute-done.6.refs_6_), channel_id=1, source_target_pairs={{0,14},{1,3},{2,0},{3,5},{4,2},{5,7},{6,4},{7,9},{8,6},{9,11},{10,... | collective-permute-start | bytes 1572872 | tf_op jit(solution)/shard_map/ppermute | solution.py:38
  63.5 8.7 %collective-permute-start.10 = (f32[2,8,64,128]{3,2,1,0:T(8,128)S(1)}, f32[2,8,64,128]{3,2,1,0:T(8,128)S(1)}, u32[]{:S(2)}, u32[]{:S(2)}) collective-permute-start(f32[2,8,64,128]{3,2,1,0:T(8,128)S(1)} %pad_maximum_fusion.refs_0_), channel_id=1, source_target_pairs={{0,1},{1,0},{2,3},{3,2},{4,5},{5,4},{6,7},{7,6},{8,9},{9,8},{10,11... | collective-permute-start | bytes 1572872 | tf_op jit(solution)/shard_map/ppermute | solution.py:38
  72.3 1.9 %collective-permute-start.11 = (f32[2,8,64,128]{3,2,1,0:T(8,128)S(1)}, f32[2,8,64,128]{3,2,1,0:T(8,128)S(1)}, u32[]{:S(2)}, u32[]{:S(2)}) collective-permute-start(f32[2,8,64,128]{3,2,1,0:T(8,128)S(1)} %collective-permute-done.2.refs_1_), channel_id=1, source_target_pairs={{0,1},{1,0},{2,3},{3,2},{4,5},{5,4},{6,7},{7,6},{8,9},{9,8},{10,11... | collective-permute-start | bytes 1572872 | tf_op jit(solution)/shard_map/ppermute | solution.py:38
  74.2 0.0 collective-permute-done.7
  74.2 2.4 %collective-permute-start.17 = (f32[2,8,64,128]{3,2,1,0:T(8,128)S(1)}, f32[2,8,64,128]{3,2,1,0:T(8,128)S(1)}, u32[]{:S(2)}, u32[]{:S(2)}) collective-permute-start(f32[2,8,64,128]{3,2,1,0:T(8,128)S(1)} %collective-permute-done.4.refs_7_), channel_id=1, source_target_pairs={{0,1},{1,0},{2,3},{3,2},{4,5},{5,4},{6,7},{7,6},{8,9},{9,8},{10,11... | collective-permute-start | bytes 1572872 | tf_op jit(solution)/shard_map/ppermute | solution.py:38
  76.6 0.0 collective-permute-done.5.refs_3_
  76.6 4.1 %collective-permute-start.8 = (f32[2,8,64,128]{3,2,1,0:T(8,128)S(1)}, f32[2,8,64,128]{3,2,1,0:T(8,128)}, u32[]{:S(2)}, u32[]{:S(2)}) collective-permute-start(f32[2,8,64,128]{3,2,1,0:T(8,128)S(1)} %collective-permute-done.5.refs_3_), channel_id=1, source_target_pairs={{0,2},{1,15},{2,4},{3,1},{4,6},{5,3},{6,8},{7,5},{8,10},{9,7},{10,... | collective-permute-start | bytes 1572872 | tf_op jit(solution)/shard_map/ppermute | solution.py:38
  80.8 4.2 %split_amplitudes.1 = (bf16[4096,128]{1,0:T(8,128)(2,1)}, bf16[4096,128]{1,0:T(8,128)(2,1)}) custom-call(f32[2048,128]{1,0:T(8,128)} %bitcast.18, f32[2048,128]{1,0:T(8,128)} %bitcast.19), custom_call_target="tpu_custom_call" | custom-call | flops 1048576 | bytes 4194304 | tf_op jit(solution)/shard_map/split_amplitudes/pallas_call | solution.py:83
  85.0 0.0 collective-permute-done.9.refs_5_
  85.0 1.9 %collective-permute-start.16 = (f32[2,8,64,128]{3,2,1,0:T(8,128)S(1)}, f32[2,8,64,128]{3,2,1,0:T(8,128)}, u32[]{:S(2)}, u32[]{:S(2)}) collective-permute-start(f32[2,8,64,128]{3,2,1,0:T(8,128)S(1)} %collective-permute-done.6.refs_6_), channel_id=1, source_target_pairs={{0,1},{1,0},{2,3},{3,2},{4,5},{5,4},{6,7},{7,6},{8,9},{9,8},{10,11... | collective-permute-start | bytes 1572872 | tf_op jit(solution)/shard_map/ppermute | solution.py:38
  86.9 0.0 collective-permute-done.10.refs_8_
  86.9 2.4 %collective-permute-start.12 = (f32[2,8,64,128]{3,2,1,0:T(8,128)S(1)}, f32[2,8,64,128]{3,2,1,0:T(8,128)}, u32[]{:S(2)}, u32[]{:S(2)}) collective-permute-start(f32[2,8,64,128]{3,2,1,0:T(8,128)S(1)} %collective-permute-done.3.refs_2_), channel_id=1, source_target_pairs={{0,1},{1,0},{2,3},{3,2},{4,5},{5,4},{6,7},{7,6},{8,9},{9,8},{10,11... | collective-permute-start | bytes 1572872 | tf_op jit(solution)/shard_map/ppermute | solution.py:38
  89.3 0.0 collective-permute-done.11.refs_9_
  89.4 1.9 %collective-permute-start.15 = (f32[2,8,64,128]{3,2,1,0:T(8,128)}, f32[2,8,64,128]{3,2,1,0:T(8,128)}, u32[]{:S(2)}, u32[]{:S(2)}) collective-permute-start(f32[2,8,64,128]{3,2,1,0:T(8,128)} %collective-permute-done.9.refs_5_), channel_id=1, source_target_pairs={{0,1},{1,0},{2,3},{3,2},{4,5},{5,4},{6,7},{7,6},{8,9},{9,8},{10,11... | collective-permute-start | bytes 1572872 | tf_op jit(solution)/shard_map/ppermute | solution.py:38
  91.3 0.0 collective-permute-done.17.refs_15_
  91.3 2.4 %collective-permute-start.13 = (f32[2,8,64,128]{3,2,1,0:T(8,128)S(1)}, f32[2,8,64,128]{3,2,1,0:T(8,128)}, u32[]{:S(2)}, u32[]{:S(2)}) collective-permute-start(f32[2,8,64,128]{3,2,1,0:T(8,128)S(1)} %collective-permute-done.5.refs_3_), channel_id=1, source_target_pairs={{0,1},{1,0},{2,3},{3,2},{4,5},{5,4},{6,7},{7,6},{8,9},{9,8},{10,11... | collective-permute-start | bytes 1572872 | tf_op jit(solution)/shard_map/ppermute | solution.py:38
  93.7 0.0 collective-permute-done.8.refs_4_
  93.8 2.1 %collective-permute-start.14 = (f32[2,8,64,128]{3,2,1,0:T(8,128)}, f32[2,8,64,128]{3,2,1,0:T(8,128)}, u32[]{:S(2)}, u32[]{:S(2)}) collective-permute-start(f32[2,8,64,128]{3,2,1,0:T(8,128)} %collective-permute-done.8.refs_4_), channel_id=1, source_target_pairs={{0,1},{1,0},{2,3},{3,2},{4,5},{5,4},{6,7},{7,6},{8,9},{9,8},{10,11... | collective-permute-start | bytes 1572872 | tf_op jit(solution)/shard_map/ppermute | solution.py:38
  95.9 0.6 stack.32.place
  96.5 0.0 collective-permute-done.16.refs_14_
  96.5 0.0 collective-permute-done.12.refs_10_
  96.5 0.0 collective-permute-done.15.refs_13_
  96.5 0.0 collective-permute-done.13.refs_11_
  96.5 1.4 collective-permute-done.14.refs_12_
  97.9 14.9 %ladder.1 = f32[8,32,128]{2,1,0:T(8,128)} custom-call(s32[5]{0:T(128)} %stack.32.place, f32[8,16,32,256]{3,2,1,0:T(8,128)} %bitcast.24, f32[2,8,64,128]{3,2,1,0:T(8,128)} %copy-done.1, f32[2,8,64,128]{3,2,1,0:T(8,128)} %copy-done.2, f32[2,8,64,128]{3,2,1,0:T(8,128)} %copy-done.4, f32[2,8,64,128]{3,2,1,0:T(8,128)} %copy-done.6, ...), custom_call_target="tpu_custom_call" | custom-call | flops 6442450944 | bytes 16777216 | tf_op jit(solution)/shard_map/ladder/pallas_call | solution.py:179
  112.8 9.4 %all_to_all.14.near = f32[8,32,128]{2,1,0:T(8,128)} all-to-all(f32[8,32,128]{2,1,0:T(8,128)} %ladder.1), channel_id=1, replica_groups=mesh['z'=8,'xh'=2,'xl'=2,'y'=8,'core'=2] {'xh','xl','core'}, dimensions={0} | all-to-all | bytes 262144 | tf_op jit(solution)/shard_map/all_to_all | solution.py:245
  122.2 1.6 %pack.1 = f32[64,128]{1,0:T(8,128)} custom-call(f32[8,32,128]{2,1,0:T(8,128)} %all_to_all.14.near), custom_call_target="tpu_custom_call" | custom-call | tf_op jit(solution)/shard_map/pack/pallas_call | solution.py:220
  123.8 17.1 %all-to-all-start.1 = ((f32[64,1,128]{2,1,0:T(1,128)}), f32[64,1,128]{2,1,0:T(1,128)S(1)}, u32[]{:S(2)}, u32[]{:S(2)}) async-start(f32[64,1,128]{2,1,0:T(1,128)} %bitcast.22), calls=%async_computation.1 | async-start | bytes 65536 | tf_op jit(solution)/shard_map/all_to_all | solution.py:246
  141.0 10.8 %all-to-all-done.1 = f32[64,1,128]{2,1,0:T(1,128)S(1)} async-done(((f32[64,1,128]{2,1,0:T(1,128)}), f32[64,1,128]{2,1,0:T(1,128)S(1)}, u32[]{:S(2)}, u32[]{:S(2)}) %all-to-all-start.1) | async-done | bytes 32800 | tf_op jit(solution)/shard_map/all_to_all | solution.py:246
  151.8 0.1 reduce_sum.9
  151.9 0.1 reshape.24
  152.0 0.6 dynamic-slice_bitcast_fusion
  (22 shorter events, 0.1 us)
Async XLA Ops:
  6.5 91.4 %all-gather.3.cloned.1.call-start = ((), (), s32[]{:S(2)}) async-start(), calls=%async_computation.2 | async-start | bytes 4718592 | tf_op jit(solution)/shard_map/all_gather | solution.py:231
  7.3 5.6 %collective-permute-start = (f32[8,64,128]{2,1,0:T(8,128)}, f32[8,64,128]{2,1,0:T(8,128)S(1)}, u32[]{:S(2)}, u32[]{:S(2)}) collective-permute-start(f32[8,64,128]{2,1,0:T(8,128)} %param.3), channel_id=1, source_target_pairs={{0,0},{1,1},{2,32},{3,33},{4,4},{5,5},{6,36},{7,37},{8,8},{9,9},{1... | collective-permute-start | bytes 786440 | tf_op jit(solution)/shard_map/ppermute | solution.py:38
  8.9 15.0 %collective-permute-start.1 = (f32[8,64,128]{2,1,0:T(8,128)}, f32[8,64,128]{2,1,0:T(8,128)S(1)}, u32[]{:S(2)}, u32[]{:S(2)}) collective-permute-start(f32[8,64,128]{2,1,0:T(8,128)} %param.3), channel_id=1, source_target_pairs={{0,16},{1,17},{2,48},{3,49},{4,20},{5,21},{6,52},{7,53},{8,24},{9,... | collective-permute-start | bytes 786440 | tf_op jit(solution)/shard_map/ppermute | solution.py:38
  23.9 74.0 %copy-start.1 = (f32[2,8,64,128]{3,2,1,0:T(8,128)}, f32[2,8,64,128]{3,2,1,0:T(8,128)S(1)}, u32[]{:S(2)}) copy-start(f32[2,8,64,128]{3,2,1,0:T(8,128)S(1)} %pad_maximum_fusion.refs_0_) | copy-start | bytes 1572868
  23.9 15.2 %collective-permute-start.2 = (f32[2,8,64,128]{3,2,1,0:T(8,128)S(1)}, f32[2,8,64,128]{3,2,1,0:T(8,128)S(1)}, u32[]{:S(2)}, u32[]{:S(2)}) collective-permute-start(f32[2,8,64,128]{3,2,1,0:T(8,128)S(1)} %pad_maximum_fusion.refs_0_), channel_id=1, source_target_pairs={{0,2},{1,15},{2,4},{3,1},{4,6},{5,3},{6,8},{7,5},{8,10},{9,7},{10,... | collective-permute-start | bytes 1572872 | tf_op jit(solution)/shard_map/ppermute | solution.py:38
  31.3 17.5 %collective-permute-start.4 = (f32[2,8,64,128]{3,2,1,0:T(8,128)S(1)}, f32[2,8,64,128]{3,2,1,0:T(8,128)S(1)}, u32[]{:S(2)}, u32[]{:S(2)}) collective-permute-start(f32[2,8,64,128]{3,2,1,0:T(8,128)S(1)} %pad_maximum_fusion.refs_0_), channel_id=1, source_target_pairs={{0,14},{1,3},{2,0},{3,5},{4,2},{5,7},{6,4},{7,9},{8,6},{9,11},{10,... | collective-permute-start | bytes 1572872 | tf_op jit(solution)/shard_map/ppermute | solution.py:38
  39.1 58.8 %copy-start.2 = (f32[2,8,64,128]{3,2,1,0:T(8,128)}, f32[2,8,64,128]{3,2,1,0:T(8,128)S(1)}, u32[]{:S(2)}) copy-start(f32[2,8,64,128]{3,2,1,0:T(8,128)S(1)} %collective-permute-done.2.refs_1_) | copy-start | bytes 1572868
  39.1 11.6 %collective-permute-start.3 = (f32[2,8,64,128]{3,2,1,0:T(8,128)S(1)}, f32[2,8,64,128]{3,2,1,0:T(8,128)S(1)}, u32[]{:S(2)}, u32[]{:S(2)}) collective-permute-start(f32[2,8,64,128]{3,2,1,0:T(8,128)S(1)} %collective-permute-done.2.refs_1_), channel_id=1, source_target_pairs={{0,2},{1,15},{2,4},{3,1},{4,6},{5,3},{6,8},{7,5},{8,10},{9,7},{10,... | collective-permute-start | bytes 1572872 | tf_op jit(solution)/shard_map/ppermute | solution.py:38
  44.5 29.7 %collective-permute-start.7 = (f32[64,32,128]{2,1,0:T(8,128)}, f32[64,32,128]{2,1,0:T(8,128)S(1)}, u32[]{:S(2)}, u32[]{:S(2)}) collective-permute-start(f32[64,32,128]{2,1,0:T(8,128)} %param.5), channel_id=1, source_target_pairs={{0,32},{1,33},{2,34},{3,35},{4,36},{5,37},{6,38},{7,39},{8,40},{9,... | collective-permute-start | bytes 3145736 | tf_op jit(solution)/shard_map/ppermute | solution.py:38
  48.8 49.2 %copy-start.3 = (f32[2,8,64,128]{3,2,1,0:T(8,128)}, f32[2,8,64,128]{3,2,1,0:T(8,128)S(1)}, u32[]{:S(2)}) copy-start(f32[2,8,64,128]{3,2,1,0:T(8,128)S(1)} %collective-permute-done.4.refs_7_) | copy-start | bytes 1572868
  48.8 12.8 %collective-permute-start.6 = (f32[2,8,64,128]{3,2,1,0:T(8,128)S(1)}, f32[2,8,64,128]{3,2,1,0:T(8,128)S(1)}, u32[]{:S(2)}, u32[]{:S(2)}) collective-permute-start(f32[2,8,64,128]{3,2,1,0:T(8,128)S(1)} %collective-permute-done.4.refs_7_), channel_id=1, source_target_pairs={{0,14},{1,3},{2,0},{3,5},{4,2},{5,7},{6,4},{7,9},{8,6},{9,11},{10,... | collective-permute-start | bytes 1572872 | tf_op jit(solution)/shard_map/ppermute | solution.py:38
  50.7 47.2 %copy-start.4 = (f32[2,8,64,128]{3,2,1,0:T(8,128)}, f32[2,8,64,128]{3,2,1,0:T(8,128)S(1)}, u32[]{:S(2)}) copy-start(f32[2,8,64,128]{3,2,1,0:T(8,128)S(1)} %collective-permute-done.3.refs_2_) | copy-start | bytes 1572868
  50.7 25.9 %collective-permute-start.5 = (f32[2,8,64,128]{3,2,1,0:T(8,128)S(1)}, f32[2,8,64,128]{3,2,1,0:T(8,128)S(1)}, u32[]{:S(2)}, u32[]{:S(2)}) collective-permute-start(f32[2,8,64,128]{3,2,1,0:T(8,128)S(1)} %collective-permute-done.3.refs_2_), channel_id=1, source_target_pairs={{0,2},{1,15},{2,4},{3,1},{4,6},{5,3},{6,8},{7,5},{8,10},{9,7},{10,... | collective-permute-start | bytes 1572872 | tf_op jit(solution)/shard_map/ppermute | solution.py:38
  61.6 36.3 %copy-start.5 = (f32[2,8,64,128]{3,2,1,0:T(8,128)}, f32[2,8,64,128]{3,2,1,0:T(8,128)S(1)}, u32[]{:S(2)}) copy-start(f32[2,8,64,128]{3,2,1,0:T(8,128)S(1)} %collective-permute-done.6.refs_6_) | copy-start | bytes 1572868
  61.6 23.4 %collective-permute-start.9 = (f32[2,8,64,128]{3,2,1,0:T(8,128)S(1)}, f32[2,8,64,128]{3,2,1,0:T(8,128)}, u32[]{:S(2)}, u32[]{:S(2)}) collective-permute-start(f32[2,8,64,128]{3,2,1,0:T(8,128)S(1)} %collective-permute-done.6.refs_6_), channel_id=1, source_target_pairs={{0,14},{1,3},{2,0},{3,5},{4,2},{5,7},{6,4},{7,9},{8,6},{9,11},{10,... | collective-permute-start | bytes 1572872 | tf_op jit(solution)/shard_map/ppermute | solution.py:38
  63.5 23.4 %collective-permute-start.10 = (f32[2,8,64,128]{3,2,1,0:T(8,128)S(1)}, f32[2,8,64,128]{3,2,1,0:T(8,128)S(1)}, u32[]{:S(2)}, u32[]{:S(2)}) collective-permute-start(f32[2,8,64,128]{3,2,1,0:T(8,128)S(1)} %pad_maximum_fusion.refs_0_), channel_id=1, source_target_pairs={{0,1},{1,0},{2,3},{3,2},{4,5},{5,4},{6,7},{7,6},{8,9},{9,8},{10,11... | collective-permute-start | bytes 1572872 | tf_op jit(solution)/shard_map/ppermute | solution.py:38
  72.3 17.1 %collective-permute-start.11 = (f32[2,8,64,128]{3,2,1,0:T(8,128)S(1)}, f32[2,8,64,128]{3,2,1,0:T(8,128)S(1)}, u32[]{:S(2)}, u32[]{:S(2)}) collective-permute-start(f32[2,8,64,128]{3,2,1,0:T(8,128)S(1)} %collective-permute-done.2.refs_1_), channel_id=1, source_target_pairs={{0,1},{1,0},{2,3},{3,2},{4,5},{5,4},{6,7},{7,6},{8,9},{9,8},{10,11... | collective-permute-start | bytes 1572872 | tf_op jit(solution)/shard_map/ppermute | solution.py:38
  74.2 6.6 %copy-start = (f32[64,32,128]{2,1,0:T(8,128)}, f32[64,32,128]{2,1,0:T(8,128)S(1)}, u32[]{:S(2)}) copy-start(f32[64,32,128]{2,1,0:T(8,128)S(1)} %collective-permute-done.7) | copy-start | bytes 3145732
  74.2 17.1 %collective-permute-start.17 = (f32[2,8,64,128]{3,2,1,0:T(8,128)S(1)}, f32[2,8,64,128]{3,2,1,0:T(8,128)S(1)}, u32[]{:S(2)}, u32[]{:S(2)}) collective-permute-start(f32[2,8,64,128]{3,2,1,0:T(8,128)S(1)} %collective-permute-done.4.refs_7_), channel_id=1, source_target_pairs={{0,1},{1,0},{2,3},{3,2},{4,5},{5,4},{6,7},{7,6},{8,9},{9,8},{10,11... | collective-permute-start | bytes 1572872 | tf_op jit(solution)/shard_map/ppermute | solution.py:38
  76.6 21.3 %copy-start.6 = (f32[2,8,64,128]{3,2,1,0:T(8,128)}, f32[2,8,64,128]{3,2,1,0:T(8,128)S(1)}, u32[]{:S(2)}) copy-start(f32[2,8,64,128]{3,2,1,0:T(8,128)S(1)} %collective-permute-done.5.refs_3_) | copy-start | bytes 1572868
  76.6 17.1 %collective-permute-start.8 = (f32[2,8,64,128]{3,2,1,0:T(8,128)S(1)}, f32[2,8,64,128]{3,2,1,0:T(8,128)}, u32[]{:S(2)}, u32[]{:S(2)}) collective-permute-start(f32[2,8,64,128]{3,2,1,0:T(8,128)S(1)} %collective-permute-done.5.refs_3_), channel_id=1, source_target_pairs={{0,2},{1,15},{2,4},{3,1},{4,6},{5,3},{6,8},{7,5},{8,10},{9,7},{10,... | collective-permute-start | bytes 1572872 | tf_op jit(solution)/shard_map/ppermute | solution.py:38
  85.0 11.5 %collective-permute-start.16 = (f32[2,8,64,128]{3,2,1,0:T(8,128)S(1)}, f32[2,8,64,128]{3,2,1,0:T(8,128)}, u32[]{:S(2)}, u32[]{:S(2)}) collective-permute-start(f32[2,8,64,128]{3,2,1,0:T(8,128)S(1)} %collective-permute-done.6.refs_6_), channel_id=1, source_target_pairs={{0,1},{1,0},{2,3},{3,2},{4,5},{5,4},{6,7},{7,6},{8,9},{9,8},{10,11... | collective-permute-start | bytes 1572872 | tf_op jit(solution)/shard_map/ppermute | solution.py:38
  86.9 6.8 %copy-start.7 = (f32[2,8,64,128]{3,2,1,0:T(8,128)}, f32[2,8,64,128]{3,2,1,0:T(8,128)S(1)}, u32[]{:S(2)}) copy-start(f32[2,8,64,128]{3,2,1,0:T(8,128)S(1)} %collective-permute-done.10.refs_8_) | copy-start | bytes 1572868
  86.9 9.6 %collective-permute-start.12 = (f32[2,8,64,128]{3,2,1,0:T(8,128)S(1)}, f32[2,8,64,128]{3,2,1,0:T(8,128)}, u32[]{:S(2)}, u32[]{:S(2)}) collective-permute-start(f32[2,8,64,128]{3,2,1,0:T(8,128)S(1)} %collective-permute-done.3.refs_2_), channel_id=1, source_target_pairs={{0,1},{1,0},{2,3},{3,2},{4,5},{5,4},{6,7},{7,6},{8,9},{9,8},{10,11... | collective-permute-start | bytes 1572872 | tf_op jit(solution)/shard_map/ppermute | solution.py:38
  89.4 6.5 %copy-start.8 = (f32[2,8,64,128]{3,2,1,0:T(8,128)}, f32[2,8,64,128]{3,2,1,0:T(8,128)S(1)}, u32[]{:S(2)}) copy-start(f32[2,8,64,128]{3,2,1,0:T(8,128)S(1)} %collective-permute-done.11.refs_9_) | copy-start | bytes 1572868
  89.4 7.2 %collective-permute-start.15 = (f32[2,8,64,128]{3,2,1,0:T(8,128)}, f32[2,8,64,128]{3,2,1,0:T(8,128)}, u32[]{:S(2)}, u32[]{:S(2)}) collective-permute-start(f32[2,8,64,128]{3,2,1,0:T(8,128)} %collective-permute-done.9.refs_5_), channel_id=1, source_target_pairs={{0,1},{1,0},{2,3},{3,2},{4,5},{5,4},{6,7},{7,6},{8,9},{9,8},{10,11... | collective-permute-start | bytes 1572872 | tf_op jit(solution)/shard_map/ppermute | solution.py:38
  91.3 4.6 %copy-start.9 = (f32[2,8,64,128]{3,2,1,0:T(8,128)}, f32[2,8,64,128]{3,2,1,0:T(8,128)S(1)}, u32[]{:S(2)}) copy-start(f32[2,8,64,128]{3,2,1,0:T(8,128)S(1)} %collective-permute-done.17.refs_15_) | copy-start | bytes 1572868
  91.3 5.2 %collective-permute-start.13 = (f32[2,8,64,128]{3,2,1,0:T(8,128)S(1)}, f32[2,8,64,128]{3,2,1,0:T(8,128)}, u32[]{:S(2)}, u32[]{:S(2)}) collective-permute-start(f32[2,8,64,128]{3,2,1,0:T(8,128)S(1)} %collective-permute-done.5.refs_3_), channel_id=1, source_target_pairs={{0,1},{1,0},{2,3},{3,2},{4,5},{5,4},{6,7},{7,6},{8,9},{9,8},{10,11... | collective-permute-start | bytes 1572872 | tf_op jit(solution)/shard_map/ppermute | solution.py:38
  93.8 4.1 %collective-permute-start.14 = (f32[2,8,64,128]{3,2,1,0:T(8,128)}, f32[2,8,64,128]{3,2,1,0:T(8,128)}, u32[]{:S(2)}, u32[]{:S(2)}) collective-permute-start(f32[2,8,64,128]{3,2,1,0:T(8,128)} %collective-permute-done.8.refs_4_), channel_id=1, source_target_pairs={{0,1},{1,0},{2,3},{3,2},{4,5},{5,4},{6,7},{7,6},{8,9},{9,8},{10,11... | collective-permute-start | bytes 1572872 | tf_op jit(solution)/shard_map/ppermute | solution.py:38
  123.8 28.0 %all-to-all-start.1 = ((f32[64,1,128]{2,1,0:T(1,128)}), f32[64,1,128]{2,1,0:T(1,128)S(1)}, u32[]{:S(2)}, u32[]{:S(2)}) async-start(f32[64,1,128]{2,1,0:T(1,128)} %bitcast.22), calls=%async_computation.1 | async-start | bytes 65536 | tf_op jit(solution)/shard_map/all_to_all | solution.py:246
Sparse Core Ops, SparseCore 0:
  9.4 63.7 all-gather.2

commit v6 on v5

--- a/solution.py
+++ b/solution.py
@@ -30,6 +30,7 @@
 RING_Y = table(lambda z, xh, xl, y, core: (z, xh, xl, y - 1 + 2 * core, core))
 SWAP_CORE = table(lambda z, xh, xl, y, core: (z, xh, xl, y, 1 - core))
 SWAP_XH = table(lambda z, xh, xl, y, core: (z, 1 - xh, xl, y, core))
+GROUPS = ((0, 1, 7, 2), (6, 3, 5), (4,))
 PAIRS = (0, 1, 3, 2)
 NEEDED = ((0, 1, 7), (2, 6, 3, 5), (4,), ())
 
@@ -95,8 +96,9 @@
 
 
 def ladder_kernel(place, right, *refs):
-    pieces, (t_high_in, t_low_in, out) = (refs[:8], refs[8:16]), refs[16:19]
-    r_buf, raw, parts, t_high, t_low, acc, y_high, y_low, flip, r_sem, l_sem, t_sem = refs[19:]
+    own, oth, (t_high_in, t_low_in, out) = refs[:8], refs[8:11], refs[11:14]
+    r_buf, raw, parts, t_high, t_low, acc, y_high, y_low, flip, r_sem, l_sem, t_sem = refs[14:]
+    swapped = {slot: ref.at[i] for group, ref in zip(GROUPS, oth) for i, slot in enumerate(group)}
     y, sign, xl_here, xh, core = (place[i] for i in range(5))
 
     def pair(k):
@@ -107,7 +109,7 @@
         return pltpu.make_async_copy(right.at[where], r_buf.at[k, order], r_sem.at[k, order])
 
     def left_copy(side, slot):
-        return pltpu.make_async_copy(pieces[side][slot], raw.at[side, slot], l_sem.at[side, slot])
+        return pltpu.make_async_copy(swapped[slot] if side else own[slot], raw.at[side, slot], l_sem.at[side, slot])
 
     def left(k, q_half, half, order):
         at = 2 * pair(k) + lax.bitwise_xor(half, xh)
@@ -179,7 +181,7 @@
     return pl.pallas_call(
         ladder_kernel,
         out_shape=jax.ShapeDtypeStruct((8, 32, 128), jnp.float32),
-        in_specs=[pl.BlockSpec(memory_space=pltpu.SMEM)] + [pl.BlockSpec(memory_space=pl.ANY)] * 19,
+        in_specs=[pl.BlockSpec(memory_space=pltpu.SMEM)] + [pl.BlockSpec(memory_space=pl.ANY)] * 14,
         out_specs=pl.BlockSpec(memory_space=pltpu.VMEM),
         scratch_shapes=[
             pltpu.VMEM((4, 2, 16, 32, 256), jnp.float32),
@@ -225,6 +227,23 @@
     )(near)
 
 
+def hold_kernel(place, piece, out):
+    for i in range(5):
+        out[i] = place[i]
+
+
+def hold(place, piece):
+    smem = pl.BlockSpec(memory_space=pltpu.SMEM)
+    return pl.pallas_call(
+        hold_kernel,
+        out_shape=jax.ShapeDtypeStruct((5,), jnp.int32),
+        in_specs=[smem, pl.BlockSpec(memory_space=pl.ANY)],
+        out_specs=smem,
+        cost_estimate=pl.CostEstimate(flops=30 << 30, bytes_accessed=1 << 10, transcendentals=0),
+        name="hold",
+    )(place, piece)
+
+
 def shards(vectors_left, vectors_right, amplitudes):
     xh, y, core = (lax.axis_index(name) for name in ("xh", "y", "core"))
     place = jnp.stack([y, 1 - 2 * core, lax.axis_index("xl"), xh, core]).astype(jnp.int32)
@@ -237,11 +256,14 @@
     y2 = send(after(y1, x1), RING_Y)
     x3 = send(after(x2, y1), RING_X)
     y3 = send(after(y2, x2), RING_Y)
-    x4 = send(after(x3, y2, t_oth), RING_X)
+    x4 = send(after(x3, y2), RING_X)
     t_split = split_amplitudes(amplitudes, t_oth)
     left_own = [own, x1, x2, x3, x4, y3, y2, y1]
-    left_oth = [send(after(piece, *t_split) if piece is y3 else piece, SWAP_CORE) for piece in left_own]
-    partial = contract(place, right, left_own, left_oth, t_split)
+    gates = ((x3, t_oth), t_split, ())
+    left_oth = [
+        send(after(jnp.stack([left_own[slot] for slot in group]), *gate), SWAP_CORE) for group, gate in zip(GROUPS, gates)
+    ]
+    partial = contract(hold(place, x4), right, left_own, left_oth, t_split)
     near = pack(lax.all_to_all(partial, ("xh", "xl", "core"), 0, 0, tiled=True))
     far = jnp.sum(lax.all_to_all(near, ("z", "y"), 0, 0, tiled=True), axis=0)
     return lax.dynamic_slice(far[:64].reshape(4, 2, 8), (0, xh, 0), (4, 1, 8)).reshape(4, 8, 1)

time: 160 us -> 162 us (1.012)
  starting transfers between devices: 78.7 us -> 72 us
  other arithmetic: 0.12 us -> 3.23 us
  waiting for transfers between devices: 35.4 us -> 37.5 us
  local copies, waits for them, and re-layouts: 1.34 us -> 3.13 us
    ppermute x18 -> x13, starting transfers between devices: 61.6 us -> 53 us  [send(): return lax.ppermute(array, AXES, pairs)]
    another operation x1 -> x3, other arithmetic: 0.04 us -> 3.15 us  [shards(): jnp.stack([left_own[slot] for slot in group])]
    ppermute x18 -> x13, waiting for transfers between devices: 23.8 us -> 26 us  [send(): return lax.ppermute(array, AXES, pairs)]
    all_to_all x1, starting transfers between devices: 17.1 us -> 18.9 us  [shards(): far = jnp.sum(lax.all_to_all(near, ('z', 'y'), 0, 0, tiled=True), axis=0)]
    unnamed x20, local copies, waits for them, and re-layouts: 0.04 us -> 1.8 us
  transfers between devices with their start and end apart: 20 -> 15, of which waited for: 5 -> 6; matrix products, arithmetic and copies ran while one was open for 0% -> 2% of each run, Pallas kernels for 3% -> 3%
where the time goes in v6:
time: 162 us
  starting transfers between devices  72 us (44%)
  waiting for transfers between devices  37.5 us (23%)
  Pallas kernels  21.8 us (13%)
  between operations  13.7 us (8%)
  blocking collectives  10.2 us (6%)
  other arithmetic  3.23 us (2%)
  local copies, waits for them, and re-layouts  3.13 us (2%)
    ppermute x13, starting transfers between devices, send(): return lax.ppermute(array, AXES, pairs)  53 us
    ppermute x13, waiting for transfers between devices, send(): return lax.ppermute(array, AXES, pairs)  26 us
    all_to_all x1, starting transfers between devices, shards(): far = jnp.sum(lax.all_to_all(near, ('z', 'y'), 0, 0, tiled=True), axis=0)  18.9 us
    pallas_call x1, Pallas kernels, contract(): pl.pallas_call(ladder_kernel, out_shape=jax.ShapeDtypeStruct((8, 32, 128)...  14.9 us
    all_to_all x1, waiting for transfers between devices, shards(): far = jnp.sum(lax.all_to_all(near, ('z', 'y'), 0, 0, tiled=True), axis=0)  10.8 us
    all_to_all x1, blocking collectives, shards(): near = pack(lax.all_to_all(partial, ('xh', 'xl', 'core'), 0, 0, tiled=True))  10.2 us
    pallas_call x1, Pallas kernels, split_amplitudes(): pl.pallas_call(amplitudes_kernel, out_shape=(shape, shape), in_specs=[any...  4.12 us
  transfers between devices with their start and end apart: 15, of which 6 were waited for; matrix products, arithmetic and copies ran while one was open for 2% of the time, Pallas kernels for 3%

profile of v6, /device:TPU:1, one launch (start us, length us, event | category | flops | bytes accessed | tf_op | source)
XLA Modules:
  0.0 161.6 jit_solution(8646487167122159167)
XLA Ops:
  6.5 0.7 all-gather.3.cloned.1.call-update
  7.3 1.6 collective-permute-start
  8.9 3.9 %collective-permute-start.1 = (f32[8,64,128]{2,1,0:T(8,128)}, f32[8,64,128]{2,1,0:T(8,128)S(1)}, u32[]{:S(2)}, u32[]{:S(2)}) collective-permute-start(f32[8,64,128]{2,1,0:T(8,128)} %param.3), channel_id=1, source_target_pairs={{0,16},{1,17},{2,48},{3,49},{4,20},{5,21},{6,52},{7,53},{8,24},{9,... | collective-permute-start | bytes 786440 | tf_op jit(solution)/shard_map/ppermute | solution.py:39
  12.8 0.0 collective-permute-done
  12.8 11.0 %collective-permute-done.1 = f32[8,64,128]{2,1,0:T(8,128)S(1)} collective-permute-done((f32[8,64,128]{2,1,0:T(8,128)}, f32[8,64,128]{2,1,0:T(8,128)S(1)}, u32[]{:S(2)}, u32[]{:S(2)}) %collective-permute-start.1) | collective-permute-done | bytes 262176 | tf_op jit(solution)/shard_map/ppermute | solution.py:39
  23.8 0.1 fusion
  24.0 7.4 %collective-permute-start.2 = (f32[2,8,64,128]{3,2,1,0:T(8,128)S(1)}, f32[2,8,64,128]{3,2,1,0:T(8,128)S(1)}, u32[]{:S(2)}, u32[]{:S(2)}) collective-permute-start(f32[2,8,64,128]{3,2,1,0:T(8,128)S(1)} %get-tuple-element.22.refs_0_), channel_id=1, source_target_pairs={{0,2},{1,15},{2,4},{3,1},{4,6},{5,3},{6,8},{7,5},{8,10},{9,7},{10,... | collective-permute-start | bytes 1572872 | tf_op jit(solution)/shard_map/ppermute | solution.py:39
  31.4 1.9 %collective-permute-start.4 = (f32[2,8,64,128]{3,2,1,0:T(8,128)S(1)}, f32[2,8,64,128]{3,2,1,0:T(8,128)S(1)}, u32[]{:S(2)}, u32[]{:S(2)}) collective-permute-start(f32[2,8,64,128]{3,2,1,0:T(8,128)S(1)} %get-tuple-element.22.refs_0_), channel_id=1, source_target_pairs={{0,14},{1,3},{2,0},{3,5},{4,2},{5,7},{6,4},{7,9},{8,6},{9,11},{10,... | collective-permute-start | bytes 1572872 | tf_op jit(solution)/shard_map/ppermute | solution.py:39
  33.3 5.9 %collective-permute-done.2.refs_1_ = f32[2,8,64,128]{3,2,1,0:T(8,128)S(1)} collective-permute-done((f32[2,8,64,128]{3,2,1,0:T(8,128)S(1)}, f32[2,8,64,128]{3,2,1,0:T(8,128)S(1)}, u32[]{:S(2)}, u32[]{:S(2)}) %collective-permute-start.2) | collective-permute-done | bytes 524320 | tf_op jit(solution)/shard_map/ppermute | solution.py:39
  39.2 5.4 %collective-permute-start.3 = (f32[2,8,64,128]{3,2,1,0:T(8,128)S(1)}, f32[2,8,64,128]{3,2,1,0:T(8,128)S(1)}, u32[]{:S(2)}, u32[]{:S(2)}) collective-permute-start(f32[2,8,64,128]{3,2,1,0:T(8,128)S(1)} %collective-permute-done.2.refs_1_), channel_id=1, source_target_pairs={{0,2},{1,15},{2,4},{3,1},{4,6},{5,3},{6,8},{7,5},{8,10},{9,7},{10,... | collective-permute-start | bytes 1572872 | tf_op jit(solution)/shard_map/ppermute | solution.py:39
  44.6 0.0 copy-done
  44.6 4.2 %collective-permute-start.9 = (f32[64,32,128]{2,1,0:T(8,128)S(1)}, f32[64,32,128]{2,1,0:T(8,128)S(1)}, u32[]{:S(2)}, u32[]{:S(2)}) collective-permute-start(f32[64,32,128]{2,1,0:T(8,128)S(1)} %copy-done), channel_id=1, source_target_pairs={{0,32},{1,33},{2,34},{3,35},{4,36},{5,37},{6,38},{7,39},{8,40},{9,... | collective-permute-start | bytes 3145736 | tf_op jit(solution)/shard_map/ppermute | solution.py:39
  48.8 0.0 collective-permute-done.4.refs_7_
  48.9 1.9 %collective-permute-start.6 = (f32[2,8,64,128]{3,2,1,0:T(8,128)S(1)}, f32[2,8,64,128]{3,2,1,0:T(8,128)}, u32[]{:S(2)}, u32[]{:S(2)}) collective-permute-start(f32[2,8,64,128]{3,2,1,0:T(8,128)S(1)} %collective-permute-done.4.refs_7_), channel_id=1, source_target_pairs={{0,14},{1,3},{2,0},{3,5},{4,2},{5,7},{6,4},{7,9},{8,6},{9,11},{10,... | collective-permute-start | bytes 1572872 | tf_op jit(solution)/shard_map/ppermute | solution.py:39
  50.8 0.0 collective-permute-done.3.refs_2_
  50.8 5.3 %collective-permute-start.5 = (f32[2,8,64,128]{3,2,1,0:T(8,128)S(1)}, f32[2,8,64,128]{3,2,1,0:T(8,128)}, u32[]{:S(2)}, u32[]{:S(2)}) collective-permute-start(f32[2,8,64,128]{3,2,1,0:T(8,128)S(1)} %collective-permute-done.3.refs_2_), channel_id=1, source_target_pairs={{0,2},{1,15},{2,4},{3,1},{4,6},{5,3},{6,8},{7,5},{8,10},{9,7},{10,... | collective-permute-start | bytes 1572872 | tf_op jit(solution)/shard_map/ppermute | solution.py:39
  56.1 5.6 %collective-permute-done.6.refs_6_ = f32[2,8,64,128]{3,2,1,0:T(8,128)} collective-permute-done((f32[2,8,64,128]{3,2,1,0:T(8,128)S(1)}, f32[2,8,64,128]{3,2,1,0:T(8,128)}, u32[]{:S(2)}, u32[]{:S(2)}) %collective-permute-start.6) | collective-permute-done | bytes 524320 | tf_op jit(solution)/shard_map/ppermute | solution.py:39
  61.7 1.9 %collective-permute-start.8 = (f32[2,8,64,128]{3,2,1,0:T(8,128)}, f32[2,8,64,128]{3,2,1,0:T(8,128)}, u32[]{:S(2)}, u32[]{:S(2)}) collective-permute-start(f32[2,8,64,128]{3,2,1,0:T(8,128)} %collective-permute-done.6.refs_6_), channel_id=1, source_target_pairs={{0,14},{1,3},{2,0},{3,5},{4,2},{5,7},{6,4},{7,9},{8,6},{9,11},{10,... | collective-permute-start | bytes 1572872 | tf_op jit(solution)/shard_map/ppermute | solution.py:39
  63.6 2.2 %collective-permute-done.5.refs_3_ = f32[2,8,64,128]{3,2,1,0:T(8,128)} collective-permute-done((f32[2,8,64,128]{3,2,1,0:T(8,128)S(1)}, f32[2,8,64,128]{3,2,1,0:T(8,128)}, u32[]{:S(2)}, u32[]{:S(2)}) %collective-permute-start.5) | collective-permute-done | bytes 524320 | tf_op jit(solution)/shard_map/ppermute | solution.py:39
  65.8 5.4 %collective-permute-start.7 = (f32[2,8,64,128]{3,2,1,0:T(8,128)}, f32[2,8,64,128]{3,2,1,0:T(8,128)}, u32[]{:S(2)}, u32[]{:S(2)}) collective-permute-start(f32[2,8,64,128]{3,2,1,0:T(8,128)} %collective-permute-done.5.refs_3_), channel_id=1, source_target_pairs={{0,2},{1,15},{2,4},{3,1},{4,6},{5,3},{6,8},{7,5},{8,10},{9,7},{10,... | collective-permute-start | bytes 1572872 | tf_op jit(solution)/shard_map/ppermute | solution.py:39
  71.3 0.7 stack.62.place
  71.9 0.0 collective-permute-done.9
  71.9 1.0 copy-done.1
  72.9 4.1 %split_amplitudes.1 = (bf16[4096,128]{1,0:T(8,128)(2,1)}, bf16[4096,128]{1,0:T(8,128)(2,1)}) custom-call(f32[2048,128]{1,0:T(8,128)} %bitcast.27, f32[2048,128]{1,0:T(8,128)} %bitcast.28), custom_call_target="tpu_custom_call" | custom-call | flops 1048576 | bytes 4194304 | tf_op jit(solution)/shard_map/split_amplitudes/pallas_call | solution.py:84
  77.0 0.0 copy-done.4
  77.1 0.0 copy-done.6
  77.1 0.0 copy-done.8
  77.1 0.2 pad_maximum_fusion
  77.3 0.0 collective-permute-done.8.refs_5_
  77.3 2.8 %pad_maximum_fusion.1 = f32[3,2,8,64,128]{4,3,2,1,0:T(8,128)} fusion(f32[1,2,8,64,128]{4,3,2,1,0:T(8,128)} %bitcast.14, f32[1,2,8,64,128]{4,3,2,1,0:T(8,128)} %bitcast.13, f32[1,2,8,64,128]{4,3,2,1,0:T(8,128)} %bitcast.12), kind=kLoop, calls=%fused_computation.1 | loop fusion | flops 786432 | bytes 3145728 | tf_op jit(solution)/shard_map/stack | solution.py:264
  80.1 9.5 %collective-permute-start.11 = (f32[3,2,8,64,128]{4,3,2,1,0:T(8,128)}, f32[3,2,8,64,128]{4,3,2,1,0:T(8,128)}, u32[]{:S(2)}, u32[]{:S(2)}) collective-permute-start(f32[3,2,8,64,128]{4,3,2,1,0:T(8,128)} %pad_maximum_fusion.1), channel_id=1, source_target_pairs={{0,1},{1,0},{2,3},{3,2},{4,5},{5,4},{6,7},{7,6},{8,9},{9,8},{10,11... | collective-permute-start | bytes 4718600 | tf_op jit(solution)/shard_map/ppermute | solution.py:39
  89.6 1.9 %collective-permute-start.10 = (f32[4,2,8,64,128]{4,3,2,1,0:T(8,128)S(1)}, f32[4,2,8,64,128]{4,3,2,1,0:T(8,128)}, u32[]{:S(2)}, u32[]{:S(2)}) collective-permute-start(f32[4,2,8,64,128]{4,3,2,1,0:T(8,128)S(1)} %pad_maximum_fusion), channel_id=1, source_target_pairs={{0,1},{1,0},{2,3},{3,2},{4,5},{5,4},{6,7},{7,6},{8,9},{9,8},{10,11... | collective-permute-start | bytes 6291464 | tf_op jit(solution)/shard_map/ppermute | solution.py:39
  91.6 0.0 collective-permute-done.7.piece.refs_4_
  91.6 2.6 %collective-permute-start.12 = (f32[1,2,8,64,128]{4,3,2,1,0:T(8,128)}, f32[1,2,8,64,128]{4,3,2,1,0:T(8,128)S(1)}, u32[]{:S(2)}, u32[]{:S(2)}) collective-permute-start(f32[1,2,8,64,128]{4,3,2,1,0:T(8,128)} %bitcast.17), channel_id=1, source_target_pairs={{0,1},{1,0},{2,3},{3,2},{4,5},{5,4},{6,7},{7,6},{8,9},{9,8},{10,11... | collective-permute-start | bytes 1572872 | tf_op jit(solution)/shard_map/ppermute | solution.py:39
  94.2 1.2 hold.1.place
  95.4 1.3 collective-permute-done.12.refs_10_
  96.7 0.0 collective-permute-done.11.refs_9_
  96.7 0.0 collective-permute-done.10.refs_8_
  96.7 0.0 all-gather.3.cloned.1.call-done
  96.7 0.8 copy-done.9
  97.5 14.9 %ladder.1 = f32[8,32,128]{2,1,0:T(8,128)} custom-call(s32[5]{0:T(128)} %hold.1.place, f32[8,16,32,256]{3,2,1,0:T(8,128)} %bitcast.36, f32[2,8,64,128]{3,2,1,0:T(8,128)} %copy-done.2, f32[2,8,64,128]{3,2,1,0:T(8,128)} %copy-done.3, f32[2,8,64,128]{3,2,1,0:T(8,128)} %copy-done.7, f32[2,8,64,128]{3,2,1,0:T(8,128)} %collective-permute-done.5.refs_3_, ...), custom_call_target="tpu_custom_call" | custom-call | flops 6442450944 | bytes 16777216 | tf_op jit(solution)/shard_map/ladder/pallas_call | solution.py:181
  112.4 10.2 %all_to_all.14.near = f32[8,32,128]{2,1,0:T(8,128)} all-to-all(f32[8,32,128]{2,1,0:T(8,128)} %ladder.1), channel_id=1, replica_groups=mesh['z'=8,'xh'=2,'xl'=2,'y'=8,'core'=2] {'xh','xl','core'}, dimensions={0} | all-to-all | bytes 262144 | tf_op jit(solution)/shard_map/all_to_all | solution.py:267
  122.6 1.6 pack.1
  124.2 18.9 %all-to-all-start.1 = ((f32[64,1,128]{2,1,0:T(1,128)}), f32[64,1,128]{2,1,0:T(1,128)S(1)}, u32[]{:S(2)}, u32[]{:S(2)}) async-start(f32[64,1,128]{2,1,0:T(1,128)} %bitcast.34), calls=%async_computation.1 | async-start | bytes 65536 | tf_op jit(solution)/shard_map/all_to_all | solution.py:268
  143.2 10.8 %all-to-all-done.1 = f32[64,1,128]{2,1,0:T(1,128)S(1)} async-done(((f32[64,1,128]{2,1,0:T(1,128)}), f32[64,1,128]{2,1,0:T(1,128)S(1)}, u32[]{:S(2)}, u32[]{:S(2)}) %all-to-all-start.1) | async-done | bytes 32800 | tf_op jit(solution)/shard_map/all_to_all | solution.py:268
  154.0 0.1 reduce_sum.9
  154.1 0.1 reshape.24
  154.2 0.6 dynamic-slice_bitcast_fusion
  (15 shorter events, 0.0 us)
Async XLA Ops:
  6.5 38.0 %copy-start = (f32[64,32,128]{2,1,0:T(8,128)S(1)}, f32[64,32,128]{2,1,0:T(8,128)}, u32[]{:S(2)}) copy-start(f32[64,32,128]{2,1,0:T(8,128)} %param.5) | copy-start | bytes 3145732
  6.5 90.2 %all-gather.3.cloned.1.call-start = ((), (), s32[]{:S(2)}) async-start(), calls=%async_computation.2 | async-start | bytes 4718592 | tf_op jit(solution)/shard_map/all_gather | solution.py:250
  7.3 5.6 %collective-permute-start = (f32[8,64,128]{2,1,0:T(8,128)}, f32[8,64,128]{2,1,0:T(8,128)S(1)}, u32[]{:S(2)}, u32[]{:S(2)}) collective-permute-start(f32[8,64,128]{2,1,0:T(8,128)} %param.3), channel_id=1, source_target_pairs={{0,0},{1,1},{2,32},{3,33},{4,4},{5,5},{6,36},{7,37},{8,8},{9,9},{1... | collective-permute-start | bytes 786440 | tf_op jit(solution)/shard_map/ppermute | solution.py:39
  8.9 15.0 %collective-permute-start.1 = (f32[8,64,128]{2,1,0:T(8,128)}, f32[8,64,128]{2,1,0:T(8,128)S(1)}, u32[]{:S(2)}, u32[]{:S(2)}) collective-permute-start(f32[8,64,128]{2,1,0:T(8,128)} %param.3), channel_id=1, source_target_pairs={{0,16},{1,17},{2,48},{3,49},{4,20},{5,21},{6,52},{7,53},{8,24},{9,... | collective-permute-start | bytes 786440 | tf_op jit(solution)/shard_map/ppermute | solution.py:39
  24.0 71.4 %copy-start.2 = (f32[2,8,64,128]{3,2,1,0:T(8,128)}, f32[2,8,64,128]{3,2,1,0:T(8,128)S(1)}, u32[]{:S(2)}) copy-start(f32[2,8,64,128]{3,2,1,0:T(8,128)S(1)} %get-tuple-element.22.refs_0_) | copy-start | bytes 1572868
  24.0 15.2 %collective-permute-start.2 = (f32[2,8,64,128]{3,2,1,0:T(8,128)S(1)}, f32[2,8,64,128]{3,2,1,0:T(8,128)S(1)}, u32[]{:S(2)}, u32[]{:S(2)}) collective-permute-start(f32[2,8,64,128]{3,2,1,0:T(8,128)S(1)} %get-tuple-element.22.refs_0_), channel_id=1, source_target_pairs={{0,2},{1,15},{2,4},{3,1},{4,6},{5,3},{6,8},{7,5},{8,10},{9,7},{10,... | collective-permute-start | bytes 1572872 | tf_op jit(solution)/shard_map/ppermute | solution.py:39
  31.4 17.5 %collective-permute-start.4 = (f32[2,8,64,128]{3,2,1,0:T(8,128)S(1)}, f32[2,8,64,128]{3,2,1,0:T(8,128)S(1)}, u32[]{:S(2)}, u32[]{:S(2)}) collective-permute-start(f32[2,8,64,128]{3,2,1,0:T(8,128)S(1)} %get-tuple-element.22.refs_0_), channel_id=1, source_target_pairs={{0,14},{1,3},{2,0},{3,5},{4,2},{5,7},{6,4},{7,9},{8,6},{9,11},{10,... | collective-permute-start | bytes 1572872 | tf_op jit(solution)/shard_map/ppermute | solution.py:39
  39.2 9.7 %copy-start.3 = (f32[2,8,64,128]{3,2,1,0:T(8,128)}, f32[2,8,64,128]{3,2,1,0:T(8,128)S(1)}, u32[]{:S(2)}) copy-start(f32[2,8,64,128]{3,2,1,0:T(8,128)S(1)} %collective-permute-done.2.refs_1_) | copy-start | bytes 1572868
  39.2 11.6 %collective-permute-start.3 = (f32[2,8,64,128]{3,2,1,0:T(8,128)S(1)}, f32[2,8,64,128]{3,2,1,0:T(8,128)S(1)}, u32[]{:S(2)}, u32[]{:S(2)}) collective-permute-start(f32[2,8,64,128]{3,2,1,0:T(8,128)S(1)} %collective-permute-done.2.refs_1_), channel_id=1, source_target_pairs={{0,2},{1,15},{2,4},{3,1},{4,6},{5,3},{6,8},{7,5},{8,10},{9,7},{10,... | collective-permute-start | bytes 1572872 | tf_op jit(solution)/shard_map/ppermute | solution.py:39
  44.6 27.3 %collective-permute-start.9 = (f32[64,32,128]{2,1,0:T(8,128)S(1)}, f32[64,32,128]{2,1,0:T(8,128)S(1)}, u32[]{:S(2)}, u32[]{:S(2)}) collective-permute-start(f32[64,32,128]{2,1,0:T(8,128)S(1)} %copy-done), channel_id=1, source_target_pairs={{0,32},{1,33},{2,34},{3,35},{4,36},{5,37},{6,38},{7,39},{8,40},{9,... | collective-permute-start | bytes 3145736 | tf_op jit(solution)/shard_map/ppermute | solution.py:39
  48.8 2.0 %copy-start.5 = (f32[2,8,64,128]{3,2,1,0:T(8,128)}, f32[2,8,64,128]{3,2,1,0:T(8,128)S(1)}, u32[]{:S(2)}) copy-start(f32[2,8,64,128]{3,2,1,0:T(8,128)S(1)} %collective-permute-done.4.refs_7_) | copy-start | bytes 1572868
  48.9 12.8 %collective-permute-start.6 = (f32[2,8,64,128]{3,2,1,0:T(8,128)S(1)}, f32[2,8,64,128]{3,2,1,0:T(8,128)}, u32[]{:S(2)}, u32[]{:S(2)}) collective-permute-start(f32[2,8,64,128]{3,2,1,0:T(8,128)S(1)} %collective-permute-done.4.refs_7_), channel_id=1, source_target_pairs={{0,14},{1,3},{2,0},{3,5},{4,2},{5,7},{6,4},{7,9},{8,6},{9,11},{10,... | collective-permute-start | bytes 1572872 | tf_op jit(solution)/shard_map/ppermute | solution.py:39
  50.8 10.9 %copy-start.7 = (f32[2,8,64,128]{3,2,1,0:T(8,128)}, f32[2,8,64,128]{3,2,1,0:T(8,128)S(1)}, u32[]{:S(2)}) copy-start(f32[2,8,64,128]{3,2,1,0:T(8,128)S(1)} %collective-permute-done.3.refs_2_) | copy-start | bytes 1572868
  50.8 15.0 %collective-permute-start.5 = (f32[2,8,64,128]{3,2,1,0:T(8,128)S(1)}, f32[2,8,64,128]{3,2,1,0:T(8,128)}, u32[]{:S(2)}, u32[]{:S(2)}) collective-permute-start(f32[2,8,64,128]{3,2,1,0:T(8,128)S(1)} %collective-permute-done.3.refs_2_), channel_id=1, source_target_pairs={{0,2},{1,15},{2,4},{3,1},{4,6},{5,3},{6,8},{7,5},{8,10},{9,7},{10,... | collective-permute-start | bytes 1572872 | tf_op jit(solution)/shard_map/ppermute | solution.py:39
  61.7 15.7 %collective-permute-start.8 = (f32[2,8,64,128]{3,2,1,0:T(8,128)}, f32[2,8,64,128]{3,2,1,0:T(8,128)}, u32[]{:S(2)}, u32[]{:S(2)}) collective-permute-start(f32[2,8,64,128]{3,2,1,0:T(8,128)} %collective-permute-done.6.refs_6_), channel_id=1, source_target_pairs={{0,14},{1,3},{2,0},{3,5},{4,2},{5,7},{6,4},{7,9},{8,6},{9,11},{10,... | collective-permute-start | bytes 1572872 | tf_op jit(solution)/shard_map/ppermute | solution.py:39
  65.8 25.8 %collective-permute-start.7 = (f32[2,8,64,128]{3,2,1,0:T(8,128)}, f32[2,8,64,128]{3,2,1,0:T(8,128)}, u32[]{:S(2)}, u32[]{:S(2)}) collective-permute-start(f32[2,8,64,128]{3,2,1,0:T(8,128)} %collective-permute-done.5.refs_3_), channel_id=1, source_target_pairs={{0,2},{1,15},{2,4},{3,1},{4,6},{5,3},{6,8},{7,5},{8,10},{9,7},{10,... | collective-permute-start | bytes 1572872 | tf_op jit(solution)/shard_map/ppermute | solution.py:39
  71.9 5.1 %copy-start.4 = (f32[2,8,64,128]{3,2,1,0:T(8,128)S(1)}, f32[2,8,64,128]{3,2,1,0:T(8,128)}, u32[]{:S(2)}) copy-start(f32[2,8,64,128]{3,2,1,0:T(8,128)} %copy-done.3) | copy-start | bytes 1572868
  71.9 5.1 %copy-start.6 = (f32[2,8,64,128]{3,2,1,0:T(8,128)S(1)}, f32[2,8,64,128]{3,2,1,0:T(8,128)}, u32[]{:S(2)}) copy-start(f32[2,8,64,128]{3,2,1,0:T(8,128)} %copy-done.5) | copy-start | bytes 1572868
  71.9 5.2 %copy-start.8 = (f32[2,8,64,128]{3,2,1,0:T(8,128)S(1)}, f32[2,8,64,128]{3,2,1,0:T(8,128)}, u32[]{:S(2)}) copy-start(f32[2,8,64,128]{3,2,1,0:T(8,128)} %copy-done.7) | copy-start | bytes 1572868
  71.9 1.0 copy-start.1
  80.1 16.5 %collective-permute-start.11 = (f32[3,2,8,64,128]{4,3,2,1,0:T(8,128)}, f32[3,2,8,64,128]{4,3,2,1,0:T(8,128)}, u32[]{:S(2)}, u32[]{:S(2)}) collective-permute-start(f32[3,2,8,64,128]{4,3,2,1,0:T(8,128)} %pad_maximum_fusion.1), channel_id=1, source_target_pairs={{0,1},{1,0},{2,3},{3,2},{4,5},{5,4},{6,7},{7,6},{8,9},{9,8},{10,11... | collective-permute-start | bytes 4718600 | tf_op jit(solution)/shard_map/ppermute | solution.py:39
  89.6 7.0 %collective-permute-start.10 = (f32[4,2,8,64,128]{4,3,2,1,0:T(8,128)S(1)}, f32[4,2,8,64,128]{4,3,2,1,0:T(8,128)}, u32[]{:S(2)}, u32[]{:S(2)}) collective-permute-start(f32[4,2,8,64,128]{4,3,2,1,0:T(8,128)S(1)} %pad_maximum_fusion), channel_id=1, source_target_pairs={{0,1},{1,0},{2,3},{3,2},{4,5},{5,4},{6,7},{7,6},{8,9},{9,8},{10,11... | collective-permute-start | bytes 6291464 | tf_op jit(solution)/shard_map/ppermute | solution.py:39
  91.6 5.1 %collective-permute-start.12 = (f32[1,2,8,64,128]{4,3,2,1,0:T(8,128)}, f32[1,2,8,64,128]{4,3,2,1,0:T(8,128)S(1)}, u32[]{:S(2)}, u32[]{:S(2)}) collective-permute-start(f32[1,2,8,64,128]{4,3,2,1,0:T(8,128)} %bitcast.17), channel_id=1, source_target_pairs={{0,1},{1,0},{2,3},{3,2},{4,5},{5,4},{6,7},{7,6},{8,9},{9,8},{10,11... | collective-permute-start | bytes 1572872 | tf_op jit(solution)/shard_map/ppermute | solution.py:39
  96.7 0.8 copy-start.9
  124.2 29.8 %all-to-all-start.1 = ((f32[64,1,128]{2,1,0:T(1,128)}), f32[64,1,128]{2,1,0:T(1,128)S(1)}, u32[]{:S(2)}, u32[]{:S(2)}) async-start(f32[64,1,128]{2,1,0:T(1,128)} %bitcast.34), calls=%async_computation.1 | async-start | bytes 65536 | tf_op jit(solution)/shard_map/all_to_all | solution.py:268
Sparse Core Ops, SparseCore 0:
  9.4 63.7 all-gather.2

commit v7 on v4

--- a/solution.py
+++ b/solution.py
@@ -56,28 +56,39 @@
     return lax.dot_general(a, b, (((1,), (0,)), ((), ())), preferred_element_type=jnp.float32)
 
 
-def amplitudes_kernel(t_own, t_oth, high_out, low_out):
+def amplitudes_kernel(block, out, raw, parts, sems):
+    copy = pltpu.make_async_copy(block, raw, sems.at[0])
+    copy.start()
+    copy.wait()
     for d in range(32):
-        for half, ref in enumerate((t_own, t_oth)):
-            high, low = split(ref[pl.ds(d, 64, 32), :])
-            high_out[d * 128 + half * 64 : d * 128 + half * 64 + 64, :] = high
-            low_out[d * 128 + half * 64 : d * 128 + half * 64 + 64, :] = low
-
-
-def split_amplitudes(t_own, t_oth):
-    shape = jax.ShapeDtypeStruct((4096, 128), jnp.bfloat16)
+        high, low = split(raw[pl.ds(d, 64, 32), :])
+        parts[0, d] = high
+        parts[1, d] = low
+    copy = pltpu.make_async_copy(parts, out, sems.at[1])
+    copy.start()
+    copy.wait()
+
+
+def split_amplitudes(block):
     return pl.pallas_call(
         amplitudes_kernel,
-        out_shape=(shape, shape),
+        out_shape=pltpu.HBM((2, 32, 64, 128), jnp.bfloat16),
+        in_specs=[pl.BlockSpec(memory_space=pl.ANY)],
+        out_specs=pl.BlockSpec(memory_space=pltpu.HBM),
+        scratch_shapes=[
+            pltpu.VMEM((2048, 128), jnp.float32),
+            pltpu.VMEM((2, 32, 64, 128), jnp.bfloat16),
+            pltpu.SemaphoreType.DMA((2,)),
+        ],
         compiler_params=pltpu.CompilerParams(vmem_limit_bytes=8 * 1024 * 1024),
-        cost_estimate=pl.CostEstimate(flops=1 << 20, bytes_accessed=4 << 20, transcendentals=0),
+        cost_estimate=pl.CostEstimate(flops=1 << 20, bytes_accessed=2 << 20, transcendentals=0),
         name="split_amplitudes",
-    )(t_own.reshape(2048, 128), t_oth.reshape(2048, 128))
+    )(pltpu.with_memory_space_constraint(block.reshape(2048, 128), pltpu.HBM))
 
 
 def ladder_kernel(place, right, *refs):
-    pieces, (t_high_in, t_low_in, out) = (refs[:8], refs[8:16]), refs[16:19]
-    r_buf, raw, parts, t_high, t_low, acc, y_high, y_low, flip, r_sem, l_sem, t_sem = refs[19:]
+    pieces, (t_own, t_oth, out) = (refs[:8], refs[8:16]), refs[16:19]
+    r_buf, raw, parts, t_buf, acc, y_high, y_low, flip, r_sem, l_sem, t_sem = refs[19:]
     y, sign, xl_here, xh, core = (place[i] for i in range(5))
 
     def pair(k):
@@ -98,8 +109,7 @@
         return parts[side, slot, order]
 
     t_copies = [
-        pltpu.make_async_copy(t_high_in, t_high, t_sem.at[0]),
-        pltpu.make_async_copy(t_low_in, t_low, t_sem.at[1]),
+        pltpu.make_async_copy(ref, t_buf.at[:, :, half], t_sem.at[half]) for half, ref in enumerate((t_own, t_oth))
     ]
     for k in range(4):
         for slot in NEEDED[k]:
@@ -144,7 +154,8 @@
             high, low = split(acc[a, pl.ds(d, 16, 32), :])
             y_high[a * 16 : a * 16 + 16, d * 128 : d * 128 + 128] = high
             y_low[a * 16 : a * 16 + 16, d * 128 : d * 128 + 128] = low
-    total = dot_nn(y_high[...], t_high[...]) + dot_nn(y_high[...], t_low[...]) + dot_nn(y_low[...], t_high[...])
+    t_high, t_low = (t_buf[i].reshape(4096, 128) for i in range(2))
+    total = dot_nn(y_high[...], t_high) + dot_nn(y_high[...], t_low) + dot_nn(y_low[...], t_high)
     for a in range(8):
         flip[pl.ds(a, 16, 8), :] = total[a * 16 : a * 16 + 16]
     total = flip[...].T
@@ -166,8 +177,7 @@
             pltpu.VMEM((4, 2, 16, 32, 256), jnp.float32),
             pltpu.VMEM((2, 8, 2, 8, 64, 128), jnp.float32),
             pltpu.VMEM((2, 8, 2, 8, 64, 256), jnp.bfloat16),
-            pltpu.VMEM((4096, 128), jnp.bfloat16),
-            pltpu.VMEM((4096, 128), jnp.bfloat16),
+            pltpu.VMEM((2, 32, 2, 64, 128), jnp.bfloat16),
             pltpu.VMEM((8, 512, 128), jnp.float32),
             pltpu.VMEM((128, 4096), jnp.bfloat16),
             pltpu.VMEM((128, 4096), jnp.bfloat16),
@@ -210,18 +220,22 @@
     xh, y, core = (lax.axis_index(name) for name in ("xh", "y", "core"))
     place = jnp.stack([y, 1 - 2 * core, lax.axis_index("xl"), xh, core]).astype(jnp.int32)
     right = lax.all_gather(vectors_right, "z", axis=0)
-    own = jnp.stack([send(vectors_left, SAME_XL), send(vectors_left, OTHER_XL)])
+    t_own_split = split_amplitudes(amplitudes)
+    same, other = send(vectors_left, SAME_XL), send(vectors_left, OTHER_XL)
+    own = jnp.stack([after(same, t_own_split), other])
+    x1 = send(own, RING_X)
     t_oth = send(amplitudes, SWAP_XH)
-    x1 = send(own, RING_X)
     y1 = send(own, RING_Y)
+    own_swapped = send(own, SWAP_CORE)
     x2 = send(x1, RING_X)
     y2 = send(after(y1, x1), RING_Y)
-    x3 = send(after(x2, y1, t_oth), RING_X)
+    x1_swapped = send(after(x1, own_swapped), SWAP_CORE)
+    x3 = send(after(x2, y1), RING_X)
     y3 = send(after(y2, x2), RING_Y)
-    x4 = send(after(x3, y2), RING_X)
+    x4 = send(after(x3, y2, t_oth), RING_X)
+    t_split = (t_own_split, split_amplitudes(after(t_oth, x4)))
     left_own = [own, x1, x2, x3, x4, y3, y2, y1]
-    t_split = split_amplitudes(amplitudes, t_oth)
-    left_oth = [send(after(piece, *t_split) if piece is y3 else piece, SWAP_CORE) for piece in left_own]
+    left_oth = [own_swapped, x1_swapped] + [send(piece, SWAP_CORE) for piece in left_own[2:]]
     partial = contract(place, right, left_own, left_oth, t_split)
     near = pack(lax.all_to_all(partial, ("xh", "xl", "core"), 0, 0, tiled=True))
     far = jnp.sum(lax.all_to_all(near, ("z", "y"), 0, 0, tiled=True), axis=0)

time: 161 us -> 158 us (0.981)
  waiting for transfers between devices: 33.6 us -> 28.8 us
  Pallas kernels: 18.3 us -> 22.3 us
  local copies, waits for them, and re-layouts: 4.63 us -> 1.32 us
    all_to_all x1, starting transfers between devices: 15.7 us -> 20.6 us  [shards(): far = jnp.sum(lax.all_to_all(near, ('z', 'y'), 0, 0, tiled=True), axis=0)]
    ppermute x18, waiting for transfers between devices: 22.1 us -> 17.3 us  [send(): return lax.ppermute(array, AXES, pairs)]
    pallas_call x1 -> x2, Pallas kernels: 1.76 us -> 5.82 us  [split_amplitudes(): pl.pallas_call(amplitudes_kernel, out_shape=pltpu.HBM((2, 32, 64, 128), j...]
    ppermute x18, starting transfers between devices: 64.4 us -> 60.6 us  [send(): return lax.ppermute(array, AXES, pairs)]
    unnamed x24 -> x16, local copies, waits for them, and re-layouts: 3.27 us -> 0.03 us
  transfers between devices with their start and end apart: 20 -> 20, of which waited for: 7 -> 5; matrix products, arithmetic and copies ran while one was open for 0% -> 0% of each run, Pallas kernels for 1% -> 4%
where the time goes in v7:
time: 158 us; the launch traced here: 157 us
  starting transfers between devices  81.2 us (51%)
  waiting for transfers between devices  28.8 us (18%)
  Pallas kernels  22.3 us (14%)
  between operations  13.8 us (9%)
  blocking collectives  9.72 us (6%)
    ppermute x18, starting transfers between devices, send(): return lax.ppermute(array, AXES, pairs)  60.6 us
    all_to_all x1, starting transfers between devices, shards(): far = jnp.sum(lax.all_to_all(near, ('z', 'y'), 0, 0, tiled=True), axis=0)  20.6 us
    ppermute x18, waiting for transfers between devices, send(): return lax.ppermute(array, AXES, pairs)  17.3 us
    pallas_call x1, Pallas kernels, contract(): pl.pallas_call(ladder_kernel, out_shape=jax.ShapeDtypeStruct((8, 32, 128)...  14.9 us
    all_to_all x1, waiting for transfers between devices, shards(): far = jnp.sum(lax.all_to_all(near, ('z', 'y'), 0, 0, tiled=True), axis=0)  10.8 us
    all_to_all x1, blocking collectives, shards(): near = pack(lax.all_to_all(partial, ('xh', 'xl', 'core'), 0, 0, tiled=True))  9.72 us
    pallas_call x2, Pallas kernels, split_amplitudes(): pl.pallas_call(amplitudes_kernel, out_shape=pltpu.HBM((2, 32, 64, 128), j...  5.82 us
  transfers between devices with their start and end apart: 20, of which 5 were waited for; matrix products, arithmetic and copies ran while one was open for 0% of the time, Pallas kernels for 4%

profile of v7, /device:TPU:1, one launch (start us, length us, event | category | flops | bytes accessed | tf_op | source)
XLA Modules:
  0.0 157.3 jit_solution(2506497106592636241)
XLA Ops:
  6.5 0.7 all-gather.3.cloned.1.call-update
  7.3 1.6 %collective-permute-start = (f32[8,64,128]{2,1,0:T(8,128)}, f32[8,64,128]{2,1,0:T(8,128)S(1)}, u32[]{:S(2)}, u32[]{:S(2)}) collective-permute-start(f32[8,64,128]{2,1,0:T(8,128)} %param.3), channel_id=1, source_target_pairs={{0,0},{1,1},{2,32},{3,33},{4,4},{5,5},{6,36},{7,37},{8,8},{9,9},{1... | collective-permute-start | bytes 786440 | tf_op jit(solution)/shard_map/ppermute | solution.py:38
  8.9 3.9 %collective-permute-start.1 = (f32[8,64,128]{2,1,0:T(8,128)}, f32[8,64,128]{2,1,0:T(8,128)S(1)}, u32[]{:S(2)}, u32[]{:S(2)}) collective-permute-start(f32[8,64,128]{2,1,0:T(8,128)} %param.3), channel_id=1, source_target_pairs={{0,16},{1,17},{2,48},{3,49},{4,20},{5,21},{6,52},{7,53},{8,24},{9,... | collective-permute-start | bytes 786440 | tf_op jit(solution)/shard_map/ppermute | solution.py:38
  12.8 2.9 %split_amplitudes.2.refs_16_ = bf16[2,32,64,128]{3,2,1,0:T(8,128)(2,1)} custom-call(f32[2048,128]{1,0:T(8,128)} %bitcast.18), custom_call_target="tpu_custom_call" | custom-call | flops 1048576 | bytes 2097152 | tf_op jit(solution)/shard_map/split_amplitudes/pallas_call | solution.py:73
  15.7 0.0 collective-permute-done
  15.8 8.1 %collective-permute-done.1 = f32[8,64,128]{2,1,0:T(8,128)S(1)} collective-permute-done((f32[8,64,128]{2,1,0:T(8,128)}, f32[8,64,128]{2,1,0:T(8,128)S(1)}, u32[]{:S(2)}, u32[]{:S(2)}) %collective-permute-start.1) | collective-permute-done | bytes 262176 | tf_op jit(solution)/shard_map/ppermute | solution.py:38
  23.9 7.4 %collective-permute-start.2 = (f32[2,8,64,128]{3,2,1,0:T(8,128)S(1)}, f32[2,8,64,128]{3,2,1,0:T(8,128)S(1)}, u32[]{:S(2)}, u32[]{:S(2)}) collective-permute-start(f32[2,8,64,128]{3,2,1,0:T(8,128)S(1)} %pad_maximum_fusion.refs_0_), channel_id=1, source_target_pairs={{0,2},{1,15},{2,4},{3,1},{4,6},{5,3},{6,8},{7,5},{8,10},{9,7},{10,... | collective-permute-start | bytes 1572872 | tf_op jit(solution)/shard_map/ppermute | solution.py:38
  31.3 1.9 %collective-permute-start.4 = (f32[2,8,64,128]{3,2,1,0:T(8,128)S(1)}, f32[2,8,64,128]{3,2,1,0:T(8,128)S(1)}, u32[]{:S(2)}, u32[]{:S(2)}) collective-permute-start(f32[2,8,64,128]{3,2,1,0:T(8,128)S(1)} %pad_maximum_fusion.refs_0_), channel_id=1, source_target_pairs={{0,14},{1,3},{2,0},{3,5},{4,2},{5,7},{6,4},{7,9},{8,6},{9,11},{10,... | collective-permute-start | bytes 1572872 | tf_op jit(solution)/shard_map/ppermute | solution.py:38
  33.2 5.9 %collective-permute-done.2.refs_1_ = f32[2,8,64,128]{3,2,1,0:T(8,128)S(1)} collective-permute-done((f32[2,8,64,128]{3,2,1,0:T(8,128)S(1)}, f32[2,8,64,128]{3,2,1,0:T(8,128)S(1)}, u32[]{:S(2)}, u32[]{:S(2)}) %collective-permute-start.2) | collective-permute-done | bytes 524320 | tf_op jit(solution)/shard_map/ppermute | solution.py:38
  39.1 5.4 %collective-permute-start.3 = (f32[2,8,64,128]{3,2,1,0:T(8,128)S(1)}, f32[2,8,64,128]{3,2,1,0:T(8,128)S(1)}, u32[]{:S(2)}, u32[]{:S(2)}) collective-permute-start(f32[2,8,64,128]{3,2,1,0:T(8,128)S(1)} %collective-permute-done.2.refs_1_), channel_id=1, source_target_pairs={{0,2},{1,15},{2,4},{3,1},{4,6},{5,3},{6,8},{7,5},{8,10},{9,7},{10,... | collective-permute-start | bytes 1572872 | tf_op jit(solution)/shard_map/ppermute | solution.py:38
  44.5 4.2 %collective-permute-start.7 = (f32[64,32,128]{2,1,0:T(8,128)}, f32[64,32,128]{2,1,0:T(8,128)S(1)}, u32[]{:S(2)}, u32[]{:S(2)}) collective-permute-start(f32[64,32,128]{2,1,0:T(8,128)} %param.5), channel_id=1, source_target_pairs={{0,32},{1,33},{2,34},{3,35},{4,36},{5,37},{6,38},{7,39},{8,40},{9,... | collective-permute-start | bytes 3145736 | tf_op jit(solution)/shard_map/ppermute | solution.py:38
  48.7 4.4 %collective-permute-start.10 = (f32[2,8,64,128]{3,2,1,0:T(8,128)S(1)}, f32[2,8,64,128]{3,2,1,0:T(8,128)S(1)}, u32[]{:S(2)}, u32[]{:S(2)}) collective-permute-start(f32[2,8,64,128]{3,2,1,0:T(8,128)S(1)} %pad_maximum_fusion.refs_0_), channel_id=1, source_target_pairs={{0,1},{1,0},{2,3},{3,2},{4,5},{5,4},{6,7},{7,6},{8,9},{9,8},{10,11... | collective-permute-start | bytes 1572872 | tf_op jit(solution)/shard_map/ppermute | solution.py:38
  53.1 0.0 collective-permute-done.4.refs_7_
  53.1 4.1 %collective-permute-start.6 = (f32[2,8,64,128]{3,2,1,0:T(8,128)S(1)}, f32[2,8,64,128]{3,2,1,0:T(8,128)}, u32[]{:S(2)}, u32[]{:S(2)}) collective-permute-start(f32[2,8,64,128]{3,2,1,0:T(8,128)S(1)} %collective-permute-done.4.refs_7_), channel_id=1, source_target_pairs={{0,14},{1,3},{2,0},{3,5},{4,2},{5,7},{6,4},{7,9},{8,6},{9,11},{10,... | collective-permute-start | bytes 1572872 | tf_op jit(solution)/shard_map/ppermute | solution.py:38
  57.2 0.0 collective-permute-done.3.refs_2_
  57.3 2.4 %collective-permute-start.5 = (f32[2,8,64,128]{3,2,1,0:T(8,128)S(1)}, f32[2,8,64,128]{3,2,1,0:T(8,128)}, u32[]{:S(2)}, u32[]{:S(2)}) collective-permute-start(f32[2,8,64,128]{3,2,1,0:T(8,128)S(1)} %collective-permute-done.3.refs_2_), channel_id=1, source_target_pairs={{0,2},{1,15},{2,4},{3,1},{4,6},{5,3},{6,8},{7,5},{8,10},{9,7},{10,... | collective-permute-start | bytes 1572872 | tf_op jit(solution)/shard_map/ppermute | solution.py:38
  59.7 0.0 collective-permute-done.10.refs_8_
  59.7 1.9 %collective-permute-start.11 = (f32[2,8,64,128]{3,2,1,0:T(8,128)S(1)}, f32[2,8,64,128]{3,2,1,0:T(8,128)S(1)}, u32[]{:S(2)}, u32[]{:S(2)}) collective-permute-start(f32[2,8,64,128]{3,2,1,0:T(8,128)S(1)} %collective-permute-done.2.refs_1_), channel_id=1, source_target_pairs={{0,1},{1,0},{2,3},{3,2},{4,5},{5,4},{6,7},{7,6},{8,9},{9,8},{10,11... | collective-permute-start | bytes 1572872 | tf_op jit(solution)/shard_map/ppermute | solution.py:38
  61.6 2.4 %collective-permute-start.17 = (f32[2,8,64,128]{3,2,1,0:T(8,128)S(1)}, f32[2,8,64,128]{3,2,1,0:T(8,128)S(1)}, u32[]{:S(2)}, u32[]{:S(2)}) collective-permute-start(f32[2,8,64,128]{3,2,1,0:T(8,128)S(1)} %collective-permute-done.4.refs_7_), channel_id=1, source_target_pairs={{0,1},{1,0},{2,3},{3,2},{4,5},{5,4},{6,7},{7,6},{8,9},{9,8},{10,11... | collective-permute-start | bytes 1572872 | tf_op jit(solution)/shard_map/ppermute | solution.py:38
  64.0 2.6 %collective-permute-done.6.refs_6_ = f32[2,8,64,128]{3,2,1,0:T(8,128)} collective-permute-done((f32[2,8,64,128]{3,2,1,0:T(8,128)S(1)}, f32[2,8,64,128]{3,2,1,0:T(8,128)}, u32[]{:S(2)}, u32[]{:S(2)}) %collective-permute-start.6) | collective-permute-done | bytes 524320 | tf_op jit(solution)/shard_map/ppermute | solution.py:38
  66.6 4.0 %collective-permute-start.9 = (f32[2,8,64,128]{3,2,1,0:T(8,128)}, f32[2,8,64,128]{3,2,1,0:T(8,128)}, u32[]{:S(2)}, u32[]{:S(2)}) collective-permute-start(f32[2,8,64,128]{3,2,1,0:T(8,128)} %collective-permute-done.6.refs_6_), channel_id=1, source_target_pairs={{0,14},{1,3},{2,0},{3,5},{4,2},{5,7},{6,4},{7,9},{8,6},{9,11},{10,... | collective-permute-start | bytes 1572872 | tf_op jit(solution)/shard_map/ppermute | solution.py:38
  70.7 0.7 collective-permute-done.7
  71.4 0.0 collective-permute-done.5.refs_3_
  71.4 1.9 %collective-permute-start.8 = (f32[2,8,64,128]{3,2,1,0:T(8,128)}, f32[2,8,64,128]{3,2,1,0:T(8,128)}, u32[]{:S(2)}, u32[]{:S(2)}) collective-permute-start(f32[2,8,64,128]{3,2,1,0:T(8,128)} %collective-permute-done.5.refs_3_), channel_id=1, source_target_pairs={{0,2},{1,15},{2,4},{3,1},{4,6},{5,3},{6,8},{7,5},{8,10},{9,7},{10,... | collective-permute-start | bytes 1572872 | tf_op jit(solution)/shard_map/ppermute | solution.py:38
  73.3 4.2 %collective-permute-start.16 = (f32[2,8,64,128]{3,2,1,0:T(8,128)}, f32[2,8,64,128]{3,2,1,0:T(8,128)}, u32[]{:S(2)}, u32[]{:S(2)}) collective-permute-start(f32[2,8,64,128]{3,2,1,0:T(8,128)} %collective-permute-done.6.refs_6_), channel_id=1, source_target_pairs={{0,1},{1,0},{2,3},{3,2},{4,5},{5,4},{6,7},{7,6},{8,9},{9,8},{10,11... | collective-permute-start | bytes 1572872 | tf_op jit(solution)/shard_map/ppermute | solution.py:38
  77.5 0.0 collective-permute-done.11.refs_9_
  77.5 1.9 %collective-permute-start.12 = (f32[2,8,64,128]{3,2,1,0:T(8,128)S(1)}, f32[2,8,64,128]{3,2,1,0:T(8,128)}, u32[]{:S(2)}, u32[]{:S(2)}) collective-permute-start(f32[2,8,64,128]{3,2,1,0:T(8,128)S(1)} %collective-permute-done.3.refs_2_), channel_id=1, source_target_pairs={{0,1},{1,0},{2,3},{3,2},{4,5},{5,4},{6,7},{7,6},{8,9},{9,8},{10,11... | collective-permute-start | bytes 1572872 | tf_op jit(solution)/shard_map/ppermute | solution.py:38
  79.5 0.0 collective-permute-done.17.refs_15_
  79.5 2.4 %collective-permute-start.13 = (f32[2,8,64,128]{3,2,1,0:T(8,128)}, f32[2,8,64,128]{3,2,1,0:T(8,128)}, u32[]{:S(2)}, u32[]{:S(2)}) collective-permute-start(f32[2,8,64,128]{3,2,1,0:T(8,128)} %collective-permute-done.5.refs_3_), channel_id=1, source_target_pairs={{0,1},{1,0},{2,3},{3,2},{4,5},{5,4},{6,7},{7,6},{8,9},{9,8},{10,11... | collective-permute-start | bytes 1572872 | tf_op jit(solution)/shard_map/ppermute | solution.py:38
  81.9 0.0 collective-permute-done.9.refs_5_
  82.0 1.9 %collective-permute-start.15 = (f32[2,8,64,128]{3,2,1,0:T(8,128)}, f32[2,8,64,128]{3,2,1,0:T(8,128)}, u32[]{:S(2)}, u32[]{:S(2)}) collective-permute-start(f32[2,8,64,128]{3,2,1,0:T(8,128)} %collective-permute-done.9.refs_5_), channel_id=1, source_target_pairs={{0,1},{1,0},{2,3},{3,2},{4,5},{5,4},{6,7},{7,6},{8,9},{9,8},{10,11... | collective-permute-start | bytes 1572872 | tf_op jit(solution)/shard_map/ppermute | solution.py:38
  83.9 0.0 collective-permute-done.8.refs_4_
  83.9 4.5 %collective-permute-start.14 = (f32[2,8,64,128]{3,2,1,0:T(8,128)}, f32[2,8,64,128]{3,2,1,0:T(8,128)}, u32[]{:S(2)}, u32[]{:S(2)}) collective-permute-start(f32[2,8,64,128]{3,2,1,0:T(8,128)} %collective-permute-done.8.refs_4_), channel_id=1, source_target_pairs={{0,1},{1,0},{2,3},{3,2},{4,5},{5,4},{6,7},{7,6},{8,9},{9,8},{10,11... | collective-permute-start | bytes 1572872 | tf_op jit(solution)/shard_map/ppermute | solution.py:38
  88.4 0.6 stack.32.place
  89.0 2.9 %split_amplitudes.3.refs_17_ = bf16[2,32,64,128]{3,2,1,0:T(8,128)(2,1)} custom-call(f32[2048,128]{1,0:T(8,128)} %bitcast.19), custom_call_target="tpu_custom_call" | custom-call | flops 1048576 | bytes 2097152 | tf_op jit(solution)/shard_map/split_amplitudes/pallas_call | solution.py:73
  91.9 0.0 collective-permute-done.16.refs_14_
  91.9 0.0 collective-permute-done.12.refs_10_
  91.9 0.0 collective-permute-done.13.refs_11_
  91.9 0.0 collective-permute-done.14.refs_12_
  91.9 0.0 all-gather.3.cloned.1.call-done
  92.0 14.9 %ladder.1 = f32[8,32,128]{2,1,0:T(8,128)} custom-call(s32[5]{0:T(128)} %stack.32.place, f32[8,16,32,256]{3,2,1,0:T(8,128)} %bitcast.24, f32[2,8,64,128]{3,2,1,0:T(8,128)} %copy-done.1, f32[2,8,64,128]{3,2,1,0:T(8,128)} %copy-done.2, f32[2,8,64,128]{3,2,1,0:T(8,128)} %copy-done.4, f32[2,8,64,128]{3,2,1,0:T(8,128)} %collective-permute-done.5.refs_3_, ...), custom_call_target="tpu_custom_call" | custom-call | flops 6442450944 | bytes 16777216 | tf_op jit(solution)/shard_map/ladder/pallas_call | solution.py:171
  106.9 9.7 %all_to_all.14.near = f32[8,32,128]{2,1,0:T(8,128)} all-to-all(f32[8,32,128]{2,1,0:T(8,128)} %ladder.1), channel_id=1, replica_groups=mesh['z'=8,'xh'=2,'xl'=2,'y'=8,'core'=2] {'xh','xl','core'}, dimensions={0} | all-to-all | bytes 262144 | tf_op jit(solution)/shard_map/all_to_all | solution.py:240
  116.6 1.6 %pack.1 = f32[64,128]{1,0:T(8,128)} custom-call(f32[8,32,128]{2,1,0:T(8,128)} %all_to_all.14.near), custom_call_target="tpu_custom_call" | custom-call | tf_op jit(solution)/shard_map/pack/pallas_call | solution.py:211
  118.2 20.6 %all-to-all-start.1 = ((f32[64,1,128]{2,1,0:T(1,128)}), f32[64,1,128]{2,1,0:T(1,128)S(1)}, u32[]{:S(2)}, u32[]{:S(2)}) async-start(f32[64,1,128]{2,1,0:T(1,128)} %bitcast.22), calls=%async_computation.1 | async-start | bytes 65536 | tf_op jit(solution)/shard_map/all_to_all | solution.py:241
  138.8 10.8 %all-to-all-done.1 = f32[64,1,128]{2,1,0:T(1,128)S(1)} async-done(((f32[64,1,128]{2,1,0:T(1,128)}), f32[64,1,128]{2,1,0:T(1,128)S(1)}, u32[]{:S(2)}, u32[]{:S(2)}) %all-to-all-start.1) | async-done | bytes 32800 | tf_op jit(solution)/shard_map/all_to_all | solution.py:241
  149.7 0.1 reduce_sum.9
  149.8 0.1 reshape.24
  149.9 0.6 dynamic-slice_bitcast_fusion
  (19 shorter events, 0.1 us)
Async XLA Ops:
  6.5 85.4 %all-gather.3.cloned.1.call-start = ((), (), s32[]{:S(2)}) async-start(), calls=%async_computation.2 | async-start | bytes 4718592 | tf_op jit(solution)/shard_map/all_gather | solution.py:222
  7.3 8.5 %collective-permute-start = (f32[8,64,128]{2,1,0:T(8,128)}, f32[8,64,128]{2,1,0:T(8,128)S(1)}, u32[]{:S(2)}, u32[]{:S(2)}) collective-permute-start(f32[8,64,128]{2,1,0:T(8,128)} %param.3), channel_id=1, source_target_pairs={{0,0},{1,1},{2,32},{3,33},{4,4},{5,5},{6,36},{7,37},{8,8},{9,9},{1... | collective-permute-start | bytes 786440 | tf_op jit(solution)/shard_map/ppermute | solution.py:38
  8.9 15.0 %collective-permute-start.1 = (f32[8,64,128]{2,1,0:T(8,128)}, f32[8,64,128]{2,1,0:T(8,128)S(1)}, u32[]{:S(2)}, u32[]{:S(2)}) collective-permute-start(f32[8,64,128]{2,1,0:T(8,128)} %param.3), channel_id=1, source_target_pairs={{0,16},{1,17},{2,48},{3,49},{4,20},{5,21},{6,52},{7,53},{8,24},{9,... | collective-permute-start | bytes 786440 | tf_op jit(solution)/shard_map/ppermute | solution.py:38
  23.9 68.1 %copy-start.1 = (f32[2,8,64,128]{3,2,1,0:T(8,128)}, f32[2,8,64,128]{3,2,1,0:T(8,128)S(1)}, u32[]{:S(2)}) copy-start(f32[2,8,64,128]{3,2,1,0:T(8,128)S(1)} %pad_maximum_fusion.refs_0_) | copy-start | bytes 1572868
  23.9 15.2 %collective-permute-start.2 = (f32[2,8,64,128]{3,2,1,0:T(8,128)S(1)}, f32[2,8,64,128]{3,2,1,0:T(8,128)S(1)}, u32[]{:S(2)}, u32[]{:S(2)}) collective-permute-start(f32[2,8,64,128]{3,2,1,0:T(8,128)S(1)} %pad_maximum_fusion.refs_0_), channel_id=1, source_target_pairs={{0,2},{1,15},{2,4},{3,1},{4,6},{5,3},{6,8},{7,5},{8,10},{9,7},{10,... | collective-permute-start | bytes 1572872 | tf_op jit(solution)/shard_map/ppermute | solution.py:38
  31.3 21.8 %collective-permute-start.4 = (f32[2,8,64,128]{3,2,1,0:T(8,128)S(1)}, f32[2,8,64,128]{3,2,1,0:T(8,128)S(1)}, u32[]{:S(2)}, u32[]{:S(2)}) collective-permute-start(f32[2,8,64,128]{3,2,1,0:T(8,128)S(1)} %pad_maximum_fusion.refs_0_), channel_id=1, source_target_pairs={{0,14},{1,3},{2,0},{3,5},{4,2},{5,7},{6,4},{7,9},{8,6},{9,11},{10,... | collective-permute-start | bytes 1572872 | tf_op jit(solution)/shard_map/ppermute | solution.py:38
  39.1 52.9 %copy-start.2 = (f32[2,8,64,128]{3,2,1,0:T(8,128)}, f32[2,8,64,128]{3,2,1,0:T(8,128)S(1)}, u32[]{:S(2)}) copy-start(f32[2,8,64,128]{3,2,1,0:T(8,128)S(1)} %collective-permute-done.2.refs_1_) | copy-start | bytes 1572868
  39.1 18.2 %collective-permute-start.3 = (f32[2,8,64,128]{3,2,1,0:T(8,128)S(1)}, f32[2,8,64,128]{3,2,1,0:T(8,128)S(1)}, u32[]{:S(2)}, u32[]{:S(2)}) collective-permute-start(f32[2,8,64,128]{3,2,1,0:T(8,128)S(1)} %collective-permute-done.2.refs_1_), channel_id=1, source_target_pairs={{0,2},{1,15},{2,4},{3,1},{4,6},{5,3},{6,8},{7,5},{8,10},{9,7},{10,... | collective-permute-start | bytes 1572872 | tf_op jit(solution)/shard_map/ppermute | solution.py:38
  44.5 26.9 %collective-permute-start.7 = (f32[64,32,128]{2,1,0:T(8,128)}, f32[64,32,128]{2,1,0:T(8,128)S(1)}, u32[]{:S(2)}, u32[]{:S(2)}) collective-permute-start(f32[64,32,128]{2,1,0:T(8,128)} %param.5), channel_id=1, source_target_pairs={{0,32},{1,33},{2,34},{3,35},{4,36},{5,37},{6,38},{7,39},{8,40},{9,... | collective-permute-start | bytes 3145736 | tf_op jit(solution)/shard_map/ppermute | solution.py:38
  48.7 10.9 %collective-permute-start.10 = (f32[2,8,64,128]{3,2,1,0:T(8,128)S(1)}, f32[2,8,64,128]{3,2,1,0:T(8,128)S(1)}, u32[]{:S(2)}, u32[]{:S(2)}) collective-permute-start(f32[2,8,64,128]{3,2,1,0:T(8,128)S(1)} %pad_maximum_fusion.refs_0_), channel_id=1, source_target_pairs={{0,1},{1,0},{2,3},{3,2},{4,5},{5,4},{6,7},{7,6},{8,9},{9,8},{10,11... | collective-permute-start | bytes 1572872 | tf_op jit(solution)/shard_map/ppermute | solution.py:38
  53.1 38.9 %copy-start.3 = (f32[2,8,64,128]{3,2,1,0:T(8,128)}, f32[2,8,64,128]{3,2,1,0:T(8,128)S(1)}, u32[]{:S(2)}) copy-start(f32[2,8,64,128]{3,2,1,0:T(8,128)S(1)} %collective-permute-done.4.refs_7_) | copy-start | bytes 1572868
  53.1 13.5 %collective-permute-start.6 = (f32[2,8,64,128]{3,2,1,0:T(8,128)S(1)}, f32[2,8,64,128]{3,2,1,0:T(8,128)}, u32[]{:S(2)}, u32[]{:S(2)}) collective-permute-start(f32[2,8,64,128]{3,2,1,0:T(8,128)S(1)} %collective-permute-done.4.refs_7_), channel_id=1, source_target_pairs={{0,14},{1,3},{2,0},{3,5},{4,2},{5,7},{6,4},{7,9},{8,6},{9,11},{10,... | collective-permute-start | bytes 1572872 | tf_op jit(solution)/shard_map/ppermute | solution.py:38
  57.3 34.7 %copy-start.4 = (f32[2,8,64,128]{3,2,1,0:T(8,128)}, f32[2,8,64,128]{3,2,1,0:T(8,128)S(1)}, u32[]{:S(2)}) copy-start(f32[2,8,64,128]{3,2,1,0:T(8,128)S(1)} %collective-permute-done.3.refs_2_) | copy-start | bytes 1572868
  57.3 14.1 %collective-permute-start.5 = (f32[2,8,64,128]{3,2,1,0:T(8,128)S(1)}, f32[2,8,64,128]{3,2,1,0:T(8,128)}, u32[]{:S(2)}, u32[]{:S(2)}) collective-permute-start(f32[2,8,64,128]{3,2,1,0:T(8,128)S(1)} %collective-permute-done.3.refs_2_), channel_id=1, source_target_pairs={{0,2},{1,15},{2,4},{3,1},{4,6},{5,3},{6,8},{7,5},{8,10},{9,7},{10,... | collective-permute-start | bytes 1572872 | tf_op jit(solution)/shard_map/ppermute | solution.py:38
  59.7 19.8 %copy-start.5 = (f32[2,8,64,128]{3,2,1,0:T(8,128)}, f32[2,8,64,128]{3,2,1,0:T(8,128)S(1)}, u32[]{:S(2)}) copy-start(f32[2,8,64,128]{3,2,1,0:T(8,128)S(1)} %collective-permute-done.10.refs_8_) | copy-start | bytes 1572868
  59.7 17.8 %collective-permute-start.11 = (f32[2,8,64,128]{3,2,1,0:T(8,128)S(1)}, f32[2,8,64,128]{3,2,1,0:T(8,128)S(1)}, u32[]{:S(2)}, u32[]{:S(2)}) collective-permute-start(f32[2,8,64,128]{3,2,1,0:T(8,128)S(1)} %collective-permute-done.2.refs_1_), channel_id=1, source_target_pairs={{0,1},{1,0},{2,3},{3,2},{4,5},{5,4},{6,7},{7,6},{8,9},{9,8},{10,11... | collective-permute-start | bytes 1572872 | tf_op jit(solution)/shard_map/ppermute | solution.py:38
  61.6 17.9 %collective-permute-start.17 = (f32[2,8,64,128]{3,2,1,0:T(8,128)S(1)}, f32[2,8,64,128]{3,2,1,0:T(8,128)S(1)}, u32[]{:S(2)}, u32[]{:S(2)}) collective-permute-start(f32[2,8,64,128]{3,2,1,0:T(8,128)S(1)} %collective-permute-done.4.refs_7_), channel_id=1, source_target_pairs={{0,1},{1,0},{2,3},{3,2},{4,5},{5,4},{6,7},{7,6},{8,9},{9,8},{10,11... | collective-permute-start | bytes 1572872 | tf_op jit(solution)/shard_map/ppermute | solution.py:38
  66.6 15.3 %collective-permute-start.9 = (f32[2,8,64,128]{3,2,1,0:T(8,128)}, f32[2,8,64,128]{3,2,1,0:T(8,128)}, u32[]{:S(2)}, u32[]{:S(2)}) collective-permute-start(f32[2,8,64,128]{3,2,1,0:T(8,128)} %collective-permute-done.6.refs_6_), channel_id=1, source_target_pairs={{0,14},{1,3},{2,0},{3,5},{4,2},{5,7},{6,4},{7,9},{8,6},{9,11},{10,... | collective-permute-start | bytes 1572872 | tf_op jit(solution)/shard_map/ppermute | solution.py:38
  71.4 17.6 %copy-start = (f32[64,32,128]{2,1,0:T(8,128)}, f32[64,32,128]{2,1,0:T(8,128)S(1)}, u32[]{:S(2)}) copy-start(f32[64,32,128]{2,1,0:T(8,128)S(1)} %collective-permute-done.7) | copy-start | bytes 3145732
  71.4 12.5 %collective-permute-start.8 = (f32[2,8,64,128]{3,2,1,0:T(8,128)}, f32[2,8,64,128]{3,2,1,0:T(8,128)}, u32[]{:S(2)}, u32[]{:S(2)}) collective-permute-start(f32[2,8,64,128]{3,2,1,0:T(8,128)} %collective-permute-done.5.refs_3_), channel_id=1, source_target_pairs={{0,2},{1,15},{2,4},{3,1},{4,6},{5,3},{6,8},{7,5},{8,10},{9,7},{10,... | collective-permute-start | bytes 1572872 | tf_op jit(solution)/shard_map/ppermute | solution.py:38
  73.3 18.6 %collective-permute-start.16 = (f32[2,8,64,128]{3,2,1,0:T(8,128)}, f32[2,8,64,128]{3,2,1,0:T(8,128)}, u32[]{:S(2)}, u32[]{:S(2)}) collective-permute-start(f32[2,8,64,128]{3,2,1,0:T(8,128)} %collective-permute-done.6.refs_6_), channel_id=1, source_target_pairs={{0,1},{1,0},{2,3},{3,2},{4,5},{5,4},{6,7},{7,6},{8,9},{9,8},{10,11... | collective-permute-start | bytes 1572872 | tf_op jit(solution)/shard_map/ppermute | solution.py:38
  77.5 4.4 %copy-start.6 = (f32[2,8,64,128]{3,2,1,0:T(8,128)}, f32[2,8,64,128]{3,2,1,0:T(8,128)S(1)}, u32[]{:S(2)}) copy-start(f32[2,8,64,128]{3,2,1,0:T(8,128)S(1)} %collective-permute-done.11.refs_9_) | copy-start | bytes 1572868
  77.5 14.4 %collective-permute-start.12 = (f32[2,8,64,128]{3,2,1,0:T(8,128)S(1)}, f32[2,8,64,128]{3,2,1,0:T(8,128)}, u32[]{:S(2)}, u32[]{:S(2)}) collective-permute-start(f32[2,8,64,128]{3,2,1,0:T(8,128)S(1)} %collective-permute-done.3.refs_2_), channel_id=1, source_target_pairs={{0,1},{1,0},{2,3},{3,2},{4,5},{5,4},{6,7},{7,6},{8,9},{9,8},{10,11... | collective-permute-start | bytes 1572872 | tf_op jit(solution)/shard_map/ppermute | solution.py:38
  79.5 2.4 %copy-start.7 = (f32[2,8,64,128]{3,2,1,0:T(8,128)}, f32[2,8,64,128]{3,2,1,0:T(8,128)S(1)}, u32[]{:S(2)}) copy-start(f32[2,8,64,128]{3,2,1,0:T(8,128)S(1)} %collective-permute-done.17.refs_15_) | copy-start | bytes 1572868
  79.5 12.4 %collective-permute-start.13 = (f32[2,8,64,128]{3,2,1,0:T(8,128)}, f32[2,8,64,128]{3,2,1,0:T(8,128)}, u32[]{:S(2)}, u32[]{:S(2)}) collective-permute-start(f32[2,8,64,128]{3,2,1,0:T(8,128)} %collective-permute-done.5.refs_3_), channel_id=1, source_target_pairs={{0,1},{1,0},{2,3},{3,2},{4,5},{5,4},{6,7},{7,6},{8,9},{9,8},{10,11... | collective-permute-start | bytes 1572872 | tf_op jit(solution)/shard_map/ppermute | solution.py:38
  82.0 10.0 %collective-permute-start.15 = (f32[2,8,64,128]{3,2,1,0:T(8,128)}, f32[2,8,64,128]{3,2,1,0:T(8,128)}, u32[]{:S(2)}, u32[]{:S(2)}) collective-permute-start(f32[2,8,64,128]{3,2,1,0:T(8,128)} %collective-permute-done.9.refs_5_), channel_id=1, source_target_pairs={{0,1},{1,0},{2,3},{3,2},{4,5},{5,4},{6,7},{7,6},{8,9},{9,8},{10,11... | collective-permute-start | bytes 1572872 | tf_op jit(solution)/shard_map/ppermute | solution.py:38
  83.9 8.0 %collective-permute-start.14 = (f32[2,8,64,128]{3,2,1,0:T(8,128)}, f32[2,8,64,128]{3,2,1,0:T(8,128)}, u32[]{:S(2)}, u32[]{:S(2)}) collective-permute-start(f32[2,8,64,128]{3,2,1,0:T(8,128)} %collective-permute-done.8.refs_4_), channel_id=1, source_target_pairs={{0,1},{1,0},{2,3},{3,2},{4,5},{5,4},{6,7},{7,6},{8,9},{9,8},{10,11... | collective-permute-start | bytes 1572872 | tf_op jit(solution)/shard_map/ppermute | solution.py:38
  118.2 31.4 %all-to-all-start.1 = ((f32[64,1,128]{2,1,0:T(1,128)}), f32[64,1,128]{2,1,0:T(1,128)S(1)}, u32[]{:S(2)}, u32[]{:S(2)}) async-start(f32[64,1,128]{2,1,0:T(1,128)} %bitcast.22), calls=%async_computation.1 | async-start | bytes 65536 | tf_op jit(solution)/shard_map/all_to_all | solution.py:241
Sparse Core Ops, SparseCore 0:
  9.4 63.7 all-gather.2

commit v8 on v7

--- a/solution.py
+++ b/solution.py
@@ -159,18 +159,14 @@
     for a in range(8):
         flip[pl.ds(a, 16, 8), :] = total[a * 16 : a * 16 + 16]
     total = flip[...].T
-    for xl in range(2):
-        for each in range(2):
-            for row in range(8):
-                first = xl * 64 + row * 8 + each * 4
-                for xh_to in range(2):
-                    out[xh_to * 4 + xl * 2 + each, row * 4 : row * 4 + 4] = total[first : first + 4]
+    for xh_to in range(2):
+        out[xh_to] = total
 
 
 def contract(place, right, own, oth, t_split):
     return pl.pallas_call(
         ladder_kernel,
-        out_shape=jax.ShapeDtypeStruct((8, 32, 128), jnp.float32),
+        out_shape=jax.ShapeDtypeStruct((2, 128, 128), jnp.float32),
         in_specs=[pl.BlockSpec(memory_space=pltpu.SMEM)] + [pl.BlockSpec(memory_space=pl.ANY)] * 19,
         out_specs=pl.BlockSpec(memory_space=pltpu.VMEM),
         scratch_shapes=[
@@ -192,32 +188,8 @@
     )(place, right, *own, *oth, *t_split)
 
 
-def pack_kernel(near, out, total):
-    value = near[0]
-    for part in range(1, 8):
-        value += near[part]
-    total[...] = value
-    lane = lax.broadcasted_iota(jnp.int32, (8, 128), 1) // 16
-    for z in range(8):
-        packed = jnp.zeros((8, 128), jnp.float32)
-        for k in range(4):
-            rows = total[pl.ds(k, 8, 4), :]
-            shift = (k - z) * 16 % 128
-            packed = jnp.where(lane == k, pltpu.roll(rows, shift, 1) if shift else rows, packed)
-        out[z * 8 : z * 8 + 8, :] = packed
-
-
-def pack(near):
-    return pl.pallas_call(
-        pack_kernel,
-        out_shape=jax.ShapeDtypeStruct((64, 128), jnp.float32),
-        scratch_shapes=[pltpu.VMEM((32, 128), jnp.float32)],
-        name="pack",
-    )(near)
-
-
 def shards(vectors_left, vectors_right, amplitudes):
-    xh, y, core = (lax.axis_index(name) for name in ("xh", "y", "core"))
+    z, xh, y, core = (lax.axis_index(name) for name in ("z", "xh", "y", "core"))
     place = jnp.stack([y, 1 - 2 * core, lax.axis_index("xl"), xh, core]).astype(jnp.int32)
     right = lax.all_gather(vectors_right, "z", axis=0)
     t_own_split = split_amplitudes(amplitudes)
@@ -237,9 +209,10 @@
     left_own = [own, x1, x2, x3, x4, y3, y2, y1]
     left_oth = [own_swapped, x1_swapped] + [send(piece, SWAP_CORE) for piece in left_own[2:]]
     partial = contract(place, right, left_own, left_oth, t_split)
-    near = pack(lax.all_to_all(partial, ("xh", "xl", "core"), 0, 0, tiled=True))
-    far = jnp.sum(lax.all_to_all(near, ("z", "y"), 0, 0, tiled=True), axis=0)
-    return lax.dynamic_slice(far[:64].reshape(4, 2, 8), (0, xh, 0), (4, 1, 8)).reshape(4, 8, 1)
+    near = lax.all_to_all(partial.reshape(64, 4, 128), ("xh", "xl", "y", "core"), 0, 0, tiled=True)
+    near = jnp.broadcast_to(jnp.sum(near, axis=0), (8, 4, 128))
+    far = jnp.sum(lax.all_to_all(near, "z", 0, 0, tiled=True), axis=0)
+    return lax.dynamic_slice(far.reshape(4, 16, 8), (0, z * 2 + xh, 0), (4, 1, 8)).reshape(4, 8, 1)
 
 
 def solution(mesh):

time: 158 us -> 156 us (0.987)
  blocking collectives: 9.72 us -> 22.8 us
  starting transfers between devices: 81.2 us -> 70.6 us
  waiting for transfers between devices: 28.8 us -> 24.6 us
  Pallas kernels: 22.3 us -> 20.7 us
    all_to_all x1, blocking collectives: 9.72 us -> 22.8 us  [shards(): lax.all_to_all(partial.reshape(64, 4, 128), ('xh', 'xl', 'y', 'core'), 0,...]
    all_to_all x1, starting transfers between devices: 20.6 us -> 10 us  [shards(): far = jnp.sum(lax.all_to_all(near, 'z', 0, 0, tiled=True), axis=0)]
    all_to_all x1, waiting for transfers between devices: 10.8 us -> 6.62 us  [shards(): far = jnp.sum(lax.all_to_all(near, 'z', 0, 0, tiled=True), axis=0)]
    pallas_call x2 -> x1, Pallas kernels: 16.5 us -> 14.9 us  [contract(): pl.pallas_call(ladder_kernel, out_shape=jax.ShapeDtypeStruct((2, 128, 128...]
where the time goes in v8:
time: 156 us; the launch traced here: 155 us
  starting transfers between devices  70.6 us (45%)
  waiting for transfers between devices  24.6 us (16%)
  blocking collectives  22.8 us (15%)
  Pallas kernels  20.7 us (13%)
  between operations  13.8 us (9%)
  local copies, waits for them, and re-layouts  1.93 us (1%)
    ppermute x18, starting transfers between devices, send(): return lax.ppermute(array, AXES, pairs)  60.6 us
    all_to_all x1, blocking collectives, shards(): lax.all_to_all(partial.reshape(64, 4, 128), ('xh', 'xl', 'y', 'core'), 0,...  22.8 us
    ppermute x18, waiting for transfers between devices, send(): return lax.ppermute(array, AXES, pairs)  17.3 us
    pallas_call x1, Pallas kernels, contract(): pl.pallas_call(ladder_kernel, out_shape=jax.ShapeDtypeStruct((2, 128, 128...  14.9 us
    all_to_all x1, starting transfers between devices, shards(): far = jnp.sum(lax.all_to_all(near, 'z', 0, 0, tiled=True), axis=0)  10 us
    all_to_all x1, waiting for transfers between devices, shards(): far = jnp.sum(lax.all_to_all(near, 'z', 0, 0, tiled=True), axis=0)  6.62 us
    pallas_call x2, Pallas kernels, split_amplitudes(): pl.pallas_call(amplitudes_kernel, out_shape=pltpu.HBM((2, 32, 64, 128), j...  5.83 us
  transfers between devices with their start and end apart: 20, of which 5 were waited for; matrix products, arithmetic and copies ran while one was open for 0% of the time, Pallas kernels for 4%

profile of v8, /device:TPU:1, one launch (start us, length us, event | category | flops | bytes accessed | tf_op | source)
XLA Modules:
  0.0 154.6 jit_solution(3034330138756925657)
XLA Ops:
  6.5 0.7 all-gather.3.cloned.1.call-update
  7.3 1.6 %collective-permute-start = (f32[8,64,128]{2,1,0:T(8,128)}, f32[8,64,128]{2,1,0:T(8,128)S(1)}, u32[]{:S(2)}, u32[]{:S(2)}) collective-permute-start(f32[8,64,128]{2,1,0:T(8,128)} %param.3), channel_id=1, source_target_pairs={{0,0},{1,1},{2,32},{3,33},{4,4},{5,5},{6,36},{7,37},{8,8},{9,9},{1... | collective-permute-start | bytes 786440 | tf_op jit(solution)/shard_map/ppermute | solution.py:38
  8.9 3.9 %collective-permute-start.1 = (f32[8,64,128]{2,1,0:T(8,128)}, f32[8,64,128]{2,1,0:T(8,128)S(1)}, u32[]{:S(2)}, u32[]{:S(2)}) collective-permute-start(f32[8,64,128]{2,1,0:T(8,128)} %param.3), channel_id=1, source_target_pairs={{0,16},{1,17},{2,48},{3,49},{4,20},{5,21},{6,52},{7,53},{8,24},{9,... | collective-permute-start | bytes 786440 | tf_op jit(solution)/shard_map/ppermute | solution.py:38
  12.8 2.9 %split_amplitudes.2.refs_16_ = bf16[2,32,64,128]{3,2,1,0:T(8,128)(2,1)} custom-call(f32[2048,128]{1,0:T(8,128)} %bitcast.15), custom_call_target="tpu_custom_call" | custom-call | flops 1048576 | bytes 2097152 | tf_op jit(solution)/shard_map/split_amplitudes/pallas_call | solution.py:73
  15.7 0.0 collective-permute-done
  15.8 8.1 %collective-permute-done.1 = f32[8,64,128]{2,1,0:T(8,128)S(1)} collective-permute-done((f32[8,64,128]{2,1,0:T(8,128)}, f32[8,64,128]{2,1,0:T(8,128)S(1)}, u32[]{:S(2)}, u32[]{:S(2)}) %collective-permute-start.1) | collective-permute-done | bytes 262176 | tf_op jit(solution)/shard_map/ppermute | solution.py:38
  23.9 7.4 %collective-permute-start.2 = (f32[2,8,64,128]{3,2,1,0:T(8,128)S(1)}, f32[2,8,64,128]{3,2,1,0:T(8,128)S(1)}, u32[]{:S(2)}, u32[]{:S(2)}) collective-permute-start(f32[2,8,64,128]{3,2,1,0:T(8,128)S(1)} %pad_maximum_fusion.refs_0_), channel_id=1, source_target_pairs={{0,2},{1,15},{2,4},{3,1},{4,6},{5,3},{6,8},{7,5},{8,10},{9,7},{10,... | collective-permute-start | bytes 1572872 | tf_op jit(solution)/shard_map/ppermute | solution.py:38
  31.3 1.9 %collective-permute-start.4 = (f32[2,8,64,128]{3,2,1,0:T(8,128)S(1)}, f32[2,8,64,128]{3,2,1,0:T(8,128)S(1)}, u32[]{:S(2)}, u32[]{:S(2)}) collective-permute-start(f32[2,8,64,128]{3,2,1,0:T(8,128)S(1)} %pad_maximum_fusion.refs_0_), channel_id=1, source_target_pairs={{0,14},{1,3},{2,0},{3,5},{4,2},{5,7},{6,4},{7,9},{8,6},{9,11},{10,... | collective-permute-start | bytes 1572872 | tf_op jit(solution)/shard_map/ppermute | solution.py:38
  33.2 5.9 %collective-permute-done.2.refs_1_ = f32[2,8,64,128]{3,2,1,0:T(8,128)S(1)} collective-permute-done((f32[2,8,64,128]{3,2,1,0:T(8,128)S(1)}, f32[2,8,64,128]{3,2,1,0:T(8,128)S(1)}, u32[]{:S(2)}, u32[]{:S(2)}) %collective-permute-start.2) | collective-permute-done | bytes 524320 | tf_op jit(solution)/shard_map/ppermute | solution.py:38
  39.1 5.4 %collective-permute-start.3 = (f32[2,8,64,128]{3,2,1,0:T(8,128)S(1)}, f32[2,8,64,128]{3,2,1,0:T(8,128)S(1)}, u32[]{:S(2)}, u32[]{:S(2)}) collective-permute-start(f32[2,8,64,128]{3,2,1,0:T(8,128)S(1)} %collective-permute-done.2.refs_1_), channel_id=1, source_target_pairs={{0,2},{1,15},{2,4},{3,1},{4,6},{5,3},{6,8},{7,5},{8,10},{9,7},{10,... | collective-permute-start | bytes 1572872 | tf_op jit(solution)/shard_map/ppermute | solution.py:38
  44.5 4.2 %collective-permute-start.7 = (f32[64,32,128]{2,1,0:T(8,128)}, f32[64,32,128]{2,1,0:T(8,128)S(1)}, u32[]{:S(2)}, u32[]{:S(2)}) collective-permute-start(f32[64,32,128]{2,1,0:T(8,128)} %param.5), channel_id=1, source_target_pairs={{0,32},{1,33},{2,34},{3,35},{4,36},{5,37},{6,38},{7,39},{8,40},{9,... | collective-permute-start | bytes 3145736 | tf_op jit(solution)/shard_map/ppermute | solution.py:38
  48.7 4.4 %collective-permute-start.10 = (f32[2,8,64,128]{3,2,1,0:T(8,128)S(1)}, f32[2,8,64,128]{3,2,1,0:T(8,128)S(1)}, u32[]{:S(2)}, u32[]{:S(2)}) collective-permute-start(f32[2,8,64,128]{3,2,1,0:T(8,128)S(1)} %pad_maximum_fusion.refs_0_), channel_id=1, source_target_pairs={{0,1},{1,0},{2,3},{3,2},{4,5},{5,4},{6,7},{7,6},{8,9},{9,8},{10,11... | collective-permute-start | bytes 1572872 | tf_op jit(solution)/shard_map/ppermute | solution.py:38
  53.1 0.0 collective-permute-done.4.refs_7_
  53.1 4.1 %collective-permute-start.6 = (f32[2,8,64,128]{3,2,1,0:T(8,128)S(1)}, f32[2,8,64,128]{3,2,1,0:T(8,128)}, u32[]{:S(2)}, u32[]{:S(2)}) collective-permute-start(f32[2,8,64,128]{3,2,1,0:T(8,128)S(1)} %collective-permute-done.4.refs_7_), channel_id=1, source_target_pairs={{0,14},{1,3},{2,0},{3,5},{4,2},{5,7},{6,4},{7,9},{8,6},{9,11},{10,... | collective-permute-start | bytes 1572872 | tf_op jit(solution)/shard_map/ppermute | solution.py:38
  57.3 0.0 collective-permute-done.3.refs_2_
  57.3 2.4 %collective-permute-start.5 = (f32[2,8,64,128]{3,2,1,0:T(8,128)S(1)}, f32[2,8,64,128]{3,2,1,0:T(8,128)}, u32[]{:S(2)}, u32[]{:S(2)}) collective-permute-start(f32[2,8,64,128]{3,2,1,0:T(8,128)S(1)} %collective-permute-done.3.refs_2_), channel_id=1, source_target_pairs={{0,2},{1,15},{2,4},{3,1},{4,6},{5,3},{6,8},{7,5},{8,10},{9,7},{10,... | collective-permute-start | bytes 1572872 | tf_op jit(solution)/shard_map/ppermute | solution.py:38
  59.7 0.0 collective-permute-done.10.refs_8_
  59.7 1.9 %collective-permute-start.11 = (f32[2,8,64,128]{3,2,1,0:T(8,128)S(1)}, f32[2,8,64,128]{3,2,1,0:T(8,128)S(1)}, u32[]{:S(2)}, u32[]{:S(2)}) collective-permute-start(f32[2,8,64,128]{3,2,1,0:T(8,128)S(1)} %collective-permute-done.2.refs_1_), channel_id=1, source_target_pairs={{0,1},{1,0},{2,3},{3,2},{4,5},{5,4},{6,7},{7,6},{8,9},{9,8},{10,11... | collective-permute-start | bytes 1572872 | tf_op jit(solution)/shard_map/ppermute | solution.py:38
  61.6 2.4 %collective-permute-start.17 = (f32[2,8,64,128]{3,2,1,0:T(8,128)S(1)}, f32[2,8,64,128]{3,2,1,0:T(8,128)S(1)}, u32[]{:S(2)}, u32[]{:S(2)}) collective-permute-start(f32[2,8,64,128]{3,2,1,0:T(8,128)S(1)} %collective-permute-done.4.refs_7_), channel_id=1, source_target_pairs={{0,1},{1,0},{2,3},{3,2},{4,5},{5,4},{6,7},{7,6},{8,9},{9,8},{10,11... | collective-permute-start | bytes 1572872 | tf_op jit(solution)/shard_map/ppermute | solution.py:38
  64.0 2.6 %collective-permute-done.6.refs_6_ = f32[2,8,64,128]{3,2,1,0:T(8,128)} collective-permute-done((f32[2,8,64,128]{3,2,1,0:T(8,128)S(1)}, f32[2,8,64,128]{3,2,1,0:T(8,128)}, u32[]{:S(2)}, u32[]{:S(2)}) %collective-permute-start.6) | collective-permute-done | bytes 524320 | tf_op jit(solution)/shard_map/ppermute | solution.py:38
  66.6 4.0 %collective-permute-start.9 = (f32[2,8,64,128]{3,2,1,0:T(8,128)}, f32[2,8,64,128]{3,2,1,0:T(8,128)}, u32[]{:S(2)}, u32[]{:S(2)}) collective-permute-start(f32[2,8,64,128]{3,2,1,0:T(8,128)} %collective-permute-done.6.refs_6_), channel_id=1, source_target_pairs={{0,14},{1,3},{2,0},{3,5},{4,2},{5,7},{6,4},{7,9},{8,6},{9,11},{10,... | collective-permute-start | bytes 1572872 | tf_op jit(solution)/shard_map/ppermute | solution.py:38
  70.7 0.7 collective-permute-done.7
  71.4 0.0 collective-permute-done.5.refs_3_
  71.4 1.9 %collective-permute-start.8 = (f32[2,8,64,128]{3,2,1,0:T(8,128)}, f32[2,8,64,128]{3,2,1,0:T(8,128)}, u32[]{:S(2)}, u32[]{:S(2)}) collective-permute-start(f32[2,8,64,128]{3,2,1,0:T(8,128)} %collective-permute-done.5.refs_3_), channel_id=1, source_target_pairs={{0,2},{1,15},{2,4},{3,1},{4,6},{5,3},{6,8},{7,5},{8,10},{9,7},{10,... | collective-permute-start | bytes 1572872 | tf_op jit(solution)/shard_map/ppermute | solution.py:38
  73.3 4.2 %collective-permute-start.16 = (f32[2,8,64,128]{3,2,1,0:T(8,128)}, f32[2,8,64,128]{3,2,1,0:T(8,128)}, u32[]{:S(2)}, u32[]{:S(2)}) collective-permute-start(f32[2,8,64,128]{3,2,1,0:T(8,128)} %collective-permute-done.6.refs_6_), channel_id=1, source_target_pairs={{0,1},{1,0},{2,3},{3,2},{4,5},{5,4},{6,7},{7,6},{8,9},{9,8},{10,11... | collective-permute-start | bytes 1572872 | tf_op jit(solution)/shard_map/ppermute | solution.py:38
  77.5 0.0 collective-permute-done.11.refs_9_
  77.6 1.9 %collective-permute-start.12 = (f32[2,8,64,128]{3,2,1,0:T(8,128)S(1)}, f32[2,8,64,128]{3,2,1,0:T(8,128)}, u32[]{:S(2)}, u32[]{:S(2)}) collective-permute-start(f32[2,8,64,128]{3,2,1,0:T(8,128)S(1)} %collective-permute-done.3.refs_2_), channel_id=1, source_target_pairs={{0,1},{1,0},{2,3},{3,2},{4,5},{5,4},{6,7},{7,6},{8,9},{9,8},{10,11... | collective-permute-start | bytes 1572872 | tf_op jit(solution)/shard_map/ppermute | solution.py:38
  79.5 0.0 collective-permute-done.17.refs_15_
  79.5 2.4 %collective-permute-start.13 = (f32[2,8,64,128]{3,2,1,0:T(8,128)}, f32[2,8,64,128]{3,2,1,0:T(8,128)}, u32[]{:S(2)}, u32[]{:S(2)}) collective-permute-start(f32[2,8,64,128]{3,2,1,0:T(8,128)} %collective-permute-done.5.refs_3_), channel_id=1, source_target_pairs={{0,1},{1,0},{2,3},{3,2},{4,5},{5,4},{6,7},{7,6},{8,9},{9,8},{10,11... | collective-permute-start | bytes 1572872 | tf_op jit(solution)/shard_map/ppermute | solution.py:38
  81.9 0.0 collective-permute-done.9.refs_5_
  82.0 1.9 %collective-permute-start.15 = (f32[2,8,64,128]{3,2,1,0:T(8,128)}, f32[2,8,64,128]{3,2,1,0:T(8,128)}, u32[]{:S(2)}, u32[]{:S(2)}) collective-permute-start(f32[2,8,64,128]{3,2,1,0:T(8,128)} %collective-permute-done.9.refs_5_), channel_id=1, source_target_pairs={{0,1},{1,0},{2,3},{3,2},{4,5},{5,4},{6,7},{7,6},{8,9},{9,8},{10,11... | collective-permute-start | bytes 1572872 | tf_op jit(solution)/shard_map/ppermute | solution.py:38
  83.9 0.0 collective-permute-done.8.refs_4_
  83.9 4.5 %collective-permute-start.14 = (f32[2,8,64,128]{3,2,1,0:T(8,128)}, f32[2,8,64,128]{3,2,1,0:T(8,128)}, u32[]{:S(2)}, u32[]{:S(2)}) collective-permute-start(f32[2,8,64,128]{3,2,1,0:T(8,128)} %collective-permute-done.8.refs_4_), channel_id=1, source_target_pairs={{0,1},{1,0},{2,3},{3,2},{4,5},{5,4},{6,7},{7,6},{8,9},{9,8},{10,11... | collective-permute-start | bytes 1572872 | tf_op jit(solution)/shard_map/ppermute | solution.py:38
  88.4 0.6 stack.32.place
  89.0 2.9 %split_amplitudes.3.refs_17_ = bf16[2,32,64,128]{3,2,1,0:T(8,128)(2,1)} custom-call(f32[2048,128]{1,0:T(8,128)} %bitcast.16), custom_call_target="tpu_custom_call" | custom-call | flops 1048576 | bytes 2097152 | tf_op jit(solution)/shard_map/split_amplitudes/pallas_call | solution.py:73
  91.9 0.0 collective-permute-done.16.refs_14_
  91.9 0.0 collective-permute-done.12.refs_10_
  91.9 0.0 collective-permute-done.13.refs_11_
  92.0 0.0 collective-permute-done.14.refs_12_
  92.0 0.0 all-gather.3.cloned.1.call-done
  92.0 14.9 %ladder.1 = f32[2,128,128]{2,1,0:T(8,128)} custom-call(s32[5]{0:T(128)} %stack.32.place, f32[8,16,32,256]{3,2,1,0:T(8,128)} %bitcast.20, f32[2,8,64,128]{3,2,1,0:T(8,128)} %copy-done.1, f32[2,8,64,128]{3,2,1,0:T(8,128)} %copy-done.2, f32[2,8,64,128]{3,2,1,0:T(8,128)} %copy-done.4, f32[2,8,64,128]{3,2,1,0:T(8,128)} %collective-permute-done.5.refs_3_, ...), custom_call_target="tpu_custom_call" | custom-call | flops 6442450944 | bytes 16777216 | tf_op jit(solution)/shard_map/ladder/pallas_call | solution.py:167
  106.9 22.8 %all_to_all.10 = f32[64,4,128]{2,1,0:T(4,128)S(1)} all-to-all(f32[64,4,128]{2,1,0:T(4,128)} %bitcast.19), channel_id=1, replica_groups=mesh['z'=8,'xh'=2,'xl'=2,'y'=8,'core'=2] {'xh','xl','y','core'}, dimensions={0} | all-to-all | bytes 262144 | tf_op jit(solution)/shard_map/all_to_all | solution.py:212
  129.7 0.1 reduce_sum.18
  129.8 0.6 broadcast_in_dim.3
  130.4 10.0 %all-to-all-start.1 = ((f32[8,4,128]{2,1,0:T(4,128)}), f32[8,4,128]{2,1,0:T(4,128)S(1)}, u32[]{:S(2)}, u32[]{:S(2)}) async-start(f32[8,4,128]{2,1,0:T(4,128)} %broadcast_in_dim.3), calls=%async_computation.1 | async-start | bytes 32768 | tf_op jit(solution)/shard_map/all_to_all | solution.py:214
  140.5 6.6 %all-to-all-done.1 = f32[8,4,128]{2,1,0:T(4,128)S(1)} async-done(((f32[8,4,128]{2,1,0:T(4,128)}), f32[8,4,128]{2,1,0:T(4,128)S(1)}, u32[]{:S(2)}, u32[]{:S(2)}) %all-to-all-start.1) | async-done | bytes 16416 | tf_op jit(solution)/shard_map/all_to_all | solution.py:214
  147.1 0.1 reshape.18
  147.2 0.6 dynamic-slice_bitcast_fusion
  (20 shorter events, 0.1 us)
Async XLA Ops:
  6.5 85.4 %all-gather.3.cloned.1.call-start = ((), (), s32[]{:S(2)}) async-start(), calls=%async_computation.2 | async-start | bytes 4718592 | tf_op jit(solution)/shard_map/all_gather | solution.py:194
  7.3 8.5 %collective-permute-start = (f32[8,64,128]{2,1,0:T(8,128)}, f32[8,64,128]{2,1,0:T(8,128)S(1)}, u32[]{:S(2)}, u32[]{:S(2)}) collective-permute-start(f32[8,64,128]{2,1,0:T(8,128)} %param.3), channel_id=1, source_target_pairs={{0,0},{1,1},{2,32},{3,33},{4,4},{5,5},{6,36},{7,37},{8,8},{9,9},{1... | collective-permute-start | bytes 786440 | tf_op jit(solution)/shard_map/ppermute | solution.py:38
  8.9 15.0 %collective-permute-start.1 = (f32[8,64,128]{2,1,0:T(8,128)}, f32[8,64,128]{2,1,0:T(8,128)S(1)}, u32[]{:S(2)}, u32[]{:S(2)}) collective-permute-start(f32[8,64,128]{2,1,0:T(8,128)} %param.3), channel_id=1, source_target_pairs={{0,16},{1,17},{2,48},{3,49},{4,20},{5,21},{6,52},{7,53},{8,24},{9,... | collective-permute-start | bytes 786440 | tf_op jit(solution)/shard_map/ppermute | solution.py:38
  23.9 68.1 %copy-start.1 = (f32[2,8,64,128]{3,2,1,0:T(8,128)}, f32[2,8,64,128]{3,2,1,0:T(8,128)S(1)}, u32[]{:S(2)}) copy-start(f32[2,8,64,128]{3,2,1,0:T(8,128)S(1)} %pad_maximum_fusion.refs_0_) | copy-start | bytes 1572868
  23.9 15.2 %collective-permute-start.2 = (f32[2,8,64,128]{3,2,1,0:T(8,128)S(1)}, f32[2,8,64,128]{3,2,1,0:T(8,128)S(1)}, u32[]{:S(2)}, u32[]{:S(2)}) collective-permute-start(f32[2,8,64,128]{3,2,1,0:T(8,128)S(1)} %pad_maximum_fusion.refs_0_), channel_id=1, source_target_pairs={{0,2},{1,15},{2,4},{3,1},{4,6},{5,3},{6,8},{7,5},{8,10},{9,7},{10,... | collective-permute-start | bytes 1572872 | tf_op jit(solution)/shard_map/ppermute | solution.py:38
  31.3 21.8 %collective-permute-start.4 = (f32[2,8,64,128]{3,2,1,0:T(8,128)S(1)}, f32[2,8,64,128]{3,2,1,0:T(8,128)S(1)}, u32[]{:S(2)}, u32[]{:S(2)}) collective-permute-start(f32[2,8,64,128]{3,2,1,0:T(8,128)S(1)} %pad_maximum_fusion.refs_0_), channel_id=1, source_target_pairs={{0,14},{1,3},{2,0},{3,5},{4,2},{5,7},{6,4},{7,9},{8,6},{9,11},{10,... | collective-permute-start | bytes 1572872 | tf_op jit(solution)/shard_map/ppermute | solution.py:38
  39.1 52.9 %copy-start.2 = (f32[2,8,64,128]{3,2,1,0:T(8,128)}, f32[2,8,64,128]{3,2,1,0:T(8,128)S(1)}, u32[]{:S(2)}) copy-start(f32[2,8,64,128]{3,2,1,0:T(8,128)S(1)} %collective-permute-done.2.refs_1_) | copy-start | bytes 1572868
  39.1 18.2 %collective-permute-start.3 = (f32[2,8,64,128]{3,2,1,0:T(8,128)S(1)}, f32[2,8,64,128]{3,2,1,0:T(8,128)S(1)}, u32[]{:S(2)}, u32[]{:S(2)}) collective-permute-start(f32[2,8,64,128]{3,2,1,0:T(8,128)S(1)} %collective-permute-done.2.refs_1_), channel_id=1, source_target_pairs={{0,2},{1,15},{2,4},{3,1},{4,6},{5,3},{6,8},{7,5},{8,10},{9,7},{10,... | collective-permute-start | bytes 1572872 | tf_op jit(solution)/shard_map/ppermute | solution.py:38
  44.5 26.9 %collective-permute-start.7 = (f32[64,32,128]{2,1,0:T(8,128)}, f32[64,32,128]{2,1,0:T(8,128)S(1)}, u32[]{:S(2)}, u32[]{:S(2)}) collective-permute-start(f32[64,32,128]{2,1,0:T(8,128)} %param.5), channel_id=1, source_target_pairs={{0,32},{1,33},{2,34},{3,35},{4,36},{5,37},{6,38},{7,39},{8,40},{9,... | collective-permute-start | bytes 3145736 | tf_op jit(solution)/shard_map/ppermute | solution.py:38
  48.7 10.9 %collective-permute-start.10 = (f32[2,8,64,128]{3,2,1,0:T(8,128)S(1)}, f32[2,8,64,128]{3,2,1,0:T(8,128)S(1)}, u32[]{:S(2)}, u32[]{:S(2)}) collective-permute-start(f32[2,8,64,128]{3,2,1,0:T(8,128)S(1)} %pad_maximum_fusion.refs_0_), channel_id=1, source_target_pairs={{0,1},{1,0},{2,3},{3,2},{4,5},{5,4},{6,7},{7,6},{8,9},{9,8},{10,11... | collective-permute-start | bytes 1572872 | tf_op jit(solution)/shard_map/ppermute | solution.py:38
  53.1 38.9 %copy-start.3 = (f32[2,8,64,128]{3,2,1,0:T(8,128)}, f32[2,8,64,128]{3,2,1,0:T(8,128)S(1)}, u32[]{:S(2)}) copy-start(f32[2,8,64,128]{3,2,1,0:T(8,128)S(1)} %collective-permute-done.4.refs_7_) | copy-start | bytes 1572868
  53.1 13.5 %collective-permute-start.6 = (f32[2,8,64,128]{3,2,1,0:T(8,128)S(1)}, f32[2,8,64,128]{3,2,1,0:T(8,128)}, u32[]{:S(2)}, u32[]{:S(2)}) collective-permute-start(f32[2,8,64,128]{3,2,1,0:T(8,128)S(1)} %collective-permute-done.4.refs_7_), channel_id=1, source_target_pairs={{0,14},{1,3},{2,0},{3,5},{4,2},{5,7},{6,4},{7,9},{8,6},{9,11},{10,... | collective-permute-start | bytes 1572872 | tf_op jit(solution)/shard_map/ppermute | solution.py:38
  57.3 34.8 %copy-start.4 = (f32[2,8,64,128]{3,2,1,0:T(8,128)}, f32[2,8,64,128]{3,2,1,0:T(8,128)S(1)}, u32[]{:S(2)}) copy-start(f32[2,8,64,128]{3,2,1,0:T(8,128)S(1)} %collective-permute-done.3.refs_2_) | copy-start | bytes 1572868
  57.3 14.1 %collective-permute-start.5 = (f32[2,8,64,128]{3,2,1,0:T(8,128)S(1)}, f32[2,8,64,128]{3,2,1,0:T(8,128)}, u32[]{:S(2)}, u32[]{:S(2)}) collective-permute-start(f32[2,8,64,128]{3,2,1,0:T(8,128)S(1)} %collective-permute-done.3.refs_2_), channel_id=1, source_target_pairs={{0,2},{1,15},{2,4},{3,1},{4,6},{5,3},{6,8},{7,5},{8,10},{9,7},{10,... | collective-permute-start | bytes 1572872 | tf_op jit(solution)/shard_map/ppermute | solution.py:38
  59.7 19.8 %copy-start.5 = (f32[2,8,64,128]{3,2,1,0:T(8,128)}, f32[2,8,64,128]{3,2,1,0:T(8,128)S(1)}, u32[]{:S(2)}) copy-start(f32[2,8,64,128]{3,2,1,0:T(8,128)S(1)} %collective-permute-done.10.refs_8_) | copy-start | bytes 1572868
  59.7 17.8 %collective-permute-start.11 = (f32[2,8,64,128]{3,2,1,0:T(8,128)S(1)}, f32[2,8,64,128]{3,2,1,0:T(8,128)S(1)}, u32[]{:S(2)}, u32[]{:S(2)}) collective-permute-start(f32[2,8,64,128]{3,2,1,0:T(8,128)S(1)} %collective-permute-done.2.refs_1_), channel_id=1, source_target_pairs={{0,1},{1,0},{2,3},{3,2},{4,5},{5,4},{6,7},{7,6},{8,9},{9,8},{10,11... | collective-permute-start | bytes 1572872 | tf_op jit(solution)/shard_map/ppermute | solution.py:38
  61.6 17.9 %collective-permute-start.17 = (f32[2,8,64,128]{3,2,1,0:T(8,128)S(1)}, f32[2,8,64,128]{3,2,1,0:T(8,128)S(1)}, u32[]{:S(2)}, u32[]{:S(2)}) collective-permute-start(f32[2,8,64,128]{3,2,1,0:T(8,128)S(1)} %collective-permute-done.4.refs_7_), channel_id=1, source_target_pairs={{0,1},{1,0},{2,3},{3,2},{4,5},{5,4},{6,7},{7,6},{8,9},{9,8},{10,11... | collective-permute-start | bytes 1572872 | tf_op jit(solution)/shard_map/ppermute | solution.py:38
  66.6 15.3 %collective-permute-start.9 = (f32[2,8,64,128]{3,2,1,0:T(8,128)}, f32[2,8,64,128]{3,2,1,0:T(8,128)}, u32[]{:S(2)}, u32[]{:S(2)}) collective-permute-start(f32[2,8,64,128]{3,2,1,0:T(8,128)} %collective-permute-done.6.refs_6_), channel_id=1, source_target_pairs={{0,14},{1,3},{2,0},{3,5},{4,2},{5,7},{6,4},{7,9},{8,6},{9,11},{10,... | collective-permute-start | bytes 1572872 | tf_op jit(solution)/shard_map/ppermute | solution.py:38
  71.4 17.6 %copy-start = (f32[64,32,128]{2,1,0:T(8,128)}, f32[64,32,128]{2,1,0:T(8,128)S(1)}, u32[]{:S(2)}) copy-start(f32[64,32,128]{2,1,0:T(8,128)S(1)} %collective-permute-done.7) | copy-start | bytes 3145732
  71.4 12.5 %collective-permute-start.8 = (f32[2,8,64,128]{3,2,1,0:T(8,128)}, f32[2,8,64,128]{3,2,1,0:T(8,128)}, u32[]{:S(2)}, u32[]{:S(2)}) collective-permute-start(f32[2,8,64,128]{3,2,1,0:T(8,128)} %collective-permute-done.5.refs_3_), channel_id=1, source_target_pairs={{0,2},{1,15},{2,4},{3,1},{4,6},{5,3},{6,8},{7,5},{8,10},{9,7},{10,... | collective-permute-start | bytes 1572872 | tf_op jit(solution)/shard_map/ppermute | solution.py:38
  73.3 18.6 %collective-permute-start.16 = (f32[2,8,64,128]{3,2,1,0:T(8,128)}, f32[2,8,64,128]{3,2,1,0:T(8,128)}, u32[]{:S(2)}, u32[]{:S(2)}) collective-permute-start(f32[2,8,64,128]{3,2,1,0:T(8,128)} %collective-permute-done.6.refs_6_), channel_id=1, source_target_pairs={{0,1},{1,0},{2,3},{3,2},{4,5},{5,4},{6,7},{7,6},{8,9},{9,8},{10,11... | collective-permute-start | bytes 1572872 | tf_op jit(solution)/shard_map/ppermute | solution.py:38
  77.5 4.4 %copy-start.6 = (f32[2,8,64,128]{3,2,1,0:T(8,128)}, f32[2,8,64,128]{3,2,1,0:T(8,128)S(1)}, u32[]{:S(2)}) copy-start(f32[2,8,64,128]{3,2,1,0:T(8,128)S(1)} %collective-permute-done.11.refs_9_) | copy-start | bytes 1572868
  77.6 14.4 %collective-permute-start.12 = (f32[2,8,64,128]{3,2,1,0:T(8,128)S(1)}, f32[2,8,64,128]{3,2,1,0:T(8,128)}, u32[]{:S(2)}, u32[]{:S(2)}) collective-permute-start(f32[2,8,64,128]{3,2,1,0:T(8,128)S(1)} %collective-permute-done.3.refs_2_), channel_id=1, source_target_pairs={{0,1},{1,0},{2,3},{3,2},{4,5},{5,4},{6,7},{7,6},{8,9},{9,8},{10,11... | collective-permute-start | bytes 1572872 | tf_op jit(solution)/shard_map/ppermute | solution.py:38
  79.5 2.4 %copy-start.7 = (f32[2,8,64,128]{3,2,1,0:T(8,128)}, f32[2,8,64,128]{3,2,1,0:T(8,128)S(1)}, u32[]{:S(2)}) copy-start(f32[2,8,64,128]{3,2,1,0:T(8,128)S(1)} %collective-permute-done.17.refs_15_) | copy-start | bytes 1572868
  79.5 12.4 %collective-permute-start.13 = (f32[2,8,64,128]{3,2,1,0:T(8,128)}, f32[2,8,64,128]{3,2,1,0:T(8,128)}, u32[]{:S(2)}, u32[]{:S(2)}) collective-permute-start(f32[2,8,64,128]{3,2,1,0:T(8,128)} %collective-permute-done.5.refs_3_), channel_id=1, source_target_pairs={{0,1},{1,0},{2,3},{3,2},{4,5},{5,4},{6,7},{7,6},{8,9},{9,8},{10,11... | collective-permute-start | bytes 1572872 | tf_op jit(solution)/shard_map/ppermute | solution.py:38
  82.0 10.0 %collective-permute-start.15 = (f32[2,8,64,128]{3,2,1,0:T(8,128)}, f32[2,8,64,128]{3,2,1,0:T(8,128)}, u32[]{:S(2)}, u32[]{:S(2)}) collective-permute-start(f32[2,8,64,128]{3,2,1,0:T(8,128)} %collective-permute-done.9.refs_5_), channel_id=1, source_target_pairs={{0,1},{1,0},{2,3},{3,2},{4,5},{5,4},{6,7},{7,6},{8,9},{9,8},{10,11... | collective-permute-start | bytes 1572872 | tf_op jit(solution)/shard_map/ppermute | solution.py:38
  83.9 8.1 %collective-permute-start.14 = (f32[2,8,64,128]{3,2,1,0:T(8,128)}, f32[2,8,64,128]{3,2,1,0:T(8,128)}, u32[]{:S(2)}, u32[]{:S(2)}) collective-permute-start(f32[2,8,64,128]{3,2,1,0:T(8,128)} %collective-permute-done.8.refs_4_), channel_id=1, source_target_pairs={{0,1},{1,0},{2,3},{3,2},{4,5},{5,4},{6,7},{7,6},{8,9},{9,8},{10,11... | collective-permute-start | bytes 1572872 | tf_op jit(solution)/shard_map/ppermute | solution.py:38
  130.4 16.7 %all-to-all-start.1 = ((f32[8,4,128]{2,1,0:T(4,128)}), f32[8,4,128]{2,1,0:T(4,128)S(1)}, u32[]{:S(2)}, u32[]{:S(2)}) async-start(f32[8,4,128]{2,1,0:T(4,128)} %broadcast_in_dim.3), calls=%async_computation.1 | async-start | bytes 32768 | tf_op jit(solution)/shard_map/all_to_all | solution.py:214
Sparse Core Ops, SparseCore 0:
  9.4 63.7 all-gather.2

commit v9 on v8

--- a/solution.py
+++ b/solution.py
@@ -88,7 +88,7 @@
 
 def ladder_kernel(place, right, *refs):
     pieces, (t_own, t_oth, out) = (refs[:8], refs[8:16]), refs[16:19]
-    r_buf, raw, parts, t_buf, acc, y_high, y_low, flip, r_sem, l_sem, t_sem = refs[19:]
+    r_buf, raw, parts, t_buf, acc, y_high, y_low, flip, rows, r_sem, l_sem, t_sem = refs[19:]
     y, sign, xl_here, xh, core = (place[i] for i in range(5))
 
     def pair(k):
@@ -156,17 +156,21 @@
             y_low[a * 16 : a * 16 + 16, d * 128 : d * 128 + 128] = low
     t_high, t_low = (t_buf[i].reshape(4096, 128) for i in range(2))
     total = dot_nn(y_high[...], t_high) + dot_nn(y_high[...], t_low) + dot_nn(y_low[...], t_high)
+    rows[...] = total
     for a in range(8):
-        flip[pl.ds(a, 16, 8), :] = total[a * 16 : a * 16 + 16]
-    total = flip[...].T
-    for xh_to in range(2):
-        out[xh_to] = total
+        for xh_to in range(2):
+            flip[pl.ds(xh_to * 64 + a, 8, 8), :] = rows[pl.ds(a * 16 + xh_to, 8, 2), :]
+    rows[...] = flip[...].T
+    even, odd = rows[pl.ds(0, 64, 2), :], rows[pl.ds(1, 64, 2), :]
+    left_half = lax.broadcasted_iota(jnp.int32, (64, 128), 1) < 64
+    out[0] = jnp.where(left_half, even, pltpu.roll(odd, 64, 1))
+    out[1] = jnp.where(left_half, pltpu.roll(even, 64, 1), odd)
 
 
 def contract(place, right, own, oth, t_split):
     return pl.pallas_call(
         ladder_kernel,
-        out_shape=jax.ShapeDtypeStruct((2, 128, 128), jnp.float32),
+        out_shape=jax.ShapeDtypeStruct((2, 64, 128), jnp.float32),
         in_specs=[pl.BlockSpec(memory_space=pltpu.SMEM)] + [pl.BlockSpec(memory_space=pl.ANY)] * 19,
         out_specs=pl.BlockSpec(memory_space=pltpu.VMEM),
         scratch_shapes=[
@@ -177,6 +181,7 @@
             pltpu.VMEM((8, 512, 128), jnp.float32),
             pltpu.VMEM((128, 4096), jnp.bfloat16),
             pltpu.VMEM((128, 4096), jnp.bfloat16),
+            pltpu.VMEM((128, 128), jnp.float32),
             pltpu.VMEM((128, 128), jnp.float32),
             pltpu.SemaphoreType.DMA((4, 2)),
             pltpu.SemaphoreType.DMA((2, 8)),
@@ -204,15 +209,16 @@
     x1_swapped = send(after(x1, own_swapped), SWAP_CORE)
     x3 = send(after(x2, y1), RING_X)
     y3 = send(after(y2, x2), RING_Y)
-    x4 = send(after(x3, y2, t_oth), RING_X)
+    x4 = send(after(x3, y2), RING_X)
     t_split = (t_own_split, split_amplitudes(after(t_oth, x4)))
     left_own = [own, x1, x2, x3, x4, y3, y2, y1]
-    left_oth = [own_swapped, x1_swapped] + [send(piece, SWAP_CORE) for piece in left_own[2:]]
+    x2_swapped = send(after(x2, x3, t_oth), SWAP_CORE)
+    left_oth = [own_swapped, x1_swapped, x2_swapped] + [send(piece, SWAP_CORE) for piece in left_own[3:]]
     partial = contract(place, right, left_own, left_oth, t_split)
-    near = lax.all_to_all(partial.reshape(64, 4, 128), ("xh", "xl", "y", "core"), 0, 0, tiled=True)
-    near = jnp.broadcast_to(jnp.sum(near, axis=0), (8, 4, 128))
+    near = lax.all_to_all(partial.reshape(64, 2, 128), ("xh", "xl", "y", "core"), 0, 0, tiled=True)
+    near = jnp.broadcast_to(jnp.sum(near, axis=0), (8, 2, 128))
     far = jnp.sum(lax.all_to_all(near, "z", 0, 0, tiled=True), axis=0)
-    return lax.dynamic_slice(far.reshape(4, 16, 8), (0, z * 2 + xh, 0), (4, 1, 8)).reshape(4, 8, 1)
+    return lax.dynamic_slice(far.reshape(4, 8, 8), (0, z, 0), (4, 1, 8)).reshape(4, 8, 1)
 
 
 def solution(mesh):

time: 156 us -> 156 us (level)
  starting transfers between devices: 70.6 us -> 67.9 us
  waiting for transfers between devices: 24.6 us -> 27 us
    ppermute x18, starting transfers between devices: 60.6 us -> 57.8 us  [send(): return lax.ppermute(array, AXES, pairs)]
    ppermute x18, waiting for transfers between devices: 17.3 us -> 19.7 us  [send(): return lax.ppermute(array, AXES, pairs)]
where the time goes in v9:
time: 156 us; the launch traced here: 155 us
  starting transfers between devices  67.9 us (44%)
  waiting for transfers between devices  27 us (17%)
  blocking collectives  23.1 us (15%)
  Pallas kernels  20.8 us (13%)
  between operations  13.8 us (9%)
  local copies, waits for them, and re-layouts  2 us (1%)
    ppermute x18, starting transfers between devices, send(): return lax.ppermute(array, AXES, pairs)  57.8 us
    all_to_all x1, blocking collectives, shards(): lax.all_to_all(partial.reshape(64, 2, 128), ('xh', 'xl', 'y', 'core'), 0,...  23.1 us
    ppermute x18, waiting for transfers between devices, send(): return lax.ppermute(array, AXES, pairs)  19.7 us
    pallas_call x1, Pallas kernels, contract(): pl.pallas_call(ladder_kernel, out_shape=jax.ShapeDtypeStruct((2, 64, 128)...  14.9 us
    all_to_all x1, starting transfers between devices, shards(): far = jnp.sum(lax.all_to_all(near, 'z', 0, 0, tiled=True), axis=0)  10 us
    all_to_all x1, waiting for transfers between devices, shards(): far = jnp.sum(lax.all_to_all(near, 'z', 0, 0, tiled=True), axis=0)  6.58 us
    pallas_call x2, Pallas kernels, split_amplitudes(): pl.pallas_call(amplitudes_kernel, out_shape=pltpu.HBM((2, 32, 64, 128), j...  5.83 us
  transfers between devices with their start and end apart: 20, of which 5 were waited for; matrix products, arithmetic and copies ran while one was open for 0% of the time, Pallas kernels for 4%

profile of v9, /device:TPU:1, one launch (start us, length us, event | category | flops | bytes accessed | tf_op | source)
XLA Modules:
  0.0 154.7 jit_solution(15713710316847586302)
XLA Ops:
  6.5 0.7 all-gather.3.cloned.1.call-update
  7.3 1.6 %collective-permute-start = (f32[8,64,128]{2,1,0:T(8,128)}, f32[8,64,128]{2,1,0:T(8,128)S(1)}, u32[]{:S(2)}, u32[]{:S(2)}) collective-permute-start(f32[8,64,128]{2,1,0:T(8,128)} %param.3), channel_id=1, source_target_pairs={{0,0},{1,1},{2,32},{3,33},{4,4},{5,5},{6,36},{7,37},{8,8},{9,9},{1... | collective-permute-start | bytes 786440 | tf_op jit(solution)/shard_map/ppermute | solution.py:38
  8.9 3.9 %collective-permute-start.1 = (f32[8,64,128]{2,1,0:T(8,128)}, f32[8,64,128]{2,1,0:T(8,128)S(1)}, u32[]{:S(2)}, u32[]{:S(2)}) collective-permute-start(f32[8,64,128]{2,1,0:T(8,128)} %param.3), channel_id=1, source_target_pairs={{0,16},{1,17},{2,48},{3,49},{4,20},{5,21},{6,52},{7,53},{8,24},{9,... | collective-permute-start | bytes 786440 | tf_op jit(solution)/shard_map/ppermute | solution.py:38
  12.8 2.9 %split_amplitudes.2.refs_16_ = bf16[2,32,64,128]{3,2,1,0:T(8,128)(2,1)} custom-call(f32[2048,128]{1,0:T(8,128)} %bitcast.15), custom_call_target="tpu_custom_call" | custom-call | flops 1048576 | bytes 2097152 | tf_op jit(solution)/shard_map/split_amplitudes/pallas_call | solution.py:73
  15.7 0.0 collective-permute-done
  15.8 8.1 %collective-permute-done.1 = f32[8,64,128]{2,1,0:T(8,128)S(1)} collective-permute-done((f32[8,64,128]{2,1,0:T(8,128)}, f32[8,64,128]{2,1,0:T(8,128)S(1)}, u32[]{:S(2)}, u32[]{:S(2)}) %collective-permute-start.1) | collective-permute-done | bytes 262176 | tf_op jit(solution)/shard_map/ppermute | solution.py:38
  23.9 7.4 %collective-permute-start.2 = (f32[2,8,64,128]{3,2,1,0:T(8,128)S(1)}, f32[2,8,64,128]{3,2,1,0:T(8,128)S(1)}, u32[]{:S(2)}, u32[]{:S(2)}) collective-permute-start(f32[2,8,64,128]{3,2,1,0:T(8,128)S(1)} %pad_maximum_fusion.refs_0_), channel_id=1, source_target_pairs={{0,2},{1,15},{2,4},{3,1},{4,6},{5,3},{6,8},{7,5},{8,10},{9,7},{10,... | collective-permute-start | bytes 1572872 | tf_op jit(solution)/shard_map/ppermute | solution.py:38
  31.3 1.9 %collective-permute-start.4 = (f32[2,8,64,128]{3,2,1,0:T(8,128)S(1)}, f32[2,8,64,128]{3,2,1,0:T(8,128)S(1)}, u32[]{:S(2)}, u32[]{:S(2)}) collective-permute-start(f32[2,8,64,128]{3,2,1,0:T(8,128)S(1)} %pad_maximum_fusion.refs_0_), channel_id=1, source_target_pairs={{0,14},{1,3},{2,0},{3,5},{4,2},{5,7},{6,4},{7,9},{8,6},{9,11},{10,... | collective-permute-start | bytes 1572872 | tf_op jit(solution)/shard_map/ppermute | solution.py:38
  33.2 5.9 %collective-permute-done.2.refs_1_ = f32[2,8,64,128]{3,2,1,0:T(8,128)S(1)} collective-permute-done((f32[2,8,64,128]{3,2,1,0:T(8,128)S(1)}, f32[2,8,64,128]{3,2,1,0:T(8,128)S(1)}, u32[]{:S(2)}, u32[]{:S(2)}) %collective-permute-start.2) | collective-permute-done | bytes 524320 | tf_op jit(solution)/shard_map/ppermute | solution.py:38
  39.1 5.4 %collective-permute-start.3 = (f32[2,8,64,128]{3,2,1,0:T(8,128)S(1)}, f32[2,8,64,128]{3,2,1,0:T(8,128)S(1)}, u32[]{:S(2)}, u32[]{:S(2)}) collective-permute-start(f32[2,8,64,128]{3,2,1,0:T(8,128)S(1)} %collective-permute-done.2.refs_1_), channel_id=1, source_target_pairs={{0,2},{1,15},{2,4},{3,1},{4,6},{5,3},{6,8},{7,5},{8,10},{9,7},{10,... | collective-permute-start | bytes 1572872 | tf_op jit(solution)/shard_map/ppermute | solution.py:38
  44.5 3.3 %collective-permute-start.9 = (f32[2,8,64,128]{3,2,1,0:T(8,128)S(1)}, f32[2,8,64,128]{3,2,1,0:T(8,128)S(1)}, u32[]{:S(2)}, u32[]{:S(2)}) collective-permute-start(f32[2,8,64,128]{3,2,1,0:T(8,128)S(1)} %pad_maximum_fusion.refs_0_), channel_id=1, source_target_pairs={{0,1},{1,0},{2,3},{3,2},{4,5},{5,4},{6,7},{7,6},{8,9},{9,8},{10,11... | collective-permute-start | bytes 1572872 | tf_op jit(solution)/shard_map/ppermute | solution.py:38
  47.8 5.0 %collective-permute-start.11 = (f32[64,32,128]{2,1,0:T(8,128)}, f32[64,32,128]{2,1,0:T(8,128)S(1)}, u32[]{:S(2)}, u32[]{:S(2)}) collective-permute-start(f32[64,32,128]{2,1,0:T(8,128)} %param.5), channel_id=1, source_target_pairs={{0,32},{1,33},{2,34},{3,35},{4,36},{5,37},{6,38},{7,39},{8,40},{9,... | collective-permute-start | bytes 3145736 | tf_op jit(solution)/shard_map/ppermute | solution.py:38
  52.8 0.0 collective-permute-done.4.refs_7_
  52.9 4.1 %collective-permute-start.6 = (f32[2,8,64,128]{3,2,1,0:T(8,128)S(1)}, f32[2,8,64,128]{3,2,1,0:T(8,128)}, u32[]{:S(2)}, u32[]{:S(2)}) collective-permute-start(f32[2,8,64,128]{3,2,1,0:T(8,128)S(1)} %collective-permute-done.4.refs_7_), channel_id=1, source_target_pairs={{0,14},{1,3},{2,0},{3,5},{4,2},{5,7},{6,4},{7,9},{8,6},{9,11},{10,... | collective-permute-start | bytes 1572872 | tf_op jit(solution)/shard_map/ppermute | solution.py:38
  57.0 0.0 collective-permute-done.3.refs_2_
  57.0 2.4 %collective-permute-start.5 = (f32[2,8,64,128]{3,2,1,0:T(8,128)S(1)}, f32[2,8,64,128]{3,2,1,0:T(8,128)}, u32[]{:S(2)}, u32[]{:S(2)}) collective-permute-start(f32[2,8,64,128]{3,2,1,0:T(8,128)S(1)} %collective-permute-done.3.refs_2_), channel_id=1, source_target_pairs={{0,2},{1,15},{2,4},{3,1},{4,6},{5,3},{6,8},{7,5},{8,10},{9,7},{10,... | collective-permute-start | bytes 1572872 | tf_op jit(solution)/shard_map/ppermute | solution.py:38
  59.4 0.0 collective-permute-done.9.refs_8_
  59.4 2.0 %collective-permute-start.10 = (f32[2,8,64,128]{3,2,1,0:T(8,128)S(1)}, f32[2,8,64,128]{3,2,1,0:T(8,128)S(1)}, u32[]{:S(2)}, u32[]{:S(2)}) collective-permute-start(f32[2,8,64,128]{3,2,1,0:T(8,128)S(1)} %collective-permute-done.2.refs_1_), channel_id=1, source_target_pairs={{0,1},{1,0},{2,3},{3,2},{4,5},{5,4},{6,7},{7,6},{8,9},{9,8},{10,11... | collective-permute-start | bytes 1572872 | tf_op jit(solution)/shard_map/ppermute | solution.py:38
  61.4 2.3 %collective-permute-start.17 = (f32[2,8,64,128]{3,2,1,0:T(8,128)S(1)}, f32[2,8,64,128]{3,2,1,0:T(8,128)S(1)}, u32[]{:S(2)}, u32[]{:S(2)}) collective-permute-start(f32[2,8,64,128]{3,2,1,0:T(8,128)S(1)} %collective-permute-done.4.refs_7_), channel_id=1, source_target_pairs={{0,1},{1,0},{2,3},{3,2},{4,5},{5,4},{6,7},{7,6},{8,9},{9,8},{10,11... | collective-permute-start | bytes 1572872 | tf_op jit(solution)/shard_map/ppermute | solution.py:38
  63.7 2.3 %collective-permute-done.6.refs_6_ = f32[2,8,64,128]{3,2,1,0:T(8,128)} collective-permute-done((f32[2,8,64,128]{3,2,1,0:T(8,128)S(1)}, f32[2,8,64,128]{3,2,1,0:T(8,128)}, u32[]{:S(2)}, u32[]{:S(2)}) %collective-permute-start.6) | collective-permute-done | bytes 524320 | tf_op jit(solution)/shard_map/ppermute | solution.py:38
  66.1 4.0 %collective-permute-start.8 = (f32[2,8,64,128]{3,2,1,0:T(8,128)}, f32[2,8,64,128]{3,2,1,0:T(8,128)}, u32[]{:S(2)}, u32[]{:S(2)}) collective-permute-start(f32[2,8,64,128]{3,2,1,0:T(8,128)} %collective-permute-done.6.refs_6_), channel_id=1, source_target_pairs={{0,14},{1,3},{2,0},{3,5},{4,2},{5,7},{6,4},{7,9},{8,6},{9,11},{10,... | collective-permute-start | bytes 1572872 | tf_op jit(solution)/shard_map/ppermute | solution.py:38
  70.1 0.0 collective-permute-done.5.refs_3_
  70.1 2.9 %collective-permute-start.7 = (f32[2,8,64,128]{3,2,1,0:T(8,128)}, f32[2,8,64,128]{3,2,1,0:T(8,128)}, u32[]{:S(2)}, u32[]{:S(2)}) collective-permute-start(f32[2,8,64,128]{3,2,1,0:T(8,128)} %collective-permute-done.5.refs_3_), channel_id=1, source_target_pairs={{0,2},{1,15},{2,4},{3,1},{4,6},{5,3},{6,8},{7,5},{8,10},{9,7},{10,... | collective-permute-start | bytes 1572872 | tf_op jit(solution)/shard_map/ppermute | solution.py:38
  73.1 3.4 %collective-permute-done.11 = f32[64,32,128]{2,1,0:T(8,128)S(1)} collective-permute-done((f32[64,32,128]{2,1,0:T(8,128)}, f32[64,32,128]{2,1,0:T(8,128)S(1)}, u32[]{:S(2)}, u32[]{:S(2)}) %collective-permute-start.11) | collective-permute-done | bytes 1048608 | tf_op jit(solution)/shard_map/ppermute | solution.py:38
  76.4 2.6 %collective-permute-start.16 = (f32[2,8,64,128]{3,2,1,0:T(8,128)}, f32[2,8,64,128]{3,2,1,0:T(8,128)}, u32[]{:S(2)}, u32[]{:S(2)}) collective-permute-start(f32[2,8,64,128]{3,2,1,0:T(8,128)} %collective-permute-done.6.refs_6_), channel_id=1, source_target_pairs={{0,1},{1,0},{2,3},{3,2},{4,5},{5,4},{6,7},{7,6},{8,9},{9,8},{10,11... | collective-permute-start | bytes 1572872 | tf_op jit(solution)/shard_map/ppermute | solution.py:38
  79.1 0.0 collective-permute-done.10.refs_9_
  79.1 1.9 %collective-permute-start.12 = (f32[2,8,64,128]{3,2,1,0:T(8,128)S(1)}, f32[2,8,64,128]{3,2,1,0:T(8,128)}, u32[]{:S(2)}, u32[]{:S(2)}) collective-permute-start(f32[2,8,64,128]{3,2,1,0:T(8,128)S(1)} %collective-permute-done.3.refs_2_), channel_id=1, source_target_pairs={{0,1},{1,0},{2,3},{3,2},{4,5},{5,4},{6,7},{7,6},{8,9},{9,8},{10,11... | collective-permute-start | bytes 1572872 | tf_op jit(solution)/shard_map/ppermute | solution.py:38
  81.0 0.0 collective-permute-done.17.refs_15_
  81.0 2.4 %collective-permute-start.13 = (f32[2,8,64,128]{3,2,1,0:T(8,128)}, f32[2,8,64,128]{3,2,1,0:T(8,128)}, u32[]{:S(2)}, u32[]{:S(2)}) collective-permute-start(f32[2,8,64,128]{3,2,1,0:T(8,128)} %collective-permute-done.5.refs_3_), channel_id=1, source_target_pairs={{0,1},{1,0},{2,3},{3,2},{4,5},{5,4},{6,7},{7,6},{8,9},{9,8},{10,11... | collective-permute-start | bytes 1572872 | tf_op jit(solution)/shard_map/ppermute | solution.py:38
  83.5 0.0 collective-permute-done.8.refs_5_
  83.5 1.9 %collective-permute-start.15 = (f32[2,8,64,128]{3,2,1,0:T(8,128)}, f32[2,8,64,128]{3,2,1,0:T(8,128)}, u32[]{:S(2)}, u32[]{:S(2)}) collective-permute-start(f32[2,8,64,128]{3,2,1,0:T(8,128)} %collective-permute-done.8.refs_5_), channel_id=1, source_target_pairs={{0,1},{1,0},{2,3},{3,2},{4,5},{5,4},{6,7},{7,6},{8,9},{9,8},{10,11... | collective-permute-start | bytes 1572872 | tf_op jit(solution)/shard_map/ppermute | solution.py:38
  85.4 0.0 collective-permute-done.7.refs_4_
  85.4 2.6 %collective-permute-start.14 = (f32[2,8,64,128]{3,2,1,0:T(8,128)}, f32[2,8,64,128]{3,2,1,0:T(8,128)}, u32[]{:S(2)}, u32[]{:S(2)}) collective-permute-start(f32[2,8,64,128]{3,2,1,0:T(8,128)} %collective-permute-done.7.refs_4_), channel_id=1, source_target_pairs={{0,1},{1,0},{2,3},{3,2},{4,5},{5,4},{6,7},{7,6},{8,9},{9,8},{10,11... | collective-permute-start | bytes 1572872 | tf_op jit(solution)/shard_map/ppermute | solution.py:38
  88.0 0.7 stack.32.place
  88.7 2.9 %split_amplitudes.3.refs_17_ = bf16[2,32,64,128]{3,2,1,0:T(8,128)(2,1)} custom-call(f32[2048,128]{1,0:T(8,128)} %bitcast.16), custom_call_target="tpu_custom_call" | custom-call | flops 1048576 | bytes 2097152 | tf_op jit(solution)/shard_map/split_amplitudes/pallas_call | solution.py:73
  91.6 0.0 collective-permute-done.16.refs_14_
  91.6 0.0 collective-permute-done.12.refs_10_
  91.7 0.0 collective-permute-done.13.refs_11_
  91.7 0.0 collective-permute-done.14.refs_12_
  91.7 0.0 all-gather.3.cloned.1.call-done
  91.7 14.9 %ladder.1 = f32[2,64,128]{2,1,0:T(8,128)} custom-call(s32[5]{0:T(128)} %stack.32.place, f32[8,16,32,256]{3,2,1,0:T(8,128)} %bitcast.20, f32[2,8,64,128]{3,2,1,0:T(8,128)} %copy-done.1, f32[2,8,64,128]{3,2,1,0:T(8,128)} %copy-done.2, f32[2,8,64,128]{3,2,1,0:T(8,128)} %copy-done.4, f32[2,8,64,128]{3,2,1,0:T(8,128)} %collective-permute-done.5.refs_3_, ...), custom_call_target="tpu_custom_call" | custom-call | flops 6442450944 | bytes 16777216 | tf_op jit(solution)/shard_map/ladder/pallas_call | solution.py:171
  106.7 23.1 %all_to_all.10 = f32[64,2,128]{2,1,0:T(2,128)S(1)} all-to-all(f32[64,2,128]{2,1,0:T(2,128)} %bitcast.19), channel_id=1, replica_groups=mesh['z'=8,'xh'=2,'xl'=2,'y'=8,'core'=2] {'xh','xl','y','core'}, dimensions={0} | all-to-all | bytes 131072 | tf_op jit(solution)/shard_map/all_to_all | solution.py:218
  129.8 0.1 reduce_sum.18
  129.9 0.6 broadcast_in_dim.3
  130.5 10.0 %all-to-all-start.1 = ((f32[8,2,128]{2,1,0:T(2,128)}), f32[8,2,128]{2,1,0:T(2,128)S(1)}, u32[]{:S(2)}, u32[]{:S(2)}) async-start(f32[8,2,128]{2,1,0:T(2,128)} %broadcast_in_dim.3), calls=%async_computation.1 | async-start | bytes 16384 | tf_op jit(solution)/shard_map/all_to_all | solution.py:220
  140.6 6.6 %all-to-all-done.1 = f32[8,2,128]{2,1,0:T(2,128)S(1)} async-done(((f32[8,2,128]{2,1,0:T(2,128)}), f32[8,2,128]{2,1,0:T(2,128)S(1)}, u32[]{:S(2)}, u32[]{:S(2)}) %all-to-all-start.1) | async-done | bytes 8224 | tf_op jit(solution)/shard_map/all_to_all | solution.py:220
  147.1 0.1 reshape.18
  147.2 0.6 dynamic-slice_bitcast_fusion
  (20 shorter events, 0.1 us)
Async XLA Ops:
  6.5 85.2 %all-gather.3.cloned.1.call-start = ((), (), s32[]{:S(2)}) async-start(), calls=%async_computation.2 | async-start | bytes 4718592 | tf_op jit(solution)/shard_map/all_gather | solution.py:199
  7.3 8.5 %collective-permute-start = (f32[8,64,128]{2,1,0:T(8,128)}, f32[8,64,128]{2,1,0:T(8,128)S(1)}, u32[]{:S(2)}, u32[]{:S(2)}) collective-permute-start(f32[8,64,128]{2,1,0:T(8,128)} %param.3), channel_id=1, source_target_pairs={{0,0},{1,1},{2,32},{3,33},{4,4},{5,5},{6,36},{7,37},{8,8},{9,9},{1... | collective-permute-start | bytes 786440 | tf_op jit(solution)/shard_map/ppermute | solution.py:38
  8.9 15.0 %collective-permute-start.1 = (f32[8,64,128]{2,1,0:T(8,128)}, f32[8,64,128]{2,1,0:T(8,128)S(1)}, u32[]{:S(2)}, u32[]{:S(2)}) collective-permute-start(f32[8,64,128]{2,1,0:T(8,128)} %param.3), channel_id=1, source_target_pairs={{0,16},{1,17},{2,48},{3,49},{4,20},{5,21},{6,52},{7,53},{8,24},{9,... | collective-permute-start | bytes 786440 | tf_op jit(solution)/shard_map/ppermute | solution.py:38
  23.9 67.8 %copy-start.1 = (f32[2,8,64,128]{3,2,1,0:T(8,128)}, f32[2,8,64,128]{3,2,1,0:T(8,128)S(1)}, u32[]{:S(2)}) copy-start(f32[2,8,64,128]{3,2,1,0:T(8,128)S(1)} %pad_maximum_fusion.refs_0_) | copy-start | bytes 1572868
  23.9 15.2 %collective-permute-start.2 = (f32[2,8,64,128]{3,2,1,0:T(8,128)S(1)}, f32[2,8,64,128]{3,2,1,0:T(8,128)S(1)}, u32[]{:S(2)}, u32[]{:S(2)}) collective-permute-start(f32[2,8,64,128]{3,2,1,0:T(8,128)S(1)} %pad_maximum_fusion.refs_0_), channel_id=1, source_target_pairs={{0,2},{1,15},{2,4},{3,1},{4,6},{5,3},{6,8},{7,5},{8,10},{9,7},{10,... | collective-permute-start | bytes 1572872 | tf_op jit(solution)/shard_map/ppermute | solution.py:38
  31.3 21.5 %collective-permute-start.4 = (f32[2,8,64,128]{3,2,1,0:T(8,128)S(1)}, f32[2,8,64,128]{3,2,1,0:T(8,128)S(1)}, u32[]{:S(2)}, u32[]{:S(2)}) collective-permute-start(f32[2,8,64,128]{3,2,1,0:T(8,128)S(1)} %pad_maximum_fusion.refs_0_), channel_id=1, source_target_pairs={{0,14},{1,3},{2,0},{3,5},{4,2},{5,7},{6,4},{7,9},{8,6},{9,11},{10,... | collective-permute-start | bytes 1572872 | tf_op jit(solution)/shard_map/ppermute | solution.py:38
  39.1 52.6 %copy-start.2 = (f32[2,8,64,128]{3,2,1,0:T(8,128)}, f32[2,8,64,128]{3,2,1,0:T(8,128)S(1)}, u32[]{:S(2)}) copy-start(f32[2,8,64,128]{3,2,1,0:T(8,128)S(1)} %collective-permute-done.2.refs_1_) | copy-start | bytes 1572868
  39.1 17.9 %collective-permute-start.3 = (f32[2,8,64,128]{3,2,1,0:T(8,128)S(1)}, f32[2,8,64,128]{3,2,1,0:T(8,128)S(1)}, u32[]{:S(2)}, u32[]{:S(2)}) collective-permute-start(f32[2,8,64,128]{3,2,1,0:T(8,128)S(1)} %collective-permute-done.2.refs_1_), channel_id=1, source_target_pairs={{0,2},{1,15},{2,4},{3,1},{4,6},{5,3},{6,8},{7,5},{8,10},{9,7},{10,... | collective-permute-start | bytes 1572872 | tf_op jit(solution)/shard_map/ppermute | solution.py:38
  44.5 14.9 %collective-permute-start.9 = (f32[2,8,64,128]{3,2,1,0:T(8,128)S(1)}, f32[2,8,64,128]{3,2,1,0:T(8,128)S(1)}, u32[]{:S(2)}, u32[]{:S(2)}) collective-permute-start(f32[2,8,64,128]{3,2,1,0:T(8,128)S(1)} %pad_maximum_fusion.refs_0_), channel_id=1, source_target_pairs={{0,1},{1,0},{2,3},{3,2},{4,5},{5,4},{6,7},{7,6},{8,9},{9,8},{10,11... | collective-permute-start | bytes 1572872 | tf_op jit(solution)/shard_map/ppermute | solution.py:38
  47.8 28.6 %collective-permute-start.11 = (f32[64,32,128]{2,1,0:T(8,128)}, f32[64,32,128]{2,1,0:T(8,128)S(1)}, u32[]{:S(2)}, u32[]{:S(2)}) collective-permute-start(f32[64,32,128]{2,1,0:T(8,128)} %param.5), channel_id=1, source_target_pairs={{0,32},{1,33},{2,34},{3,35},{4,36},{5,37},{6,38},{7,39},{8,40},{9,... | collective-permute-start | bytes 3145736 | tf_op jit(solution)/shard_map/ppermute | solution.py:38
  52.8 38.9 %copy-start.3 = (f32[2,8,64,128]{3,2,1,0:T(8,128)}, f32[2,8,64,128]{3,2,1,0:T(8,128)S(1)}, u32[]{:S(2)}) copy-start(f32[2,8,64,128]{3,2,1,0:T(8,128)S(1)} %collective-permute-done.4.refs_7_) | copy-start | bytes 1572868
  52.9 13.2 %collective-permute-start.6 = (f32[2,8,64,128]{3,2,1,0:T(8,128)S(1)}, f32[2,8,64,128]{3,2,1,0:T(8,128)}, u32[]{:S(2)}, u32[]{:S(2)}) collective-permute-start(f32[2,8,64,128]{3,2,1,0:T(8,128)S(1)} %collective-permute-done.4.refs_7_), channel_id=1, source_target_pairs={{0,14},{1,3},{2,0},{3,5},{4,2},{5,7},{6,4},{7,9},{8,6},{9,11},{10,... | collective-permute-start | bytes 1572872 | tf_op jit(solution)/shard_map/ppermute | solution.py:38
  57.0 34.8 %copy-start.4 = (f32[2,8,64,128]{3,2,1,0:T(8,128)}, f32[2,8,64,128]{3,2,1,0:T(8,128)S(1)}, u32[]{:S(2)}) copy-start(f32[2,8,64,128]{3,2,1,0:T(8,128)S(1)} %collective-permute-done.3.refs_2_) | copy-start | bytes 1572868
  57.0 13.1 %collective-permute-start.5 = (f32[2,8,64,128]{3,2,1,0:T(8,128)S(1)}, f32[2,8,64,128]{3,2,1,0:T(8,128)}, u32[]{:S(2)}, u32[]{:S(2)}) collective-permute-start(f32[2,8,64,128]{3,2,1,0:T(8,128)S(1)} %collective-permute-done.3.refs_2_), channel_id=1, source_target_pairs={{0,2},{1,15},{2,4},{3,1},{4,6},{5,3},{6,8},{7,5},{8,10},{9,7},{10,... | collective-permute-start | bytes 1572872 | tf_op jit(solution)/shard_map/ppermute | solution.py:38
  59.4 21.6 %copy-start.5 = (f32[2,8,64,128]{3,2,1,0:T(8,128)}, f32[2,8,64,128]{3,2,1,0:T(8,128)S(1)}, u32[]{:S(2)}) copy-start(f32[2,8,64,128]{3,2,1,0:T(8,128)S(1)} %collective-permute-done.9.refs_8_) | copy-start | bytes 1572868
  59.4 19.6 %collective-permute-start.10 = (f32[2,8,64,128]{3,2,1,0:T(8,128)S(1)}, f32[2,8,64,128]{3,2,1,0:T(8,128)S(1)}, u32[]{:S(2)}, u32[]{:S(2)}) collective-permute-start(f32[2,8,64,128]{3,2,1,0:T(8,128)S(1)} %collective-permute-done.2.refs_1_), channel_id=1, source_target_pairs={{0,1},{1,0},{2,3},{3,2},{4,5},{5,4},{6,7},{7,6},{8,9},{9,8},{10,11... | collective-permute-start | bytes 1572872 | tf_op jit(solution)/shard_map/ppermute | solution.py:38
  61.4 19.6 %collective-permute-start.17 = (f32[2,8,64,128]{3,2,1,0:T(8,128)S(1)}, f32[2,8,64,128]{3,2,1,0:T(8,128)S(1)}, u32[]{:S(2)}, u32[]{:S(2)}) collective-permute-start(f32[2,8,64,128]{3,2,1,0:T(8,128)S(1)} %collective-permute-done.4.refs_7_), channel_id=1, source_target_pairs={{0,1},{1,0},{2,3},{3,2},{4,5},{5,4},{6,7},{7,6},{8,9},{9,8},{10,11... | collective-permute-start | bytes 1572872 | tf_op jit(solution)/shard_map/ppermute | solution.py:38
  66.1 17.4 %collective-permute-start.8 = (f32[2,8,64,128]{3,2,1,0:T(8,128)}, f32[2,8,64,128]{3,2,1,0:T(8,128)}, u32[]{:S(2)}, u32[]{:S(2)}) collective-permute-start(f32[2,8,64,128]{3,2,1,0:T(8,128)} %collective-permute-done.6.refs_6_), channel_id=1, source_target_pairs={{0,14},{1,3},{2,0},{3,5},{4,2},{5,7},{6,4},{7,9},{8,6},{9,11},{10,... | collective-permute-start | bytes 1572872 | tf_op jit(solution)/shard_map/ppermute | solution.py:38
  70.1 15.3 %collective-permute-start.7 = (f32[2,8,64,128]{3,2,1,0:T(8,128)}, f32[2,8,64,128]{3,2,1,0:T(8,128)}, u32[]{:S(2)}, u32[]{:S(2)}) collective-permute-start(f32[2,8,64,128]{3,2,1,0:T(8,128)} %collective-permute-done.5.refs_3_), channel_id=1, source_target_pairs={{0,2},{1,15},{2,4},{3,1},{4,6},{5,3},{6,8},{7,5},{8,10},{9,7},{10,... | collective-permute-start | bytes 1572872 | tf_op jit(solution)/shard_map/ppermute | solution.py:38
  76.4 12.3 %copy-start = (f32[64,32,128]{2,1,0:T(8,128)}, f32[64,32,128]{2,1,0:T(8,128)S(1)}, u32[]{:S(2)}) copy-start(f32[64,32,128]{2,1,0:T(8,128)S(1)} %collective-permute-done.11) | copy-start | bytes 3145732
  76.4 15.2 %collective-permute-start.16 = (f32[2,8,64,128]{3,2,1,0:T(8,128)}, f32[2,8,64,128]{3,2,1,0:T(8,128)}, u32[]{:S(2)}, u32[]{:S(2)}) collective-permute-start(f32[2,8,64,128]{3,2,1,0:T(8,128)} %collective-permute-done.6.refs_6_), channel_id=1, source_target_pairs={{0,1},{1,0},{2,3},{3,2},{4,5},{5,4},{6,7},{7,6},{8,9},{9,8},{10,11... | collective-permute-start | bytes 1572872 | tf_op jit(solution)/shard_map/ppermute | solution.py:38
  79.1 4.4 %copy-start.6 = (f32[2,8,64,128]{3,2,1,0:T(8,128)}, f32[2,8,64,128]{3,2,1,0:T(8,128)S(1)}, u32[]{:S(2)}) copy-start(f32[2,8,64,128]{3,2,1,0:T(8,128)S(1)} %collective-permute-done.10.refs_9_) | copy-start | bytes 1572868
  79.1 12.6 %collective-permute-start.12 = (f32[2,8,64,128]{3,2,1,0:T(8,128)S(1)}, f32[2,8,64,128]{3,2,1,0:T(8,128)}, u32[]{:S(2)}, u32[]{:S(2)}) collective-permute-start(f32[2,8,64,128]{3,2,1,0:T(8,128)S(1)} %collective-permute-done.3.refs_2_), channel_id=1, source_target_pairs={{0,1},{1,0},{2,3},{3,2},{4,5},{5,4},{6,7},{7,6},{8,9},{9,8},{10,11... | collective-permute-start | bytes 1572872 | tf_op jit(solution)/shard_map/ppermute | solution.py:38
  81.0 2.4 %copy-start.7 = (f32[2,8,64,128]{3,2,1,0:T(8,128)}, f32[2,8,64,128]{3,2,1,0:T(8,128)S(1)}, u32[]{:S(2)}) copy-start(f32[2,8,64,128]{3,2,1,0:T(8,128)S(1)} %collective-permute-done.17.refs_15_) | copy-start | bytes 1572868
  81.0 10.6 %collective-permute-start.13 = (f32[2,8,64,128]{3,2,1,0:T(8,128)}, f32[2,8,64,128]{3,2,1,0:T(8,128)}, u32[]{:S(2)}, u32[]{:S(2)}) collective-permute-start(f32[2,8,64,128]{3,2,1,0:T(8,128)} %collective-permute-done.5.refs_3_), channel_id=1, source_target_pairs={{0,1},{1,0},{2,3},{3,2},{4,5},{5,4},{6,7},{7,6},{8,9},{9,8},{10,11... | collective-permute-start | bytes 1572872 | tf_op jit(solution)/shard_map/ppermute | solution.py:38
  83.5 8.2 %collective-permute-start.15 = (f32[2,8,64,128]{3,2,1,0:T(8,128)}, f32[2,8,64,128]{3,2,1,0:T(8,128)}, u32[]{:S(2)}, u32[]{:S(2)}) collective-permute-start(f32[2,8,64,128]{3,2,1,0:T(8,128)} %collective-permute-done.8.refs_5_), channel_id=1, source_target_pairs={{0,1},{1,0},{2,3},{3,2},{4,5},{5,4},{6,7},{7,6},{8,9},{9,8},{10,11... | collective-permute-start | bytes 1572872 | tf_op jit(solution)/shard_map/ppermute | solution.py:38
  85.4 6.2 %collective-permute-start.14 = (f32[2,8,64,128]{3,2,1,0:T(8,128)}, f32[2,8,64,128]{3,2,1,0:T(8,128)}, u32[]{:S(2)}, u32[]{:S(2)}) collective-permute-start(f32[2,8,64,128]{3,2,1,0:T(8,128)} %collective-permute-done.7.refs_4_), channel_id=1, source_target_pairs={{0,1},{1,0},{2,3},{3,2},{4,5},{5,4},{6,7},{7,6},{8,9},{9,8},{10,11... | collective-permute-start | bytes 1572872 | tf_op jit(solution)/shard_map/ppermute | solution.py:38
  130.5 16.6 %all-to-all-start.1 = ((f32[8,2,128]{2,1,0:T(2,128)}), f32[8,2,128]{2,1,0:T(2,128)S(1)}, u32[]{:S(2)}, u32[]{:S(2)}) async-start(f32[8,2,128]{2,1,0:T(2,128)} %broadcast_in_dim.3), calls=%async_computation.1 | async-start | bytes 16384 | tf_op jit(solution)/shard_map/all_to_all | solution.py:220
Sparse Core Ops, SparseCore 0:
  9.4 63.7 all-gather.2

commit v10 on v9

--- a/solution.py
+++ b/solution.py
@@ -31,6 +31,7 @@
 SWAP_CORE = table(lambda z, xh, xl, y, core: (z, xh, xl, y, 1 - core))
 SWAP_XH = table(lambda z, xh, xl, y, core: (z, 1 - xh, xl, y, core))
 PAIRS = (0, 1, 3, 2)
+GROUPS = ((0,), (1,), (7,), (2, 6), (3, 5), (4,))
 NEEDED = ((0, 1, 7), (2, 6, 3, 5), (4,), ())
 
 
@@ -69,7 +70,7 @@
     copy.wait()
 
 
-def split_amplitudes(block):
+def split_amplitudes(block, flops=1 << 20):
     return pl.pallas_call(
         amplitudes_kernel,
         out_shape=pltpu.HBM((2, 32, 64, 128), jnp.bfloat16),
@@ -81,14 +82,15 @@
             pltpu.SemaphoreType.DMA((2,)),
         ],
         compiler_params=pltpu.CompilerParams(vmem_limit_bytes=8 * 1024 * 1024),
-        cost_estimate=pl.CostEstimate(flops=1 << 20, bytes_accessed=2 << 20, transcendentals=0),
+        cost_estimate=pl.CostEstimate(flops=flops, bytes_accessed=2 << 20, transcendentals=0),
         name="split_amplitudes",
     )(pltpu.with_memory_space_constraint(block.reshape(2048, 128), pltpu.HBM))
 
 
 def ladder_kernel(place, right, *refs):
-    pieces, (t_own, t_oth, out) = (refs[:8], refs[8:16]), refs[16:19]
-    r_buf, raw, parts, t_buf, acc, y_high, y_low, flip, rows, r_sem, l_sem, t_sem = refs[19:]
+    own, oth, (t_own, t_oth, out) = refs[:8], refs[8:14], refs[14:17]
+    swapped = {slot: ref.at[i] for group, ref in zip(GROUPS, oth) for i, slot in enumerate(group)}
+    r_buf, raw, parts, t_buf, acc, y_high, y_low, flip, rows, r_sem, l_sem, t_sem = refs[17:]
     y, sign, xl_here, xh, core = (place[i] for i in range(5))
 
     def pair(k):
@@ -99,7 +101,7 @@
         return pltpu.make_async_copy(right.at[where], r_buf.at[k, order], r_sem.at[k, order])
 
     def left_copy(side, slot):
-        return pltpu.make_async_copy(pieces[side][slot], raw.at[side, slot], l_sem.at[side, slot])
+        return pltpu.make_async_copy(swapped[slot] if side else own[slot], raw.at[side, slot], l_sem.at[side, slot])
 
     def left(k, q_half, half, order):
         at = 2 * pair(k) + lax.bitwise_xor(half, xh)
@@ -171,7 +173,7 @@
     return pl.pallas_call(
         ladder_kernel,
         out_shape=jax.ShapeDtypeStruct((2, 64, 128), jnp.float32),
-        in_specs=[pl.BlockSpec(memory_space=pltpu.SMEM)] + [pl.BlockSpec(memory_space=pl.ANY)] * 19,
+        in_specs=[pl.BlockSpec(memory_space=pltpu.SMEM)] + [pl.BlockSpec(memory_space=pl.ANY)] * 17,
         out_specs=pl.BlockSpec(memory_space=pltpu.VMEM),
         scratch_shapes=[
             pltpu.VMEM((4, 2, 16, 32, 256), jnp.float32),
@@ -199,7 +201,7 @@
     right = lax.all_gather(vectors_right, "z", axis=0)
     t_own_split = split_amplitudes(amplitudes)
     same, other = send(vectors_left, SAME_XL), send(vectors_left, OTHER_XL)
-    own = jnp.stack([after(same, t_own_split), other])
+    own = jnp.stack([after(same, t_own_split, place), other])
     x1 = send(own, RING_X)
     t_oth = send(amplitudes, SWAP_XH)
     y1 = send(own, RING_Y)
@@ -210,10 +212,16 @@
     x3 = send(after(x2, y1), RING_X)
     y3 = send(after(y2, x2), RING_Y)
     x4 = send(after(x3, y2), RING_X)
-    t_split = (t_own_split, split_amplitudes(after(t_oth, x4)))
+    t_split = (t_own_split, split_amplitudes(after(t_oth, x4), 30 << 30))
     left_own = [own, x1, x2, x3, x4, y3, y2, y1]
-    x2_swapped = send(after(x2, x3, t_oth), SWAP_CORE)
-    left_oth = [own_swapped, x1_swapped, x2_swapped] + [send(piece, SWAP_CORE) for piece in left_own[3:]]
+    left_oth = [
+        own_swapped[None],
+        x1_swapped[None],
+        send(y1, SWAP_CORE)[None],
+        send(after(jnp.stack([x2, y2]), x3, t_oth), SWAP_CORE),
+        send(jnp.stack([x3, y3]), SWAP_CORE),
+        send(x4, SWAP_CORE)[None],
+    ]
     partial = contract(place, right, left_own, left_oth, t_split)
     near = lax.all_to_all(partial.reshape(64, 2, 128), ("xh", "xl", "y", "core"), 0, 0, tiled=True)
     near = jnp.broadcast_to(jnp.sum(near, axis=0), (8, 2, 128))

time: 156 us -> 157 us (level)
  starting transfers between devices: 67.9 us -> 73.7 us
  waiting for transfers between devices: 27 us -> 21.7 us
  local copies, waits for them, and re-layouts: 2 us -> 4.24 us
  blocking collectives: 23.1 us -> 21.4 us
    ppermute x18 -> x16, starting transfers between devices: 57.8 us -> 63.6 us  [send(): return lax.ppermute(array, AXES, pairs)]
    ppermute x18 -> x16, waiting for transfers between devices: 19.7 us -> 14.4 us  [send(): return lax.ppermute(array, AXES, pairs)]
    unnamed x16 -> x28, local copies, waits for them, and re-layouts: 0.03 us -> 2.34 us
    all_to_all x1, blocking collectives: 23.1 us -> 21.4 us  [shards(): lax.all_to_all(partial.reshape(64, 2, 128), ('xh', 'xl', 'y', 'core'), 0,...]
  transfers between devices with their start and end apart: 20 -> 18, of which waited for: 5 -> 4; matrix products, arithmetic and copies ran while one was open for 0% -> 1% of each run, Pallas kernels for 4% -> 4%
where the time goes in v10:
time: 157 us; the launch traced here: 156 us
  starting transfers between devices  73.7 us (47%)
  waiting for transfers between devices  21.7 us (14%)
  blocking collectives  21.4 us (14%)
  Pallas kernels  20.8 us (13%)
  between operations  13.8 us (9%)
  local copies, waits for them, and re-layouts  4.24 us (3%)
    ppermute x16, starting transfers between devices, send(): return lax.ppermute(array, AXES, pairs)  63.6 us
    all_to_all x1, blocking collectives, shards(): lax.all_to_all(partial.reshape(64, 2, 128), ('xh', 'xl', 'y', 'core'), 0,...  21.4 us
    pallas_call x1, Pallas kernels, contract(): pl.pallas_call(ladder_kernel, out_shape=jax.ShapeDtypeStruct((2, 64, 128)...  14.9 us
    ppermute x16, waiting for transfers between devices, send(): return lax.ppermute(array, AXES, pairs)  14.4 us
    all_to_all x1, starting transfers between devices, shards(): far = jnp.sum(lax.all_to_all(near, 'z', 0, 0, tiled=True), axis=0)  10.1 us
    all_to_all x1, waiting for transfers between devices, shards(): far = jnp.sum(lax.all_to_all(near, 'z', 0, 0, tiled=True), axis=0)  6.58 us
    pallas_call x2, Pallas kernels, split_amplitudes(): pl.pallas_call(amplitudes_kernel, out_shape=pltpu.HBM((2, 32, 64, 128), j...  5.83 us
  transfers between devices with their start and end apart: 18, of which 4 were waited for; matrix products, arithmetic and copies ran while one was open for 1% of the time, Pallas kernels for 4%

profile of v10, /device:TPU:1, one launch (start us, length us, event | category | flops | bytes accessed | tf_op | source)
XLA Modules:
  0.0 155.9 jit_solution(10796773943146633370)
XLA Ops:
  6.5 0.7 all-gather.3.cloned.1.call-update
  7.3 1.6 %collective-permute-start = (f32[8,64,128]{2,1,0:T(8,128)}, f32[8,64,128]{2,1,0:T(8,128)S(1)}, u32[]{:S(2)}, u32[]{:S(2)}) collective-permute-start(f32[8,64,128]{2,1,0:T(8,128)} %param.3), channel_id=1, source_target_pairs={{0,0},{1,1},{2,32},{3,33},{4,4},{5,5},{6,36},{7,37},{8,8},{9,9},{1... | collective-permute-start | bytes 786440 | tf_op jit(solution)/shard_map/ppermute | solution.py:39
  8.9 3.9 %collective-permute-start.1 = (f32[8,64,128]{2,1,0:T(8,128)}, f32[8,64,128]{2,1,0:T(8,128)S(1)}, u32[]{:S(2)}, u32[]{:S(2)}) collective-permute-start(f32[8,64,128]{2,1,0:T(8,128)} %param.3), channel_id=1, source_target_pairs={{0,16},{1,17},{2,48},{3,49},{4,20},{5,21},{6,52},{7,53},{8,24},{9,... | collective-permute-start | bytes 786440 | tf_op jit(solution)/shard_map/ppermute | solution.py:39
  12.8 0.6 stack.50.place
  13.4 2.9 %split_amplitudes.2.refs_14_ = bf16[2,32,64,128]{3,2,1,0:T(8,128)(2,1)} custom-call(f32[2048,128]{1,0:T(8,128)} %bitcast.23), custom_call_target="tpu_custom_call" | custom-call | flops 1048576 | bytes 2097152 | tf_op jit(solution)/shard_map/split_amplitudes/pallas_call | solution.py:74
  16.4 0.0 collective-permute-done
  16.4 7.5 %collective-permute-done.1 = f32[8,64,128]{2,1,0:T(8,128)S(1)} collective-permute-done((f32[8,64,128]{2,1,0:T(8,128)}, f32[8,64,128]{2,1,0:T(8,128)S(1)}, u32[]{:S(2)}, u32[]{:S(2)}) %collective-permute-start.1) | collective-permute-done | bytes 262176 | tf_op jit(solution)/shard_map/ppermute | solution.py:39
  23.9 7.4 %collective-permute-start.2 = (f32[2,8,64,128]{3,2,1,0:T(8,128)S(1)}, f32[2,8,64,128]{3,2,1,0:T(8,128)S(1)}, u32[]{:S(2)}, u32[]{:S(2)}) collective-permute-start(f32[2,8,64,128]{3,2,1,0:T(8,128)S(1)} %pad_maximum_fusion.2.refs_0_), channel_id=1, source_target_pairs={{0,2},{1,15},{2,4},{3,1},{4,6},{5,3},{6,8},{7,5},{8,10},{9,7},{10,... | collective-permute-start | bytes 1572872 | tf_op jit(solution)/shard_map/ppermute | solution.py:39
  31.3 1.9 %collective-permute-start.4 = (f32[2,8,64,128]{3,2,1,0:T(8,128)S(1)}, f32[2,8,64,128]{3,2,1,0:T(8,128)S(1)}, u32[]{:S(2)}, u32[]{:S(2)}) collective-permute-start(f32[2,8,64,128]{3,2,1,0:T(8,128)S(1)} %pad_maximum_fusion.2.refs_0_), channel_id=1, source_target_pairs={{0,14},{1,3},{2,0},{3,5},{4,2},{5,7},{6,4},{7,9},{8,6},{9,11},{10,... | collective-permute-start | bytes 1572872 | tf_op jit(solution)/shard_map/ppermute | solution.py:39
  33.2 5.9 %collective-permute-done.2.refs_1_ = f32[2,8,64,128]{3,2,1,0:T(8,128)S(1)} collective-permute-done((f32[2,8,64,128]{3,2,1,0:T(8,128)S(1)}, f32[2,8,64,128]{3,2,1,0:T(8,128)S(1)}, u32[]{:S(2)}, u32[]{:S(2)}) %collective-permute-start.2) | collective-permute-done | bytes 524320 | tf_op jit(solution)/shard_map/ppermute | solution.py:39
  39.1 5.4 %collective-permute-start.3 = (f32[2,8,64,128]{3,2,1,0:T(8,128)S(1)}, f32[2,8,64,128]{3,2,1,0:T(8,128)S(1)}, u32[]{:S(2)}, u32[]{:S(2)}) collective-permute-start(f32[2,8,64,128]{3,2,1,0:T(8,128)S(1)} %collective-permute-done.2.refs_1_), channel_id=1, source_target_pairs={{0,2},{1,15},{2,4},{3,1},{4,6},{5,3},{6,8},{7,5},{8,10},{9,7},{10,... | collective-permute-start | bytes 1572872 | tf_op jit(solution)/shard_map/ppermute | solution.py:39
  44.5 1.0 collective-permute-done.4.refs_7_
  45.5 1.9 %collective-permute-start.6 = (f32[2,8,64,128]{3,2,1,0:T(8,128)S(1)}, f32[2,8,64,128]{3,2,1,0:T(8,128)S(1)}, u32[]{:S(2)}, u32[]{:S(2)}) collective-permute-start(f32[2,8,64,128]{3,2,1,0:T(8,128)S(1)} %collective-permute-done.4.refs_7_), channel_id=1, source_target_pairs={{0,14},{1,3},{2,0},{3,5},{4,2},{5,7},{6,4},{7,9},{8,6},{9,11},{10,... | collective-permute-start | bytes 1572872 | tf_op jit(solution)/shard_map/ppermute | solution.py:39
  47.4 3.8 %collective-permute-start.12 = (f32[64,32,128]{2,1,0:T(8,128)}, f32[64,32,128]{2,1,0:T(8,128)S(1)}, u32[]{:S(2)}, u32[]{:S(2)}) collective-permute-start(f32[64,32,128]{2,1,0:T(8,128)} %param.5), channel_id=1, source_target_pairs={{0,32},{1,33},{2,34},{3,35},{4,36},{5,37},{6,38},{7,39},{8,40},{9,... | collective-permute-start | bytes 3145736 | tf_op jit(solution)/shard_map/ppermute | solution.py:39
  51.3 0.0 collective-permute-done.3.refs_2_
  51.3 4.7 %collective-permute-start.5 = (f32[2,8,64,128]{3,2,1,0:T(8,128)S(1)}, f32[2,8,64,128]{3,2,1,0:T(8,128)S(1)}, u32[]{:S(2)}, u32[]{:S(2)}) collective-permute-start(f32[2,8,64,128]{3,2,1,0:T(8,128)S(1)} %collective-permute-done.3.refs_2_), channel_id=1, source_target_pairs={{0,2},{1,15},{2,4},{3,1},{4,6},{5,3},{6,8},{7,5},{8,10},{9,7},{10,... | collective-permute-start | bytes 1572872 | tf_op jit(solution)/shard_map/ppermute | solution.py:39
  56.0 8.6 %collective-permute-start.9 = (f32[2,8,64,128]{3,2,1,0:T(8,128)S(1)}, f32[2,8,64,128]{3,2,1,0:T(8,128)S(1)}, u32[]{:S(2)}, u32[]{:S(2)}) collective-permute-start(f32[2,8,64,128]{3,2,1,0:T(8,128)S(1)} %pad_maximum_fusion.2.refs_0_), channel_id=1, source_target_pairs={{0,1},{1,0},{2,3},{3,2},{4,5},{5,4},{6,7},{7,6},{8,9},{9,8},{10,11... | collective-permute-start | bytes 1572872 | tf_op jit(solution)/shard_map/ppermute | solution.py:39
  64.6 0.0 collective-permute-done.6.refs_6_
  64.6 3.2 %collective-permute-start.8 = (f32[2,8,64,128]{3,2,1,0:T(8,128)S(1)}, f32[2,8,64,128]{3,2,1,0:T(8,128)S(1)}, u32[]{:S(2)}, u32[]{:S(2)}) collective-permute-start(f32[2,8,64,128]{3,2,1,0:T(8,128)S(1)} %collective-permute-done.6.refs_6_), channel_id=1, source_target_pairs={{0,14},{1,3},{2,0},{3,5},{4,2},{5,7},{6,4},{7,9},{8,6},{9,11},{10,... | collective-permute-start | bytes 1572872 | tf_op jit(solution)/shard_map/ppermute | solution.py:39
  67.9 0.0 collective-permute-done.5.refs_3_
  67.9 3.6 %collective-permute-start.7 = (f32[2,8,64,128]{3,2,1,0:T(8,128)S(1)}, f32[2,8,64,128]{3,2,1,0:T(8,128)S(1)}, u32[]{:S(2)}, u32[]{:S(2)}) collective-permute-start(f32[2,8,64,128]{3,2,1,0:T(8,128)S(1)} %collective-permute-done.5.refs_3_), channel_id=1, source_target_pairs={{0,2},{1,15},{2,4},{3,1},{4,6},{5,3},{6,8},{7,5},{8,10},{9,7},{10,... | collective-permute-start | bytes 1572872 | tf_op jit(solution)/shard_map/ppermute | solution.py:39
  71.5 0.0 collective-permute-done.9
  71.5 7.3 %collective-permute-start.10 = (f32[2,8,64,128]{3,2,1,0:T(8,128)S(1)}, f32[2,8,64,128]{3,2,1,0:T(8,128)S(1)}, u32[]{:S(2)}, u32[]{:S(2)}) collective-permute-start(f32[2,8,64,128]{3,2,1,0:T(8,128)S(1)} %collective-permute-done.2.refs_1_), channel_id=1, source_target_pairs={{0,1},{1,0},{2,3},{3,2},{4,5},{5,4},{6,7},{7,6},{8,9},{9,8},{10,11... | collective-permute-start | bytes 1572872 | tf_op jit(solution)/shard_map/ppermute | solution.py:39
  78.8 1.9 %collective-permute-start.11 = (f32[2,8,64,128]{3,2,1,0:T(8,128)S(1)}, f32[2,8,64,128]{3,2,1,0:T(8,128)S(1)}, u32[]{:S(2)}, u32[]{:S(2)}) collective-permute-start(f32[2,8,64,128]{3,2,1,0:T(8,128)S(1)} %collective-permute-done.4.refs_7_), channel_id=1, source_target_pairs={{0,1},{1,0},{2,3},{3,2},{4,5},{5,4},{6,7},{7,6},{8,9},{9,8},{10,11... | collective-permute-start | bytes 1572872 | tf_op jit(solution)/shard_map/ppermute | solution.py:39
  80.7 0.1 pad_maximum_fusion
  80.8 0.0 collective-permute-done.8.refs_5_
  80.8 0.1 pad_maximum_fusion.1
  80.9 2.4 %collective-permute-start.14 = (f32[2,2,8,64,128]{4,3,2,1,0:T(8,128)S(1)}, f32[2,2,8,64,128]{4,3,2,1,0:T(8,128)S(1)}, u32[]{:S(2)}, u32[]{:S(2)}) collective-permute-start(f32[2,2,8,64,128]{4,3,2,1,0:T(8,128)S(1)} %pad_maximum_fusion.1), channel_id=1, source_target_pairs={{0,1},{1,0},{2,3},{3,2},{4,5},{5,4},{6,7},{7,6},{8,9},{9,8},{10,11... | collective-permute-start | bytes 3145736 | tf_op jit(solution)/shard_map/ppermute | solution.py:39
  83.3 1.9 %collective-permute-start.13 = (f32[2,2,8,64,128]{4,3,2,1,0:T(8,128)S(1)}, f32[2,2,8,64,128]{4,3,2,1,0:T(8,128)S(1)}, u32[]{:S(2)}, u32[]{:S(2)}) collective-permute-start(f32[2,2,8,64,128]{4,3,2,1,0:T(8,128)S(1)} %pad_maximum_fusion), channel_id=1, source_target_pairs={{0,1},{1,0},{2,3},{3,2},{4,5},{5,4},{6,7},{7,6},{8,9},{9,8},{10,11... | collective-permute-start | bytes 3145736 | tf_op jit(solution)/shard_map/ppermute | solution.py:39
  85.3 0.0 collective-permute-done.7.refs_4_
  85.3 4.0 %collective-permute-start.15 = (f32[2,8,64,128]{3,2,1,0:T(8,128)S(1)}, f32[2,8,64,128]{3,2,1,0:T(8,128)}, u32[]{:S(2)}, u32[]{:S(2)}) collective-permute-start(f32[2,8,64,128]{3,2,1,0:T(8,128)S(1)} %collective-permute-done.7.refs_4_), channel_id=1, source_target_pairs={{0,1},{1,0},{2,3},{3,2},{4,5},{5,4},{6,7},{7,6},{8,9},{9,8},{10,11... | collective-permute-start | bytes 1572872 | tf_op jit(solution)/shard_map/ppermute | solution.py:39
  89.3 2.9 %split_amplitudes.3.refs_15_ = bf16[2,32,64,128]{3,2,1,0:T(8,128)(2,1)} custom-call(f32[2048,128]{1,0:T(8,128)} %bitcast.32), custom_call_target="tpu_custom_call" | custom-call | flops 32212254720 | bytes 2097152 | tf_op jit(solution)/shard_map/split_amplitudes/pallas_call | solution.py:74
  92.3 0.0 collective-permute-done.10
  92.3 0.0 collective-permute-done.11
  92.4 0.0 collective-permute-done.13.refs_11_
  92.4 0.7 copy-done.12
  93.1 0.2 copy-done.13
  93.3 0.4 copy-done.6
  93.7 1.0 copy-done.7
  94.7 0.0 collective-permute-done.15
  94.7 14.9 %ladder.1 = f32[2,64,128]{2,1,0:T(8,128)} custom-call(s32[5]{0:T(128)} %stack.50.place, f32[8,16,32,256]{3,2,1,0:T(8,128)} %bitcast.31, f32[2,8,64,128]{3,2,1,0:T(8,128)} %copy-done, f32[2,8,64,128]{3,2,1,0:T(8,128)} %copy-done.8, f32[2,8,64,128]{3,2,1,0:T(8,128)} %copy-done.1, f32[2,8,64,128]{3,2,1,0:T(8,128)} %copy-done.3, f32[2,8,64,128]{3,2,1,0:T(8,128)} %copy-done.11, ...), custom_call_target="tpu_custom_call" | custom-call | flops 6442450944 | bytes 16777216 | tf_op jit(solution)/shard_map/ladder/pallas_call | solution.py:173
  109.6 21.4 %all_to_all.10 = f32[64,2,128]{2,1,0:T(2,128)S(1)} all-to-all(f32[64,2,128]{2,1,0:T(2,128)} %bitcast.30), channel_id=1, replica_groups=mesh['z'=8,'xh'=2,'xl'=2,'y'=8,'core'=2] {'xh','xl','y','core'}, dimensions={0} | all-to-all | bytes 131072 | tf_op jit(solution)/shard_map/all_to_all | solution.py:226
  131.0 0.1 reduce_sum.18
  131.1 0.6 broadcast_in_dim.19
  131.7 10.1 %all-to-all-start.1 = ((f32[8,2,128]{2,1,0:T(2,128)}), f32[8,2,128]{2,1,0:T(2,128)S(1)}, u32[]{:S(2)}, u32[]{:S(2)}) async-start(f32[8,2,128]{2,1,0:T(2,128)} %broadcast_in_dim.19), calls=%async_computation.1 | async-start | bytes 16384 | tf_op jit(solution)/shard_map/all_to_all | solution.py:228
  141.7 6.6 %all-to-all-done.1 = f32[8,2,128]{2,1,0:T(2,128)S(1)} async-done(((f32[8,2,128]{2,1,0:T(2,128)}), f32[8,2,128]{2,1,0:T(2,128)S(1)}, u32[]{:S(2)}, u32[]{:S(2)}) %all-to-all-start.1) | async-done | bytes 8224 | tf_op jit(solution)/shard_map/all_to_all | solution.py:228
  148.3 0.1 reshape.18
  148.4 0.6 dynamic-slice_bitcast_fusion
  (30 shorter events, 0.1 us)
Async XLA Ops:
  6.5 88.1 %all-gather.3.cloned.1.call-start = ((), (), s32[]{:S(2)}) async-start(), calls=%async_computation.2 | async-start | bytes 4718592 | tf_op jit(solution)/shard_map/all_gather | solution.py:201
  7.3 9.1 %collective-permute-start = (f32[8,64,128]{2,1,0:T(8,128)}, f32[8,64,128]{2,1,0:T(8,128)S(1)}, u32[]{:S(2)}, u32[]{:S(2)}) collective-permute-start(f32[8,64,128]{2,1,0:T(8,128)} %param.3), channel_id=1, source_target_pairs={{0,0},{1,1},{2,32},{3,33},{4,4},{5,5},{6,36},{7,37},{8,8},{9,9},{1... | collective-permute-start | bytes 786440 | tf_op jit(solution)/shard_map/ppermute | solution.py:39
  8.9 15.0 %collective-permute-start.1 = (f32[8,64,128]{2,1,0:T(8,128)}, f32[8,64,128]{2,1,0:T(8,128)S(1)}, u32[]{:S(2)}, u32[]{:S(2)}) collective-permute-start(f32[8,64,128]{2,1,0:T(8,128)} %param.3), channel_id=1, source_target_pairs={{0,16},{1,17},{2,48},{3,49},{4,20},{5,21},{6,52},{7,53},{8,24},{9,... | collective-permute-start | bytes 786440 | tf_op jit(solution)/shard_map/ppermute | solution.py:39
  23.9 68.3 %copy-start = (f32[2,8,64,128]{3,2,1,0:T(8,128)}, f32[2,8,64,128]{3,2,1,0:T(8,128)S(1)}, u32[]{:S(2)}) copy-start(f32[2,8,64,128]{3,2,1,0:T(8,128)S(1)} %pad_maximum_fusion.2.refs_0_) | copy-start | bytes 1572868
  23.9 15.2 %collective-permute-start.2 = (f32[2,8,64,128]{3,2,1,0:T(8,128)S(1)}, f32[2,8,64,128]{3,2,1,0:T(8,128)S(1)}, u32[]{:S(2)}, u32[]{:S(2)}) collective-permute-start(f32[2,8,64,128]{3,2,1,0:T(8,128)S(1)} %pad_maximum_fusion.2.refs_0_), channel_id=1, source_target_pairs={{0,2},{1,15},{2,4},{3,1},{4,6},{5,3},{6,8},{7,5},{8,10},{9,7},{10,... | collective-permute-start | bytes 1572872 | tf_op jit(solution)/shard_map/ppermute | solution.py:39
  31.3 14.2 %collective-permute-start.4 = (f32[2,8,64,128]{3,2,1,0:T(8,128)S(1)}, f32[2,8,64,128]{3,2,1,0:T(8,128)S(1)}, u32[]{:S(2)}, u32[]{:S(2)}) collective-permute-start(f32[2,8,64,128]{3,2,1,0:T(8,128)S(1)} %pad_maximum_fusion.2.refs_0_), channel_id=1, source_target_pairs={{0,14},{1,3},{2,0},{3,5},{4,2},{5,7},{6,4},{7,9},{8,6},{9,11},{10,... | collective-permute-start | bytes 1572872 | tf_op jit(solution)/shard_map/ppermute | solution.py:39
  39.1 53.1 %copy-start.8 = (f32[2,8,64,128]{3,2,1,0:T(8,128)}, f32[2,8,64,128]{3,2,1,0:T(8,128)S(1)}, u32[]{:S(2)}) copy-start(f32[2,8,64,128]{3,2,1,0:T(8,128)S(1)} %collective-permute-done.2.refs_1_) | copy-start | bytes 1572868
  39.1 12.2 %collective-permute-start.3 = (f32[2,8,64,128]{3,2,1,0:T(8,128)S(1)}, f32[2,8,64,128]{3,2,1,0:T(8,128)S(1)}, u32[]{:S(2)}, u32[]{:S(2)}) collective-permute-start(f32[2,8,64,128]{3,2,1,0:T(8,128)S(1)} %collective-permute-done.2.refs_1_), channel_id=1, source_target_pairs={{0,2},{1,15},{2,4},{3,1},{4,6},{5,3},{6,8},{7,5},{8,10},{9,7},{10,... | collective-permute-start | bytes 1572872 | tf_op jit(solution)/shard_map/ppermute | solution.py:39
  45.5 46.7 %copy-start.9 = (f32[2,8,64,128]{3,2,1,0:T(8,128)}, f32[2,8,64,128]{3,2,1,0:T(8,128)S(1)}, u32[]{:S(2)}) copy-start(f32[2,8,64,128]{3,2,1,0:T(8,128)S(1)} %collective-permute-done.4.refs_7_) | copy-start | bytes 1572868
  45.5 19.1 %collective-permute-start.6 = (f32[2,8,64,128]{3,2,1,0:T(8,128)S(1)}, f32[2,8,64,128]{3,2,1,0:T(8,128)S(1)}, u32[]{:S(2)}, u32[]{:S(2)}) collective-permute-start(f32[2,8,64,128]{3,2,1,0:T(8,128)S(1)} %collective-permute-done.4.refs_7_), channel_id=1, source_target_pairs={{0,14},{1,3},{2,0},{3,5},{4,2},{5,7},{6,4},{7,9},{8,6},{9,11},{10,... | collective-permute-start | bytes 1572872 | tf_op jit(solution)/shard_map/ppermute | solution.py:39
  47.4 35.9 %collective-permute-start.12 = (f32[64,32,128]{2,1,0:T(8,128)}, f32[64,32,128]{2,1,0:T(8,128)S(1)}, u32[]{:S(2)}, u32[]{:S(2)}) collective-permute-start(f32[64,32,128]{2,1,0:T(8,128)} %param.5), channel_id=1, source_target_pairs={{0,32},{1,33},{2,34},{3,35},{4,36},{5,37},{6,38},{7,39},{8,40},{9,... | collective-permute-start | bytes 3145736 | tf_op jit(solution)/shard_map/ppermute | solution.py:39
  51.3 41.0 %copy-start.1 = (f32[2,8,64,128]{3,2,1,0:T(8,128)}, f32[2,8,64,128]{3,2,1,0:T(8,128)S(1)}, u32[]{:S(2)}) copy-start(f32[2,8,64,128]{3,2,1,0:T(8,128)S(1)} %collective-permute-done.3.refs_2_) | copy-start | bytes 1572868
  51.3 16.6 %collective-permute-start.5 = (f32[2,8,64,128]{3,2,1,0:T(8,128)S(1)}, f32[2,8,64,128]{3,2,1,0:T(8,128)S(1)}, u32[]{:S(2)}, u32[]{:S(2)}) collective-permute-start(f32[2,8,64,128]{3,2,1,0:T(8,128)S(1)} %collective-permute-done.3.refs_2_), channel_id=1, source_target_pairs={{0,2},{1,15},{2,4},{3,1},{4,6},{5,3},{6,8},{7,5},{8,10},{9,7},{10,... | collective-permute-start | bytes 1572872 | tf_op jit(solution)/shard_map/ppermute | solution.py:39
  56.0 15.4 %collective-permute-start.9 = (f32[2,8,64,128]{3,2,1,0:T(8,128)S(1)}, f32[2,8,64,128]{3,2,1,0:T(8,128)S(1)}, u32[]{:S(2)}, u32[]{:S(2)}) collective-permute-start(f32[2,8,64,128]{3,2,1,0:T(8,128)S(1)} %pad_maximum_fusion.2.refs_0_), channel_id=1, source_target_pairs={{0,1},{1,0},{2,3},{3,2},{4,5},{5,4},{6,7},{7,6},{8,9},{9,8},{10,11... | collective-permute-start | bytes 1572872 | tf_op jit(solution)/shard_map/ppermute | solution.py:39
  64.6 27.6 %copy-start.2 = (f32[2,8,64,128]{3,2,1,0:T(8,128)}, f32[2,8,64,128]{3,2,1,0:T(8,128)S(1)}, u32[]{:S(2)}) copy-start(f32[2,8,64,128]{3,2,1,0:T(8,128)S(1)} %collective-permute-done.6.refs_6_) | copy-start | bytes 1572868
  64.6 16.2 %collective-permute-start.8 = (f32[2,8,64,128]{3,2,1,0:T(8,128)S(1)}, f32[2,8,64,128]{3,2,1,0:T(8,128)S(1)}, u32[]{:S(2)}, u32[]{:S(2)}) collective-permute-start(f32[2,8,64,128]{3,2,1,0:T(8,128)S(1)} %collective-permute-done.6.refs_6_), channel_id=1, source_target_pairs={{0,14},{1,3},{2,0},{3,5},{4,2},{5,7},{6,4},{7,9},{8,6},{9,11},{10,... | collective-permute-start | bytes 1572872 | tf_op jit(solution)/shard_map/ppermute | solution.py:39
  67.9 24.4 %copy-start.3 = (f32[2,8,64,128]{3,2,1,0:T(8,128)}, f32[2,8,64,128]{3,2,1,0:T(8,128)S(1)}, u32[]{:S(2)}) copy-start(f32[2,8,64,128]{3,2,1,0:T(8,128)S(1)} %collective-permute-done.5.refs_3_) | copy-start | bytes 1572868
  67.9 17.4 %collective-permute-start.7 = (f32[2,8,64,128]{3,2,1,0:T(8,128)S(1)}, f32[2,8,64,128]{3,2,1,0:T(8,128)S(1)}, u32[]{:S(2)}, u32[]{:S(2)}) collective-permute-start(f32[2,8,64,128]{3,2,1,0:T(8,128)S(1)} %collective-permute-done.5.refs_3_), channel_id=1, source_target_pairs={{0,2},{1,15},{2,4},{3,1},{4,6},{5,3},{6,8},{7,5},{8,10},{9,7},{10,... | collective-permute-start | bytes 1572872 | tf_op jit(solution)/shard_map/ppermute | solution.py:39
  71.5 9.3 %copy-start.10 = (f32[2,8,64,128]{3,2,1,0:T(8,128)}, f32[2,8,64,128]{3,2,1,0:T(8,128)S(1)}, u32[]{:S(2)}) copy-start(f32[2,8,64,128]{3,2,1,0:T(8,128)S(1)} %collective-permute-done.9) | copy-start | bytes 1572868
  71.5 20.8 %collective-permute-start.10 = (f32[2,8,64,128]{3,2,1,0:T(8,128)S(1)}, f32[2,8,64,128]{3,2,1,0:T(8,128)S(1)}, u32[]{:S(2)}, u32[]{:S(2)}) collective-permute-start(f32[2,8,64,128]{3,2,1,0:T(8,128)S(1)} %collective-permute-done.2.refs_1_), channel_id=1, source_target_pairs={{0,1},{1,0},{2,3},{3,2},{4,5},{5,4},{6,7},{7,6},{8,9},{9,8},{10,11... | collective-permute-start | bytes 1572872 | tf_op jit(solution)/shard_map/ppermute | solution.py:39
  78.8 13.5 %collective-permute-start.11 = (f32[2,8,64,128]{3,2,1,0:T(8,128)S(1)}, f32[2,8,64,128]{3,2,1,0:T(8,128)S(1)}, u32[]{:S(2)}, u32[]{:S(2)}) collective-permute-start(f32[2,8,64,128]{3,2,1,0:T(8,128)S(1)} %collective-permute-done.4.refs_7_), channel_id=1, source_target_pairs={{0,1},{1,0},{2,3},{3,2},{4,5},{5,4},{6,7},{7,6},{8,9},{9,8},{10,11... | collective-permute-start | bytes 1572872 | tf_op jit(solution)/shard_map/ppermute | solution.py:39
  80.8 11.5 %copy-start.4 = (f32[2,8,64,128]{3,2,1,0:T(8,128)}, f32[2,8,64,128]{3,2,1,0:T(8,128)S(1)}, u32[]{:S(2)}) copy-start(f32[2,8,64,128]{3,2,1,0:T(8,128)S(1)} %collective-permute-done.8.refs_5_) | copy-start | bytes 1572868
  80.9 11.4 %collective-permute-start.14 = (f32[2,2,8,64,128]{4,3,2,1,0:T(8,128)S(1)}, f32[2,2,8,64,128]{4,3,2,1,0:T(8,128)S(1)}, u32[]{:S(2)}, u32[]{:S(2)}) collective-permute-start(f32[2,2,8,64,128]{4,3,2,1,0:T(8,128)S(1)} %pad_maximum_fusion.1), channel_id=1, source_target_pairs={{0,1},{1,0},{2,3},{3,2},{4,5},{5,4},{6,7},{7,6},{8,9},{9,8},{10,11... | collective-permute-start | bytes 3145736 | tf_op jit(solution)/shard_map/ppermute | solution.py:39
  83.3 6.0 %copy-start.5 = (f32[64,32,128]{2,1,0:T(8,128)}, f32[64,32,128]{2,1,0:T(8,128)S(1)}, u32[]{:S(2)}) copy-start(f32[64,32,128]{2,1,0:T(8,128)S(1)} %collective-permute-done.12) | copy-start | bytes 3145732
  83.3 9.0 %collective-permute-start.13 = (f32[2,2,8,64,128]{4,3,2,1,0:T(8,128)S(1)}, f32[2,2,8,64,128]{4,3,2,1,0:T(8,128)S(1)}, u32[]{:S(2)}, u32[]{:S(2)}) collective-permute-start(f32[2,2,8,64,128]{4,3,2,1,0:T(8,128)S(1)} %pad_maximum_fusion), channel_id=1, source_target_pairs={{0,1},{1,0},{2,3},{3,2},{4,5},{5,4},{6,7},{7,6},{8,9},{9,8},{10,11... | collective-permute-start | bytes 3145736 | tf_op jit(solution)/shard_map/ppermute | solution.py:39
  85.3 7.0 %copy-start.11 = (f32[2,8,64,128]{3,2,1,0:T(8,128)}, f32[2,8,64,128]{3,2,1,0:T(8,128)S(1)}, u32[]{:S(2)}) copy-start(f32[2,8,64,128]{3,2,1,0:T(8,128)S(1)} %collective-permute-done.7.refs_4_) | copy-start | bytes 1572868
  85.3 9.4 %collective-permute-start.15 = (f32[2,8,64,128]{3,2,1,0:T(8,128)S(1)}, f32[2,8,64,128]{3,2,1,0:T(8,128)}, u32[]{:S(2)}, u32[]{:S(2)}) collective-permute-start(f32[2,8,64,128]{3,2,1,0:T(8,128)S(1)} %collective-permute-done.7.refs_4_), channel_id=1, source_target_pairs={{0,1},{1,0},{2,3},{3,2},{4,5},{5,4},{6,7},{7,6},{8,9},{9,8},{10,11... | collective-permute-start | bytes 1572872 | tf_op jit(solution)/shard_map/ppermute | solution.py:39
  92.3 0.8 copy-start.12
  92.3 0.9 copy-start.13
  92.3 1.4 copy-start.6
  93.7 1.0 copy-start.7
  131.7 16.6 %all-to-all-start.1 = ((f32[8,2,128]{2,1,0:T(2,128)}), f32[8,2,128]{2,1,0:T(2,128)S(1)}, u32[]{:S(2)}, u32[]{:S(2)}) async-start(f32[8,2,128]{2,1,0:T(2,128)} %broadcast_in_dim.19), calls=%async_computation.1 | async-start | bytes 16384 | tf_op jit(solution)/shard_map/all_to_all | solution.py:228
Sparse Core Ops, SparseCore 0:
  9.4 63.7 all-gather.2

commit v11 on v9

--- a/solution.py
+++ b/solution.py
@@ -199,7 +199,7 @@
     right = lax.all_gather(vectors_right, "z", axis=0)
     t_own_split = split_amplitudes(amplitudes)
     same, other = send(vectors_left, SAME_XL), send(vectors_left, OTHER_XL)
-    own = jnp.stack([after(same, t_own_split), other])
+    own = jnp.stack([after(same, t_own_split, place), other])
     x1 = send(own, RING_X)
     t_oth = send(amplitudes, SWAP_XH)
     y1 = send(own, RING_Y)

time: 156 us -> 156 us (level)
  local copies, waits for them, and re-layouts: 2 us -> 3.84 us
    unnamed x16 -> x32, local copies, waits for them, and re-layouts: 0.03 us -> 1.96 us
where the time goes in v11:
time: 156 us; the launch traced here: 155 us
  starting transfers between devices  67.8 us (43%)
  waiting for transfers between devices  26.3 us (17%)
  blocking collectives  22.6 us (14%)
  Pallas kernels  20.8 us (13%)
  between operations  13.9 us (9%)
  local copies, waits for them, and re-layouts  3.84 us (2%)
    ppermute x18, starting transfers between devices, send(): return lax.ppermute(array, AXES, pairs)  57.8 us
    all_to_all x1, blocking collectives, shards(): lax.all_to_all(partial.reshape(64, 2, 128), ('xh', 'xl', 'y', 'core'), 0,...  22.6 us
    ppermute x18, waiting for transfers between devices, send(): return lax.ppermute(array, AXES, pairs)  19 us
    pallas_call x1, Pallas kernels, contract(): pl.pallas_call(ladder_kernel, out_shape=jax.ShapeDtypeStruct((2, 64, 128)...  15 us
    all_to_all x1, starting transfers between devices, shards(): far = jnp.sum(lax.all_to_all(near, 'z', 0, 0, tiled=True), axis=0)  10 us
    all_to_all x1, waiting for transfers between devices, shards(): far = jnp.sum(lax.all_to_all(near, 'z', 0, 0, tiled=True), axis=0)  6.58 us
    pallas_call x2, Pallas kernels, split_amplitudes(): pl.pallas_call(amplitudes_kernel, out_shape=pltpu.HBM((2, 32, 64, 128), j...  5.86 us
  transfers between devices with their start and end apart: 20, of which 5 were waited for; matrix products, arithmetic and copies ran while one was open for 0% of the time, Pallas kernels for 4%

profile of v11, /device:TPU:1, one launch (start us, length us, event | category | flops | bytes accessed | tf_op | source)
XLA Modules:
  0.0 155.5 jit_solution(586064996743834176)
XLA Ops:
  6.5 0.7 all-gather.3.cloned.1.call-update
  7.3 1.6 %collective-permute-start = (f32[8,64,128]{2,1,0:T(8,128)}, f32[8,64,128]{2,1,0:T(8,128)S(1)}, u32[]{:S(2)}, u32[]{:S(2)}) collective-permute-start(f32[8,64,128]{2,1,0:T(8,128)} %param.3), channel_id=1, source_target_pairs={{0,0},{1,1},{2,32},{3,33},{4,4},{5,5},{6,36},{7,37},{8,8},{9,9},{1... | collective-permute-start | bytes 786440 | tf_op jit(solution)/shard_map/ppermute | solution.py:38
  8.9 3.9 %collective-permute-start.1 = (f32[8,64,128]{2,1,0:T(8,128)}, f32[8,64,128]{2,1,0:T(8,128)S(1)}, u32[]{:S(2)}, u32[]{:S(2)}) collective-permute-start(f32[8,64,128]{2,1,0:T(8,128)} %param.3), channel_id=1, source_target_pairs={{0,16},{1,17},{2,48},{3,49},{4,20},{5,21},{6,52},{7,53},{8,24},{9,... | collective-permute-start | bytes 786440 | tf_op jit(solution)/shard_map/ppermute | solution.py:38
  12.8 0.6 stack.32.place
  13.4 2.9 %split_amplitudes.2.refs_16_ = bf16[2,32,64,128]{3,2,1,0:T(8,128)(2,1)} custom-call(f32[2048,128]{1,0:T(8,128)} %bitcast.15), custom_call_target="tpu_custom_call" | custom-call | flops 1048576 | bytes 2097152 | tf_op jit(solution)/shard_map/split_amplitudes/pallas_call | solution.py:73
  16.4 0.0 collective-permute-done
  16.4 7.5 %collective-permute-done.1 = f32[8,64,128]{2,1,0:T(8,128)S(1)} collective-permute-done((f32[8,64,128]{2,1,0:T(8,128)}, f32[8,64,128]{2,1,0:T(8,128)S(1)}, u32[]{:S(2)}, u32[]{:S(2)}) %collective-permute-start.1) | collective-permute-done | bytes 262176 | tf_op jit(solution)/shard_map/ppermute | solution.py:38
  23.9 7.4 %collective-permute-start.2 = (f32[2,8,64,128]{3,2,1,0:T(8,128)S(1)}, f32[2,8,64,128]{3,2,1,0:T(8,128)S(1)}, u32[]{:S(2)}, u32[]{:S(2)}) collective-permute-start(f32[2,8,64,128]{3,2,1,0:T(8,128)S(1)} %pad_maximum_fusion.refs_0_), channel_id=1, source_target_pairs={{0,2},{1,15},{2,4},{3,1},{4,6},{5,3},{6,8},{7,5},{8,10},{9,7},{10,... | collective-permute-start | bytes 1572872 | tf_op jit(solution)/shard_map/ppermute | solution.py:38
  31.3 1.9 %collective-permute-start.4 = (f32[2,8,64,128]{3,2,1,0:T(8,128)S(1)}, f32[2,8,64,128]{3,2,1,0:T(8,128)S(1)}, u32[]{:S(2)}, u32[]{:S(2)}) collective-permute-start(f32[2,8,64,128]{3,2,1,0:T(8,128)S(1)} %pad_maximum_fusion.refs_0_), channel_id=1, source_target_pairs={{0,14},{1,3},{2,0},{3,5},{4,2},{5,7},{6,4},{7,9},{8,6},{9,11},{10,... | collective-permute-start | bytes 1572872 | tf_op jit(solution)/shard_map/ppermute | solution.py:38
  33.2 5.9 %collective-permute-done.2.refs_1_ = f32[2,8,64,128]{3,2,1,0:T(8,128)S(1)} collective-permute-done((f32[2,8,64,128]{3,2,1,0:T(8,128)S(1)}, f32[2,8,64,128]{3,2,1,0:T(8,128)S(1)}, u32[]{:S(2)}, u32[]{:S(2)}) %collective-permute-start.2) | collective-permute-done | bytes 524320 | tf_op jit(solution)/shard_map/ppermute | solution.py:38
  39.1 5.4 %collective-permute-start.3 = (f32[2,8,64,128]{3,2,1,0:T(8,128)S(1)}, f32[2,8,64,128]{3,2,1,0:T(8,128)S(1)}, u32[]{:S(2)}, u32[]{:S(2)}) collective-permute-start(f32[2,8,64,128]{3,2,1,0:T(8,128)S(1)} %collective-permute-done.2.refs_1_), channel_id=1, source_target_pairs={{0,2},{1,15},{2,4},{3,1},{4,6},{5,3},{6,8},{7,5},{8,10},{9,7},{10,... | collective-permute-start | bytes 1572872 | tf_op jit(solution)/shard_map/ppermute | solution.py:38
  44.5 3.3 %collective-permute-start.9 = (f32[2,8,64,128]{3,2,1,0:T(8,128)S(1)}, f32[2,8,64,128]{3,2,1,0:T(8,128)S(1)}, u32[]{:S(2)}, u32[]{:S(2)}) collective-permute-start(f32[2,8,64,128]{3,2,1,0:T(8,128)S(1)} %pad_maximum_fusion.refs_0_), channel_id=1, source_target_pairs={{0,1},{1,0},{2,3},{3,2},{4,5},{5,4},{6,7},{7,6},{8,9},{9,8},{10,11... | collective-permute-start | bytes 1572872 | tf_op jit(solution)/shard_map/ppermute | solution.py:38
  47.8 5.0 %collective-permute-start.11 = (f32[64,32,128]{2,1,0:T(8,128)}, f32[64,32,128]{2,1,0:T(8,128)S(1)}, u32[]{:S(2)}, u32[]{:S(2)}) collective-permute-start(f32[64,32,128]{2,1,0:T(8,128)} %param.5), channel_id=1, source_target_pairs={{0,32},{1,33},{2,34},{3,35},{4,36},{5,37},{6,38},{7,39},{8,40},{9,... | collective-permute-start | bytes 3145736 | tf_op jit(solution)/shard_map/ppermute | solution.py:38
  52.8 0.0 collective-permute-done.4.refs_7_
  52.9 4.1 %collective-permute-start.6 = (f32[2,8,64,128]{3,2,1,0:T(8,128)S(1)}, f32[2,8,64,128]{3,2,1,0:T(8,128)S(1)}, u32[]{:S(2)}, u32[]{:S(2)}) collective-permute-start(f32[2,8,64,128]{3,2,1,0:T(8,128)S(1)} %collective-permute-done.4.refs_7_), channel_id=1, source_target_pairs={{0,14},{1,3},{2,0},{3,5},{4,2},{5,7},{6,4},{7,9},{8,6},{9,11},{10,... | collective-permute-start | bytes 1572872 | tf_op jit(solution)/shard_map/ppermute | solution.py:38
  57.0 0.0 collective-permute-done.3.refs_2_
  57.0 2.4 %collective-permute-start.5 = (f32[2,8,64,128]{3,2,1,0:T(8,128)S(1)}, f32[2,8,64,128]{3,2,1,0:T(8,128)S(1)}, u32[]{:S(2)}, u32[]{:S(2)}) collective-permute-start(f32[2,8,64,128]{3,2,1,0:T(8,128)S(1)} %collective-permute-done.3.refs_2_), channel_id=1, source_target_pairs={{0,2},{1,15},{2,4},{3,1},{4,6},{5,3},{6,8},{7,5},{8,10},{9,7},{10,... | collective-permute-start | bytes 1572872 | tf_op jit(solution)/shard_map/ppermute | solution.py:38
  59.4 0.0 collective-permute-done.9.refs_8_
  59.4 2.0 %collective-permute-start.10 = (f32[2,8,64,128]{3,2,1,0:T(8,128)S(1)}, f32[2,8,64,128]{3,2,1,0:T(8,128)S(1)}, u32[]{:S(2)}, u32[]{:S(2)}) collective-permute-start(f32[2,8,64,128]{3,2,1,0:T(8,128)S(1)} %collective-permute-done.2.refs_1_), channel_id=1, source_target_pairs={{0,1},{1,0},{2,3},{3,2},{4,5},{5,4},{6,7},{7,6},{8,9},{9,8},{10,11... | collective-permute-start | bytes 1572872 | tf_op jit(solution)/shard_map/ppermute | solution.py:38
  61.4 2.3 %collective-permute-start.17 = (f32[2,8,64,128]{3,2,1,0:T(8,128)S(1)}, f32[2,8,64,128]{3,2,1,0:T(8,128)S(1)}, u32[]{:S(2)}, u32[]{:S(2)}) collective-permute-start(f32[2,8,64,128]{3,2,1,0:T(8,128)S(1)} %collective-permute-done.4.refs_7_), channel_id=1, source_target_pairs={{0,1},{1,0},{2,3},{3,2},{4,5},{5,4},{6,7},{7,6},{8,9},{9,8},{10,11... | collective-permute-start | bytes 1572872 | tf_op jit(solution)/shard_map/ppermute | solution.py:38
  63.8 2.3 %collective-permute-done.6.refs_6_ = f32[2,8,64,128]{3,2,1,0:T(8,128)S(1)} collective-permute-done((f32[2,8,64,128]{3,2,1,0:T(8,128)S(1)}, f32[2,8,64,128]{3,2,1,0:T(8,128)S(1)}, u32[]{:S(2)}, u32[]{:S(2)}) %collective-permute-start.6) | collective-permute-done | bytes 524320 | tf_op jit(solution)/shard_map/ppermute | solution.py:38
  66.1 4.0 %collective-permute-start.8 = (f32[2,8,64,128]{3,2,1,0:T(8,128)S(1)}, f32[2,8,64,128]{3,2,1,0:T(8,128)S(1)}, u32[]{:S(2)}, u32[]{:S(2)}) collective-permute-start(f32[2,8,64,128]{3,2,1,0:T(8,128)S(1)} %collective-permute-done.6.refs_6_), channel_id=1, source_target_pairs={{0,14},{1,3},{2,0},{3,5},{4,2},{5,7},{6,4},{7,9},{8,6},{9,11},{10,... | collective-permute-start | bytes 1572872 | tf_op jit(solution)/shard_map/ppermute | solution.py:38
  70.1 0.0 collective-permute-done.5.refs_3_
  70.2 2.9 %collective-permute-start.7 = (f32[2,8,64,128]{3,2,1,0:T(8,128)S(1)}, f32[2,8,64,128]{3,2,1,0:T(8,128)S(1)}, u32[]{:S(2)}, u32[]{:S(2)}) collective-permute-start(f32[2,8,64,128]{3,2,1,0:T(8,128)S(1)} %collective-permute-done.5.refs_3_), channel_id=1, source_target_pairs={{0,2},{1,15},{2,4},{3,1},{4,6},{5,3},{6,8},{7,5},{8,10},{9,7},{10,... | collective-permute-start | bytes 1572872 | tf_op jit(solution)/shard_map/ppermute | solution.py:38
  73.1 3.4 %collective-permute-done.11 = f32[64,32,128]{2,1,0:T(8,128)S(1)} collective-permute-done((f32[64,32,128]{2,1,0:T(8,128)}, f32[64,32,128]{2,1,0:T(8,128)S(1)}, u32[]{:S(2)}, u32[]{:S(2)}) %collective-permute-start.11) | collective-permute-done | bytes 1048608 | tf_op jit(solution)/shard_map/ppermute | solution.py:38
  76.4 2.6 %collective-permute-start.16 = (f32[2,8,64,128]{3,2,1,0:T(8,128)S(1)}, f32[2,8,64,128]{3,2,1,0:T(8,128)S(1)}, u32[]{:S(2)}, u32[]{:S(2)}) collective-permute-start(f32[2,8,64,128]{3,2,1,0:T(8,128)S(1)} %collective-permute-done.6.refs_6_), channel_id=1, source_target_pairs={{0,1},{1,0},{2,3},{3,2},{4,5},{5,4},{6,7},{7,6},{8,9},{9,8},{10,11... | collective-permute-start | bytes 1572872 | tf_op jit(solution)/shard_map/ppermute | solution.py:38
  79.1 0.0 collective-permute-done.10.refs_9_
  79.1 1.9 %collective-permute-start.12 = (f32[2,8,64,128]{3,2,1,0:T(8,128)S(1)}, f32[2,8,64,128]{3,2,1,0:T(8,128)S(1)}, u32[]{:S(2)}, u32[]{:S(2)}) collective-permute-start(f32[2,8,64,128]{3,2,1,0:T(8,128)S(1)} %collective-permute-done.3.refs_2_), channel_id=1, source_target_pairs={{0,1},{1,0},{2,3},{3,2},{4,5},{5,4},{6,7},{7,6},{8,9},{9,8},{10,11... | collective-permute-start | bytes 1572872 | tf_op jit(solution)/shard_map/ppermute | solution.py:38
  81.0 0.0 collective-permute-done.17.refs_15_
  81.0 2.4 %collective-permute-start.13 = (f32[2,8,64,128]{3,2,1,0:T(8,128)S(1)}, f32[2,8,64,128]{3,2,1,0:T(8,128)S(1)}, u32[]{:S(2)}, u32[]{:S(2)}) collective-permute-start(f32[2,8,64,128]{3,2,1,0:T(8,128)S(1)} %collective-permute-done.5.refs_3_), channel_id=1, source_target_pairs={{0,1},{1,0},{2,3},{3,2},{4,5},{5,4},{6,7},{7,6},{8,9},{9,8},{10,11... | collective-permute-start | bytes 1572872 | tf_op jit(solution)/shard_map/ppermute | solution.py:38
  83.4 0.0 collective-permute-done.8.refs_5_
  83.5 1.9 %collective-permute-start.15 = (f32[2,8,64,128]{3,2,1,0:T(8,128)S(1)}, f32[2,8,64,128]{3,2,1,0:T(8,128)S(1)}, u32[]{:S(2)}, u32[]{:S(2)}) collective-permute-start(f32[2,8,64,128]{3,2,1,0:T(8,128)S(1)} %collective-permute-done.8.refs_5_), channel_id=1, source_target_pairs={{0,1},{1,0},{2,3},{3,2},{4,5},{5,4},{6,7},{7,6},{8,9},{9,8},{10,11... | collective-permute-start | bytes 1572872 | tf_op jit(solution)/shard_map/ppermute | solution.py:38
  85.4 0.0 collective-permute-done.7.refs_4_
  85.4 2.6 %collective-permute-start.14 = (f32[2,8,64,128]{3,2,1,0:T(8,128)S(1)}, f32[2,8,64,128]{3,2,1,0:T(8,128)}, u32[]{:S(2)}, u32[]{:S(2)}) collective-permute-start(f32[2,8,64,128]{3,2,1,0:T(8,128)S(1)} %collective-permute-done.7.refs_4_), channel_id=1, source_target_pairs={{0,1},{1,0},{2,3},{3,2},{4,5},{5,4},{6,7},{7,6},{8,9},{9,8},{10,11... | collective-permute-start | bytes 1572872 | tf_op jit(solution)/shard_map/ppermute | solution.py:38
  88.0 2.9 %split_amplitudes.3.refs_17_ = bf16[2,32,64,128]{3,2,1,0:T(8,128)(2,1)} custom-call(f32[2048,128]{1,0:T(8,128)} %bitcast.16), custom_call_target="tpu_custom_call" | custom-call | flops 1048576 | bytes 2097152 | tf_op jit(solution)/shard_map/split_amplitudes/pallas_call | solution.py:73
  91.0 0.0 collective-permute-done.12.refs_10_
  91.1 0.7 copy-done.12
  91.8 0.2 copy-done.13
  92.0 0.2 copy-done.15
  92.2 0.8 copy-done.14
  93.0 15.0 %ladder.1 = f32[2,64,128]{2,1,0:T(8,128)} custom-call(s32[5]{0:T(128)} %stack.32.place, f32[8,16,32,256]{3,2,1,0:T(8,128)} %bitcast.20, f32[2,8,64,128]{3,2,1,0:T(8,128)} %copy-done.1, f32[2,8,64,128]{3,2,1,0:T(8,128)} %copy-done.2, f32[2,8,64,128]{3,2,1,0:T(8,128)} %copy-done.4, f32[2,8,64,128]{3,2,1,0:T(8,128)} %copy-done.7, f32[2,8,64,128]{3,2,1,0:T(8,128)} %copy-done.11, ...), custom_call_target="tpu_custom_call" | custom-call | flops 6442450944 | bytes 16777216 | tf_op jit(solution)/shard_map/ladder/pallas_call | solution.py:171
  108.0 22.6 %all_to_all.10 = f32[64,2,128]{2,1,0:T(2,128)S(1)} all-to-all(f32[64,2,128]{2,1,0:T(2,128)} %bitcast.19), channel_id=1, replica_groups=mesh['z'=8,'xh'=2,'xl'=2,'y'=8,'core'=2] {'xh','xl','y','core'}, dimensions={0} | all-to-all | bytes 131072 | tf_op jit(solution)/shard_map/all_to_all | solution.py:218
  130.6 0.1 reduce_sum.18
  130.7 0.6 broadcast_in_dim.3
  131.3 10.0 %all-to-all-start.1 = ((f32[8,2,128]{2,1,0:T(2,128)}), f32[8,2,128]{2,1,0:T(2,128)S(1)}, u32[]{:S(2)}, u32[]{:S(2)}) async-start(f32[8,2,128]{2,1,0:T(2,128)} %broadcast_in_dim.3), calls=%async_computation.1 | async-start | bytes 16384 | tf_op jit(solution)/shard_map/all_to_all | solution.py:220
  141.3 6.6 %all-to-all-done.1 = f32[8,2,128]{2,1,0:T(2,128)S(1)} async-done(((f32[8,2,128]{2,1,0:T(2,128)}), f32[8,2,128]{2,1,0:T(2,128)S(1)}, u32[]{:S(2)}, u32[]{:S(2)}) %all-to-all-start.1) | async-done | bytes 8224 | tf_op jit(solution)/shard_map/all_to_all | solution.py:220
  147.9 0.1 reshape.18
  148.0 0.6 dynamic-slice_bitcast_fusion
  (36 shorter events, 0.1 us)
Async XLA Ops:
  6.5 86.4 %all-gather.3.cloned.1.call-start = ((), (), s32[]{:S(2)}) async-start(), calls=%async_computation.2 | async-start | bytes 4718592 | tf_op jit(solution)/shard_map/all_gather | solution.py:199
  7.3 9.1 %collective-permute-start = (f32[8,64,128]{2,1,0:T(8,128)}, f32[8,64,128]{2,1,0:T(8,128)S(1)}, u32[]{:S(2)}, u32[]{:S(2)}) collective-permute-start(f32[8,64,128]{2,1,0:T(8,128)} %param.3), channel_id=1, source_target_pairs={{0,0},{1,1},{2,32},{3,33},{4,4},{5,5},{6,36},{7,37},{8,8},{9,9},{1... | collective-permute-start | bytes 786440 | tf_op jit(solution)/shard_map/ppermute | solution.py:38
  8.9 15.0 %collective-permute-start.1 = (f32[8,64,128]{2,1,0:T(8,128)}, f32[8,64,128]{2,1,0:T(8,128)S(1)}, u32[]{:S(2)}, u32[]{:S(2)}) collective-permute-start(f32[8,64,128]{2,1,0:T(8,128)} %param.3), channel_id=1, source_target_pairs={{0,16},{1,17},{2,48},{3,49},{4,20},{5,21},{6,52},{7,53},{8,24},{9,... | collective-permute-start | bytes 786440 | tf_op jit(solution)/shard_map/ppermute | solution.py:38
  23.9 69.1 %copy-start.1 = (f32[2,8,64,128]{3,2,1,0:T(8,128)}, f32[2,8,64,128]{3,2,1,0:T(8,128)S(1)}, u32[]{:S(2)}) copy-start(f32[2,8,64,128]{3,2,1,0:T(8,128)S(1)} %pad_maximum_fusion.refs_0_) | copy-start | bytes 1572868
  23.9 15.2 %collective-permute-start.2 = (f32[2,8,64,128]{3,2,1,0:T(8,128)S(1)}, f32[2,8,64,128]{3,2,1,0:T(8,128)S(1)}, u32[]{:S(2)}, u32[]{:S(2)}) collective-permute-start(f32[2,8,64,128]{3,2,1,0:T(8,128)S(1)} %pad_maximum_fusion.refs_0_), channel_id=1, source_target_pairs={{0,2},{1,15},{2,4},{3,1},{4,6},{5,3},{6,8},{7,5},{8,10},{9,7},{10,... | collective-permute-start | bytes 1572872 | tf_op jit(solution)/shard_map/ppermute | solution.py:38
  31.3 21.5 %collective-permute-start.4 = (f32[2,8,64,128]{3,2,1,0:T(8,128)S(1)}, f32[2,8,64,128]{3,2,1,0:T(8,128)S(1)}, u32[]{:S(2)}, u32[]{:S(2)}) collective-permute-start(f32[2,8,64,128]{3,2,1,0:T(8,128)S(1)} %pad_maximum_fusion.refs_0_), channel_id=1, source_target_pairs={{0,14},{1,3},{2,0},{3,5},{4,2},{5,7},{6,4},{7,9},{8,6},{9,11},{10,... | collective-permute-start | bytes 1572872 | tf_op jit(solution)/shard_map/ppermute | solution.py:38
  39.1 53.9 %copy-start.2 = (f32[2,8,64,128]{3,2,1,0:T(8,128)}, f32[2,8,64,128]{3,2,1,0:T(8,128)S(1)}, u32[]{:S(2)}) copy-start(f32[2,8,64,128]{3,2,1,0:T(8,128)S(1)} %collective-permute-done.2.refs_1_) | copy-start | bytes 1572868
  39.1 17.9 %collective-permute-start.3 = (f32[2,8,64,128]{3,2,1,0:T(8,128)S(1)}, f32[2,8,64,128]{3,2,1,0:T(8,128)S(1)}, u32[]{:S(2)}, u32[]{:S(2)}) collective-permute-start(f32[2,8,64,128]{3,2,1,0:T(8,128)S(1)} %collective-permute-done.2.refs_1_), channel_id=1, source_target_pairs={{0,2},{1,15},{2,4},{3,1},{4,6},{5,3},{6,8},{7,5},{8,10},{9,7},{10,... | collective-permute-start | bytes 1572872 | tf_op jit(solution)/shard_map/ppermute | solution.py:38
  44.5 14.9 %collective-permute-start.9 = (f32[2,8,64,128]{3,2,1,0:T(8,128)S(1)}, f32[2,8,64,128]{3,2,1,0:T(8,128)S(1)}, u32[]{:S(2)}, u32[]{:S(2)}) collective-permute-start(f32[2,8,64,128]{3,2,1,0:T(8,128)S(1)} %pad_maximum_fusion.refs_0_), channel_id=1, source_target_pairs={{0,1},{1,0},{2,3},{3,2},{4,5},{5,4},{6,7},{7,6},{8,9},{9,8},{10,11... | collective-permute-start | bytes 1572872 | tf_op jit(solution)/shard_map/ppermute | solution.py:38
  47.8 28.6 %collective-permute-start.11 = (f32[64,32,128]{2,1,0:T(8,128)}, f32[64,32,128]{2,1,0:T(8,128)S(1)}, u32[]{:S(2)}, u32[]{:S(2)}) collective-permute-start(f32[64,32,128]{2,1,0:T(8,128)} %param.5), channel_id=1, source_target_pairs={{0,32},{1,33},{2,34},{3,35},{4,36},{5,37},{6,38},{7,39},{8,40},{9,... | collective-permute-start | bytes 3145736 | tf_op jit(solution)/shard_map/ppermute | solution.py:38
  52.8 40.1 %copy-start.3 = (f32[2,8,64,128]{3,2,1,0:T(8,128)}, f32[2,8,64,128]{3,2,1,0:T(8,128)S(1)}, u32[]{:S(2)}) copy-start(f32[2,8,64,128]{3,2,1,0:T(8,128)S(1)} %collective-permute-done.4.refs_7_) | copy-start | bytes 1572868
  52.9 13.2 %collective-permute-start.6 = (f32[2,8,64,128]{3,2,1,0:T(8,128)S(1)}, f32[2,8,64,128]{3,2,1,0:T(8,128)S(1)}, u32[]{:S(2)}, u32[]{:S(2)}) collective-permute-start(f32[2,8,64,128]{3,2,1,0:T(8,128)S(1)} %collective-permute-done.4.refs_7_), channel_id=1, source_target_pairs={{0,14},{1,3},{2,0},{3,5},{4,2},{5,7},{6,4},{7,9},{8,6},{9,11},{10,... | collective-permute-start | bytes 1572872 | tf_op jit(solution)/shard_map/ppermute | solution.py:38
  57.0 36.0 %copy-start.4 = (f32[2,8,64,128]{3,2,1,0:T(8,128)}, f32[2,8,64,128]{3,2,1,0:T(8,128)S(1)}, u32[]{:S(2)}) copy-start(f32[2,8,64,128]{3,2,1,0:T(8,128)S(1)} %collective-permute-done.3.refs_2_) | copy-start | bytes 1572868
  57.0 13.1 %collective-permute-start.5 = (f32[2,8,64,128]{3,2,1,0:T(8,128)S(1)}, f32[2,8,64,128]{3,2,1,0:T(8,128)S(1)}, u32[]{:S(2)}, u32[]{:S(2)}) collective-permute-start(f32[2,8,64,128]{3,2,1,0:T(8,128)S(1)} %collective-permute-done.3.refs_2_), channel_id=1, source_target_pairs={{0,2},{1,15},{2,4},{3,1},{4,6},{5,3},{6,8},{7,5},{8,10},{9,7},{10,... | collective-permute-start | bytes 1572872 | tf_op jit(solution)/shard_map/ppermute | solution.py:38
  59.4 33.6 %copy-start.5 = (f32[2,8,64,128]{3,2,1,0:T(8,128)}, f32[2,8,64,128]{3,2,1,0:T(8,128)S(1)}, u32[]{:S(2)}) copy-start(f32[2,8,64,128]{3,2,1,0:T(8,128)S(1)} %collective-permute-done.9.refs_8_) | copy-start | bytes 1572868
  59.4 19.6 %collective-permute-start.10 = (f32[2,8,64,128]{3,2,1,0:T(8,128)S(1)}, f32[2,8,64,128]{3,2,1,0:T(8,128)S(1)}, u32[]{:S(2)}, u32[]{:S(2)}) collective-permute-start(f32[2,8,64,128]{3,2,1,0:T(8,128)S(1)} %collective-permute-done.2.refs_1_), channel_id=1, source_target_pairs={{0,1},{1,0},{2,3},{3,2},{4,5},{5,4},{6,7},{7,6},{8,9},{9,8},{10,11... | collective-permute-start | bytes 1572872 | tf_op jit(solution)/shard_map/ppermute | solution.py:38
  61.4 19.6 %collective-permute-start.17 = (f32[2,8,64,128]{3,2,1,0:T(8,128)S(1)}, f32[2,8,64,128]{3,2,1,0:T(8,128)S(1)}, u32[]{:S(2)}, u32[]{:S(2)}) collective-permute-start(f32[2,8,64,128]{3,2,1,0:T(8,128)S(1)} %collective-permute-done.4.refs_7_), channel_id=1, source_target_pairs={{0,1},{1,0},{2,3},{3,2},{4,5},{5,4},{6,7},{7,6},{8,9},{9,8},{10,11... | collective-permute-start | bytes 1572872 | tf_op jit(solution)/shard_map/ppermute | solution.py:38
  66.1 26.9 %copy-start.6 = (f32[2,8,64,128]{3,2,1,0:T(8,128)}, f32[2,8,64,128]{3,2,1,0:T(8,128)S(1)}, u32[]{:S(2)}) copy-start(f32[2,8,64,128]{3,2,1,0:T(8,128)S(1)} %collective-permute-done.6.refs_6_) | copy-start | bytes 1572868
  66.1 17.4 %collective-permute-start.8 = (f32[2,8,64,128]{3,2,1,0:T(8,128)S(1)}, f32[2,8,64,128]{3,2,1,0:T(8,128)S(1)}, u32[]{:S(2)}, u32[]{:S(2)}) collective-permute-start(f32[2,8,64,128]{3,2,1,0:T(8,128)S(1)} %collective-permute-done.6.refs_6_), channel_id=1, source_target_pairs={{0,14},{1,3},{2,0},{3,5},{4,2},{5,7},{6,4},{7,9},{8,6},{9,11},{10,... | collective-permute-start | bytes 1572872 | tf_op jit(solution)/shard_map/ppermute | solution.py:38
  70.2 20.8 %copy-start.7 = (f32[2,8,64,128]{3,2,1,0:T(8,128)}, f32[2,8,64,128]{3,2,1,0:T(8,128)S(1)}, u32[]{:S(2)}) copy-start(f32[2,8,64,128]{3,2,1,0:T(8,128)S(1)} %collective-permute-done.5.refs_3_) | copy-start | bytes 1572868
  70.2 15.2 %collective-permute-start.7 = (f32[2,8,64,128]{3,2,1,0:T(8,128)S(1)}, f32[2,8,64,128]{3,2,1,0:T(8,128)S(1)}, u32[]{:S(2)}, u32[]{:S(2)}) collective-permute-start(f32[2,8,64,128]{3,2,1,0:T(8,128)S(1)} %collective-permute-done.5.refs_3_), channel_id=1, source_target_pairs={{0,2},{1,15},{2,4},{3,1},{4,6},{5,3},{6,8},{7,5},{8,10},{9,7},{10,... | collective-permute-start | bytes 1572872 | tf_op jit(solution)/shard_map/ppermute | solution.py:38
  76.4 11.6 %copy-start = (f32[64,32,128]{2,1,0:T(8,128)}, f32[64,32,128]{2,1,0:T(8,128)S(1)}, u32[]{:S(2)}) copy-start(f32[64,32,128]{2,1,0:T(8,128)S(1)} %collective-permute-done.11) | copy-start | bytes 3145732
  76.4 14.5 %collective-permute-start.16 = (f32[2,8,64,128]{3,2,1,0:T(8,128)S(1)}, f32[2,8,64,128]{3,2,1,0:T(8,128)S(1)}, u32[]{:S(2)}, u32[]{:S(2)}) collective-permute-start(f32[2,8,64,128]{3,2,1,0:T(8,128)S(1)} %collective-permute-done.6.refs_6_), channel_id=1, source_target_pairs={{0,1},{1,0},{2,3},{3,2},{4,5},{5,4},{6,7},{7,6},{8,9},{9,8},{10,11... | collective-permute-start | bytes 1572872 | tf_op jit(solution)/shard_map/ppermute | solution.py:38
  79.1 6.3 %copy-start.8 = (f32[2,8,64,128]{3,2,1,0:T(8,128)}, f32[2,8,64,128]{3,2,1,0:T(8,128)S(1)}, u32[]{:S(2)}) copy-start(f32[2,8,64,128]{3,2,1,0:T(8,128)S(1)} %collective-permute-done.10.refs_9_) | copy-start | bytes 1572868
  79.1 11.9 %collective-permute-start.12 = (f32[2,8,64,128]{3,2,1,0:T(8,128)S(1)}, f32[2,8,64,128]{3,2,1,0:T(8,128)S(1)}, u32[]{:S(2)}, u32[]{:S(2)}) collective-permute-start(f32[2,8,64,128]{3,2,1,0:T(8,128)S(1)} %collective-permute-done.3.refs_2_), channel_id=1, source_target_pairs={{0,1},{1,0},{2,3},{3,2},{4,5},{5,4},{6,7},{7,6},{8,9},{9,8},{10,11... | collective-permute-start | bytes 1572872 | tf_op jit(solution)/shard_map/ppermute | solution.py:38
  81.0 7.0 %copy-start.9 = (f32[2,8,64,128]{3,2,1,0:T(8,128)}, f32[2,8,64,128]{3,2,1,0:T(8,128)S(1)}, u32[]{:S(2)}) copy-start(f32[2,8,64,128]{3,2,1,0:T(8,128)S(1)} %collective-permute-done.17.refs_15_) | copy-start | bytes 1572868
  81.0 10.0 %collective-permute-start.13 = (f32[2,8,64,128]{3,2,1,0:T(8,128)S(1)}, f32[2,8,64,128]{3,2,1,0:T(8,128)S(1)}, u32[]{:S(2)}, u32[]{:S(2)}) collective-permute-start(f32[2,8,64,128]{3,2,1,0:T(8,128)S(1)} %collective-permute-done.5.refs_3_), channel_id=1, source_target_pairs={{0,1},{1,0},{2,3},{3,2},{4,5},{5,4},{6,7},{7,6},{8,9},{9,8},{10,11... | collective-permute-start | bytes 1572872 | tf_op jit(solution)/shard_map/ppermute | solution.py:38
  83.4 7.6 %copy-start.10 = (f32[2,8,64,128]{3,2,1,0:T(8,128)}, f32[2,8,64,128]{3,2,1,0:T(8,128)S(1)}, u32[]{:S(2)}) copy-start(f32[2,8,64,128]{3,2,1,0:T(8,128)S(1)} %collective-permute-done.8.refs_5_) | copy-start | bytes 1572868
  83.5 7.6 %collective-permute-start.15 = (f32[2,8,64,128]{3,2,1,0:T(8,128)S(1)}, f32[2,8,64,128]{3,2,1,0:T(8,128)S(1)}, u32[]{:S(2)}, u32[]{:S(2)}) collective-permute-start(f32[2,8,64,128]{3,2,1,0:T(8,128)S(1)} %collective-permute-done.8.refs_5_), channel_id=1, source_target_pairs={{0,1},{1,0},{2,3},{3,2},{4,5},{5,4},{6,7},{7,6},{8,9},{9,8},{10,11... | collective-permute-start | bytes 1572872 | tf_op jit(solution)/shard_map/ppermute | solution.py:38
  85.4 5.6 %copy-start.11 = (f32[2,8,64,128]{3,2,1,0:T(8,128)}, f32[2,8,64,128]{3,2,1,0:T(8,128)S(1)}, u32[]{:S(2)}) copy-start(f32[2,8,64,128]{3,2,1,0:T(8,128)S(1)} %collective-permute-done.7.refs_4_) | copy-start | bytes 1572868
  85.4 7.5 %collective-permute-start.14 = (f32[2,8,64,128]{3,2,1,0:T(8,128)S(1)}, f32[2,8,64,128]{3,2,1,0:T(8,128)}, u32[]{:S(2)}, u32[]{:S(2)}) collective-permute-start(f32[2,8,64,128]{3,2,1,0:T(8,128)S(1)} %collective-permute-done.7.refs_4_), channel_id=1, source_target_pairs={{0,1},{1,0},{2,3},{3,2},{4,5},{5,4},{6,7},{7,6},{8,9},{9,8},{10,11... | collective-permute-start | bytes 1572872 | tf_op jit(solution)/shard_map/ppermute | solution.py:38
  91.0 0.8 copy-start.12
  91.0 1.0 copy-start.13
  91.0 1.2 copy-start.15
  92.2 0.8 copy-start.14
  131.3 16.6 %all-to-all-start.1 = ((f32[8,2,128]{2,1,0:T(2,128)}), f32[8,2,128]{2,1,0:T(2,128)S(1)}, u32[]{:S(2)}, u32[]{:S(2)}) async-start(f32[8,2,128]{2,1,0:T(2,128)} %broadcast_in_dim.3), calls=%async_computation.1 | async-start | bytes 16384 | tf_op jit(solution)/shard_map/all_to_all | solution.py:220
Sparse Core Ops, SparseCore 0:
  9.4 63.7 all-gather.2
